TPU v7x, 256 devices: a whole 4x4x8 slice. The times are simulated.
256 devices in a mesh: pair: 32 (over z, x_hi, core), panel: 8 (over x_lo, y).
Axes of the slice: x: 4 (x_hi: 2, x_lo: 2; x = x_hi * 2 + x_lo), y: 4, z: 8, core: 2. Of those that a mesh axis runs over, the one named last changes fastest.
Arguments:
- psi: bfloat16 [1536, 3072], P('pair', 'panel'), may hold values from -6 to 6
- left_ops: bfloat16 [64, 12, 2, 128, 128], P('pair'), may hold values from -0.046875 to 0.046875
- a_rows: int32 [64, 12, 2], P('pair'), may hold values from 0 to 11
- right_ops: bfloat16 [64, 3072, 3072], P('pair', 'panel'), may hold values from -0.109375 to 0.109375
- left_sizes: int32 [12], replicated, may hold values from 32 to 128
- right_sizes: int32 [24], replicated, may hold values from 32 to 128
Outputs:
- sigma: float32 [1536, 3072], P('pair', 'panel')
All inputs are finite; a program needn't handle non-finite values.
Results may differ from a plain program's by a relative error of at most 0.0029.
Values may be sent and summed in bfloat16 or wider, within the bound.
No kernel may reach another device: no remote copies, remote signals or barrier semaphores. Data moves between devices by JAX's collectives and lax.ppermute only.
A program may use at most 128 MiB of HBM per device.

v0:
```python
import jax
import jax.numpy as jnp
from jax import lax
from jax.sharding import PartitionSpec as P

BLK = 128


def live_mask(sizes):
    count = sizes.shape[0]
    offsets = lax.broadcasted_iota(jnp.int32, (count, BLK), 1)
    return (offsets < sizes[:, None]).astype(jnp.float32).reshape(count * BLK)


def local(psi, left_ops, a_rows, right_ops, left_sizes, right_sizes):
    rows_dev = psi.shape[0]
    cols_dev = psi.shape[1]
    pair_count = right_ops.shape[0]
    left_live = live_mask(left_sizes)
    right_live = live_mask(right_sizes)
    left_total = left_live.shape[0]
    my_rows = lax.dynamic_slice_in_dim(left_live, lax.axis_index("pair") * rows_dev, rows_dev, 0)
    my_cols = lax.dynamic_slice_in_dim(right_live, lax.axis_index("panel") * cols_dev, cols_dev, 0)
    masked = (psi.astype(jnp.float32) * my_rows[:, None] * my_cols[None, :]).astype(jnp.bfloat16)
    wide = lax.all_gather(masked, "panel", axis=1, tiled=True)
    product = jnp.einsum(
        "lc,prc->plr",
        lax.all_gather(wide, "pair", axis=0, tiled=True),
        right_ops,
        preferred_element_type=jnp.float32,
    )
    right_part = (product * my_cols[None, None, :]).astype(jnp.bfloat16)
    block_count = left_total // BLK
    right_blocks = right_part.reshape(pair_count, block_count, BLK, cols_dev)
    prods = jnp.einsum(
        "pcsij,pcjk->pcsik", left_ops, right_blocks, preferred_element_type=jnp.float32
    )
    block_ids = lax.broadcasted_iota(jnp.int32, (1, 1, 1, block_count), 3)
    onehot = (a_rows[:, :, :, None] == block_ids).astype(jnp.float32)
    placed = jnp.einsum("pcsb,pcsik->bik", onehot, prods, precision=lax.Precision.HIGHEST)
    local_terms = placed.reshape(left_total, cols_dev)
    summed = lax.psum_scatter(local_terms, "pair", scatter_dimension=0, tiled=True)
    return summed * my_rows[:, None]


def solution(mesh):
    placed = (
        P("pair", "panel"),
        P("pair", None, None, None, None),
        P("pair", None, None),
        P("pair", "panel", None),
        P(),
        P(),
    )
    return jax.shard_map(
        local, mesh=mesh, in_specs=placed, out_specs=P("pair", "panel"), check_vma=False
    )
```

profile of v0, /device:TPU:24, one launch (start us, length us, event | category | flops | bytes accessed | tf_op | source)
XLA Modules:
  0.0 314.1 jit_solution(8261690272190512991)
XLA Ops:
  6.5 0.0 copy-start
  6.5 0.0 all-gather.2.cloned.1.call-start
  6.5 0.8 convert_bitcast_fusion.1
  7.4 0.7 convert_bitcast_fusion
  8.1 0.1 dynamic_slice.6
  8.2 0.1 dynamic_slice.7
  8.3 0.8 multiply_convert_fusion.1
  9.1 30.5 %all_gather.6 = bf16[48,3072]{1,0:T(8,128)(2,1)} all-gather(bf16[48,384]{1,0:T(8,128)(2,1)S(1)} %multiply_convert_fusion.1), channel_id=1, replica_groups=mesh['pair'=32,'panel'=8] {'panel'}, dimensions={1}, use_global_device_ids=true | all-gather | bytes 331776 | tf_op jit(solution)/shard_map/all_gather | solution.py:25
  39.7 0.0 all-gather.2.cloned.1.call-update
  39.7 0.0 reduce-scatter.2.cloned.1.call-start
  39.7 108.1 %all-gather.2.cloned.1.call-done = bf16[1536,3072]{1,0:T(8,128)(2,1)} async-done(((bf16[48,3072]{1,0:T(8,128)(2,1)}), bf16[1536,3072]{1,0:T(8,128)(2,1)}) %all-gather.2.cloned.1.call-update) | async-done | bytes 9437200 | tf_op jit(solution)/shard_map/all_gather | solution.py:28
  147.8 11.3 %multiply_convert_fusion = bf16[1536,2,384]{2,0,1:T(8,128)(2,1)S(1)} fusion(bf16[2,384,3072]{2,1,0:T(8,128)(2,1)} %param.9, bf16[1536,3072]{1,0:T(8,128)(2,1)} %all-gather.2.cloned.1.call-done, f32[384]{0:T(512)S(1)} %dynamic_slice.7), kind=kOutput, calls=%fused_computation.2 | convolution fusion | flops 7250116608 | bytes 16516608 | tf_op jit(solution)/shard_map/lc,prc->plr/dot_general | solution.py:26
  159.1 0.0 copy-done
  159.1 5.0 %convolution_bitcast_fusion = f32[2,12,2,128,384]{3,4,2,1,0:T(8,128)} fusion(bf16[2,12,128,384,1]{3,2,4,1,0:T(8,128)(2,1)S(1)} %bitcast.34, bf16[2,12,2,128,128]{4,3,2,1,0:T(8,128)(2,1)S(1)} %copy-done), kind=kOutput, calls=%fused_computation.3 | convolution fusion | flops 603979776 | bytes 13369344 | tf_op jit(solution)/shard_map/pcsij,pcjk->pcsik/dot_general | solution.py:35
  164.1 0.0 copy-start.1
  164.1 12.9 %copy.11 = f32[2,12,2,128,384]{4,1,2,3,0:T(8,128)} copy(f32[2,12,2,128,384]{3,4,2,1,0:T(8,128)} %convolution_bitcast_fusion) | data formatting | bytes 18874368 | tf_op jit(solution)/shard_map/pcsij,pcjk->pcsik/dot_general | solution.py:35
  177.0 0.0 copy-done.1
  177.0 9.4 %convolution_bitcast_fusion.1 = f32[12,128,384]{2,0,1:T(8,128)S(1)} fusion(f32[2,12,2,128,384]{4,1,2,3,0:T(8,128)} %copy.11, s32[2,12,2]{1,2,0:T(2,128)S(1)} %copy-done.1), kind=kOutput, calls=%fused_computation.4 | convolution fusion | flops 339739200 | bytes 11796672 | tf_op jit(solution)/shard_map/pcsb,pcsik->bik/dot_general | solution.py:40
  186.4 2.1 copy.7
  188.5 0.0 reduce-scatter.2.cloned.1.call-update
  188.6 117.1 %reduce-scatter.2.cloned.1.call-done = f32[48,384]{1,0:T(8,128)} async-done(((f32[1536,384]{1,0:T(8,128)}), f32[48,384]{1,0:T(8,128)}) %reduce-scatter.2.cloned.1.call-update) | async-done | bytes 73744 | tf_op jit(solution)/shard_map/reduce_scatter | solution.py:42
  305.6 1.6 broadcast_multiply_fusion
Async XLA Ops:
  6.5 152.6 %copy-start = (bf16[2,12,2,128,128]{4,3,2,1,0:T(8,128)(2,1)S(1)}, bf16[2,12,2,128,128]{4,3,2,1,0:T(8,128)(2,1)}, u32[]{:S(2)}) copy-start(bf16[2,12,2,128,128]{4,3,2,1,0:T(8,128)(2,1)} %param.7) | copy-start | bytes 4718596
  6.5 141.3 %all-gather.2.cloned.1.call-start = ((), (), s32[]{:S(2)}) async-start(), calls=%async_computation.1 | async-start | bytes 9732096 | tf_op jit(solution)/shard_map/all_gather | solution.py:28
  39.7 266.0 %reduce-scatter.2.cloned.1.call-start = ((), (), s32[]{:S(2)}) async-start(), calls=%async_computation.2 | async-start | bytes 2433024 | tf_op jit(solution)/shard_map/reduce_scatter | solution.py:42
  164.1 12.9 %copy-start.1 = (s32[2,12,2]{1,2,0:T(2,128)S(1)}, s32[2,12,2]{1,2,0:T(2,128)}, u32[]{:S(2)}) copy-start(s32[2,12,2]{1,2,0:T(2,128)} %param.8) | copy-start | bytes 580
Sparse Core Ops, SparseCore 0:
  39.8 107.9 all-gather.1
  188.7 116.9 reduce-scatter.1
where the time goes:
time: 315 us; the launch traced here: 314 us
  waiting for transfers between devices  225 us (71%)
  blocking collectives  30.5 us (10%)
  matrix products  25.6 us (8%)
  local copies, waits for them, and re-layouts  15.2 us (5%)
  between operations  13.4 us (4%)
  other arithmetic  4.01 us (1%)
    reduce_scatter x1, waiting for transfers between devices, local(): lax.psum_scatter(local_terms, 'pair', scatter_dimension=0, tiled=True)  117 us
    all_gather x1, waiting for transfers between devices, local(): lax.all_gather(wide, 'pair', axis=0, tiled=True)  108 us
    all_gather x1, blocking collectives, local(): wide = lax.all_gather(masked, 'panel', axis=1, tiled=True)  30.5 us
    dot_general x1, local copies, waits for them, and re-layouts, local(): jnp.einsum('pcsij,pcjk->pcsik', left_ops, right_blocks, preferred_element...  12.9 us
    dot_general x1, matrix products, local(): jnp.einsum('lc,prc->plr', lax.all_gather(wide, 'pair', axis=0, tiled=True...  11.3 us
    dot_general x1, matrix products, local(): jnp.einsum('pcsb,pcsik->bik', onehot, prods, precision=lax.Precision.HIGH...  9.37 us
  transfers between devices with their start and end apart: 2, of which 2 were waited for; matrix products, arithmetic and copies ran while one was open for 0% of the time, Pallas kernels for 0%

commit v1 on v0

v1 whole, which is shorter than its diff:
```python
import functools

import jax
import jax.numpy as jnp
from jax import lax
from jax.experimental import pallas as pl
from jax.experimental.pallas import tpu as pltpu
from jax.sharding import PartitionSpec as P

BLK = 128
NZ, NXH, NC, NXL, NY = 8, 2, 2, 2, 4
NX = NXH * NXL
RING = 4
AXES = ("pair", "panel")
VMEM_LIMIT = 26 * 1024 * 1024
SMEM_SPEC = pl.BlockSpec(memory_space=pltpu.SMEM)
VMEM_SPEC = pl.BlockSpec(memory_space=pltpu.VMEM)
ANY_SPEC = pl.BlockSpec(memory_space=pl.ANY)


def flat(z, x, y, core):
    pair = (z * NXH + x // NXL) * NC + core
    return pair * (NXL * NY) + (x % NXL) * NY + y


def everywhere():
    return [
        (z, x, y, core) for z in range(NZ) for x in range(NX) for y in range(NY) for core in range(NC)
    ]


def core_swap(value):
    return lax.ppermute(
        value, AXES, [(flat(z, x, y, 1 - c), flat(z, x, y, c)) for z, x, y, c in everywhere()]
    )


def last_shift(value, step):
    perm = []
    for z, x, y, c in everywhere():
        source = flat(z, (x + step) % NX, y, c) if c == 0 else flat(z, x, (y + step) % NY, c)
        perm.append((source, flat(z, x, y, c)))
    return lax.ppermute(value, AXES, perm)


def exchange(copies, groups):
    return lax.all_to_all(
        copies, AXES, split_axis=0, concat_axis=0, axis_index_groups=groups, tiled=True
    )


def z_groups():
    return [
        [flat(z, x, y, c) for z in range(NZ)] for x in range(NX) for y in range(NY) for c in range(NC)
    ]


def middle_groups():
    along_y = [[flat(z, x, y, 0) for y in range(NY)] for z in range(NZ) for x in range(NX)]
    along_x = [[flat(z, x, y, 1) for x in range(NX)] for z in range(NZ) for y in range(NY)]
    return along_y + along_x


def mask_kernel(where_ref, left_ref, right_ref, psi_ref, out_ref):
    rows, cols = psi_ref.shape
    base = where_ref[0] * rows
    first = base // BLK
    second = jnp.minimum(first + 1, left_ref.shape[0] - 1)
    index = base + lax.broadcasted_iota(jnp.int32, (rows, BLK), 0)
    limit = jnp.where(
        index < (first + 1) * BLK, first * BLK + left_ref[first], (first + 1) * BLK + left_ref[second]
    )
    row_live = index < limit
    lane = lax.broadcasted_iota(jnp.int32, (rows, BLK), 1)
    for block in range(cols // BLK):
        live = row_live & (lane < right_ref[where_ref[1] * (cols // BLK) + block])
        span = slice(block * BLK, (block + 1) * BLK)
        value = psi_ref[:, span].astype(jnp.float32)
        value = jnp.where(live, value, 0.0).astype(out_ref.dtype)
        for copy in range(out_ref.shape[0]):
            out_ref[copy, :, span] = value


def mask_psi(where, left_sizes, right_sizes, psi):
    return pl.pallas_call(
        mask_kernel,
        out_shape=jax.ShapeDtypeStruct((NZ,) + psi.shape, psi.dtype),
        in_specs=[SMEM_SPEC, SMEM_SPEC, SMEM_SPEC, VMEM_SPEC],
        out_specs=VMEM_SPEC,
        name="mask_psi",
    )(where, left_sizes, right_sizes, psi)


def product_kernel(steps, first, last, where_ref, *refs):
    refs = list(refs)
    rows_ref, right_ref = (refs.pop(0), refs.pop(0)) if last else (None, None)
    acc_in = None if first else refs.pop(0)
    arrays = [refs.pop(0) for _ in steps]
    r_own, r_other = refs.pop(0), refs.pop(0)
    l_own, l_other = (refs.pop(0), refs.pop(0)) if last else (None, None)
    if last:
        keep_ref, send_ref, acc, lbuf, part, total = (refs.pop(0) for _ in range(6))
    else:
        acc = refs.pop(0)
    ubuf, rbuf, sem_u, sem_r, sem_a, sem_l = refs
    z, xh, core, xl, y = (where_ref[i] for i in range(2, 7))
    x = xh * NXL + xl
    pairs, cols, depth = r_own.shape
    group = ubuf.shape[2]

    units = []
    for array, step, start in zip(arrays, *zip(*steps)):
        for spot in range(array.shape[0]):
            middle = start + spot
            far_x, far_y = lax.rem(x + step, NX), lax.rem(y + step, NY)
            unit_x = jnp.where(core == 0, far_x, middle)
            unit_y = jnp.where(core == 0, middle, far_y)
            units.append((array, spot, unit_x, unit_y))

    def unit_copy(index):
        array, spot = units[index][:2]
        return pltpu.make_async_copy(array.at[spot], ubuf.at[index], sem_u.at[index])

    def right_copies(index):
        _, _, unit_x, unit_y = units[index]
        column = pl.multiple_of((lax.rem(unit_x, NXL) * NY + unit_y) * cols, BLK)
        slot = index % 2
        return [
            pltpu.make_async_copy(
                source.at[:, :, pl.ds(column, cols)],
                rbuf.at[slot, pl.ds(side * pairs, pairs)],
                sem_r.at[slot, side],
            )
            for side, source in enumerate((r_own, r_other))
        ]

    for copy in right_copies(0):
        copy.start()
    for index in range(len(units)):
        unit_copy(index).start()
    waits = []
    if not first:
        waits.append(pltpu.make_async_copy(acc_in, acc, sem_a))
    if last:
        waits.append(pltpu.make_async_copy(l_own, lbuf.at[pl.ds(0, pairs)], sem_l.at[0]))
        waits.append(pltpu.make_async_copy(l_other, lbuf.at[pl.ds(pairs, pairs)], sem_l.at[1]))
    for copy in waits:
        copy.start()
    if first:
        acc[...] = jnp.zeros_like(acc)
    if last:
        total[...] = jnp.zeros_like(total)
        part[...] = jnp.zeros_like(part)
    if not first:
        waits.pop(0).wait()

    for index in range(len(units)):
        if index + 1 < len(units):
            for copy in right_copies(index + 1):
                copy.start()
        unit_copy(index).wait()
        for copy in right_copies(index):
            copy.wait()
        half = units[index][2] // NXL
        left = ubuf[index].reshape(NZ * group, cols)
        for pair in range(2 * pairs):
            acc[half, pair] += lax.dot_general(
                left,
                rbuf[index % 2, pair],
                (((1,), (1,)), ((), ())),
                preferred_element_type=jnp.float32,
            )

    if not last:
        return
    blocks, ka = lbuf.shape[1:3]
    lane = lax.broadcasted_iota(jnp.int32, (1, BLK), 1)
    start = (xl * NY + y) * (cols // BLK)
    live = jnp.concatenate(
        [(lane < right_ref[start + i]).astype(jnp.float32) for i in range(cols // BLK)], axis=1
    )
    for copy in waits:
        copy.wait()

    @pl.loop(0, 2 * pairs)
    def _(pair):
        for half in range(NXH):
            for dz in range(NZ):
                rounded = (acc[half, pair, dz * group : (dz + 1) * group] * live).astype(part.dtype)
                at = ((dz * NXH + half) * NC + core) * group
                part[pl.ds(pl.multiple_of(at, 16), group), :] = rounded
        for block in range(blocks):
            result = jnp.dot(
                lbuf[pair, block].reshape(ka * BLK, BLK),
                part[block * BLK : (block + 1) * BLK],
                preferred_element_type=jnp.float32,
            )
            for s in range(ka):
                row = rows_ref[(pair * blocks + block) * ka + s]
                total[pl.ds(pl.multiple_of(row * BLK, BLK), BLK), :] += result[s * BLK : (s + 1) * BLK]

    for q in range(NZ * NXH):
        mine = pl.multiple_of((q * NC + core) * group, 16)
        theirs = pl.multiple_of((q * NC + 1 - core) * group, 16)
        keep_ref[q] = total[pl.ds(mine, group), :]
        send_ref[q] = total[pl.ds(theirs, group), :].astype(send_ref.dtype)


def product(where, acc, pieces, right, left=None, rows=None, right_sizes=None):
    arrays = [array for array, _, _ in pieces]
    steps = tuple((step, start) for _, step, start in pieces)
    first, last = acc is None, left is not None
    group, cols = arrays[0].shape[2:]
    pairs = right[0].shape[0]
    units = sum(array.shape[0] for array in arrays)
    acc_shape = (NXH, 2 * pairs, NZ * group, cols)
    operands, specs = [where], [SMEM_SPEC]
    if last:
        operands += [rows, right_sizes]
        specs += [SMEM_SPEC, SMEM_SPEC]
    rest = ([] if first else [acc]) + arrays + list(right) + (list(left) if last else [])
    operands += rest
    specs += [ANY_SPEC] * len(rest)
    scratch = []
    if last:
        blocks = left[0].shape[1]
        out_shape = (
            jax.ShapeDtypeStruct((NZ * NXH, group, cols), jnp.float32),
            jax.ShapeDtypeStruct((NZ * NXH, group, cols), jnp.bfloat16),
        )
        out_specs = (VMEM_SPEC, VMEM_SPEC)
        scratch = [
            pltpu.VMEM(acc_shape, jnp.float32),
            pltpu.VMEM((2 * pairs,) + left[0].shape[1:], jnp.bfloat16),
            pltpu.VMEM((blocks * BLK, cols), jnp.bfloat16),
            pltpu.VMEM((blocks * BLK, cols), jnp.float32),
        ]
    else:
        out_shape = jax.ShapeDtypeStruct(acc_shape, jnp.float32)
        out_specs = VMEM_SPEC
    scratch += [
        pltpu.VMEM((units, NZ, group, cols), jnp.bfloat16),
        pltpu.VMEM((2, 2 * pairs, cols, cols), jnp.bfloat16),
        pltpu.SemaphoreType.DMA((units,)),
        pltpu.SemaphoreType.DMA((2, 2)),
        pltpu.SemaphoreType.DMA,
        pltpu.SemaphoreType.DMA((2,)),
    ]
    return pl.pallas_call(
        functools.partial(product_kernel, steps, first, last),
        out_shape=out_shape,
        in_specs=specs,
        out_specs=out_specs,
        scratch_shapes=scratch,
        compiler_params=pltpu.CompilerParams(vmem_limit_bytes=VMEM_LIMIT),
        cost_estimate=pl.CostEstimate(
            flops=2 * units * 2 * pairs * NZ * group * cols * cols,
            bytes_accessed=units * 2 * pairs * cols * cols * 2 + 9_000_000,
            transcendentals=0,
        ),
        name=f"product_{units}",
    )(*operands)


def local(psi, left_ops, a_rows, right_ops, left_sizes, right_sizes):
    rows_dev = psi.shape[0]
    pair, panel = lax.axis_index("pair"), lax.axis_index("panel")
    where = jnp.stack(
        [
            pair,
            panel,
            lax.shift_right_logical(pair, 2),
            lax.shift_right_logical(pair, 1) & 1,
            pair & 1,
            lax.shift_right_logical(panel, 2),
            panel & 3,
        ]
    ).astype(jnp.int32)
    copies = mask_psi(where, left_sizes, right_sizes, psi)
    right = (right_ops, core_swap(right_ops))
    left = (left_ops, core_swap(left_ops))
    rows = jnp.concatenate([a_rows.reshape(-1), core_swap(a_rows.reshape(-1))])

    along_z = exchange(copies, z_groups())
    wide = exchange(jnp.broadcast_to(along_z[None], (RING,) + along_z.shape), middle_groups())
    plus = last_shift(wide, 1)
    minus = last_shift(wide, -1)
    acc = product(where, None, [(wide, 0, 0)], right)
    half = RING // 2
    plus, minus, acc = lax.optimization_barrier((plus, minus, acc))
    far_low = last_shift(plus[:half], 1)
    far_high = last_shift(minus[half:], -1)

    acc = product(where, acc, [(plus, 1, 0), (minus, 3, 0)], right)
    keep, send = product(
        where, acc, [(far_low, 2, 0), (far_high, 2, half)], right, left, rows, right_sizes
    )
    mine = (keep + core_swap(send).astype(jnp.float32)).astype(jnp.bfloat16)
    groups = [
        [flat(z, xh * NXL + xl, y, c) for z in range(NZ) for xh in range(NXH)]
        for c in range(NC)
        for xl in range(NXL)
        for y in range(NY)
    ]
    parts = exchange(mine, groups)
    summed = parts.astype(jnp.float32).sum(axis=0)
    index = pair * rows_dev + jnp.arange(rows_dev, dtype=jnp.int32)
    blocks = jnp.arange(left_sizes.shape[0], dtype=jnp.int32)
    limit = jnp.sum(jnp.where(index[:, None] // BLK == blocks, left_sizes + blocks * BLK, 0), axis=1)
    return jnp.where((index < limit)[:, None], summed, 0.0)


def solution(mesh):
    placed = (
        P("pair", "panel"),
        P("pair", None, None, None, None),
        P("pair", None, None),
        P("pair", "panel", None),
        P(),
        P(),
    )
    return jax.shard_map(
        local, mesh=mesh, in_specs=placed, out_specs=P("pair", "panel"), check_vma=False
    )
```

time: 315 us -> 120 us (0.38)
  waiting for transfers between devices: 225 us -> 31.1 us
  Pallas kernels: 0 us -> 28 us
  matrix products: 25.6 us -> 0 us
  between operations: 13.4 us -> 0.16 us
  starting transfers between devices: 0.04 us -> 9.09 us
  blocking collectives: 30.5 us -> 35.7 us
  local copies, waits for them, and re-layouts: 15.2 us -> 11.9 us
    reduce_scatter x1 -> x0, waiting for transfers between devices: 117 us -> none  [local(): lax.psum_scatter(local_terms, 'pair', scatter_dimension=0, tiled=True)]
    all_gather x1 -> x0, waiting for transfers between devices: 108 us -> none  [local(): lax.all_gather(wide, 'pair', axis=0, tiled=True)]
    all_to_all x0 -> x2, blocking collectives: none -> 35.7 us  [exchange(): lax.all_to_all(copies, AXES, split_axis=0, concat_axis=0, axis_index_grou...]
    all_gather x1 -> x0, blocking collectives: 30.5 us -> none  [local(): wide = lax.all_gather(masked, 'panel', axis=1, tiled=True)]
    pallas_call x0 -> x4, Pallas kernels: none -> 28 us  [the longest x3 26.5 us: product(): pl.pallas_call(functools.partial(product_kernel, steps, first, last), out...]
    dot_general x3 -> x0, matrix products: 25.6 us -> none  [the longest x1 11.3 us: local(): jnp.einsum('lc,prc->plr', lax.all_gather(wide, 'pair', axis=0, tiled=True...]
    all_to_all x0 -> x1, waiting for transfers between devices: none -> 21.2 us  [exchange(): lax.all_to_all(copies, AXES, split_axis=0, concat_axis=0, axis_index_grou...]
    dot_general x2 -> x0, local copies, waits for them, and re-layouts: 15.1 us -> none  [the longest x1 12.9 us: local(): jnp.einsum('pcsij,pcjk->pcsik', left_ops, right_blocks, preferred_element...]
  transfers between devices with their start and end apart: 2 -> 9, of which waited for: 2 -> 5; matrix products, arithmetic and copies ran while one was open for 0% -> 2% of each run, Pallas kernels for 0% -> 15%
where the time goes in v1:
time: 120 us; the launch traced here: 118 us
  blocking collectives  35.7 us (30%)
  waiting for transfers between devices  31.1 us (26%)
  Pallas kernels  28 us (23%)
  local copies, waits for them, and re-layouts  11.9 us (10%)
  starting transfers between devices  9.09 us (8%)
  other arithmetic  1.96 us (2%)
    all_to_all x2, blocking collectives, exchange(): lax.all_to_all(copies, AXES, split_axis=0, concat_axis=0, axis_index_grou...  35.7 us
    pallas_call x3, Pallas kernels, product(): pl.pallas_call(functools.partial(product_kernel, steps, first, last), out...  26.5 us
    all_to_all x1, waiting for transfers between devices, exchange(): lax.all_to_all(copies, AXES, split_axis=0, concat_axis=0, axis_index_grou...  21.2 us
    unnamed x21, local copies, waits for them, and re-layouts  9.3 us
    ppermute x4, waiting for transfers between devices, last_shift(): return lax.ppermute(value, AXES, perm)  6.95 us
    ppermute x4, starting transfers between devices, last_shift(): return lax.ppermute(value, AXES, perm)  4.79 us
    all_to_all x1, starting transfers between devices, exchange(): lax.all_to_all(copies, AXES, split_axis=0, concat_axis=0, axis_index_grou...  3.71 us
    ppermute x4, waiting for transfers between devices, core_swap(): lax.ppermute(value, AXES, [(flat(z, x, y, 1 - c), flat(z, x, y, c)) for z...  2.92 us
  transfers between devices with their start and end apart: 9, of which 5 were waited for; matrix products, arithmetic and copies ran while one was open for 2% of the time, Pallas kernels for 15%

profile of v1, /device:TPU:24, one launch (start us, length us, event | category | flops | bytes accessed | tf_op | source)
XLA Modules:
  0.0 118.0 jit_solution(2729500376512086778)
XLA Ops:
  0.0 0.0 collective-permute-start.3
  0.0 0.6 stack.31.where_ref
  0.6 1.6 %mask_psi.1 = bf16[8,48,384]{2,1,0:T(8,128)(2,1)} custom-call(s32[7]{0:T(128)} %stack.31.where_ref, s32[12]{0:T(128)} %left_ref.1, s32[24]{0:T(128)} %refs_1_.3, bf16[48,384]{1,0:T(8,128)(2,1)} %psi_ref.1), custom_call_target="tpu_custom_call" | custom-call | tf_op jit(solution)/shard_map/mask_psi/pallas_call | solution.py:85
  2.2 21.7 %all_to_all.15 = bf16[8,48,384]{2,1,0:T(8,128)(2,1)S(1)} all-to-all(bf16[8,48,384]{2,1,0:T(8,128)(2,1)} %mask_psi.1), channel_id=1, replica_groups={{0,32,64,96,128,160,192,224},{8,40,72,104,136,168,200,232},{1,33,65,97,..., dimensions={0} | all-to-all | bytes 589824 | tf_op jit(solution)/shard_map/all_to_all | solution.py:47
  23.9 0.1 broadcast_in_dim.32
  24.0 0.0 copy-start.4
  24.0 14.0 %all_to_all.16.refs_0_ = bf16[4,8,48,384]{3,2,1,0:T(8,128)(2,1)S(1)} all-to-all(bf16[4,8,48,384]{3,2,1,0:T(8,128)(2,1)S(1)} %broadcast_in_dim.32), channel_id=1, replica_groups={{0,1,2,3},{4,5,6,7},{16,17,18,19},{20,21,22,23},{32,33,34,35},{36,37,38..., dimensions={0} | all-to-all | bytes 2359296 | tf_op jit(solution)/shard_map/all_to_all | solution.py:47
  38.0 2.8 %collective-permute-start.1 = (bf16[4,8,48,384]{3,2,1,0:T(8,128)(2,1)S(1)}, bf16[4,8,48,384]{3,2,1,0:T(8,128)(2,1)S(1)}, u32[]{:S(2)}, u32[]{:S(2)}) collective-permute-start(bf16[4,8,48,384]{3,2,1,0:T(8,128)(2,1)S(1)} %all_to_all.16.refs_0_), channel_id=1, source_target_pairs={{4,0},{9,8},{5,1},{10,9},{6,2},{11,10},{7,3},{8,11},{16,4},{13,12}... | collective-permute-start | bytes 3538952 | tf_op jit(solution)/shard_map/ppermute | solution.py:43
  40.8 0.0 collective-permute-start.2
  40.8 0.0 collective-permute-start.6
  40.8 0.0 collective-permute-done.3.refs_2_.refs_4_.refs_6_
  40.8 0.0 copy-done.4
  40.8 0.0 copy-start
  40.8 2.3 %copy-done = bf16[2,384,3072]{2,1,0:T(8,128)(2,1)S(1)} copy-done((bf16[2,384,3072]{2,1,0:T(8,128)(2,1)S(1)}, bf16[2,384,3072]{2,1,0:T(8,128)(2,1)}, u32[]{:S(2)}) %copy-start) | copy-done | bytes 4718616
  43.2 5.9 %product_4.2.refs_0_ = f32[2,4,384,384]{3,2,1,0:T(8,128)S(1)} custom-call(s32[7]{0:T(128)S(1)} %copy-done.4, bf16[4,8,48,384]{3,2,1,0:T(8,128)(2,1)S(1)} %all_to_all.16.refs_0_, bf16[2,384,3072]{2,1,0:T(8,128)(2,1)S(1)} %copy-done, bf16[2,384,3072]{2,1,0:T(8,128)(2,1)} %collective-permute-done.3.refs_2_.refs_4_.refs_6_), custom_call_target="tpu_custom_call" | custom-call | flops 1811939328 | bytes 13718592 | tf_op jit(solution)/shard_map/product_4/pallas_call | solution.py:249
  49.1 0.0 copy-start.2
  49.1 2.2 %copy-done.2 = f32[2,4,384,384]{3,2,1,0:T(8,128)} copy-done((f32[2,4,384,384]{3,2,1,0:T(8,128)}, f32[2,4,384,384]{3,2,1,0:T(8,128)S(1)}, u32[]{:S(2)}) %copy-start.2) | copy-done | bytes 4718616
  51.3 0.0 copy-start.6
  51.3 3.3 %collective-permute-done.1.refs_1_ = bf16[4,8,48,384]{3,2,1,0:T(8,128)(2,1)S(1)} collective-permute-done((bf16[4,8,48,384]{3,2,1,0:T(8,128)(2,1)S(1)}, bf16[4,8,48,384]{3,2,1,0:T(8,128)(2,1)S(1)}, u32[]{:S(2)}, u32[]{:S(2)}) %collective-permute-start.1) | collective-permute-done | bytes 1179680 | tf_op jit(solution)/shard_map/ppermute | solution.py:43
  54.5 3.7 %collective-permute-done.2.refs_2_ = bf16[4,8,48,384]{3,2,1,0:T(8,128)(2,1)S(1)} collective-permute-done((bf16[4,8,48,384]{3,2,1,0:T(8,128)(2,1)S(1)}, bf16[4,8,48,384]{3,2,1,0:T(8,128)(2,1)S(1)}, u32[]{:S(2)}, u32[]{:S(2)}) %collective-permute-start.2) | collective-permute-done | bytes 1179680 | tf_op jit(solution)/shard_map/ppermute | solution.py:43
  58.2 0.9 slice.6
  59.1 0.0 collective-permute-start.4
  59.1 0.0 slice-start
  59.1 0.9 slice.7
  60.0 2.0 %collective-permute-start.5 = (bf16[2,8,48,384]{3,2,1,0:T(8,128)(2,1)}, bf16[2,8,48,384]{3,2,1,0:T(8,128)(2,1)}, u32[]{:S(2)}, u32[]{:S(2)}) collective-permute-start(bf16[2,8,48,384]{3,2,1,0:T(8,128)(2,1)} %slice.7), channel_id=1, source_target_pairs={{20,0},{11,8},{21,1},{8,9},{22,2},{9,10},{23,3},{10,11},{0,4},{15,... | collective-permute-start | bytes 1769480 | tf_op jit(solution)/shard_map/ppermute | solution.py:43
  62.0 0.0 copy-done.6
  62.0 0.1 copy.9
  62.1 0.1 reshape.47
  62.2 0.3 collective-permute-start
  62.5 1.1 collective-permute-done
  63.6 0.1 pad_add_fusion.refs_0_
  63.7 0.0 copy-start.1
  63.7 2.3 %copy-done.1 = bf16[2,384,3072]{2,1,0:T(8,128)(2,1)S(1)} copy-done((bf16[2,384,3072]{2,1,0:T(8,128)(2,1)S(1)}, bf16[2,384,3072]{2,1,0:T(8,128)(2,1)}, u32[]{:S(2)}) %copy-start.1) | copy-done | bytes 4718616
  66.0 0.0 copy-start.3
  66.0 2.3 %copy-done.3 = f32[2,4,384,384]{3,2,1,0:T(8,128)S(1)} copy-done((f32[2,4,384,384]{3,2,1,0:T(8,128)S(1)}, f32[2,4,384,384]{3,2,1,0:T(8,128)}, u32[]{:S(2)}) %copy-start.3) | copy-done | bytes 4718616
  68.4 0.0 slice-start.1
  68.4 0.0 copy-start.5
  68.4 10.5 %product_8.1.refs_2_ = f32[2,4,384,384]{3,2,1,0:T(8,128)S(1)} custom-call(s32[7]{0:T(128)S(1)} %copy-done.4, f32[2,4,384,384]{3,2,1,0:T(8,128)S(1)} %copy-done.3, bf16[4,8,48,384]{3,2,1,0:T(8,128)(2,1)S(1)} %collective-permute-done.1.refs_1_, bf16[4,8,48,384]{3,2,1,0:T(8,128)(2,1)S(1)} %collective-permute-done.2.refs_2_, ...), custom_call_target="tpu_custom_call" | custom-call | flops 3623878656 | bytes 18437184 | tf_op jit(solution)/shard_map/product_8/pallas_call | solution.py:249
  78.8 0.0 collective-permute-done.6.refs_8_
  78.8 0.0 collective-permute-done.4.refs_3_
  78.9 0.0 collective-permute-done.5.refs_4_
  78.9 0.0 slice-done
  78.9 0.0 slice-done.1
  78.9 0.0 copy-done.5
  78.9 10.1 %product_4.3 = (f32[16,48,384]{2,1,0:T(8,128)S(1)}, bf16[16,48,384]{2,1,0:T(8,128)(2,1)S(1)}) custom-call(s32[7]{0:T(128)S(1)} %copy-done.4, s32[96]{0:T(128)S(1)} %pad_add_fusion.refs_0_, s32[24]{0:T(128)S(1)} %copy-done.5, f32[2,4,384,384]{3,2,1,0:T(8,128)S(1)} %product_8.1.refs_2_, bf16[2,8,48,384]{3,2,1,0:T(8,128)(2,1)S(1)} %collective-permute-done.4.refs_3_, ...), custom_call_target="tpu_custom_call" | custom-call | flops 1811939328 | bytes 13718592 | tf_op jit(solution)/shard_map/product_4/pallas_call | solution.py:249
  89.0 0.3 collective-permute-start.7
  89.3 1.8 %collective-permute-done.7 = bf16[16,48,384]{2,1,0:T(8,128)(2,1)S(1)} collective-permute-done((bf16[16,48,384]{2,1,0:T(8,128)(2,1)S(1)}, bf16[16,48,384]{2,1,0:T(8,128)(2,1)S(1)}, u32[]{:S(2)}, u32[]{:S(2)}) %collective-permute-start.7) | collective-permute-done | bytes 589856 | tf_op jit(solution)/shard_map/ppermute | solution.py:33
  91.1 1.0 add_convert_fusion
  92.1 0.0 copy-start.7
  92.1 3.7 %all-to-all-start.2 = ((bf16[16,48,384]{2,1,0:T(8,128)(2,1)}), bf16[16,48,384]{2,1,0:T(8,128)(2,1)S(1)}, u32[]{:S(2)}, u32[]{:S(2)}) async-start(bf16[16,48,384]{2,1,0:T(8,128)(2,1)} %add_convert_fusion), calls=%async_computation.2 | async-start | bytes 1179648 | tf_op jit(solution)/shard_map/all_to_all | solution.py:47
  95.8 0.0 copy-done.7
  95.8 0.1 select_reduce_fusion
  95.9 21.2 %all-to-all-done.2 = bf16[16,48,384]{2,1,0:T(8,128)(2,1)S(1)} async-done(((bf16[16,48,384]{2,1,0:T(8,128)(2,1)}), bf16[16,48,384]{2,1,0:T(8,128)(2,1)S(1)}, u32[]{:S(2)}, u32[]{:S(2)}) %all-to-all-start.2) | async-done | bytes 589856 | tf_op jit(solution)/shard_map/all_to_all | solution.py:47
  117.2 0.1 convert_reduce_fusion
  117.3 0.7 broadcast_select_fusion
  (4 shorter events, 0.0 us)
Async XLA Ops:
  0.0 40.8 %collective-permute-start.3 = (bf16[2,384,3072]{2,1,0:T(8,128)(2,1)}, bf16[2,384,3072]{2,1,0:T(8,128)(2,1)}, u32[]{:S(2)}, u32[]{:S(2)}) collective-permute-start(bf16[2,384,3072]{2,1,0:T(8,128)(2,1)} %refs_5_.1), channel_id=1, source_target_pairs={{8,0},{0,8},{9,1},{1,9},{10,2},{2,10},{11,3},{3,11},{12,4},{4,12},... | collective-permute-start | bytes 14155784 | tf_op jit(solution)/shard_map/ppermute | solution.py:33
  24.0 16.8 %copy-start.4 = (s32[7]{0:T(128)S(1)}, s32[7]{0:T(128)}, u32[]{:S(2)}) copy-start(s32[7]{0:T(128)} %stack.31.where_ref) | copy-start | bytes 88
  38.0 16.5 %collective-permute-start.1 = (bf16[4,8,48,384]{3,2,1,0:T(8,128)(2,1)S(1)}, bf16[4,8,48,384]{3,2,1,0:T(8,128)(2,1)S(1)}, u32[]{:S(2)}, u32[]{:S(2)}) collective-permute-start(bf16[4,8,48,384]{3,2,1,0:T(8,128)(2,1)S(1)} %all_to_all.16.refs_0_), channel_id=1, source_target_pairs={{4,0},{9,8},{5,1},{10,9},{6,2},{11,10},{7,3},{8,11},{16,4},{13,12}... | collective-permute-start | bytes 3538952 | tf_op jit(solution)/shard_map/ppermute | solution.py:43
  40.8 17.4 %collective-permute-start.2 = (bf16[4,8,48,384]{3,2,1,0:T(8,128)(2,1)S(1)}, bf16[4,8,48,384]{3,2,1,0:T(8,128)(2,1)S(1)}, u32[]{:S(2)}, u32[]{:S(2)}) collective-permute-start(bf16[4,8,48,384]{3,2,1,0:T(8,128)(2,1)S(1)} %all_to_all.16.refs_0_), channel_id=1, source_target_pairs={{20,0},{11,8},{21,1},{8,9},{22,2},{9,10},{23,3},{10,11},{0,4},{15,... | collective-permute-start | bytes 3538952 | tf_op jit(solution)/shard_map/ppermute | solution.py:43
  40.8 38.0 %collective-permute-start.6 = (bf16[2,12,2,128,128]{4,3,2,1,0:T(8,128)(2,1)}, bf16[2,12,2,128,128]{4,3,2,1,0:T(8,128)(2,1)}, u32[]{:S(2)}, u32[]{:S(2)}) collective-permute-start(bf16[2,12,2,128,128]{4,3,2,1,0:T(8,128)(2,1)} %refs_7_.1), channel_id=1, source_target_pairs={{8,0},{0,8},{9,1},{1,9},{10,2},{2,10},{11,3},{3,11},{12,4},{4,12},... | collective-permute-start | bytes 4718600 | tf_op jit(solution)/shard_map/ppermute | solution.py:33
  40.8 2.3 %copy-start = (bf16[2,384,3072]{2,1,0:T(8,128)(2,1)S(1)}, bf16[2,384,3072]{2,1,0:T(8,128)(2,1)}, u32[]{:S(2)}) copy-start(bf16[2,384,3072]{2,1,0:T(8,128)(2,1)} %refs_5_.1) | copy-start | bytes 14155780
  49.1 2.2 %copy-start.2 = (f32[2,4,384,384]{3,2,1,0:T(8,128)}, f32[2,4,384,384]{3,2,1,0:T(8,128)S(1)}, u32[]{:S(2)}) copy-start(f32[2,4,384,384]{3,2,1,0:T(8,128)S(1)} %product_4.2.refs_0_) | copy-start | bytes 14155780
  51.3 10.8 %copy-start.6 = (s32[2,12,2]{1,2,0:T(2,128)S(1)}, s32[2,12,2]{1,2,0:T(2,128)}, u32[]{:S(2)}) copy-start(s32[2,12,2]{1,2,0:T(2,128)} %param.8) | copy-start | bytes 580
  59.1 19.8 %collective-permute-start.4 = (bf16[2,8,48,384]{3,2,1,0:T(8,128)(2,1)}, bf16[2,8,48,384]{3,2,1,0:T(8,128)(2,1)S(1)}, u32[]{:S(2)}, u32[]{:S(2)}) collective-permute-start(bf16[2,8,48,384]{3,2,1,0:T(8,128)(2,1)} %slice.6), channel_id=1, source_target_pairs={{4,0},{9,8},{5,1},{10,9},{6,2},{11,10},{7,3},{8,11},{16,4},{13,12}... | collective-permute-start | bytes 1769480 | tf_op jit(solution)/shard_map/ppermute | solution.py:43
  59.1 19.8 %slice-start = ((s8[4718592]{0:T(1024)(128)(4,1)}), s8[524288]{0:T(1024)(128)(4,1)S(1)}, s32[]{:S(2)}) async-start(s8[4718592]{0:T(1024)(128)(4,1)} %bitcast.7), calls=%async_computation.3 | async-start | bytes 1048576
  60.0 18.9 %collective-permute-start.5 = (bf16[2,8,48,384]{3,2,1,0:T(8,128)(2,1)}, bf16[2,8,48,384]{3,2,1,0:T(8,128)(2,1)}, u32[]{:S(2)}, u32[]{:S(2)}) collective-permute-start(bf16[2,8,48,384]{3,2,1,0:T(8,128)(2,1)} %slice.7), channel_id=1, source_target_pairs={{20,0},{11,8},{21,1},{8,9},{22,2},{9,10},{23,3},{10,11},{0,4},{15,... | collective-permute-start | bytes 1769480 | tf_op jit(solution)/shard_map/ppermute | solution.py:43
  62.2 1.4 %collective-permute-start = (s32[48]{0:T(128)S(1)}, s32[48]{0:T(128)S(1)}, u32[]{:S(2)}, u32[]{:S(2)}) collective-permute-start(s32[48]{0:T(128)S(1)} %reshape.47), channel_id=1, source_target_pairs={{8,0},{0,8},{9,1},{1,9},{10,2},{2,10},{11,3},{3,11},{12,4},{4,12},... | collective-permute-start | bytes 584 | tf_op jit(solution)/shard_map/ppermute | solution.py:33
  63.7 2.3 %copy-start.1 = (bf16[2,384,3072]{2,1,0:T(8,128)(2,1)S(1)}, bf16[2,384,3072]{2,1,0:T(8,128)(2,1)}, u32[]{:S(2)}) copy-start(bf16[2,384,3072]{2,1,0:T(8,128)(2,1)} %refs_5_.1) | copy-start | bytes 14155780
  66.0 2.3 %copy-start.3 = (f32[2,4,384,384]{3,2,1,0:T(8,128)S(1)}, f32[2,4,384,384]{3,2,1,0:T(8,128)}, u32[]{:S(2)}) copy-start(f32[2,4,384,384]{3,2,1,0:T(8,128)} %copy-done.2) | copy-start | bytes 14155780
  68.4 10.5 %slice-start.1 = ((s8[4718592]{0:T(1024)(128)(4,1)}), s8[4194304]{0:T(1024)(128)(4,1)S(1)}, s32[]{:S(2)}) async-start(s8[4718592]{0:T(1024)(128)(4,1)} %bitcast.7), calls=%async_computation.4 | async-start | bytes 8388608
  68.4 10.5 %copy-start.5 = (s32[24]{0:T(128)S(1)}, s32[24]{0:T(128)}, u32[]{:S(2)}) copy-start(s32[24]{0:T(128)} %refs_1_.3) | copy-start | bytes 292
  89.0 2.1 %collective-permute-start.7 = (bf16[16,48,384]{2,1,0:T(8,128)(2,1)S(1)}, bf16[16,48,384]{2,1,0:T(8,128)(2,1)S(1)}, u32[]{:S(2)}, u32[]{:S(2)}) collective-permute-start(bf16[16,48,384]{2,1,0:T(8,128)(2,1)S(1)} %get-tuple-element.14), channel_id=1, source_target_pairs={{8,0},{0,8},{9,1},{1,9},{10,2},{2,10},{11,3},{3,11},{12,4},{4,12},... | collective-permute-start | bytes 1769480 | tf_op jit(solution)/shard_map/ppermute | solution.py:33
  92.1 3.7 %copy-start.7 = (s32[12]{0:T(128)S(1)}, s32[12]{0:T(128)}, u32[]{:S(2)}) copy-start(s32[12]{0:T(128)} %left_ref.1) | copy-start | bytes 148
  92.1 25.1 %all-to-all-start.2 = ((bf16[16,48,384]{2,1,0:T(8,128)(2,1)}), bf16[16,48,384]{2,1,0:T(8,128)(2,1)S(1)}, u32[]{:S(2)}, u32[]{:S(2)}) async-start(bf16[16,48,384]{2,1,0:T(8,128)(2,1)} %add_convert_fusion), calls=%async_computation.2 | async-start | bytes 1179648 | tf_op jit(solution)/shard_map/all_to_all | solution.py:47

commit v2 on v1

v2 whole, which is shorter than its diff:
```python
import functools

import jax
import jax.numpy as jnp
from jax import lax
from jax.experimental import pallas as pl
from jax.experimental.pallas import tpu as pltpu
from jax.sharding import PartitionSpec as P

BLK = 128
NZ, NXH, NC, NXL, NY = 8, 2, 2, 2, 4
NX = NXH * NXL
RING = 4
AXES = ("pair", "panel")
VMEM_LIMIT = 32 * 1024 * 1024
SMEM_SPEC = pl.BlockSpec(memory_space=pltpu.SMEM)
VMEM_SPEC = pl.BlockSpec(memory_space=pltpu.VMEM)
ANY_SPEC = pl.BlockSpec(memory_space=pl.ANY)


def flat(z, x, y, core):
    pair = (z * NXH + x // NXL) * NC + core
    return pair * (NXL * NY) + (x % NXL) * NY + y


def everywhere():
    return [
        (z, x, y, core) for z in range(NZ) for x in range(NX) for y in range(NY) for core in range(NC)
    ]


def core_swap(value):
    return lax.ppermute(
        value, AXES, [(flat(z, x, y, 1 - c), flat(z, x, y, c)) for z, x, y, c in everywhere()]
    )


def last_shift(value, step):
    perm = []
    for z, x, y, c in everywhere():
        source = flat(z, (x + step) % NX, y, c) if c == 0 else flat(z, x, (y + step) % NY, c)
        perm.append((source, flat(z, x, y, c)))
    return lax.ppermute(value, AXES, perm)


def exchange(copies, groups):
    return lax.all_to_all(
        copies, AXES, split_axis=0, concat_axis=0, axis_index_groups=groups, tiled=True
    )


def z_groups():
    return [
        [flat(z, x, y, c) for z in range(NZ)] for x in range(NX) for y in range(NY) for c in range(NC)
    ]


def middle_groups():
    along_y = [[flat(z, x, y, 0) for y in range(NY)] for z in range(NZ) for x in range(NX)]
    along_x = [[flat(z, x, y, 1) for x in range(NX)] for z in range(NZ) for y in range(NY)]
    return along_y + along_x


def mask_kernel(where_ref, left_ref, right_ref, psi_ref, out_ref):
    rows, cols = psi_ref.shape
    base = where_ref[0] * rows
    first = base // BLK
    second = jnp.minimum(first + 1, left_ref.shape[0] - 1)
    index = base + lax.broadcasted_iota(jnp.int32, (rows, BLK), 0)
    limit = jnp.where(
        index < (first + 1) * BLK, first * BLK + left_ref[first], (first + 1) * BLK + left_ref[second]
    )
    row_live = index < limit
    lane = lax.broadcasted_iota(jnp.int32, (rows, BLK), 1)
    for block in range(cols // BLK):
        live = row_live & (lane < right_ref[where_ref[1] * (cols // BLK) + block])
        span = slice(block * BLK, (block + 1) * BLK)
        value = psi_ref[:, span].astype(jnp.float32)
        value = jnp.where(live, value, 0.0).astype(out_ref.dtype)
        for copy in range(out_ref.shape[0]):
            out_ref[copy, :, span] = value


def mask_psi(where, left_sizes, right_sizes, psi):
    return pl.pallas_call(
        mask_kernel,
        out_shape=jax.ShapeDtypeStruct((NZ,) + psi.shape, psi.dtype),
        in_specs=[SMEM_SPEC, SMEM_SPEC, SMEM_SPEC, VMEM_SPEC],
        out_specs=VMEM_SPEC,
        name="mask_psi",
    )(where, left_sizes, right_sizes, psi)


def product_kernel(steps, first, last, where_ref, *refs):
    refs = list(refs)
    rows_ref, right_ref = (refs.pop(0), refs.pop(0)) if last else (None, None)
    acc_in = None if first else refs.pop(0)
    arrays = [refs.pop(0) for _ in steps]
    right = (refs.pop(0), refs.pop(0))
    left = (refs.pop(0), refs.pop(0)) if last else None
    acc = refs.pop(0)
    xh, core, xl, y = (where_ref[i] for i in range(3, 7))
    x = xh * NXL + xl
    pairs, cols, _ = right[0].shape
    group = arrays[0].shape[2]

    acc[...] = jnp.zeros_like(acc) if first else acc_in[...]
    for array, (step, start) in zip(arrays, steps):
        far_x, far_y = lax.rem(x + step, NX), lax.rem(y + step, NY)

        @pl.loop(0, array.shape[0] // 2)
        def _(two):
            columns = []
            for spot in range(2):
                middle = start + 2 * two + spot
                unit_x = jnp.where(core == 0, far_x, middle)
                unit_y = jnp.where(core == 0, middle, far_y)
                columns.append(pl.multiple_of((lax.rem(unit_x, NXL) * NY + unit_y) * cols, BLK))
            half = unit_x // NXL
            wide = jnp.concatenate(
                [array[2 * two + spot].reshape(NZ * group, cols) for spot in range(2)], axis=1
            )
            for side in range(2):
                operator = jnp.concatenate(
                    [right[side][:, :, pl.ds(c, cols)].reshape(pairs * cols, cols) for c in columns], axis=1
                )
                acc[half, side] += lax.dot_general(
                    wide, operator, (((1,), (1,)), ((), ())), preferred_element_type=jnp.float32
                )

    if not last:
        return
    keep_ref, send_ref, part, total = refs
    _, blocks, ka = left[0].shape[:3]
    lane = lax.broadcasted_iota(jnp.int32, (1, BLK), 1)
    start = (xl * NY + y) * (cols // BLK)
    live = jnp.concatenate(
        [(lane < right_ref[start + i]).astype(jnp.float32) for i in range(cols // BLK)], axis=1
    )
    total[...] = jnp.zeros_like(total)
    part[...] = jnp.zeros_like(part)
    for side in range(2):

        @pl.loop(0, pairs)
        def _(pair):
            column = pl.multiple_of(pair * cols, BLK)
            for half in range(NXH):
                for dz in range(NZ):
                    term = acc[half, side, pl.ds(dz * group, group), pl.ds(column, cols)]
                    at = ((dz * NXH + half) * NC + core) * group
                    part[pair, pl.ds(pl.multiple_of(at, 16), group), :] = (term * live).astype(part.dtype)
            for block in range(blocks):
                result = jnp.dot(
                    left[side][pair, block].reshape(ka * BLK, BLK),
                    part[pair, block * BLK : (block + 1) * BLK],
                    preferred_element_type=jnp.float32,
                )
                for s in range(ka):
                    row = rows_ref[((side * pairs + pair) * blocks + block) * ka + s]
                    at = pl.multiple_of(row * BLK, BLK)
                    total[pl.ds(at, BLK), :] += result[s * BLK : (s + 1) * BLK]

    for q in range(NZ * NXH):
        mine = pl.multiple_of((q * NC + core) * group, 16)
        theirs = pl.multiple_of((q * NC + 1 - core) * group, 16)
        keep_ref[q] = total[pl.ds(mine, group), :]
        send_ref[q] = total[pl.ds(theirs, group), :].astype(send_ref.dtype)


def product(where, acc, pieces, right, left=None, rows=None, right_sizes=None):
    arrays = [array for array, _, _ in pieces]
    steps = tuple((step, start) for _, step, start in pieces)
    first, last = acc is None, left is not None
    group, cols = arrays[0].shape[2:]
    pairs = right[0].shape[0]
    units = sum(array.shape[0] for array in arrays)
    acc_shape = (NXH, 2, NZ * group, pairs * cols)
    operands, specs = [where], [SMEM_SPEC]
    if last:
        operands += [rows, right_sizes]
        specs += [SMEM_SPEC, SMEM_SPEC]
    aliases = {} if first else {len(operands): 0}
    rest = ([] if first else [acc]) + arrays + list(right) + (list(left) if last else [])
    operands += rest
    specs += [VMEM_SPEC] * len(rest)
    scratch = []
    out_shape = [jax.ShapeDtypeStruct(acc_shape, jnp.float32)]
    if last:
        blocks = left[0].shape[1]
        out_shape += [
            jax.ShapeDtypeStruct((NZ * NXH, group, cols), jnp.float32),
            jax.ShapeDtypeStruct((NZ * NXH, group, cols), jnp.bfloat16),
        ]
        scratch = [
            pltpu.VMEM((pairs, blocks * BLK, cols), jnp.bfloat16),
            pltpu.VMEM((blocks * BLK, cols), jnp.float32),
        ]
    return pl.pallas_call(
        functools.partial(product_kernel, steps, first, last),
        out_shape=out_shape,
        in_specs=specs,
        out_specs=[VMEM_SPEC] * len(out_shape),
        scratch_shapes=scratch,
        input_output_aliases=aliases,
        compiler_params=pltpu.CompilerParams(vmem_limit_bytes=VMEM_LIMIT),
        cost_estimate=pl.CostEstimate(
            flops=2 * units * 2 * pairs * NZ * group * cols * cols,
            bytes_accessed=units * 2 * pairs * cols * cols * 2,
            transcendentals=0,
        ),
        name=f"product_{units}",
    )(*operands)


def local(psi, left_ops, a_rows, right_ops, left_sizes, right_sizes):
    rows_dev = psi.shape[0]
    pair, panel = lax.axis_index("pair"), lax.axis_index("panel")
    where = jnp.stack(
        [
            pair,
            panel,
            lax.shift_right_logical(pair, 2),
            lax.shift_right_logical(pair, 1) & 1,
            pair & 1,
            lax.shift_right_logical(panel, 2),
            panel & 3,
        ]
    ).astype(jnp.int32)
    copies = mask_psi(where, left_sizes, right_sizes, psi)
    right = (right_ops, core_swap(right_ops))
    left = (left_ops, core_swap(left_ops))
    rows = jnp.concatenate([a_rows.reshape(-1), core_swap(a_rows.reshape(-1))])

    along_z = exchange(copies, z_groups())
    wide = exchange(jnp.broadcast_to(along_z[None], (RING,) + along_z.shape), middle_groups())
    plus = last_shift(wide, 1)
    minus = last_shift(wide, -1)
    (acc,) = product(where, None, [(wide, 0, 0)], right)
    half = RING // 2
    plus, minus, acc, rows = lax.optimization_barrier((plus, minus, acc, rows))
    far_low = last_shift(plus[:half], 1)
    far_high = last_shift(minus[half:], -1)

    (acc,) = product(where, acc, [(plus, 1, 0), (minus, 3, 0)], right)
    _, keep, send = product(
        where, acc, [(far_low, 2, 0), (far_high, 2, half)], right, left, rows, right_sizes
    )
    mine = (keep + core_swap(send).astype(jnp.float32)).astype(jnp.bfloat16)
    groups = [
        [flat(z, xh * NXL + xl, y, c) for z in range(NZ) for xh in range(NXH)]
        for c in range(NC)
        for xl in range(NXL)
        for y in range(NY)
    ]
    parts = exchange(mine, groups)
    summed = parts.astype(jnp.float32).sum(axis=0)
    index = pair * rows_dev + jnp.arange(rows_dev, dtype=jnp.int32)
    blocks = jnp.arange(left_sizes.shape[0], dtype=jnp.int32)
    limit = jnp.sum(jnp.where(index[:, None] // BLK == blocks, left_sizes + blocks * BLK, 0), axis=1)
    return jnp.where((index < limit)[:, None], summed, 0.0)


def solution(mesh):
    placed = (
        P("pair", "panel"),
        P("pair", None, None, None, None),
        P("pair", None, None),
        P("pair", "panel", None),
        P(),
        P(),
    )
    return jax.shard_map(
        local, mesh=mesh, in_specs=placed, out_specs=P("pair", "panel"), check_vma=False
    )
```

time: 120 us -> 108 us (0.900)
  local copies, waits for them, and re-layouts: 11.9 us -> 4.76 us
  Pallas kernels: 28 us -> 24.2 us
  waiting for transfers between devices: 31.1 us -> 27.9 us
  starting transfers between devices: 9.09 us -> 11.7 us
    unnamed x21 -> x13, local copies, waits for them, and re-layouts: 9.3 us -> 3.06 us
    pallas_call x3, Pallas kernels: 26.5 us -> 22.7 us  [product(): pl.pallas_call(functools.partial(product_kernel, steps, first, last), out...]
    ppermute x4, waiting for transfers between devices: 6.95 us -> 4.05 us  [last_shift(): return lax.ppermute(value, AXES, perm)]
    ppermute x4, starting transfers between devices: 4.79 us -> 6.55 us  [last_shift(): return lax.ppermute(value, AXES, perm)]
  transfers between devices with their start and end apart: 9 -> 9, of which waited for: 5 -> 7; matrix products, arithmetic and copies ran while one was open for 2% -> 2% of each run, Pallas kernels for 15% -> 13%
where the time goes in v2:
time: 108 us; the launch traced here: 106 us
  blocking collectives  35.7 us (33%)
  waiting for transfers between devices  27.9 us (26%)
  Pallas kernels  24.2 us (22%)
  starting transfers between devices  11.7 us (11%)
  local copies, waits for them, and re-layouts  4.76 us (4%)
  other arithmetic  1.94 us (2%)
    all_to_all x2, blocking collectives, exchange(): lax.all_to_all(copies, AXES, split_axis=0, concat_axis=0, axis_index_grou...  35.7 us
    pallas_call x3, Pallas kernels, product(): pl.pallas_call(functools.partial(product_kernel, steps, first, last), out...  22.7 us
    all_to_all x1, waiting for transfers between devices, exchange(): lax.all_to_all(copies, AXES, split_axis=0, concat_axis=0, axis_index_grou...  20.6 us
    ppermute x4, starting transfers between devices, last_shift(): return lax.ppermute(value, AXES, perm)  6.55 us
    all_to_all x1, starting transfers between devices, exchange(): lax.all_to_all(copies, AXES, split_axis=0, concat_axis=0, axis_index_grou...  4.44 us
    ppermute x4, waiting for transfers between devices, last_shift(): return lax.ppermute(value, AXES, perm)  4.05 us
    ppermute x4, waiting for transfers between devices, core_swap(): lax.ppermute(value, AXES, [(flat(z, x, y, 1 - c), flat(z, x, y, c)) for z...  3.26 us
    unnamed x13, local copies, waits for them, and re-layouts  3.06 us
  transfers between devices with their start and end apart: 9, of which 7 were waited for; matrix products, arithmetic and copies ran while one was open for 2% of the time, Pallas kernels for 13%

profile of v2, /device:TPU:24, one launch (start us, length us, event | category | flops | bytes accessed | tf_op | source)
XLA Modules:
  0.0 106.4 jit_solution(4284781544251770556)
XLA Ops:
  0.0 0.0 collective-permute-start.2
  0.0 0.7 stack.31.where_ref
  0.7 1.6 %mask_psi.1 = bf16[8,48,384]{2,1,0:T(8,128)(2,1)} custom-call(s32[7]{0:T(128)} %stack.31.where_ref, s32[12]{0:T(128)} %left_ref.1, s32[24]{0:T(128)} %refs_1_.3, bf16[48,384]{1,0:T(8,128)(2,1)} %psi_ref.1), custom_call_target="tpu_custom_call" | custom-call | tf_op jit(solution)/shard_map/mask_psi/pallas_call | solution.py:85
  2.2 21.7 %all_to_all.15 = bf16[8,48,384]{2,1,0:T(8,128)(2,1)S(1)} all-to-all(bf16[8,48,384]{2,1,0:T(8,128)(2,1)} %mask_psi.1), channel_id=1, replica_groups={{0,32,64,96,128,160,192,224},{8,40,72,104,136,168,200,232},{1,33,65,97,..., dimensions={0} | all-to-all | bytes 589824 | tf_op jit(solution)/shard_map/all_to_all | solution.py:47
  23.9 0.1 broadcast_in_dim.32
  24.0 0.0 copy-start.4
  24.1 0.0 copy-start.2
  24.1 14.0 %all_to_all.16.refs_0_ = bf16[4,8,48,384]{3,2,1,0:T(8,128)(2,1)S(1)} all-to-all(bf16[4,8,48,384]{3,2,1,0:T(8,128)(2,1)S(1)} %broadcast_in_dim.32), channel_id=1, replica_groups={{0,1,2,3},{4,5,6,7},{16,17,18,19},{20,21,22,23},{32,33,34,35},{36,37,38..., dimensions={0} | all-to-all | bytes 2359296 | tf_op jit(solution)/shard_map/all_to_all | solution.py:47
  38.1 1.5 %collective-permute-start.1 = (bf16[4,8,48,384]{3,2,1,0:T(8,128)(2,1)S(1)}, bf16[4,8,48,384]{3,2,1,0:T(8,128)(2,1)S(1)}, u32[]{:S(2)}, u32[]{:S(2)}) collective-permute-start(bf16[4,8,48,384]{3,2,1,0:T(8,128)(2,1)S(1)} %all_to_all.16.refs_0_), channel_id=1, source_target_pairs={{20,0},{11,8},{21,1},{8,9},{22,2},{9,10},{23,3},{10,11},{0,4},{15,... | collective-permute-start | bytes 3538952 | tf_op jit(solution)/shard_map/ppermute | solution.py:43
  39.6 1.7 %collective-permute-start = (bf16[4,8,48,384]{3,2,1,0:T(8,128)(2,1)S(1)}, bf16[4,8,48,384]{3,2,1,0:T(8,128)(2,1)S(1)}, u32[]{:S(2)}, u32[]{:S(2)}) collective-permute-start(bf16[4,8,48,384]{3,2,1,0:T(8,128)(2,1)S(1)} %all_to_all.16.refs_0_), channel_id=1, source_target_pairs={{4,0},{9,8},{5,1},{10,9},{6,2},{11,10},{7,3},{8,11},{16,4},{13,12}... | collective-permute-start | bytes 3538952 | tf_op jit(solution)/shard_map/ppermute | solution.py:43
  41.3 0.0 collective-permute-start.6
  41.3 0.0 copy-done.4
  41.3 0.7 copy.11
  42.0 0.8 reshape.47
  42.8 0.6 collective-permute-start.3
  43.4 1.3 %collective-permute-done.3 = s32[48]{0:T(128)S(1)} collective-permute-done((s32[48]{0:T(128)S(1)}, s32[48]{0:T(128)S(1)}, u32[]{:S(2)}, u32[]{:S(2)}) %collective-permute-start.3) | collective-permute-done | bytes 224 | tf_op jit(solution)/shard_map/ppermute | solution.py:33
  44.7 0.1 pad_add_fusion.refs_0_
  44.8 0.0 collective-permute-done.2.refs_2_.refs_4_.refs_6_
  44.8 0.0 copy-done.2
  44.8 0.0 copy-start
  44.8 2.3 %copy-done = bf16[2,384,3072]{2,1,0:T(8,128)(2,1)S(1)} copy-done((bf16[2,384,3072]{2,1,0:T(8,128)(2,1)S(1)}, bf16[2,384,3072]{2,1,0:T(8,128)(2,1)}, u32[]{:S(2)}) %copy-start) | copy-done | bytes 4718616
  47.1 0.0 copy-start.1
  47.1 5.1 %product_4.2.refs_0_ = f32[2,2,384,768]{3,2,1,0:T(8,128)S(1)} custom-call(s32[7]{0:T(128)S(1)} %copy-done.2, bf16[4,8,48,384]{3,2,1,0:T(8,128)(2,1)S(1)} %all_to_all.16.refs_0_, bf16[2,384,3072]{2,1,0:T(8,128)(2,1)S(1)} %copy-done, bf16[2,384,3072]{2,1,0:T(8,128)(2,1)} %collective-permute-done.2.refs_2_.refs_4_.refs_6_), custom_call_target="tpu_custom_call" | custom-call | flops 1811939328 | bytes 4718592 | tf_op jit(solution)/shard_map/product_4/pallas_call | solution.py:198
  52.2 3.3 %collective-permute-done.1.refs_2_ = bf16[4,8,48,384]{3,2,1,0:T(8,128)(2,1)S(1)} collective-permute-done((bf16[4,8,48,384]{3,2,1,0:T(8,128)(2,1)S(1)}, bf16[4,8,48,384]{3,2,1,0:T(8,128)(2,1)S(1)}, u32[]{:S(2)}, u32[]{:S(2)}) %collective-permute-start.1) | collective-permute-done | bytes 1179680 | tf_op jit(solution)/shard_map/ppermute | solution.py:43
  55.5 0.3 collective-permute-done.refs_1_
  55.8 0.1 slice.6
  55.8 0.1 slice.7
  55.9 0.0 copy-start.3
  55.9 1.6 %collective-permute-start.5 = (bf16[2,8,48,384]{3,2,1,0:T(8,128)(2,1)S(1)}, bf16[2,8,48,384]{3,2,1,0:T(8,128)(2,1)S(1)}, u32[]{:S(2)}, u32[]{:S(2)}) collective-permute-start(bf16[2,8,48,384]{3,2,1,0:T(8,128)(2,1)S(1)} %slice.7), channel_id=1, source_target_pairs={{20,0},{11,8},{21,1},{8,9},{22,2},{9,10},{23,3},{10,11},{0,4},{15,... | collective-permute-start | bytes 1769480 | tf_op jit(solution)/shard_map/ppermute | solution.py:43
  57.5 1.7 %collective-permute-start.4 = (bf16[2,8,48,384]{3,2,1,0:T(8,128)(2,1)S(1)}, bf16[2,8,48,384]{3,2,1,0:T(8,128)(2,1)S(1)}, u32[]{:S(2)}, u32[]{:S(2)}) collective-permute-start(bf16[2,8,48,384]{3,2,1,0:T(8,128)(2,1)S(1)} %slice.6), channel_id=1, source_target_pairs={{4,0},{9,8},{5,1},{10,9},{6,2},{11,10},{7,3},{8,11},{16,4},{13,12}... | collective-permute-start | bytes 1769480 | tf_op jit(solution)/shard_map/ppermute | solution.py:43
  59.2 0.0 copy-done.1
  59.2 7.6 %product_8.1.refs_2_ = f32[2,2,384,768]{3,2,1,0:T(8,128)S(1)} custom-call(s32[7]{0:T(128)S(1)} %copy-done.2, f32[2,2,384,768]{3,2,1,0:T(8,128)S(1)} %product_4.2.refs_0_, bf16[4,8,48,384]{3,2,1,0:T(8,128)(2,1)S(1)} %collective-permute-done.refs_1_, bf16[4,8,48,384]{3,2,1,0:T(8,128)(2,1)S(1)} %collective-permute-done.1.refs_2_, ...), custom_call_target="tpu_custom_call", output_to_operand_aliasing={{}: (1, {})} | custom-call | flops 3623878656 | bytes 9437184 | tf_op jit(solution)/shard_map/product_8/pallas_call | solution.py:198
  66.9 0.0 collective-permute-done.6.refs_8_
  66.9 0.2 collective-permute-done.5.refs_4_
  67.1 0.3 collective-permute-done.4.refs_3_
  67.4 0.0 copy-done.3
  67.4 9.9 %product_4.3 = (f32[2,2,384,768]{3,2,1,0:T(8,128)S(1)}, f32[16,48,384]{2,1,0:T(8,128)S(1)}, bf16[16,48,384]{2,1,0:T(8,128)(2,1)S(1)}) custom-call(s32[7]{0:T(128)S(1)} %copy-done.2, s32[96]{0:T(128)S(1)} %pad_add_fusion.refs_0_, s32[24]{0:T(128)S(1)} %copy-done.3, f32[2,2,384,768]{3,2,1,0:T(8,128)S(1)} %product_8.1.refs_2_, ...), custom_call_target="tpu_custom_call", output_to_operand_aliasing={{0}: (3, {})} | custom-call | flops 1811939328 | bytes 4718592 | tf_op jit(solution)/shard_map/product_4/pallas_call | solution.py:198
  77.3 0.1 collective-permute-start.7
  77.4 2.0 %collective-permute-done.7 = bf16[16,48,384]{2,1,0:T(8,128)(2,1)S(1)} collective-permute-done((bf16[16,48,384]{2,1,0:T(8,128)(2,1)S(1)}, bf16[16,48,384]{2,1,0:T(8,128)(2,1)S(1)}, u32[]{:S(2)}, u32[]{:S(2)}) %collective-permute-start.7) | collective-permute-done | bytes 589856 | tf_op jit(solution)/shard_map/ppermute | solution.py:33
  79.4 1.0 add_convert_fusion
  80.4 0.0 copy-start.5
  80.4 4.4 %all-to-all-start.2 = ((bf16[16,48,384]{2,1,0:T(8,128)(2,1)}), bf16[16,48,384]{2,1,0:T(8,128)(2,1)S(1)}, u32[]{:S(2)}, u32[]{:S(2)}) async-start(bf16[16,48,384]{2,1,0:T(8,128)(2,1)} %add_convert_fusion), calls=%async_computation.2 | async-start | bytes 1179648 | tf_op jit(solution)/shard_map/all_to_all | solution.py:47
  84.9 0.0 copy-done.5
  84.9 0.1 select_reduce_fusion
  85.0 20.6 %all-to-all-done.2 = bf16[16,48,384]{2,1,0:T(8,128)(2,1)S(1)} async-done(((bf16[16,48,384]{2,1,0:T(8,128)(2,1)}), bf16[16,48,384]{2,1,0:T(8,128)(2,1)S(1)}, u32[]{:S(2)}, u32[]{:S(2)}) %all-to-all-start.2) | async-done | bytes 589856 | tf_op jit(solution)/shard_map/all_to_all | solution.py:47
  105.6 0.1 convert_reduce_fusion
  105.7 0.7 broadcast_select_fusion
  (3 shorter events, 0.0 us)
Async XLA Ops:
  0.0 44.8 %collective-permute-start.2 = (bf16[2,384,3072]{2,1,0:T(8,128)(2,1)}, bf16[2,384,3072]{2,1,0:T(8,128)(2,1)}, u32[]{:S(2)}, u32[]{:S(2)}) collective-permute-start(bf16[2,384,3072]{2,1,0:T(8,128)(2,1)} %refs_5_.1), channel_id=1, source_target_pairs={{8,0},{0,8},{9,1},{1,9},{10,2},{2,10},{11,3},{3,11},{12,4},{4,12},... | collective-permute-start | bytes 14155784 | tf_op jit(solution)/shard_map/ppermute | solution.py:33
  24.0 17.3 %copy-start.4 = (s32[2,12,2]{1,2,0:T(2,128)S(1)}, s32[2,12,2]{1,2,0:T(2,128)}, u32[]{:S(2)}) copy-start(s32[2,12,2]{1,2,0:T(2,128)} %param.8) | copy-start | bytes 580
  24.1 20.7 %copy-start.2 = (s32[7]{0:T(128)S(1)}, s32[7]{0:T(128)}, u32[]{:S(2)}) copy-start(s32[7]{0:T(128)} %stack.31.where_ref) | copy-start | bytes 88
  38.1 17.4 %collective-permute-start.1 = (bf16[4,8,48,384]{3,2,1,0:T(8,128)(2,1)S(1)}, bf16[4,8,48,384]{3,2,1,0:T(8,128)(2,1)S(1)}, u32[]{:S(2)}, u32[]{:S(2)}) collective-permute-start(bf16[4,8,48,384]{3,2,1,0:T(8,128)(2,1)S(1)} %all_to_all.16.refs_0_), channel_id=1, source_target_pairs={{20,0},{11,8},{21,1},{8,9},{22,2},{9,10},{23,3},{10,11},{0,4},{15,... | collective-permute-start | bytes 3538952 | tf_op jit(solution)/shard_map/ppermute | solution.py:43
  39.6 16.2 %collective-permute-start = (bf16[4,8,48,384]{3,2,1,0:T(8,128)(2,1)S(1)}, bf16[4,8,48,384]{3,2,1,0:T(8,128)(2,1)S(1)}, u32[]{:S(2)}, u32[]{:S(2)}) collective-permute-start(bf16[4,8,48,384]{3,2,1,0:T(8,128)(2,1)S(1)} %all_to_all.16.refs_0_), channel_id=1, source_target_pairs={{4,0},{9,8},{5,1},{10,9},{6,2},{11,10},{7,3},{8,11},{16,4},{13,12}... | collective-permute-start | bytes 3538952 | tf_op jit(solution)/shard_map/ppermute | solution.py:43
  41.3 25.5 %collective-permute-start.6 = (bf16[2,12,2,128,128]{4,3,2,1,0:T(8,128)(2,1)}, bf16[2,12,2,128,128]{4,3,2,1,0:T(8,128)(2,1)}, u32[]{:S(2)}, u32[]{:S(2)}) collective-permute-start(bf16[2,12,2,128,128]{4,3,2,1,0:T(8,128)(2,1)} %refs_7_.1), channel_id=1, source_target_pairs={{8,0},{0,8},{9,1},{1,9},{10,2},{2,10},{11,3},{3,11},{12,4},{4,12},... | collective-permute-start | bytes 4718600 | tf_op jit(solution)/shard_map/ppermute | solution.py:33
  42.8 1.9 %collective-permute-start.3 = (s32[48]{0:T(128)S(1)}, s32[48]{0:T(128)S(1)}, u32[]{:S(2)}, u32[]{:S(2)}) collective-permute-start(s32[48]{0:T(128)S(1)} %reshape.47), channel_id=1, source_target_pairs={{8,0},{0,8},{9,1},{1,9},{10,2},{2,10},{11,3},{3,11},{12,4},{4,12},... | collective-permute-start | bytes 584 | tf_op jit(solution)/shard_map/ppermute | solution.py:33
  44.8 2.3 %copy-start = (bf16[2,384,3072]{2,1,0:T(8,128)(2,1)S(1)}, bf16[2,384,3072]{2,1,0:T(8,128)(2,1)}, u32[]{:S(2)}) copy-start(bf16[2,384,3072]{2,1,0:T(8,128)(2,1)} %refs_5_.1) | copy-start | bytes 14155780
  47.1 12.1 %copy-start.1 = (bf16[2,384,3072]{2,1,0:T(8,128)(2,1)S(1)}, bf16[2,384,3072]{2,1,0:T(8,128)(2,1)}, u32[]{:S(2)}) copy-start(bf16[2,384,3072]{2,1,0:T(8,128)(2,1)} %refs_5_.1) | copy-start | bytes 14155780
  55.9 11.5 %copy-start.3 = (s32[24]{0:T(128)S(1)}, s32[24]{0:T(128)}, u32[]{:S(2)}) copy-start(s32[24]{0:T(128)} %refs_1_.3) | copy-start | bytes 292
  55.9 11.2 %collective-permute-start.5 = (bf16[2,8,48,384]{3,2,1,0:T(8,128)(2,1)S(1)}, bf16[2,8,48,384]{3,2,1,0:T(8,128)(2,1)S(1)}, u32[]{:S(2)}, u32[]{:S(2)}) collective-permute-start(bf16[2,8,48,384]{3,2,1,0:T(8,128)(2,1)S(1)} %slice.7), channel_id=1, source_target_pairs={{20,0},{11,8},{21,1},{8,9},{22,2},{9,10},{23,3},{10,11},{0,4},{15,... | collective-permute-start | bytes 1769480 | tf_op jit(solution)/shard_map/ppermute | solution.py:43
  57.5 9.9 %collective-permute-start.4 = (bf16[2,8,48,384]{3,2,1,0:T(8,128)(2,1)S(1)}, bf16[2,8,48,384]{3,2,1,0:T(8,128)(2,1)S(1)}, u32[]{:S(2)}, u32[]{:S(2)}) collective-permute-start(bf16[2,8,48,384]{3,2,1,0:T(8,128)(2,1)S(1)} %slice.6), channel_id=1, source_target_pairs={{4,0},{9,8},{5,1},{10,9},{6,2},{11,10},{7,3},{8,11},{16,4},{13,12}... | collective-permute-start | bytes 1769480 | tf_op jit(solution)/shard_map/ppermute | solution.py:43
  77.3 2.1 %collective-permute-start.7 = (bf16[16,48,384]{2,1,0:T(8,128)(2,1)S(1)}, bf16[16,48,384]{2,1,0:T(8,128)(2,1)S(1)}, u32[]{:S(2)}, u32[]{:S(2)}) collective-permute-start(bf16[16,48,384]{2,1,0:T(8,128)(2,1)S(1)} %get-tuple-element.16), channel_id=1, source_target_pairs={{8,0},{0,8},{9,1},{1,9},{10,2},{2,10},{11,3},{3,11},{12,4},{4,12},... | collective-permute-start | bytes 1769480 | tf_op jit(solution)/shard_map/ppermute | solution.py:33
  80.4 4.5 %copy-start.5 = (s32[12]{0:T(128)S(1)}, s32[12]{0:T(128)}, u32[]{:S(2)}) copy-start(s32[12]{0:T(128)} %left_ref.1) | copy-start | bytes 148
  80.4 25.2 %all-to-all-start.2 = ((bf16[16,48,384]{2,1,0:T(8,128)(2,1)}), bf16[16,48,384]{2,1,0:T(8,128)(2,1)S(1)}, u32[]{:S(2)}, u32[]{:S(2)}) async-start(bf16[16,48,384]{2,1,0:T(8,128)(2,1)} %add_convert_fusion), calls=%async_computation.2 | async-start | bytes 1179648 | tf_op jit(solution)/shard_map/all_to_all | solution.py:47

commit v3 on v2

v3 whole, which is shorter than its diff:
```python
import functools

import jax
import jax.numpy as jnp
from jax import lax
from jax.experimental import pallas as pl
from jax.experimental.pallas import tpu as pltpu
from jax.sharding import PartitionSpec as P

BLK = 128
NZ, NXH, NC, NXL, NY = 8, 2, 2, 2, 4
NX = NXH * NXL
RING = 4
AXES = ("pair", "panel")
VMEM_LIMIT = 32 * 1024 * 1024
SMEM_SPEC = pl.BlockSpec(memory_space=pltpu.SMEM)
VMEM_SPEC = pl.BlockSpec(memory_space=pltpu.VMEM)
ANY_SPEC = pl.BlockSpec(memory_space=pl.ANY)


def flat(z, x, y, core):
    pair = (z * NXH + x // NXL) * NC + core
    return pair * (NXL * NY) + (x % NXL) * NY + y


def everywhere():
    return [
        (z, x, y, core) for z in range(NZ) for x in range(NX) for y in range(NY) for core in range(NC)
    ]


def core_swap(value):
    return lax.ppermute(
        value, AXES, [(flat(z, x, y, 1 - c), flat(z, x, y, c)) for z, x, y, c in everywhere()]
    )


def last_shift(value, step):
    perm = []
    for z, x, y, c in everywhere():
        source = flat(z, (x + step) % NX, y, c) if c == 0 else flat(z, x, (y + step) % NY, c)
        perm.append((source, flat(z, x, y, c)))
    return lax.ppermute(value, AXES, perm)


def exchange(copies, groups):
    return lax.all_to_all(
        copies, AXES, split_axis=0, concat_axis=0, axis_index_groups=groups, tiled=True
    )


def z_groups():
    return [
        [flat(z, x, y, c) for z in range(NZ)] for x in range(NX) for y in range(NY) for c in range(NC)
    ]


def middle_groups():
    along_y = [[flat(z, x, y, 0) for y in range(NY)] for z in range(NZ) for x in range(NX)]
    along_x = [[flat(z, x, y, 1) for x in range(NX)] for z in range(NZ) for y in range(NY)]
    return along_y + along_x


def position():
    pair, panel = lax.axis_index("pair"), lax.axis_index("panel")
    return pair // (NXH * NC), (pair // NC) % NXH, pair % NC, panel // NY, panel % NY


def mask_kernel(left_ref, right_ref, psi_ref, out_ref):
    rows, cols = psi_ref.shape
    base = lax.axis_index("pair") * rows
    panel = lax.axis_index("panel")
    first = base // BLK
    second = jnp.minimum(first + 1, left_ref.shape[0] - 1)
    index = base + lax.broadcasted_iota(jnp.int32, (rows, BLK), 0)
    limit = jnp.where(
        index < (first + 1) * BLK, first * BLK + left_ref[first], (first + 1) * BLK + left_ref[second]
    )
    row_live = index < limit
    lane = lax.broadcasted_iota(jnp.int32, (rows, BLK), 1)
    for block in range(cols // BLK):
        live = row_live & (lane < right_ref[panel * (cols // BLK) + block])
        span = slice(block * BLK, (block + 1) * BLK)
        value = psi_ref[:, span].astype(jnp.float32)
        value = jnp.where(live, value, 0.0).astype(out_ref.dtype)
        for copy in range(out_ref.shape[0]):
            out_ref[copy, :, span] = value


def mask_psi(left_sizes, right_sizes, psi):
    return pl.pallas_call(
        mask_kernel,
        out_shape=jax.ShapeDtypeStruct((NZ,) + psi.shape, psi.dtype),
        in_specs=[SMEM_SPEC, SMEM_SPEC, VMEM_SPEC],
        out_specs=VMEM_SPEC,
        name="mask_psi",
    )(left_sizes, right_sizes, psi)


def product_kernel(steps, first, last, *refs):
    refs = list(refs)
    rows_ref, right_ref = (refs.pop(0), refs.pop(0)) if last else (None, None)
    acc_in = None if first else refs.pop(0)
    arrays = [refs.pop(0) for _ in steps]
    right = (refs.pop(0), refs.pop(0))
    left = (refs.pop(0), refs.pop(0)) if last else None
    _, xh, core, xl, y = position()
    x = xh * NXL + xl
    pairs, cols, _ = right[0].shape
    group = arrays[0].shape[2]
    if last:
        keep_ref, send_ref, rbuf, sem_r, lbuf, sem_l, part, total = refs
    else:
        acc, rbuf, sem_r = refs

    twos = []
    copies = []
    for array, (step, start) in zip(arrays, steps):
        far_x, far_y = lax.rem(x + step, NX), lax.rem(y + step, NY)
        for spot in range(0, array.shape[0], 2):
            for side in range(2):
                copies.append([])
                for way in range(2):
                    middle = start + spot + way
                    unit_x = jnp.where(core == 0, far_x, middle)
                    unit_y = jnp.where(core == 0, middle, far_y)
                    column = pl.multiple_of((lax.rem(unit_x, NXL) * NY + unit_y) * cols, BLK)
                    copies[-1].append(
                        pltpu.make_async_copy(
                            right[side].at[:, :, pl.ds(column, cols)],
                            rbuf.at[len(twos), side, :, :, pl.ds(way * cols, cols)],
                            sem_r.at[len(twos), side, way],
                        )
                    )
            twos.append((array, spot, unit_x // NXL))
    for copy in sum(copies, []):
        copy.start()

    def wide(array, spot):
        return jnp.concatenate(
            [array[spot + way].reshape(NZ * group, cols) for way in range(2)], axis=1
        )

    def times(left_side, right_side):
        return lax.dot_general(
            left_side, right_side, (((1,), (1,)), ((), ())), preferred_element_type=jnp.float32
        )

    def operator(index, side):
        return rbuf[index, side].reshape(pairs * cols, 2 * cols)

    if not last:
        acc[...] = jnp.zeros_like(acc) if first else acc_in[...]
        for index, (array, spot, half) in enumerate(twos):
            for side in range(2):
                for copy in copies[2 * index + side]:
                    copy.wait()

            @pl.loop(0, 2)
            def _(side):
                acc[half, side] += times(wide(array, spot), operator(index, side))

        return

    left_copies = [
        pltpu.make_async_copy(left[side], lbuf.at[pl.ds(side * pairs, pairs)], sem_l.at[side])
        for side in range(2)
    ]
    for copy in left_copies:
        copy.start()
    blocks, ka = lbuf.shape[1:3]
    lane = lax.broadcasted_iota(jnp.int32, (1, BLK), 1)
    start = (xl * NY + y) * (cols // BLK)
    live = jnp.concatenate(
        [(lane < right_ref[start + i]).astype(jnp.float32) for i in range(cols // BLK)], axis=1
    )
    total[...] = jnp.zeros_like(total)
    part[...] = jnp.zeros_like(part)
    for copy in sum(copies, []):
        copy.wait()

    def place(half, side, sums):
        for pair in range(pairs):
            rounded = (sums[:, pair * cols : (pair + 1) * cols] * live).astype(part.dtype)
            for dz in range(NZ):
                at = ((dz * NXH + half) * NC + core) * group
                part[side * pairs + pair, pl.ds(pl.multiple_of(at, 16), group), :] = rounded[
                    dz * group : (dz + 1) * group
                ]

    @pl.loop(0, 2)
    def _(side):
        @pl.when(core == 0)
        def _():
            far = 1 - xh
            place(xh, side, acc_in[xh, side])
            left_side = jnp.concatenate([wide(array, spot) for array, spot, _ in twos], axis=1)
            right_side = jnp.concatenate([operator(index, side) for index in range(len(twos))], axis=1)
            place(far, side, acc_in[far, side] + times(left_side, right_side))

        @pl.when(core == 1)
        def _():
            for index, (array, spot, half) in enumerate(twos):
                place(half, side, acc_in[half, side] + times(wide(array, spot), operator(index, side)))

    for copy in left_copies:
        copy.wait()

    @pl.loop(0, 2 * pairs)
    def _(pair):
        for block in range(blocks):
            result = jnp.dot(
                lbuf[pair, block].reshape(ka * BLK, BLK),
                part[pair, block * BLK : (block + 1) * BLK],
                preferred_element_type=jnp.float32,
            )
            for s in range(ka):
                row = rows_ref[(pair * blocks + block) * ka + s]
                total[pl.ds(pl.multiple_of(row * BLK, BLK), BLK), :] += result[s * BLK : (s + 1) * BLK]

    for q in range(NZ * NXH):
        mine = pl.multiple_of((q * NC + core) * group, 16)
        theirs = pl.multiple_of((q * NC + 1 - core) * group, 16)
        keep_ref[q] = total[pl.ds(mine, group), :]
        send_ref[q] = total[pl.ds(theirs, group), :].astype(send_ref.dtype)


def product(acc, pieces, right, left=None, rows=None, right_sizes=None):
    arrays = [array for array, _, _ in pieces]
    steps = tuple((step, start) for _, step, start in pieces)
    first, last = acc is None, left is not None
    group, cols = arrays[0].shape[2:]
    pairs = right[0].shape[0]
    units = sum(array.shape[0] for array in arrays)
    acc_shape = (NXH, 2, NZ * group, pairs * cols)
    operands = [rows, right_sizes] if last else []
    specs = [SMEM_SPEC] * len(operands)
    aliases = {} if first or last else {len(operands): 0}
    near = ([] if first else [acc]) + arrays
    away = list(right) + (list(left) if last else [])
    operands += near + away
    specs += [VMEM_SPEC] * len(near) + [ANY_SPEC] * len(away)
    scratch = [
        pltpu.VMEM((units // 2, 2, pairs, cols, 2 * cols), jnp.bfloat16),
        pltpu.SemaphoreType.DMA((units // 2, 2, 2)),
    ]
    if last:
        blocks = left[0].shape[1]
        out_shape = [
            jax.ShapeDtypeStruct((NZ * NXH, group, cols), jnp.float32),
            jax.ShapeDtypeStruct((NZ * NXH, group, cols), jnp.bfloat16),
        ]
        scratch += [
            pltpu.VMEM((2 * pairs,) + left[0].shape[1:], jnp.bfloat16),
            pltpu.SemaphoreType.DMA((2,)),
            pltpu.VMEM((2 * pairs, blocks * BLK, cols), jnp.bfloat16),
            pltpu.VMEM((blocks * BLK, cols), jnp.float32),
        ]
    else:
        out_shape = [jax.ShapeDtypeStruct(acc_shape, jnp.float32)]
    return pl.pallas_call(
        functools.partial(product_kernel, steps, first, last),
        out_shape=out_shape,
        in_specs=specs,
        out_specs=[VMEM_SPEC] * len(out_shape),
        scratch_shapes=scratch,
        input_output_aliases=aliases,
        compiler_params=pltpu.CompilerParams(vmem_limit_bytes=VMEM_LIMIT),
        cost_estimate=pl.CostEstimate(
            flops=2 * units * 2 * pairs * NZ * group * cols * cols,
            bytes_accessed=units * 2 * pairs * cols * cols * 2,
            transcendentals=0,
        ),
        name=f"product_{units}",
    )(*operands)


def local(psi, left_ops, a_rows, right_ops, left_sizes, right_sizes):
    rows_dev = psi.shape[0]
    pair = lax.axis_index("pair")
    copies = mask_psi(left_sizes, right_sizes, psi)
    right = (right_ops, core_swap(right_ops))
    left = (left_ops, core_swap(left_ops))
    rows = jnp.concatenate([a_rows.reshape(-1), core_swap(a_rows.reshape(-1))])

    along_z = exchange(copies, z_groups())
    wide = exchange(jnp.broadcast_to(along_z[None], (RING,) + along_z.shape), middle_groups())
    plus = last_shift(wide, 1)
    minus = last_shift(wide, -1)
    (acc,) = product(None, [(wide, 0, 0)], right)
    half = RING // 2
    plus, minus, acc, rows = lax.optimization_barrier((plus, minus, acc, rows))
    far_low = last_shift(plus[:half], 1)
    far_high = last_shift(minus[half:], -1)

    (acc,) = product(acc, [(plus, 1, 0), (minus, 3, 0)], right)
    keep, send = product(
        acc, [(far_low, 2, 0), (far_high, 2, half)], right, left, rows, right_sizes
    )
    mine = (keep + core_swap(send).astype(jnp.float32)).astype(jnp.bfloat16)
    groups = [
        [flat(z, xh * NXL + xl, y, c) for z in range(NZ) for xh in range(NXH)]
        for c in range(NC)
        for xl in range(NXL)
        for y in range(NY)
    ]
    parts = exchange(mine, groups)
    summed = parts.astype(jnp.float32).sum(axis=0)
    index = pair * rows_dev + jnp.arange(rows_dev, dtype=jnp.int32)
    blocks = jnp.arange(left_sizes.shape[0], dtype=jnp.int32)
    limit = jnp.sum(jnp.where(index[:, None] // BLK == blocks, left_sizes + blocks * BLK, 0), axis=1)
    return jnp.where((index < limit)[:, None], summed, 0.0)


def solution(mesh):
    placed = (
        P("pair", "panel"),
        P("pair", None, None, None, None),
        P("pair", None, None),
        P("pair", "panel", None),
        P(),
        P(),
    )
    return jax.shard_map(
        local, mesh=mesh, in_specs=placed, out_specs=P("pair", "panel"), check_vma=False
    )
```

time: 108 us -> 108 us (level)
  waiting for transfers between devices: 27.9 us -> 33.4 us
  Pallas kernels: 24.2 us -> 21.5 us
  starting transfers between devices: 11.7 us -> 9.43 us
    ppermute x4, waiting for transfers between devices: 4.05 us -> 8.6 us  [last_shift(): return lax.ppermute(value, AXES, perm)]
    pallas_call x3, Pallas kernels: 22.7 us -> 19.9 us  [product(): pl.pallas_call(functools.partial(product_kernel, steps, first, last), out...]
    ppermute x4, starting transfers between devices: 6.55 us -> 5.11 us  [last_shift(): return lax.ppermute(value, AXES, perm)]
    unnamed x13 -> x9, local copies, waits for them, and re-layouts: 3.06 us -> 3.13 us
  transfers between devices with their start and end apart: 9 -> 9, of which waited for: 7 -> 7; matrix products, arithmetic and copies ran while one was open for 2% -> 2% of each run, Pallas kernels for 13% -> 12%
where the time goes in v3:
time: 108 us; the launch traced here: 107 us
  blocking collectives  35.7 us (33%)
  waiting for transfers between devices  33.4 us (31%)
  Pallas kernels  21.5 us (20%)
  starting transfers between devices  9.43 us (9%)
  local copies, waits for them, and re-layouts  3.96 us (4%)
  other arithmetic  2.58 us (2%)
    all_to_all x2, blocking collectives, exchange(): lax.all_to_all(copies, AXES, split_axis=0, concat_axis=0, axis_index_grou...  35.7 us
    all_to_all x1, waiting for transfers between devices, exchange(): lax.all_to_all(copies, AXES, split_axis=0, concat_axis=0, axis_index_grou...  21.2 us
    pallas_call x3, Pallas kernels, product(): pl.pallas_call(functools.partial(product_kernel, steps, first, last), out...  19.9 us
    ppermute x4, waiting for transfers between devices, last_shift(): return lax.ppermute(value, AXES, perm)  8.6 us
    ppermute x4, starting transfers between devices, last_shift(): return lax.ppermute(value, AXES, perm)  5.11 us
    all_to_all x1, starting transfers between devices, exchange(): lax.all_to_all(copies, AXES, split_axis=0, concat_axis=0, axis_index_grou...  3.71 us
    ppermute x4, waiting for transfers between devices, core_swap(): lax.ppermute(value, AXES, [(flat(z, x, y, 1 - c), flat(z, x, y, c)) for z...  3.6 us
    unnamed x9, local copies, waits for them, and re-layouts  3.13 us
  transfers between devices with their start and end apart: 9, of which 7 were waited for; matrix products, arithmetic and copies ran while one was open for 2% of the time, Pallas kernels for 12%

profile of v3, /device:TPU:24, one launch (start us, length us, event | category | flops | bytes accessed | tf_op | source)
XLA Modules:
  0.0 106.7 jit_solution(16603849651925602809)
XLA Ops:
  0.0 0.0 collective-permute-start.2
  0.0 1.6 %mask_psi.1 = bf16[8,48,384]{2,1,0:T(8,128)(2,1)} custom-call(s32[12]{0:T(128)} %left_ref.1, s32[24]{0:T(128)} %refs_1_.3, bf16[48,384]{1,0:T(8,128)(2,1)} %psi_ref.1), custom_call_target="tpu_custom_call" | custom-call | tf_op jit(solution)/shard_map/mask_psi/pallas_call | solution.py:91
  1.6 21.7 %all_to_all.15 = bf16[8,48,384]{2,1,0:T(8,128)(2,1)S(1)} all-to-all(bf16[8,48,384]{2,1,0:T(8,128)(2,1)} %mask_psi.1), channel_id=1, replica_groups={{0,32,64,96,128,160,192,224},{8,40,72,104,136,168,200,232},{1,33,65,97,..., dimensions={0} | all-to-all | bytes 589824 | tf_op jit(solution)/shard_map/all_to_all | solution.py:47
  23.3 0.1 broadcast_in_dim.32
  23.4 14.0 %all_to_all.16.refs_0_ = bf16[4,8,48,384]{3,2,1,0:T(8,128)(2,1)S(1)} all-to-all(bf16[4,8,48,384]{3,2,1,0:T(8,128)(2,1)S(1)} %broadcast_in_dim.32), channel_id=1, replica_groups={{0,1,2,3},{4,5,6,7},{16,17,18,19},{20,21,22,23},{32,33,34,35},{36,37,38..., dimensions={0} | all-to-all | bytes 2359296 | tf_op jit(solution)/shard_map/all_to_all | solution.py:47
  37.4 2.8 %collective-permute-start = (bf16[4,8,48,384]{3,2,1,0:T(8,128)(2,1)S(1)}, bf16[4,8,48,384]{3,2,1,0:T(8,128)(2,1)S(1)}, u32[]{:S(2)}, u32[]{:S(2)}) collective-permute-start(bf16[4,8,48,384]{3,2,1,0:T(8,128)(2,1)S(1)} %all_to_all.16.refs_0_), channel_id=1, source_target_pairs={{4,0},{9,8},{5,1},{10,9},{6,2},{11,10},{7,3},{8,11},{16,4},{13,12}... | collective-permute-start | bytes 3538952 | tf_op jit(solution)/shard_map/ppermute | solution.py:43
  40.2 0.0 collective-permute-start.1
  40.2 0.0 collective-permute-start.6
  40.2 0.8 copy.10
  41.0 0.6 reshape.47
  41.6 0.5 collective-permute-start.3
  42.1 1.6 %collective-permute-done.3 = s32[48]{0:T(128)S(1)} collective-permute-done((s32[48]{0:T(128)}, s32[48]{0:T(128)S(1)}, u32[]{:S(2)}, u32[]{:S(2)}) %collective-permute-start.3) | collective-permute-done | bytes 224 | tf_op jit(solution)/shard_map/ppermute | solution.py:33
  43.7 0.7 pad_add_fusion.refs_0_
  44.4 0.0 collective-permute-done.2.refs_2_.refs_4_.refs_6_
  44.4 0.0 copy-start
  44.4 2.3 %copy-done = bf16[2,384,3072]{2,1,0:T(8,128)(2,1)S(1)} copy-done((bf16[2,384,3072]{2,1,0:T(8,128)(2,1)S(1)}, bf16[2,384,3072]{2,1,0:T(8,128)(2,1)}, u32[]{:S(2)}) %copy-start) | copy-done | bytes 4718616
  46.7 0.0 copy-start.1
  46.7 4.3 %product_4.2.refs_0_ = f32[2,2,384,768]{3,2,1,0:T(8,128)S(1)} custom-call(bf16[4,8,48,384]{3,2,1,0:T(8,128)(2,1)S(1)} %all_to_all.16.refs_0_, bf16[2,384,3072]{2,1,0:T(8,128)(2,1)S(1)} %copy-done, bf16[2,384,3072]{2,1,0:T(8,128)(2,1)} %collective-permute-done.2.refs_2_.refs_4_.refs_6_), custom_call_target="tpu_custom_call" | custom-call | flops 1811939328 | bytes 4718592 | tf_op jit(solution)/shard_map/product_4/pallas_call | solution.py:261
  51.1 2.8 %collective-permute-done.refs_1_ = bf16[4,8,48,384]{3,2,1,0:T(8,128)(2,1)S(1)} collective-permute-done((bf16[4,8,48,384]{3,2,1,0:T(8,128)(2,1)S(1)}, bf16[4,8,48,384]{3,2,1,0:T(8,128)(2,1)S(1)}, u32[]{:S(2)}, u32[]{:S(2)}) %collective-permute-start) | collective-permute-done | bytes 1179680 | tf_op jit(solution)/shard_map/ppermute | solution.py:43
  53.9 3.7 %collective-permute-done.1.refs_2_ = bf16[4,8,48,384]{3,2,1,0:T(8,128)(2,1)S(1)} collective-permute-done((bf16[4,8,48,384]{3,2,1,0:T(8,128)(2,1)S(1)}, bf16[4,8,48,384]{3,2,1,0:T(8,128)(2,1)S(1)}, u32[]{:S(2)}, u32[]{:S(2)}) %collective-permute-start.1) | collective-permute-done | bytes 1179680 | tf_op jit(solution)/shard_map/ppermute | solution.py:43
  57.6 0.1 slice.6
  57.6 0.1 collective-permute-start.4
  57.7 0.1 slice.7
  57.8 0.0 copy-start.2
  57.8 2.3 %collective-permute-start.5 = (bf16[2,8,48,384]{3,2,1,0:T(8,128)(2,1)S(1)}, bf16[2,8,48,384]{3,2,1,0:T(8,128)(2,1)S(1)}, u32[]{:S(2)}, u32[]{:S(2)}) collective-permute-start(bf16[2,8,48,384]{3,2,1,0:T(8,128)(2,1)S(1)} %slice.7), channel_id=1, source_target_pairs={{20,0},{11,8},{21,1},{8,9},{22,2},{9,10},{23,3},{10,11},{0,4},{15,... | collective-permute-start | bytes 1769480 | tf_op jit(solution)/shard_map/ppermute | solution.py:43
  60.1 0.0 copy-done.1
  60.1 7.0 %product_8.1.refs_2_ = f32[2,2,384,768]{3,2,1,0:T(8,128)S(1)} custom-call(f32[2,2,384,768]{3,2,1,0:T(8,128)S(1)} %product_4.2.refs_0_, bf16[4,8,48,384]{3,2,1,0:T(8,128)(2,1)S(1)} %collective-permute-done.refs_1_, bf16[4,8,48,384]{3,2,1,0:T(8,128)(2,1)S(1)} %collective-permute-done.1.refs_2_, ...), custom_call_target="tpu_custom_call", output_to_operand_aliasing={{}: (0, {})} | custom-call | flops 3623878656 | bytes 9437184 | tf_op jit(solution)/shard_map/product_8/pallas_call | solution.py:261
  67.0 0.0 collective-permute-done.6.refs_8_
  67.1 0.5 collective-permute-done.4.refs_3_
  67.6 1.6 %collective-permute-done.5.refs_4_ = bf16[2,8,48,384]{3,2,1,0:T(8,128)(2,1)S(1)} collective-permute-done((bf16[2,8,48,384]{3,2,1,0:T(8,128)(2,1)S(1)}, bf16[2,8,48,384]{3,2,1,0:T(8,128)(2,1)S(1)}, u32[]{:S(2)}, u32[]{:S(2)}) %collective-permute-start.5) | collective-permute-done | bytes 589856 | tf_op jit(solution)/shard_map/ppermute | solution.py:43
  69.2 0.0 copy-done.2
  69.2 8.6 %product_4.3 = (f32[16,48,384]{2,1,0:T(8,128)S(1)}, bf16[16,48,384]{2,1,0:T(8,128)(2,1)S(1)}) custom-call(s32[96]{0:T(128)S(1)} %pad_add_fusion.refs_0_, s32[24]{0:T(128)S(1)} %copy-done.2, f32[2,2,384,768]{3,2,1,0:T(8,128)S(1)} %product_8.1.refs_2_, bf16[2,8,48,384]{3,2,1,0:T(8,128)(2,1)S(1)} %collective-permute-done.4.refs_3_, ...), custom_call_target="tpu_custom_call" | custom-call | flops 1811939328 | bytes 4718592 | tf_op jit(solution)/shard_map/product_4/pallas_call | solution.py:261
  77.8 0.1 collective-permute-start.7
  77.9 2.0 %collective-permute-done.7 = bf16[16,48,384]{2,1,0:T(8,128)(2,1)S(1)} collective-permute-done((bf16[16,48,384]{2,1,0:T(8,128)(2,1)S(1)}, bf16[16,48,384]{2,1,0:T(8,128)(2,1)S(1)}, u32[]{:S(2)}, u32[]{:S(2)}) %collective-permute-start.7) | collective-permute-done | bytes 589856 | tf_op jit(solution)/shard_map/ppermute | solution.py:33
  79.9 0.9 add_convert_fusion
  80.8 0.0 copy-start.3
  80.8 3.7 %all-to-all-start.2 = ((bf16[16,48,384]{2,1,0:T(8,128)(2,1)}), bf16[16,48,384]{2,1,0:T(8,128)(2,1)S(1)}, u32[]{:S(2)}, u32[]{:S(2)}) async-start(bf16[16,48,384]{2,1,0:T(8,128)(2,1)} %add_convert_fusion), calls=%async_computation.2 | async-start | bytes 1179648 | tf_op jit(solution)/shard_map/all_to_all | solution.py:47
  84.6 0.0 copy-done.3
  84.6 0.1 select_reduce_fusion
  84.7 21.2 %all-to-all-done.2 = bf16[16,48,384]{2,1,0:T(8,128)(2,1)S(1)} async-done(((bf16[16,48,384]{2,1,0:T(8,128)(2,1)}), bf16[16,48,384]{2,1,0:T(8,128)(2,1)S(1)}, u32[]{:S(2)}, u32[]{:S(2)}) %all-to-all-start.2) | async-done | bytes 589856 | tf_op jit(solution)/shard_map/all_to_all | solution.py:47
  105.9 0.1 convert_reduce_fusion
  105.9 0.7 broadcast_select_fusion
  (3 shorter events, 0.0 us)
Async XLA Ops:
  0.0 44.4 %collective-permute-start.2 = (bf16[2,384,3072]{2,1,0:T(8,128)(2,1)}, bf16[2,384,3072]{2,1,0:T(8,128)(2,1)}, u32[]{:S(2)}, u32[]{:S(2)}) collective-permute-start(bf16[2,384,3072]{2,1,0:T(8,128)(2,1)} %refs_5_.1), channel_id=1, source_target_pairs={{8,0},{0,8},{9,1},{1,9},{10,2},{2,10},{11,3},{3,11},{12,4},{4,12},... | collective-permute-start | bytes 14155784 | tf_op jit(solution)/shard_map/ppermute | solution.py:33
  37.4 16.5 %collective-permute-start = (bf16[4,8,48,384]{3,2,1,0:T(8,128)(2,1)S(1)}, bf16[4,8,48,384]{3,2,1,0:T(8,128)(2,1)S(1)}, u32[]{:S(2)}, u32[]{:S(2)}) collective-permute-start(bf16[4,8,48,384]{3,2,1,0:T(8,128)(2,1)S(1)} %all_to_all.16.refs_0_), channel_id=1, source_target_pairs={{4,0},{9,8},{5,1},{10,9},{6,2},{11,10},{7,3},{8,11},{16,4},{13,12}... | collective-permute-start | bytes 3538952 | tf_op jit(solution)/shard_map/ppermute | solution.py:43
  40.2 17.4 %collective-permute-start.1 = (bf16[4,8,48,384]{3,2,1,0:T(8,128)(2,1)S(1)}, bf16[4,8,48,384]{3,2,1,0:T(8,128)(2,1)S(1)}, u32[]{:S(2)}, u32[]{:S(2)}) collective-permute-start(bf16[4,8,48,384]{3,2,1,0:T(8,128)(2,1)S(1)} %all_to_all.16.refs_0_), channel_id=1, source_target_pairs={{20,0},{11,8},{21,1},{8,9},{22,2},{9,10},{23,3},{10,11},{0,4},{15,... | collective-permute-start | bytes 3538952 | tf_op jit(solution)/shard_map/ppermute | solution.py:43
  40.2 26.9 %collective-permute-start.6 = (bf16[2,12,2,128,128]{4,3,2,1,0:T(8,128)(2,1)}, bf16[2,12,2,128,128]{4,3,2,1,0:T(8,128)(2,1)}, u32[]{:S(2)}, u32[]{:S(2)}) collective-permute-start(bf16[2,12,2,128,128]{4,3,2,1,0:T(8,128)(2,1)} %refs_7_.1), channel_id=1, source_target_pairs={{8,0},{0,8},{9,1},{1,9},{10,2},{2,10},{11,3},{3,11},{12,4},{4,12},... | collective-permute-start | bytes 4718600 | tf_op jit(solution)/shard_map/ppermute | solution.py:33
  41.6 2.1 %collective-permute-start.3 = (s32[48]{0:T(128)}, s32[48]{0:T(128)S(1)}, u32[]{:S(2)}, u32[]{:S(2)}) collective-permute-start(s32[48]{0:T(128)} %reshape.47), channel_id=1, source_target_pairs={{8,0},{0,8},{9,1},{1,9},{10,2},{2,10},{11,3},{3,11},{12,4},{4,12},... | collective-permute-start | bytes 584 | tf_op jit(solution)/shard_map/ppermute | solution.py:33
  44.4 2.3 %copy-start = (bf16[2,384,3072]{2,1,0:T(8,128)(2,1)S(1)}, bf16[2,384,3072]{2,1,0:T(8,128)(2,1)}, u32[]{:S(2)}) copy-start(bf16[2,384,3072]{2,1,0:T(8,128)(2,1)} %refs_5_.1) | copy-start | bytes 14155780
  46.7 13.3 %copy-start.1 = (bf16[2,384,3072]{2,1,0:T(8,128)(2,1)S(1)}, bf16[2,384,3072]{2,1,0:T(8,128)(2,1)}, u32[]{:S(2)}) copy-start(bf16[2,384,3072]{2,1,0:T(8,128)(2,1)} %refs_5_.1) | copy-start | bytes 14155780
  57.6 10.0 %collective-permute-start.4 = (bf16[2,8,48,384]{3,2,1,0:T(8,128)(2,1)S(1)}, bf16[2,8,48,384]{3,2,1,0:T(8,128)(2,1)S(1)}, u32[]{:S(2)}, u32[]{:S(2)}) collective-permute-start(bf16[2,8,48,384]{3,2,1,0:T(8,128)(2,1)S(1)} %slice.6), channel_id=1, source_target_pairs={{4,0},{9,8},{5,1},{10,9},{6,2},{11,10},{7,3},{8,11},{16,4},{13,12}... | collective-permute-start | bytes 1769480 | tf_op jit(solution)/shard_map/ppermute | solution.py:43
  57.8 11.4 %copy-start.2 = (s32[24]{0:T(128)S(1)}, s32[24]{0:T(128)}, u32[]{:S(2)}) copy-start(s32[24]{0:T(128)} %refs_1_.3) | copy-start | bytes 292
  57.8 11.4 %collective-permute-start.5 = (bf16[2,8,48,384]{3,2,1,0:T(8,128)(2,1)S(1)}, bf16[2,8,48,384]{3,2,1,0:T(8,128)(2,1)S(1)}, u32[]{:S(2)}, u32[]{:S(2)}) collective-permute-start(bf16[2,8,48,384]{3,2,1,0:T(8,128)(2,1)S(1)} %slice.7), channel_id=1, source_target_pairs={{20,0},{11,8},{21,1},{8,9},{22,2},{9,10},{23,3},{10,11},{0,4},{15,... | collective-permute-start | bytes 1769480 | tf_op jit(solution)/shard_map/ppermute | solution.py:43
  77.8 2.1 %collective-permute-start.7 = (bf16[16,48,384]{2,1,0:T(8,128)(2,1)S(1)}, bf16[16,48,384]{2,1,0:T(8,128)(2,1)S(1)}, u32[]{:S(2)}, u32[]{:S(2)}) collective-permute-start(bf16[16,48,384]{2,1,0:T(8,128)(2,1)S(1)} %get-tuple-element.16), channel_id=1, source_target_pairs={{8,0},{0,8},{9,1},{1,9},{10,2},{2,10},{11,3},{3,11},{12,4},{4,12},... | collective-permute-start | bytes 1769480 | tf_op jit(solution)/shard_map/ppermute | solution.py:33
  80.8 3.7 %copy-start.3 = (s32[12]{0:T(128)S(1)}, s32[12]{0:T(128)}, u32[]{:S(2)}) copy-start(s32[12]{0:T(128)} %left_ref.1) | copy-start | bytes 148
  80.8 25.0 %all-to-all-start.2 = ((bf16[16,48,384]{2,1,0:T(8,128)(2,1)}), bf16[16,48,384]{2,1,0:T(8,128)(2,1)S(1)}, u32[]{:S(2)}, u32[]{:S(2)}) async-start(bf16[16,48,384]{2,1,0:T(8,128)(2,1)} %add_convert_fusion), calls=%async_computation.2 | async-start | bytes 1179648 | tf_op jit(solution)/shard_map/all_to_all | solution.py:47

commit v4 on v3

v4 whole, which is shorter than its diff:
```python
import functools

import jax
import jax.numpy as jnp
from jax import lax
from jax.experimental import pallas as pl
from jax.experimental.pallas import tpu as pltpu
from jax.sharding import PartitionSpec as P

BLK = 128
NZ, NXH, NC, NXL, NY = 8, 2, 2, 2, 4
NX = NXH * NXL
RING = 4
AXES = ("pair", "panel")
VMEM_LIMIT = 32 * 1024 * 1024
SMEM_SPEC = pl.BlockSpec(memory_space=pltpu.SMEM)
VMEM_SPEC = pl.BlockSpec(memory_space=pltpu.VMEM)
HBM_SPEC = pl.BlockSpec(memory_space=pltpu.HBM)


def flat(z, x, y, core):
    pair = (z * NXH + x // NXL) * NC + core
    return pair * (NXL * NY) + (x % NXL) * NY + y


def everywhere():
    return [
        (z, x, y, core) for z in range(NZ) for x in range(NX) for y in range(NY) for core in range(NC)
    ]


def core_swap(value):
    return lax.ppermute(
        value, AXES, [(flat(z, x, y, 1 - c), flat(z, x, y, c)) for z, x, y, c in everywhere()]
    )


def last_shift(value, step):
    perm = []
    for z, x, y, c in everywhere():
        source = flat(z, (x + step) % NX, y, c) if c == 0 else flat(z, x, (y + step) % NY, c)
        perm.append((source, flat(z, x, y, c)))
    return lax.ppermute(value, AXES, perm)


def exchange(copies, groups):
    return lax.all_to_all(
        copies, AXES, split_axis=0, concat_axis=0, axis_index_groups=groups, tiled=True
    )


def z_groups():
    return [
        [flat(z, x, y, c) for z in range(NZ)] for x in range(NX) for y in range(NY) for c in range(NC)
    ]


def middle_groups():
    along_y = [[flat(z, x, y, 0) for y in range(NY)] for z in range(NZ) for x in range(NX)]
    along_x = [[flat(z, x, y, 1) for x in range(NX)] for z in range(NZ) for y in range(NY)]
    return along_y + along_x


def position():
    pair, panel = lax.axis_index("pair"), lax.axis_index("panel")
    return pair // (NXH * NC), (pair // NC) % NXH, pair % NC, panel // NY, panel % NY


def mask_kernel(left_ref, right_ref, psi_ref, out_ref):
    rows, cols = psi_ref.shape
    base = lax.axis_index("pair") * rows
    panel = lax.axis_index("panel")
    first = base // BLK
    second = jnp.minimum(first + 1, left_ref.shape[0] - 1)
    index = base + lax.broadcasted_iota(jnp.int32, (rows, BLK), 0)
    limit = jnp.where(
        index < (first + 1) * BLK, first * BLK + left_ref[first], (first + 1) * BLK + left_ref[second]
    )
    row_live = index < limit
    lane = lax.broadcasted_iota(jnp.int32, (rows, BLK), 1)
    for block in range(cols // BLK):
        live = row_live & (lane < right_ref[panel * (cols // BLK) + block])
        span = slice(block * BLK, (block + 1) * BLK)
        value = psi_ref[:, span].astype(jnp.float32)
        value = jnp.where(live, value, 0.0).astype(out_ref.dtype)
        for copy in range(out_ref.shape[0]):
            out_ref[copy, :, span] = value


def mask_psi(left_sizes, right_sizes, psi):
    return pl.pallas_call(
        mask_kernel,
        out_shape=jax.ShapeDtypeStruct((NZ,) + psi.shape, psi.dtype),
        in_specs=[SMEM_SPEC, SMEM_SPEC, VMEM_SPEC],
        out_specs=VMEM_SPEC,
        name="mask_psi",
    )(left_sizes, right_sizes, psi)


def plan_kernel(own_ref, other_ref, slots_ref, rows_ref, next_ref):
    shape = own_ref.shape
    count = own_ref.size
    slots = [
        (side, pair, block, s)
        for side in range(2)
        for pair in range(shape[0])
        for block in range(shape[1])
        for s in range(shape[2])
    ]

    def row_of(slot):
        return (own_ref, other_ref)[slot[0]][slot[1], slot[2], slot[3]]

    for place in range(slots_ref.shape[0]):
        slots_ref[place] = 2 * count
    for place in range(rows_ref.shape[0]):
        rows_ref[place] = 0
    for row in range(shape[1]):
        next_ref[row] = 0
    for slot in slots:
        row = row_of(slot)
        next_ref[row] = next_ref[row] + 1
    start = jnp.int32(0)
    for row in range(shape[1]):
        pairs = (next_ref[row] + 1) // 2
        next_ref[row] = 2 * start

        @pl.loop(0, pairs)
        def _(i):
            rows_ref[start + i] = row

        start = start + pairs
    for number, slot in enumerate(slots):
        row = row_of(slot)
        place = next_ref[row]
        slots_ref[place] = number
        next_ref[row] = place + 1


def plan(own, other):
    pairs = own.size + own.shape[1] // 2
    return pl.pallas_call(
        plan_kernel,
        out_shape=(
            jax.ShapeDtypeStruct((2 * pairs,), jnp.int32),
            jax.ShapeDtypeStruct((pairs,), jnp.int32),
        ),
        in_specs=[SMEM_SPEC, SMEM_SPEC],
        out_specs=(SMEM_SPEC, SMEM_SPEC),
        scratch_shapes=[pltpu.SMEM((own.shape[1],), jnp.int32)],
        name="plan",
    )(own, other)


def two_specs(steps, counts):
    return [
        (number, spot, step, start + spot)
        for number, ((step, start), count) in enumerate(zip(steps, counts))
        for spot in range(0, count, 2)
    ]


def two_copies(twos, right, buffer, sem):
    _, xh, core, xl, y = position()
    x = xh * NXL + xl
    cols = right[0].shape[1]
    copies, halves = [], []
    for index, (_, _, step, place) in enumerate(twos):
        far_x, far_y = lax.rem(x + step, NX), lax.rem(y + step, NY)
        copies.append([])
        for way in range(2):
            unit_x = jnp.where(core == 0, far_x, place + way)
            unit_y = jnp.where(core == 0, place + way, far_y)
            column = pl.multiple_of((lax.rem(unit_x, NXL) * NY + unit_y) * cols, BLK)
            for side in range(2):
                copies[-1].append(
                    pltpu.make_async_copy(
                        right[side].at[:, :, pl.ds(column, cols)],
                        buffer.at[index, side, :, :, pl.ds(way * cols, cols)],
                        sem.at[index, side, way],
                    )
                )
        halves.append(unit_x // NXL)
    return copies, halves


def wide(array, spot):
    rows = array.shape[1] * array.shape[2]
    return jnp.concatenate([array[spot + way].reshape(rows, array.shape[3]) for way in range(2)], axis=1)


def times(left_side, right_side):
    return lax.dot_general(
        left_side, right_side, (((1,), (1,)), ((), ())), preferred_element_type=jnp.float32
    )


def operator(buffer, index, side):
    return buffer[index, side].reshape(buffer.shape[2] * buffer.shape[3], buffer.shape[4])


def sums_kernel(steps, ahead, *refs):
    refs = list(refs)
    acc_in = refs.pop(0) if ahead else None
    arrays = [refs.pop(0) for _ in steps]
    right = (refs.pop(0), refs.pop(0))
    left = (refs.pop(0), refs.pop(0)) if ahead else None
    acc = refs.pop(0)
    if ahead:
        far_ref, left_ref = refs.pop(0), refs.pop(0)
        far_sem, left_sem = refs.pop(), refs.pop()
    rbuf, sem = refs
    twos = two_specs(steps, [array.shape[0] for array in arrays])
    copies, halves = two_copies(twos, right, rbuf, sem)
    later = []
    if ahead:
        later = sum(two_copies(two_specs(ahead, [RING // 2] * 2), right, far_ref, far_sem)[0], [])
        count = left[0].shape[0]
        for side in range(2):
            later.append(
                pltpu.make_async_copy(
                    left[side], left_ref.at[pl.ds(side * count, count)], left_sem.at[side]
                )
            )
        left_ref[2 * count] = jnp.zeros(left_ref.shape[1:], left_ref.dtype)
    for copy in sum(copies, []) + later:
        copy.start()
    acc[...] = acc_in[...] if ahead else jnp.zeros_like(acc)
    for index, (number, spot, _, _) in enumerate(twos):
        for copy in copies[index]:
            copy.wait()

        @pl.loop(0, 2)
        def _(side):
            acc[halves[index], side] += times(wide(arrays[number], spot), operator(rbuf, index, side))

    for copy in later:
        copy.wait()


def sums(acc, pieces, right, left=None, ahead=()):
    arrays = [array for array, _, _ in pieces]
    steps = tuple((step, start) for _, step, start in pieces)
    group, cols = arrays[0].shape[2:]
    pairs = right[0].shape[0]
    units = sum(array.shape[0] for array in arrays)
    out_shape = [jax.ShapeDtypeStruct((NXH, 2, NZ * group, pairs * cols), jnp.float32)]
    scratch = [
        pltpu.VMEM((units // 2, 2, pairs, cols, 2 * cols), jnp.bfloat16),
        pltpu.SemaphoreType.DMA((units // 2, 2, 2)),
    ]
    near, away = arrays, list(right)
    if ahead:
        near, away = [acc] + arrays, list(right) + list(left)
        out_shape += [
            jax.ShapeDtypeStruct((2, 2, pairs, cols, 2 * cols), jnp.bfloat16),
            jax.ShapeDtypeStruct((2 * left[0].shape[0] + 1,) + left[0].shape[1:], jnp.bfloat16),
        ]
        scratch += [pltpu.SemaphoreType.DMA((2,)), pltpu.SemaphoreType.DMA((2, 2, 2))]
    return pl.pallas_call(
        functools.partial(sums_kernel, steps, ahead),
        out_shape=out_shape,
        in_specs=[VMEM_SPEC] * len(near) + [HBM_SPEC] * len(away),
        out_specs=[VMEM_SPEC] * len(out_shape),
        scratch_shapes=scratch,
        input_output_aliases={0: 0} if ahead else {},
        compiler_params=pltpu.CompilerParams(vmem_limit_bytes=VMEM_LIMIT),
        cost_estimate=pl.CostEstimate(
            flops=2 * units * 2 * pairs * NZ * group * cols * cols,
            bytes_accessed=units * 2 * pairs * cols * cols * 2,
            transcendentals=0,
        ),
        name=f"sums_{units}",
    )(*near, *away)


UNROLL = 6


def terms_kernel(steps, slots_ref, rows_ref, right_ref, acc, low, high, far_ref, left_ref, *refs):
    keep_ref, send_ref, part, total = refs
    _, xh, core, xl, y = position()
    arrays = (low, high)
    group, cols = low.shape[2:]
    pairs = far_ref.shape[2]
    twos = two_specs(steps, [array.shape[0] for array in arrays])
    lane = lax.broadcasted_iota(jnp.int32, (1, BLK), 1)
    start = (xl * NY + y) * (cols // BLK)
    live = jnp.concatenate(
        [(lane < right_ref[start + i]).astype(jnp.float32) for i in range(cols // BLK)], axis=1
    )
    height = total.shape[0]
    total[...] = jnp.zeros_like(total)
    for pair in range(2 * pairs):
        for q in range(NZ * NXH):
            at = pl.multiple_of(pair * height + (q * NC + 1 - core) * group, 16)
            part[pl.ds(at, group), :] = jnp.zeros((group, cols), part.dtype)

    def place(half, side, values):
        for pair in range(pairs):
            rounded = (values[:, pair * cols : (pair + 1) * cols] * live).astype(part.dtype)
            for dz in range(NZ):
                at = (side * pairs + pair) * height + ((dz * NXH + half) * NC + core) * group
                part[pl.ds(pl.multiple_of(at, 16), group), :] = rounded[dz * group : (dz + 1) * group]

    @pl.loop(0, 2)
    def _(side):
        @pl.when(core == 0)
        def _():
            far = 1 - xh
            place(xh, side, acc[xh, side])
            left_side = jnp.concatenate([wide(arrays[n], spot) for n, spot, _, _ in twos], axis=1)
            right_side = jnp.concatenate([operator(far_ref, i, side) for i in range(len(twos))], axis=1)
            place(far, side, acc[far, side] + times(left_side, right_side))

        @pl.when(core == 1)
        def _():
            for index, (n, spot, _, middle) in enumerate(twos):
                half = middle // NXL
                place(half, side, acc[half, side] + times(wide(arrays[n], spot), operator(far_ref, index, side)))

    last_block = 2 * pairs * height // BLK - 1

    @pl.loop(0, rows_ref.shape[0] // UNROLL)
    def _(step):
        for turn in range(UNROLL):
            number = step * UNROLL + turn
            slots = [slots_ref[2 * number + way] for way in range(2)]
            blocks = [jnp.minimum(slot // 2, last_block) for slot in slots]
            result = jnp.dot(
                jnp.concatenate([left_ref[slot] for slot in slots], axis=1),
                jnp.concatenate(
                    [part[pl.ds(pl.multiple_of(block * BLK, BLK), BLK), :] for block in blocks], axis=0
                ),
                preferred_element_type=jnp.float32,
            )
            total[pl.ds(pl.multiple_of(rows_ref[number] * BLK, BLK), BLK), :] += result

    for q in range(NZ * NXH):
        mine = pl.multiple_of((q * NC + core) * group, 16)
        theirs = pl.multiple_of((q * NC + 1 - core) * group, 16)
        keep_ref[q] = total[pl.ds(mine, group), :]
        send_ref[q] = total[pl.ds(theirs, group), :].astype(send_ref.dtype)


def terms(steps, slots, rows, right_sizes, acc, low, high, far, left):
    group, cols = low.shape[2:]
    height = NZ * NXH * NC * group
    pairs = 2 * far.shape[2]
    assert rows.shape[0] % UNROLL == 0
    return pl.pallas_call(
        functools.partial(terms_kernel, steps),
        out_shape=(
            jax.ShapeDtypeStruct((NZ * NXH, group, cols), jnp.float32),
            jax.ShapeDtypeStruct((NZ * NXH, group, cols), jnp.bfloat16),
        ),
        in_specs=[SMEM_SPEC] * 3 + [VMEM_SPEC] * 5,
        out_specs=(VMEM_SPEC, VMEM_SPEC),
        scratch_shapes=[
            pltpu.VMEM((pairs * height, cols), jnp.bfloat16),
            pltpu.VMEM((height, cols), jnp.float32),
        ],
        compiler_params=pltpu.CompilerParams(vmem_limit_bytes=VMEM_LIMIT),
        name="terms",
    )(slots, rows, right_sizes, acc, low, high, far, left)


def local(psi, left_ops, a_rows, right_ops, left_sizes, right_sizes):
    rows_dev = psi.shape[0]
    pair = lax.axis_index("pair")
    copies = mask_psi(left_sizes, right_sizes, psi)
    right = (right_ops, core_swap(right_ops))
    flat_left = left_ops.reshape((-1, BLK, BLK))
    left = (flat_left, core_swap(flat_left))
    slots, rows = plan(a_rows, core_swap(a_rows))

    along_z = exchange(copies, z_groups())
    near = exchange(jnp.broadcast_to(along_z[None], (RING,) + along_z.shape), middle_groups())
    plus = last_shift(near, 1)
    minus = last_shift(near, -1)
    (acc,) = sums(None, [(near, 0, 0)], right)
    half = RING // 2
    plus, minus, acc, slots, rows = lax.optimization_barrier((plus, minus, acc, slots, rows))
    far_low = last_shift(plus[:half], 1)
    far_high = last_shift(minus[half:], -1)
    last_steps = ((2, 0), (2, half))
    acc, far, both = sums(acc, [(plus, 1, 0), (minus, 3, 0)], right, left, last_steps)
    keep, send = terms(last_steps, slots, rows, right_sizes, acc, far_low, far_high, far, both)
    mine = (keep + core_swap(send).astype(jnp.float32)).astype(jnp.bfloat16)
    groups = [
        [flat(z, xh * NXL + xl, y, c) for z in range(NZ) for xh in range(NXH)]
        for c in range(NC)
        for xl in range(NXL)
        for y in range(NY)
    ]
    parts = exchange(mine, groups)
    summed = parts.astype(jnp.float32).sum(axis=0)
    index = pair * rows_dev + jnp.arange(rows_dev, dtype=jnp.int32)
    blocks = jnp.arange(left_sizes.shape[0], dtype=jnp.int32)
    limit = jnp.sum(jnp.where(index[:, None] // BLK == blocks, left_sizes + blocks * BLK, 0), axis=1)
    return jnp.where((index < limit)[:, None], summed, 0.0)


def solution(mesh):
    placed = (
        P("pair", "panel"),
        P("pair", None, None, None, None),
        P("pair", None, None),
        P("pair", "panel", None),
        P(),
        P(),
    )
    return jax.shard_map(
        local, mesh=mesh, in_specs=placed, out_specs=P("pair", "panel"), check_vma=False
    )
```

time: 108 us -> 109 us (level)
  blocking collectives: 35.7 us -> 21.7 us
  waiting for transfers between devices: 33.4 us -> 40.6 us
  starting transfers between devices: 9.43 us -> 13.8 us
  Pallas kernels: 21.5 us -> 24 us
  local copies, waits for them, and re-layouts: 3.96 us -> 5.36 us
    all_to_all x2 -> x1, blocking collectives: 35.7 us -> 21.7 us  [exchange(): lax.all_to_all(copies, AXES, split_axis=0, concat_axis=0, axis_index_grou...]
    all_to_all x1 -> x2, waiting for transfers between devices: 21.2 us -> 30.7 us  [exchange(): lax.all_to_all(copies, AXES, split_axis=0, concat_axis=0, axis_index_grou...]
    all_to_all x1 -> x2, starting transfers between devices: 3.71 us -> 8.53 us  [exchange(): lax.all_to_all(copies, AXES, split_axis=0, concat_axis=0, axis_index_grou...]
    pallas_call x3 -> x4, Pallas kernels: 19.9 us -> 22.4 us  [the longest x2 12.4 us: sums(): pl.pallas_call(functools.partial(sums_kernel, steps, ahead), out_shape=ou...]
    ppermute x4, waiting for transfers between devices: 8.6 us -> 6.74 us  [last_shift(): return lax.ppermute(value, AXES, perm)]
    unnamed x9 -> x17, local copies, waits for them, and re-layouts: 3.13 us -> 3.06 us
  transfers between devices with their start and end apart: 9 -> 10, of which waited for: 7 -> 7; matrix products, arithmetic and copies ran while one was open for 2% -> 2% of each run, Pallas kernels for 12% -> 16%
where the time goes in v4:
time: 109 us; the launch traced here: 107 us
  waiting for transfers between devices  40.6 us (37%)
  Pallas kernels  24 us (22%)
  blocking collectives  21.7 us (20%)
  starting transfers between devices  13.8 us (13%)
  local copies, waits for them, and re-layouts  5.36 us (5%)
  other arithmetic  1.85 us (2%)
    all_to_all x2, waiting for transfers between devices, exchange(): lax.all_to_all(copies, AXES, split_axis=0, concat_axis=0, axis_index_grou...  30.7 us
    all_to_all x1, blocking collectives, exchange(): lax.all_to_all(copies, AXES, split_axis=0, concat_axis=0, axis_index_grou...  21.7 us
    pallas_call x2, Pallas kernels, sums(): pl.pallas_call(functools.partial(sums_kernel, steps, ahead), out_shape=ou...  12.4 us
    all_to_all x2, starting transfers between devices, exchange(): lax.all_to_all(copies, AXES, split_axis=0, concat_axis=0, axis_index_grou...  8.53 us
    pallas_call x1, Pallas kernels, terms(): pl.pallas_call(functools.partial(terms_kernel, steps), out_shape=(jax.Sha...  6.89 us
    ppermute x4, waiting for transfers between devices, last_shift(): return lax.ppermute(value, AXES, perm)  6.74 us
    ppermute x4, starting transfers between devices, last_shift(): return lax.ppermute(value, AXES, perm)  5.11 us
    ppermute x4, waiting for transfers between devices, core_swap(): lax.ppermute(value, AXES, [(flat(z, x, y, 1 - c), flat(z, x, y, c)) for z...  3.15 us
  transfers between devices with their start and end apart: 10, of which 7 were waited for; matrix products, arithmetic and copies ran while one was open for 2% of the time, Pallas kernels for 16%

profile of v4, /device:TPU:24, one launch (start us, length us, event | category | flops | bytes accessed | tf_op | source)
XLA Modules:
  0.0 107.5 jit_solution(16556533972449341041)
XLA Ops:
  0.0 0.0 collective-permute-start.2
  0.0 1.6 %mask_psi.1 = bf16[8,48,384]{2,1,0:T(8,128)(2,1)} custom-call(s32[12]{0:T(128)} %left_ref.1, s32[24]{0:T(128)} %right_ref.3, bf16[48,384]{1,0:T(8,128)(2,1)} %psi_ref.1), custom_call_target="tpu_custom_call" | custom-call | tf_op jit(solution)/shard_map/mask_psi/pallas_call | solution.py:91
  1.6 21.7 %all_to_all.15 = bf16[8,48,384]{2,1,0:T(8,128)(2,1)S(1)} all-to-all(bf16[8,48,384]{2,1,0:T(8,128)(2,1)} %mask_psi.1), channel_id=1, replica_groups={{0,32,64,96,128,160,192,224},{8,40,72,104,136,168,200,232},{1,33,65,97,..., dimensions={0} | all-to-all | bytes 589824 | tf_op jit(solution)/shard_map/all_to_all | solution.py:47
  23.3 1.1 %broadcast_in_dim.32 = bf16[4,8,48,384]{3,2,1,0:T(8,128)(2,1)} broadcast(bf16[8,48,384]{2,1,0:T(8,128)(2,1)S(1)} %all_to_all.15), dimensions={1,2,3} | broadcast | bytes 1474560 | tf_op jit(solution)/shard_map/broadcast_in_dim | solution.py:378
  24.4 0.0 copy-start.6
  24.4 4.8 %all-to-all-start.1 = ((bf16[4,8,48,384]{3,2,1,0:T(8,128)(2,1)}), bf16[4,8,48,384]{3,2,1,0:T(8,128)(2,1)S(1)}, u32[]{:S(2)}, u32[]{:S(2)}) async-start(bf16[4,8,48,384]{3,2,1,0:T(8,128)(2,1)} %broadcast_in_dim.32), calls=%async_computation.1 | async-start | bytes 2359296 | tf_op jit(solution)/shard_map/all_to_all | solution.py:47
  29.2 0.0 collective-permute-start.4
  29.2 9.5 %all-to-all-done.1.refs_0_ = bf16[4,8,48,384]{3,2,1,0:T(8,128)(2,1)S(1)} async-done(((bf16[4,8,48,384]{3,2,1,0:T(8,128)(2,1)}), bf16[4,8,48,384]{3,2,1,0:T(8,128)(2,1)S(1)}, u32[]{:S(2)}, u32[]{:S(2)}) %all-to-all-start.1) | async-done | bytes 1179680 | tf_op jit(solution)/shard_map/all_to_all | solution.py:47
  38.7 2.8 %collective-permute-start = (bf16[4,8,48,384]{3,2,1,0:T(8,128)(2,1)S(1)}, bf16[4,8,48,384]{3,2,1,0:T(8,128)(2,1)S(1)}, u32[]{:S(2)}, u32[]{:S(2)}) collective-permute-start(bf16[4,8,48,384]{3,2,1,0:T(8,128)(2,1)S(1)} %all-to-all-done.1.refs_0_), channel_id=1, source_target_pairs={{4,0},{9,8},{5,1},{10,9},{6,2},{11,10},{7,3},{8,11},{16,4},{13,12}... | collective-permute-start | bytes 3538952 | tf_op jit(solution)/shard_map/ppermute | solution.py:43
  41.5 0.0 collective-permute-start.1
  41.5 0.0 copy-done.6
  41.5 0.1 copy.11.own_ref
  41.6 0.0 copy-start.4
  41.6 0.1 collective-permute-start.3
  41.7 1.2 %collective-permute-done.3.other_ref = s32[2,12,2]{2,1,0:T(8,128)S(1)} collective-permute-done((s32[2,12,2]{2,1,0:T(8,128)S(1)}, s32[2,12,2]{2,1,0:T(8,128)S(1)}, u32[]{:S(2)}, u32[]{:S(2)}) %collective-permute-start.3) | collective-permute-done | bytes 224 | tf_op jit(solution)/shard_map/ppermute | solution.py:33
  42.9 0.0 copy-done.4
  42.9 0.0 copy-start.5
  42.9 0.6 copy-done.5
  43.5 3.1 %plan.1 = (s32[108]{0:T(128)}, s32[54]{0:T(128)}) custom-call(s32[2,12,2]{2,1,0:T(8,128)} %copy-done.4, s32[2,12,2]{2,1,0:T(8,128)} %copy-done.5), custom_call_target="tpu_custom_call" | custom-call | tf_op jit(solution)/shard_map/plan/pallas_call | solution.py:142
  46.5 0.0 collective-permute-done.2.refs_2_.refs_4_
  46.5 0.0 copy-start
  46.6 2.3 %copy-done = bf16[2,384,3072]{2,1,0:T(8,128)(2,1)S(1)} copy-done((bf16[2,384,3072]{2,1,0:T(8,128)(2,1)S(1)}, bf16[2,384,3072]{2,1,0:T(8,128)(2,1)}, u32[]{:S(2)}) %copy-start) | copy-done | bytes 4718616
  48.9 4.1 %sums_4.1.refs_0_ = f32[2,2,384,768]{3,2,1,0:T(8,128)S(1)} custom-call(bf16[4,8,48,384]{3,2,1,0:T(8,128)(2,1)S(1)} %all-to-all-done.1.refs_0_, bf16[2,384,3072]{2,1,0:T(8,128)(2,1)S(1)} %copy-done, bf16[2,384,3072]{2,1,0:T(8,128)(2,1)} %collective-permute-done.2.refs_2_.refs_4_), custom_call_target="tpu_custom_call" | custom-call | flops 1811939328 | bytes 4718592 | tf_op jit(solution)/shard_map/sums_4/pallas_call | solution.py:260
  53.0 2.3 %collective-permute-done.refs_1_ = bf16[4,8,48,384]{3,2,1,0:T(8,128)(2,1)S(1)} collective-permute-done((bf16[4,8,48,384]{3,2,1,0:T(8,128)(2,1)S(1)}, bf16[4,8,48,384]{3,2,1,0:T(8,128)(2,1)S(1)}, u32[]{:S(2)}, u32[]{:S(2)}) %collective-permute-start) | collective-permute-done | bytes 1179680 | tf_op jit(solution)/shard_map/ppermute | solution.py:43
  55.2 3.8 %collective-permute-done.1.refs_2_ = bf16[4,8,48,384]{3,2,1,0:T(8,128)(2,1)} collective-permute-done((bf16[4,8,48,384]{3,2,1,0:T(8,128)(2,1)S(1)}, bf16[4,8,48,384]{3,2,1,0:T(8,128)(2,1)}, u32[]{:S(2)}, u32[]{:S(2)}) %collective-permute-start.1) | collective-permute-done | bytes 1179680 | tf_op jit(solution)/shard_map/ppermute | solution.py:43
  59.0 0.1 slice.6
  59.1 0.1 collective-permute-start.5
  59.2 1.1 %slice.7 = bf16[2,8,48,384]{3,2,1,0:T(8,128)(2,1)S(1)} slice(bf16[4,8,48,384]{3,2,1,0:T(8,128)(2,1)} %collective-permute-done.1.refs_2_), slice={[2:4], [0:8], [0:48], [0:384]} | slice | bytes 1179648 | tf_op jit(solution)/shard_map/slice | solution.py:385
  60.3 0.0 copy-start.1
  60.3 0.0 copy-start.2
  60.3 0.0 copy-start.3
  60.3 2.3 %collective-permute-start.6 = (bf16[2,8,48,384]{3,2,1,0:T(8,128)(2,1)S(1)}, bf16[2,8,48,384]{3,2,1,0:T(8,128)(2,1)S(1)}, u32[]{:S(2)}, u32[]{:S(2)}) collective-permute-start(bf16[2,8,48,384]{3,2,1,0:T(8,128)(2,1)S(1)} %slice.7), channel_id=1, source_target_pairs={{20,0},{11,8},{21,1},{8,9},{22,2},{9,10},{23,3},{10,11},{0,4},{15,... | collective-permute-start | bytes 1769480 | tf_op jit(solution)/shard_map/ppermute | solution.py:43
  62.6 0.0 collective-permute-done.4.refs_6_
  62.6 8.4 %sums_8.1 = (f32[2,2,384,768]{3,2,1,0:T(8,128)S(1)}, bf16[2,2,2,384,768]{4,3,2,1,0:T(8,128)(2,1)S(1)}, bf16[97,128,128]{2,1,0:T(8,128)(2,1)S(1)}) custom-call(f32[2,2,384,768]{3,2,1,0:T(8,128)S(1)} %sums_4.1.refs_0_, bf16[4,8,48,384]{3,2,1,0:T(8,128)(2,1)S(1)} %collective-permute-done.refs_1_, ...), custom_call_target="tpu_custom_call", output_to_operand_aliasing={{0}: (0, {})} | custom-call | flops 3623878656 | bytes 9437184 | tf_op jit(solution)/shard_map/sums_8/pallas_call | solution.py:260
  71.0 0.0 collective-permute-done.5.low
  71.0 0.7 collective-permute-done.6.high
  71.7 0.0 copy-done.1
  71.7 0.0 copy-done.2
  71.7 0.0 copy-done.3
  71.7 6.9 %terms.1 = (f32[16,48,384]{2,1,0:T(8,128)S(1)}, bf16[16,48,384]{2,1,0:T(8,128)(2,1)S(1)}) custom-call(s32[108]{0:T(128)S(1)} %copy-done.2, s32[54]{0:T(128)S(1)} %copy-done.3, s32[24]{0:T(128)S(1)} %copy-done.1, f32[2,2,384,768]{3,2,1,0:T(8,128)S(1)} %get-tuple-element.24.acc, bf16[2,8,48,384]{3,2,1,0:T(8,128)(2,1)S(1)} %collective-permute-done.5.low, ...), custom_call_target="tpu_custom_call" | custom-call | tf_op jit(solution)/shard_map/terms/pallas_call | solution.py:351
  78.6 0.1 collective-permute-start.7
  78.7 2.0 %collective-permute-done.7 = bf16[16,48,384]{2,1,0:T(8,128)(2,1)S(1)} collective-permute-done((bf16[16,48,384]{2,1,0:T(8,128)(2,1)S(1)}, bf16[16,48,384]{2,1,0:T(8,128)(2,1)S(1)}, u32[]{:S(2)}, u32[]{:S(2)}) %collective-permute-start.7) | collective-permute-done | bytes 589856 | tf_op jit(solution)/shard_map/ppermute | solution.py:33
  80.7 0.9 add_convert_fusion
  81.6 0.0 copy-start.7
  81.6 3.7 %all-to-all-start.2 = ((bf16[16,48,384]{2,1,0:T(8,128)(2,1)}), bf16[16,48,384]{2,1,0:T(8,128)(2,1)S(1)}, u32[]{:S(2)}, u32[]{:S(2)}) async-start(bf16[16,48,384]{2,1,0:T(8,128)(2,1)} %add_convert_fusion), calls=%async_computation.2 | async-start | bytes 1179648 | tf_op jit(solution)/shard_map/all_to_all | solution.py:47
  85.4 0.0 copy-done.7
  85.4 0.1 select_reduce_fusion
  85.5 21.2 %all-to-all-done.2 = bf16[16,48,384]{2,1,0:T(8,128)(2,1)S(1)} async-done(((bf16[16,48,384]{2,1,0:T(8,128)(2,1)}), bf16[16,48,384]{2,1,0:T(8,128)(2,1)S(1)}, u32[]{:S(2)}, u32[]{:S(2)}) %all-to-all-start.2) | async-done | bytes 589856 | tf_op jit(solution)/shard_map/all_to_all | solution.py:47
  106.7 0.1 convert_reduce_fusion
  106.8 0.7 broadcast_select_fusion
  (3 shorter events, 0.0 us)
Async XLA Ops:
  0.0 46.5 %collective-permute-start.2 = (bf16[2,384,3072]{2,1,0:T(8,128)(2,1)}, bf16[2,384,3072]{2,1,0:T(8,128)(2,1)}, u32[]{:S(2)}, u32[]{:S(2)}) collective-permute-start(bf16[2,384,3072]{2,1,0:T(8,128)(2,1)} %refs_3_.1), channel_id=1, source_target_pairs={{8,0},{0,8},{9,1},{1,9},{10,2},{2,10},{11,3},{3,11},{12,4},{4,12},... | collective-permute-start | bytes 14155784 | tf_op jit(solution)/shard_map/ppermute | solution.py:33
  24.4 17.1 %copy-start.6 = (s32[2,12,2]{1,2,0:T(2,128)S(1)}, s32[2,12,2]{1,2,0:T(2,128)}, u32[]{:S(2)}) copy-start(s32[2,12,2]{1,2,0:T(2,128)} %param.8) | copy-start | bytes 580
  24.4 14.3 %all-to-all-start.1 = ((bf16[4,8,48,384]{3,2,1,0:T(8,128)(2,1)}), bf16[4,8,48,384]{3,2,1,0:T(8,128)(2,1)S(1)}, u32[]{:S(2)}, u32[]{:S(2)}) async-start(bf16[4,8,48,384]{3,2,1,0:T(8,128)(2,1)} %broadcast_in_dim.32), calls=%async_computation.1 | async-start | bytes 2359296 | tf_op jit(solution)/shard_map/all_to_all | solution.py:47
  29.2 33.4 %collective-permute-start.4 = (bf16[48,128,128]{2,1,0:T(8,128)(2,1)}, bf16[48,128,128]{2,1,0:T(8,128)(2,1)}, u32[]{:S(2)}, u32[]{:S(2)}) collective-permute-start(bf16[48,128,128]{2,1,0:T(8,128)(2,1)} %bitcast.refs_5_), channel_id=1, source_target_pairs={{8,0},{0,8},{9,1},{1,9},{10,2},{2,10},{11,3},{3,11},{12,4},{4,12},... | collective-permute-start | bytes 4718600 | tf_op jit(solution)/shard_map/ppermute | solution.py:33
  38.7 16.5 %collective-permute-start = (bf16[4,8,48,384]{3,2,1,0:T(8,128)(2,1)S(1)}, bf16[4,8,48,384]{3,2,1,0:T(8,128)(2,1)S(1)}, u32[]{:S(2)}, u32[]{:S(2)}) collective-permute-start(bf16[4,8,48,384]{3,2,1,0:T(8,128)(2,1)S(1)} %all-to-all-done.1.refs_0_), channel_id=1, source_target_pairs={{4,0},{9,8},{5,1},{10,9},{6,2},{11,10},{7,3},{8,11},{16,4},{13,12}... | collective-permute-start | bytes 3538952 | tf_op jit(solution)/shard_map/ppermute | solution.py:43
  41.5 17.5 %collective-permute-start.1 = (bf16[4,8,48,384]{3,2,1,0:T(8,128)(2,1)S(1)}, bf16[4,8,48,384]{3,2,1,0:T(8,128)(2,1)}, u32[]{:S(2)}, u32[]{:S(2)}) collective-permute-start(bf16[4,8,48,384]{3,2,1,0:T(8,128)(2,1)S(1)} %all-to-all-done.1.refs_0_), channel_id=1, source_target_pairs={{20,0},{11,8},{21,1},{8,9},{22,2},{9,10},{23,3},{10,11},{0,4},{15,... | collective-permute-start | bytes 3538952 | tf_op jit(solution)/shard_map/ppermute | solution.py:43
  41.6 1.2 %copy-start.4 = (s32[2,12,2]{2,1,0:T(8,128)}, s32[2,12,2]{2,1,0:T(8,128)S(1)}, u32[]{:S(2)}) copy-start(s32[2,12,2]{2,1,0:T(8,128)S(1)} %copy.11.own_ref) | copy-start | bytes 580
  41.6 1.2 %collective-permute-start.3 = (s32[2,12,2]{2,1,0:T(8,128)S(1)}, s32[2,12,2]{2,1,0:T(8,128)S(1)}, u32[]{:S(2)}, u32[]{:S(2)}) collective-permute-start(s32[2,12,2]{2,1,0:T(8,128)S(1)} %copy.11.own_ref), channel_id=1, source_target_pairs={{8,0},{0,8},{9,1},{1,9},{10,2},{2,10},{11,3},{3,11},{12,4},{4,12},... | collective-permute-start | bytes 584 | tf_op jit(solution)/shard_map/ppermute | solution.py:33
  42.9 0.6 copy-start.5
  46.5 2.3 %copy-start = (bf16[2,384,3072]{2,1,0:T(8,128)(2,1)S(1)}, bf16[2,384,3072]{2,1,0:T(8,128)(2,1)}, u32[]{:S(2)}) copy-start(bf16[2,384,3072]{2,1,0:T(8,128)(2,1)} %refs_3_.1) | copy-start | bytes 14155780
  59.1 11.9 %collective-permute-start.5 = (bf16[2,8,48,384]{3,2,1,0:T(8,128)(2,1)S(1)}, bf16[2,8,48,384]{3,2,1,0:T(8,128)(2,1)S(1)}, u32[]{:S(2)}, u32[]{:S(2)}) collective-permute-start(bf16[2,8,48,384]{3,2,1,0:T(8,128)(2,1)S(1)} %slice.6), channel_id=1, source_target_pairs={{4,0},{9,8},{5,1},{10,9},{6,2},{11,10},{7,3},{8,11},{16,4},{13,12}... | collective-permute-start | bytes 1769480 | tf_op jit(solution)/shard_map/ppermute | solution.py:43
  60.3 11.4 %copy-start.1 = (s32[24]{0:T(128)S(1)}, s32[24]{0:T(128)}, u32[]{:S(2)}) copy-start(s32[24]{0:T(128)} %right_ref.3) | copy-start | bytes 292
  60.3 11.4 %copy-start.2 = (s32[108]{0:T(128)S(1)}, s32[108]{0:T(128)}, u32[]{:S(2)}) copy-start(s32[108]{0:T(128)} %get-tuple-element.19.slots_ref) | copy-start | bytes 1300
  60.3 11.4 %copy-start.3 = (s32[54]{0:T(128)S(1)}, s32[54]{0:T(128)}, u32[]{:S(2)}) copy-start(s32[54]{0:T(128)} %get-tuple-element.20.rows_ref) | copy-start | bytes 652
  60.3 11.4 %collective-permute-start.6 = (bf16[2,8,48,384]{3,2,1,0:T(8,128)(2,1)S(1)}, bf16[2,8,48,384]{3,2,1,0:T(8,128)(2,1)S(1)}, u32[]{:S(2)}, u32[]{:S(2)}) collective-permute-start(bf16[2,8,48,384]{3,2,1,0:T(8,128)(2,1)S(1)} %slice.7), channel_id=1, source_target_pairs={{20,0},{11,8},{21,1},{8,9},{22,2},{9,10},{23,3},{10,11},{0,4},{15,... | collective-permute-start | bytes 1769480 | tf_op jit(solution)/shard_map/ppermute | solution.py:43
  78.6 2.1 %collective-permute-start.7 = (bf16[16,48,384]{2,1,0:T(8,128)(2,1)S(1)}, bf16[16,48,384]{2,1,0:T(8,128)(2,1)S(1)}, u32[]{:S(2)}, u32[]{:S(2)}) collective-permute-start(bf16[16,48,384]{2,1,0:T(8,128)(2,1)S(1)} %get-tuple-element.28), channel_id=1, source_target_pairs={{8,0},{0,8},{9,1},{1,9},{10,2},{2,10},{11,3},{3,11},{12,4},{4,12},... | collective-permute-start | bytes 1769480 | tf_op jit(solution)/shard_map/ppermute | solution.py:33
  81.6 3.7 %copy-start.7 = (s32[12]{0:T(128)S(1)}, s32[12]{0:T(128)}, u32[]{:S(2)}) copy-start(s32[12]{0:T(128)} %left_ref.1) | copy-start | bytes 148
  81.6 25.0 %all-to-all-start.2 = ((bf16[16,48,384]{2,1,0:T(8,128)(2,1)}), bf16[16,48,384]{2,1,0:T(8,128)(2,1)S(1)}, u32[]{:S(2)}, u32[]{:S(2)}) async-start(bf16[16,48,384]{2,1,0:T(8,128)(2,1)} %add_convert_fusion), calls=%async_computation.2 | async-start | bytes 1179648 | tf_op jit(solution)/shard_map/all_to_all | solution.py:47

commit v5 on v4

--- a/solution.py
+++ b/solution.py
@@ -12,7 +12,8 @@
 NX = NXH * NXL
 RING = 4
 AXES = ("pair", "panel")
-VMEM_LIMIT = 32 * 1024 * 1024
+VMEM_LIMIT = 28 * 1024 * 1024
+SMALL_LIMIT = 2 * 1024 * 1024
 SMEM_SPEC = pl.BlockSpec(memory_space=pltpu.SMEM)
 VMEM_SPEC = pl.BlockSpec(memory_space=pltpu.VMEM)
 HBM_SPEC = pl.BlockSpec(memory_space=pltpu.HBM)
@@ -66,20 +67,21 @@
     return pair // (NXH * NC), (pair // NC) % NXH, pair % NC, panel // NY, panel % NY
 
 
+def row_live(base, left_ref, count):
+    first = base // BLK
+    second = jnp.minimum(first + 1, left_ref.shape[0] - 1)
+    index = base + lax.broadcasted_iota(jnp.int32, (count, 1), 0)
+    end = (first + 1) * BLK
+    return index < jnp.where(index < end, first * BLK + left_ref[first], end + left_ref[second])
+
+
 def mask_kernel(left_ref, right_ref, psi_ref, out_ref):
     rows, cols = psi_ref.shape
-    base = lax.axis_index("pair") * rows
     panel = lax.axis_index("panel")
-    first = base // BLK
-    second = jnp.minimum(first + 1, left_ref.shape[0] - 1)
-    index = base + lax.broadcasted_iota(jnp.int32, (rows, BLK), 0)
-    limit = jnp.where(
-        index < (first + 1) * BLK, first * BLK + left_ref[first], (first + 1) * BLK + left_ref[second]
-    )
-    row_live = index < limit
+    rows_live = row_live(lax.axis_index("pair") * rows, left_ref, rows)
     lane = lax.broadcasted_iota(jnp.int32, (rows, BLK), 1)
     for block in range(cols // BLK):
-        live = row_live & (lane < right_ref[panel * (cols // BLK) + block])
+        live = rows_live & (lane < right_ref[panel * (cols // BLK) + block])
         span = slice(block * BLK, (block + 1) * BLK)
         value = psi_ref[:, span].astype(jnp.float32)
         value = jnp.where(live, value, 0.0).astype(out_ref.dtype)
@@ -93,6 +95,7 @@
         out_shape=jax.ShapeDtypeStruct((NZ,) + psi.shape, psi.dtype),
         in_specs=[SMEM_SPEC, SMEM_SPEC, VMEM_SPEC],
         out_specs=VMEM_SPEC,
+        compiler_params=pltpu.CompilerParams(vmem_limit_bytes=SMALL_LIMIT),
         name="mask_psi",
     )(left_sizes, right_sizes, psi)
 
@@ -148,6 +151,7 @@
         in_specs=[SMEM_SPEC, SMEM_SPEC],
         out_specs=(SMEM_SPEC, SMEM_SPEC),
         scratch_shapes=[pltpu.SMEM((own.shape[1],), jnp.int32)],
+        compiler_params=pltpu.CompilerParams(vmem_limit_bytes=SMALL_LIMIT),
         name="plan",
     )(own, other)
 
@@ -204,25 +208,21 @@
     acc_in = refs.pop(0) if ahead else None
     arrays = [refs.pop(0) for _ in steps]
     right = (refs.pop(0), refs.pop(0))
-    left = (refs.pop(0), refs.pop(0)) if ahead else None
-    acc = refs.pop(0)
-    if ahead:
-        far_ref, left_ref = refs.pop(0), refs.pop(0)
-        far_sem, left_sem = refs.pop(), refs.pop()
-    rbuf, sem = refs
+    left = None if ahead else (refs.pop(0), refs.pop(0))
+    acc, later_ref, rbuf, sem, later_sem = refs
     twos = two_specs(steps, [array.shape[0] for array in arrays])
     copies, halves = two_copies(twos, right, rbuf, sem)
-    later = []
     if ahead:
-        later = sum(two_copies(two_specs(ahead, [RING // 2] * 2), right, far_ref, far_sem)[0], [])
+        later = sum(two_copies(two_specs(ahead, [RING // 2] * 2), right, later_ref, later_sem)[0], [])
+    else:
         count = left[0].shape[0]
-        for side in range(2):
-            later.append(
-                pltpu.make_async_copy(
-                    left[side], left_ref.at[pl.ds(side * count, count)], left_sem.at[side]
-                )
+        later = [
+            pltpu.make_async_copy(
+                left[side], later_ref.at[pl.ds(side * count, count)], later_sem.at[side]
             )
-        left_ref[2 * count] = jnp.zeros(left_ref.shape[1:], left_ref.dtype)
+            for side in range(2)
+        ]
+        later_ref[2 * count] = jnp.zeros(later_ref.shape[1:], later_ref.dtype)
     for copy in sum(copies, []) + later:
         copy.start()
     acc[...] = acc_in[...] if ahead else jnp.zeros_like(acc)
@@ -244,25 +244,24 @@
     group, cols = arrays[0].shape[2:]
     pairs = right[0].shape[0]
     units = sum(array.shape[0] for array in arrays)
-    out_shape = [jax.ShapeDtypeStruct((NXH, 2, NZ * group, pairs * cols), jnp.float32)]
-    scratch = [
-        pltpu.VMEM((units // 2, 2, pairs, cols, 2 * cols), jnp.bfloat16),
-        pltpu.SemaphoreType.DMA((units // 2, 2, 2)),
-    ]
-    near, away = arrays, list(right)
+    near, away = ([acc] if ahead else []) + arrays, list(right) + ([] if ahead else list(left))
     if ahead:
-        near, away = [acc] + arrays, list(right) + list(left)
-        out_shape += [
-            jax.ShapeDtypeStruct((2, 2, pairs, cols, 2 * cols), jnp.bfloat16),
-            jax.ShapeDtypeStruct((2 * left[0].shape[0] + 1,) + left[0].shape[1:], jnp.bfloat16),
-        ]
-        scratch += [pltpu.SemaphoreType.DMA((2,)), pltpu.SemaphoreType.DMA((2, 2, 2))]
+        later = (2, 2, pairs, cols, 2 * cols)
+    else:
+        later = (2 * left[0].shape[0] + 1,) + left[0].shape[1:]
     return pl.pallas_call(
         functools.partial(sums_kernel, steps, ahead),
-        out_shape=out_shape,
+        out_shape=[
+            jax.ShapeDtypeStruct((NXH, 2, NZ * group, pairs * cols), jnp.float32),
+            jax.ShapeDtypeStruct(later, jnp.bfloat16),
+        ],
         in_specs=[VMEM_SPEC] * len(near) + [HBM_SPEC] * len(away),
-        out_specs=[VMEM_SPEC] * len(out_shape),
-        scratch_shapes=scratch,
+        out_specs=[VMEM_SPEC] * 2,
+        scratch_shapes=[
+            pltpu.VMEM((units // 2, 2, pairs, cols, 2 * cols), jnp.bfloat16),
+            pltpu.SemaphoreType.DMA((units // 2, 2, 2)),
+            pltpu.SemaphoreType.DMA((2, 2, 2) if ahead else (2,)),
+        ],
         input_output_aliases={0: 0} if ahead else {},
         compiler_params=pltpu.CompilerParams(vmem_limit_bytes=VMEM_LIMIT),
         cost_estimate=pl.CostEstimate(
@@ -277,7 +276,7 @@
 UNROLL = 6
 
 
-def terms_kernel(steps, slots_ref, rows_ref, right_ref, acc, low, high, far_ref, left_ref, *refs):
+def terms_kernel(steps, slots_ref, rows_ref, sizes_ref, right_ref, acc, low, high, far_ref, left_ref, *refs):
     keep_ref, send_ref, part, total = refs
     _, xh, core, xl, y = position()
     arrays = (low, high)
@@ -339,11 +338,12 @@
     for q in range(NZ * NXH):
         mine = pl.multiple_of((q * NC + core) * group, 16)
         theirs = pl.multiple_of((q * NC + 1 - core) * group, 16)
-        keep_ref[q] = total[pl.ds(mine, group), :]
-        send_ref[q] = total[pl.ds(theirs, group), :].astype(send_ref.dtype)
-
-
-def terms(steps, slots, rows, right_sizes, acc, low, high, far, left):
+        keep_ref[q] = jnp.where(row_live(mine, sizes_ref, group), total[pl.ds(mine, group), :], 0.0)
+        other = jnp.where(row_live(theirs, sizes_ref, group), total[pl.ds(theirs, group), :], 0.0)
+        send_ref[q] = other.astype(send_ref.dtype)
+
+
+def terms(steps, slots, rows, left_sizes, right_sizes, acc, low, high, far, left):
     group, cols = low.shape[2:]
     height = NZ * NXH * NC * group
     pairs = 2 * far.shape[2]
@@ -354,7 +354,7 @@
             jax.ShapeDtypeStruct((NZ * NXH, group, cols), jnp.float32),
             jax.ShapeDtypeStruct((NZ * NXH, group, cols), jnp.bfloat16),
         ),
-        in_specs=[SMEM_SPEC] * 3 + [VMEM_SPEC] * 5,
+        in_specs=[SMEM_SPEC] * 4 + [VMEM_SPEC] * 5,
         out_specs=(VMEM_SPEC, VMEM_SPEC),
         scratch_shapes=[
             pltpu.VMEM((pairs * height, cols), jnp.bfloat16),
@@ -362,12 +362,10 @@
         ],
         compiler_params=pltpu.CompilerParams(vmem_limit_bytes=VMEM_LIMIT),
         name="terms",
-    )(slots, rows, right_sizes, acc, low, high, far, left)
+    )(slots, rows, left_sizes, right_sizes, acc, low, high, far, left)
 
 
 def local(psi, left_ops, a_rows, right_ops, left_sizes, right_sizes):
-    rows_dev = psi.shape[0]
-    pair = lax.axis_index("pair")
     copies = mask_psi(left_sizes, right_sizes, psi)
     right = (right_ops, core_swap(right_ops))
     flat_left = left_ops.reshape((-1, BLK, BLK))
@@ -378,14 +376,16 @@
     near = exchange(jnp.broadcast_to(along_z[None], (RING,) + along_z.shape), middle_groups())
     plus = last_shift(near, 1)
     minus = last_shift(near, -1)
-    (acc,) = sums(None, [(near, 0, 0)], right)
+    acc, both = sums(None, [(near, 0, 0)], right, left)
     half = RING // 2
     plus, minus, acc, slots, rows = lax.optimization_barrier((plus, minus, acc, slots, rows))
     far_low = last_shift(plus[:half], 1)
     far_high = last_shift(minus[half:], -1)
     last_steps = ((2, 0), (2, half))
-    acc, far, both = sums(acc, [(plus, 1, 0), (minus, 3, 0)], right, left, last_steps)
-    keep, send = terms(last_steps, slots, rows, right_sizes, acc, far_low, far_high, far, both)
+    acc, far = sums(acc, [(plus, 1, 0), (minus, 3, 0)], right, ahead=last_steps)
+    keep, send = terms(
+        last_steps, slots, rows, left_sizes, right_sizes, acc, far_low, far_high, far, both
+    )
     mine = (keep + core_swap(send).astype(jnp.float32)).astype(jnp.bfloat16)
     groups = [
         [flat(z, xh * NXL + xl, y, c) for z in range(NZ) for xh in range(NXH)]
@@ -394,11 +394,7 @@
         for y in range(NY)
     ]
     parts = exchange(mine, groups)
-    summed = parts.astype(jnp.float32).sum(axis=0)
-    index = pair * rows_dev + jnp.arange(rows_dev, dtype=jnp.int32)
-    blocks = jnp.arange(left_sizes.shape[0], dtype=jnp.int32)
-    limit = jnp.sum(jnp.where(index[:, None] // BLK == blocks, left_sizes + blocks * BLK, 0), axis=1)
-    return jnp.where((index < limit)[:, None], summed, 0.0)
+    return parts.astype(jnp.float32).sum(axis=0)
 
 
 def solution(mesh):

time: 109 us -> 108 us (level)
  the two profiles are of different devices: /device:TPU:24 before, /device:TPU:1 now
where the time goes in v5:
time: 108 us; the launch traced here: 107 us
  blocking collectives  42.1 us (39%)
  Pallas kernels  22.1 us (20%)
  starting transfers between devices  19.4 us (18%)
  waiting for transfers between devices  14.7 us (14%)
  local copies, waits for them, and re-layouts  8.09 us (7%)
    all_to_all x2, blocking collectives, exchange(): lax.all_to_all(copies, AXES, split_axis=0, concat_axis=0, axis_index_grou...  42.1 us
    pallas_call x2, Pallas kernels, sums(): pl.pallas_call(functools.partial(sums_kernel, steps, ahead), out_shape=[j...  11.5 us
    ppermute x4, starting transfers between devices, core_swap(): lax.ppermute(value, AXES, [(flat(z, x, y, 1 - c), flat(z, x, y, c)) for z...  10.9 us
    all_to_all x1, waiting for transfers between devices, exchange(): lax.all_to_all(copies, AXES, split_axis=0, concat_axis=0, axis_index_grou...  9.44 us
    pallas_call x1, Pallas kernels, terms(): pl.pallas_call(functools.partial(terms_kernel, steps), out_shape=(jax.Sha...  6.94 us
    unnamed x19, local copies, waits for them, and re-layouts  6.85 us
    ppermute x4, starting transfers between devices, last_shift(): return lax.ppermute(value, AXES, perm)  4.44 us
    all_to_all x1, starting transfers between devices, exchange(): lax.all_to_all(copies, AXES, split_axis=0, concat_axis=0, axis_index_grou...  4.01 us
  transfers between devices with their start and end apart: 9, of which 5 were waited for; matrix products, arithmetic and copies ran while one was open for 2% of the time, Pallas kernels for 14%

profile of v5, /device:TPU:1, one launch (start us, length us, event | category | flops | bytes accessed | tf_op | source)
XLA Modules:
  0.0 107.4 jit_solution(6238394641481959489)
XLA Ops:
  0.0 3.2 %collective-permute-start.2 = (bf16[2,384,3072]{2,1,0:T(8,128)(2,1)}, bf16[2,384,3072]{2,1,0:T(8,128)(2,1)}, u32[]{:S(2)}, u32[]{:S(2)}) collective-permute-start(bf16[2,384,3072]{2,1,0:T(8,128)(2,1)} %refs_3_.1), channel_id=1, source_target_pairs={{8,0},{0,8},{9,1},{1,9},{10,2},{2,10},{11,3},{3,11},{12,4},{4,12},... | collective-permute-start | bytes 14155784 | tf_op jit(solution)/shard_map/ppermute | solution.py:34
  3.2 0.0 copy-start.4
  3.2 0.8 copy-done.4
  4.0 0.0 copy-start.5
  4.0 0.7 copy-done.5
  4.7 0.0 copy-start.7
  4.7 0.7 copy-done.7
  5.3 0.6 mask_psi.1
  5.9 18.9 %all_to_all.15 = bf16[8,48,384]{2,1,0:T(8,128)(2,1)S(1)} all-to-all(bf16[8,48,384]{2,1,0:T(8,128)(2,1)S(1)} %mask_psi.1), channel_id=1, replica_groups={{0,32,64,96,128,160,192,224},{8,40,72,104,136,168,200,232},{1,33,65,97,..., dimensions={0} | all-to-all | bytes 589824 | tf_op jit(solution)/shard_map/all_to_all | solution.py:48
  24.9 1.1 %broadcast_in_dim.2 = bf16[4,8,48,384]{3,2,1,0:T(8,128)(2,1)} broadcast(bf16[8,48,384]{2,1,0:T(8,128)(2,1)S(1)} %all_to_all.15), dimensions={1,2,3} | broadcast | bytes 1474560 | tf_op jit(solution)/shard_map/broadcast_in_dim | solution.py:376
  26.0 4.0 %all-to-all-start.1 = ((bf16[4,8,48,384]{3,2,1,0:T(8,128)(2,1)}), bf16[4,8,48,384]{3,2,1,0:T(8,128)(2,1)S(1)}, u32[]{:S(2)}, u32[]{:S(2)}) async-start(bf16[4,8,48,384]{3,2,1,0:T(8,128)(2,1)} %broadcast_in_dim.2), calls=%async_computation.1 | async-start | bytes 2359296 | tf_op jit(solution)/shard_map/all_to_all | solution.py:48
  30.0 1.3 %collective-permute-start.3 = (bf16[48,128,128]{2,1,0:T(8,128)(2,1)}, bf16[48,128,128]{2,1,0:T(8,128)(2,1)}, u32[]{:S(2)}, u32[]{:S(2)}) collective-permute-start(bf16[48,128,128]{2,1,0:T(8,128)(2,1)} %bitcast.refs_3_), channel_id=1, source_target_pairs={{8,0},{0,8},{9,1},{1,9},{10,2},{2,10},{11,3},{3,11},{12,4},{4,12},... | collective-permute-start | bytes 4718600 | tf_op jit(solution)/shard_map/ppermute | solution.py:34
  31.3 9.4 %all-to-all-done.1.refs_0_ = bf16[4,8,48,384]{3,2,1,0:T(8,128)(2,1)S(1)} async-done(((bf16[4,8,48,384]{3,2,1,0:T(8,128)(2,1)}), bf16[4,8,48,384]{3,2,1,0:T(8,128)(2,1)S(1)}, u32[]{:S(2)}, u32[]{:S(2)}) %all-to-all-start.1) | async-done | bytes 1179680 | tf_op jit(solution)/shard_map/all_to_all | solution.py:48
  40.7 2.6 %collective-permute-start = (bf16[4,8,48,384]{3,2,1,0:T(8,128)(2,1)S(1)}, bf16[4,8,48,384]{3,2,1,0:T(8,128)(2,1)S(1)}, u32[]{:S(2)}, u32[]{:S(2)}) collective-permute-start(bf16[4,8,48,384]{3,2,1,0:T(8,128)(2,1)S(1)} %all-to-all-done.1.refs_0_), channel_id=1, source_target_pairs={{4,0},{9,8},{5,1},{10,9},{6,2},{11,10},{7,3},{8,11},{16,4},{13,12}... | collective-permute-start | bytes 3538952 | tf_op jit(solution)/shard_map/ppermute | solution.py:44
  43.4 0.0 collective-permute-start.1
  43.4 0.8 copy.9.own_ref
  44.2 2.3 %collective-permute-start.4 = (s32[2,12,2]{2,1,0:T(8,128)S(1)}, s32[2,12,2]{2,1,0:T(8,128)S(1)}, u32[]{:S(2)}, u32[]{:S(2)}) collective-permute-start(s32[2,12,2]{2,1,0:T(8,128)S(1)} %copy.9.own_ref), channel_id=1, source_target_pairs={{8,0},{0,8},{9,1},{1,9},{10,2},{2,10},{11,3},{3,11},{12,4},{4,12},... | collective-permute-start | bytes 584 | tf_op jit(solution)/shard_map/ppermute | solution.py:34
  46.4 0.8 collective-permute-done.4.other_ref
  47.3 3.0 %plan.1 = (s32[108]{0:T(128)S(1)}, s32[54]{0:T(128)S(1)}) custom-call(s32[2,12,2]{2,1,0:T(8,128)S(1)} %copy.9.own_ref, s32[2,12,2]{2,1,0:T(8,128)S(1)} %collective-permute-done.4.other_ref), custom_call_target="tpu_custom_call" | custom-call | tf_op jit(solution)/shard_map/plan/pallas_call | solution.py:145
  50.3 0.0 collective-permute-done.3.refs_4_
  50.3 0.0 collective-permute-done.2.refs_2_.refs_4_
  50.3 0.0 copy-start
  50.3 2.3 %copy-done = bf16[2,384,3072]{2,1,0:T(8,128)(2,1)S(1)} copy-done((bf16[2,384,3072]{2,1,0:T(8,128)(2,1)S(1)}, bf16[2,384,3072]{2,1,0:T(8,128)(2,1)}, u32[]{:S(2)}) %copy-start) | copy-done | bytes 4718616
  52.7 0.0 copy-start.1
  52.7 4.3 %sums_4.1 = (f32[2,2,384,768]{3,2,1,0:T(8,128)S(1)}, bf16[97,128,128]{2,1,0:T(8,128)(2,1)S(1)}) custom-call(bf16[4,8,48,384]{3,2,1,0:T(8,128)(2,1)S(1)} %all-to-all-done.1.refs_0_, bf16[2,384,3072]{2,1,0:T(8,128)(2,1)S(1)} %copy-done, bf16[2,384,3072]{2,1,0:T(8,128)(2,1)} %collective-permute-done.2.refs_2_.refs_4_, bf16[48,128,128]{2,1,0:T(8,128)(2,1)} %bitcast.refs_3_, ...), custom_call_target="tpu_custom_call" | custom-call | flops 1811939328 | bytes 4718592 | tf_op jit(solution)/shard_map/sums_4/pallas_call | solution.py:252
  57.0 0.0 copy-start.2
  57.0 1.6 %copy-done.2 = bf16[97,128,128]{2,1,0:T(8,128)(2,1)} copy-done((bf16[97,128,128]{2,1,0:T(8,128)(2,1)}, bf16[97,128,128]{2,1,0:T(8,128)(2,1)S(1)}, u32[]{:S(2)}) %copy-start.2) | copy-done | bytes 3178520
  58.7 0.0 collective-permute-done.refs_1_
  58.7 1.3 %collective-permute-done.1.refs_2_ = bf16[4,8,48,384]{3,2,1,0:T(8,128)(2,1)S(1)} collective-permute-done((bf16[4,8,48,384]{3,2,1,0:T(8,128)(2,1)S(1)}, bf16[4,8,48,384]{3,2,1,0:T(8,128)(2,1)S(1)}, u32[]{:S(2)}, u32[]{:S(2)}) %collective-permute-start.1) | collective-permute-done | bytes 1179680 | tf_op jit(solution)/shard_map/ppermute | solution.py:44
  59.9 0.1 slice.6
  60.0 0.1 collective-permute-start.5
  60.1 0.1 slice.7
  60.2 0.0 copy-start.6
  60.2 0.0 copy-start.8
  60.2 1.7 %collective-permute-start.6 = (bf16[2,8,48,384]{3,2,1,0:T(8,128)(2,1)S(1)}, bf16[2,8,48,384]{3,2,1,0:T(8,128)(2,1)S(1)}, u32[]{:S(2)}, u32[]{:S(2)}) collective-permute-start(bf16[2,8,48,384]{3,2,1,0:T(8,128)(2,1)S(1)} %slice.7), channel_id=1, source_target_pairs={{20,0},{11,8},{21,1},{8,9},{22,2},{9,10},{23,3},{10,11},{0,4},{15,... | collective-permute-start | bytes 1769480 | tf_op jit(solution)/shard_map/ppermute | solution.py:44
  61.9 0.0 copy-done.1
  61.9 0.0 copy-start.3
  61.9 7.2 %sums_8.1 = (f32[2,2,384,768]{3,2,1,0:T(8,128)S(1)}, bf16[2,2,2,384,768]{4,3,2,1,0:T(8,128)(2,1)S(1)}) custom-call(f32[2,2,384,768]{3,2,1,0:T(8,128)S(1)} %get-tuple-element.23.refs_0_, bf16[4,8,48,384]{3,2,1,0:T(8,128)(2,1)S(1)} %collective-permute-done.refs_1_, ...), custom_call_target="tpu_custom_call", output_to_operand_aliasing={{0}: (0, {})} | custom-call | flops 3623878656 | bytes 9437184 | tf_op jit(solution)/shard_map/sums_8/pallas_call | solution.py:252
  69.1 0.0 collective-permute-done.5.low
  69.1 1.5 %collective-permute-done.6.high = bf16[2,8,48,384]{3,2,1,0:T(8,128)(2,1)S(1)} collective-permute-done((bf16[2,8,48,384]{3,2,1,0:T(8,128)(2,1)S(1)}, bf16[2,8,48,384]{3,2,1,0:T(8,128)(2,1)S(1)}, u32[]{:S(2)}, u32[]{:S(2)}) %collective-permute-start.6) | collective-permute-done | bytes 589856 | tf_op jit(solution)/shard_map/ppermute | solution.py:44
  70.7 0.0 copy-done.6
  70.7 0.0 copy-done.8
  70.7 0.0 copy-done.3
  70.7 6.9 %terms.1 = (f32[16,48,384]{2,1,0:T(8,128)S(1)}, bf16[16,48,384]{2,1,0:T(8,128)(2,1)S(1)}) custom-call(s32[108]{0:T(128)S(1)} %get-tuple-element.21.slots_ref, s32[54]{0:T(128)S(1)} %get-tuple-element.22.rows_ref, s32[12]{0:T(128)S(1)} %copy-done.6, s32[24]{0:T(128)S(1)} %copy-done.8, f32[2,2,384,768]{3,2,1,0:T(8,128)S(1)} %get-tuple-element.26.acc, ...), custom_call_target="tpu_custom_call" | custom-call | tf_op jit(solution)/shard_map/terms/pallas_call | solution.py:351
  77.6 4.1 %collective-permute-start.7 = (bf16[16,48,384]{2,1,0:T(8,128)(2,1)S(1)}, bf16[16,48,384]{2,1,0:T(8,128)(2,1)S(1)}, u32[]{:S(2)}, u32[]{:S(2)}) collective-permute-start(bf16[16,48,384]{2,1,0:T(8,128)(2,1)S(1)} %get-tuple-element.30), channel_id=1, source_target_pairs={{8,0},{0,8},{9,1},{1,9},{10,2},{2,10},{11,3},{3,11},{12,4},{4,12},... | collective-permute-start | bytes 1769480 | tf_op jit(solution)/shard_map/ppermute | solution.py:34
  81.7 1.6 %collective-permute-done.7 = bf16[16,48,384]{2,1,0:T(8,128)(2,1)S(1)} collective-permute-done((bf16[16,48,384]{2,1,0:T(8,128)(2,1)S(1)}, bf16[16,48,384]{2,1,0:T(8,128)(2,1)S(1)}, u32[]{:S(2)}, u32[]{:S(2)}) %collective-permute-start.7) | collective-permute-done | bytes 589856 | tf_op jit(solution)/shard_map/ppermute | solution.py:34
  83.4 0.2 add_convert_fusion
  83.5 23.1 %all_to_all.16 = bf16[16,48,384]{2,1,0:T(8,128)(2,1)S(1)} all-to-all(bf16[16,48,384]{2,1,0:T(8,128)(2,1)S(1)} %add_convert_fusion), channel_id=1, replica_groups={{0,16,32,48,64,80,96,112,128,144,160,176,192,208,224,240},{1,17,33,49,6..., dimensions={0} | all-to-all | bytes 1179648 | tf_op jit(solution)/shard_map/all_to_all | solution.py:48
  106.7 0.7 convert_reduce_fusion
Async XLA Ops:
  0.0 50.3 %collective-permute-start.2 = (bf16[2,384,3072]{2,1,0:T(8,128)(2,1)}, bf16[2,384,3072]{2,1,0:T(8,128)(2,1)}, u32[]{:S(2)}, u32[]{:S(2)}) collective-permute-start(bf16[2,384,3072]{2,1,0:T(8,128)(2,1)} %refs_3_.1), channel_id=1, source_target_pairs={{8,0},{0,8},{9,1},{1,9},{10,2},{2,10},{11,3},{3,11},{12,4},{4,12},... | collective-permute-start | bytes 14155784 | tf_op jit(solution)/shard_map/ppermute | solution.py:34
  3.2 0.8 copy-start.4
  4.0 0.7 copy-start.5
  4.7 0.7 copy-start.7
  26.0 14.8 %all-to-all-start.1 = ((bf16[4,8,48,384]{3,2,1,0:T(8,128)(2,1)}), bf16[4,8,48,384]{3,2,1,0:T(8,128)(2,1)S(1)}, u32[]{:S(2)}, u32[]{:S(2)}) async-start(bf16[4,8,48,384]{3,2,1,0:T(8,128)(2,1)} %broadcast_in_dim.2), calls=%async_computation.1 | async-start | bytes 2359296 | tf_op jit(solution)/shard_map/all_to_all | solution.py:48
  30.0 20.3 %collective-permute-start.3 = (bf16[48,128,128]{2,1,0:T(8,128)(2,1)}, bf16[48,128,128]{2,1,0:T(8,128)(2,1)}, u32[]{:S(2)}, u32[]{:S(2)}) collective-permute-start(bf16[48,128,128]{2,1,0:T(8,128)(2,1)} %bitcast.refs_3_), channel_id=1, source_target_pairs={{8,0},{0,8},{9,1},{1,9},{10,2},{2,10},{11,3},{3,11},{12,4},{4,12},... | collective-permute-start | bytes 4718600 | tf_op jit(solution)/shard_map/ppermute | solution.py:34
  40.7 17.9 %collective-permute-start = (bf16[4,8,48,384]{3,2,1,0:T(8,128)(2,1)S(1)}, bf16[4,8,48,384]{3,2,1,0:T(8,128)(2,1)S(1)}, u32[]{:S(2)}, u32[]{:S(2)}) collective-permute-start(bf16[4,8,48,384]{3,2,1,0:T(8,128)(2,1)S(1)} %all-to-all-done.1.refs_0_), channel_id=1, source_target_pairs={{4,0},{9,8},{5,1},{10,9},{6,2},{11,10},{7,3},{8,11},{16,4},{13,12}... | collective-permute-start | bytes 3538952 | tf_op jit(solution)/shard_map/ppermute | solution.py:44
  43.4 16.6 %collective-permute-start.1 = (bf16[4,8,48,384]{3,2,1,0:T(8,128)(2,1)S(1)}, bf16[4,8,48,384]{3,2,1,0:T(8,128)(2,1)S(1)}, u32[]{:S(2)}, u32[]{:S(2)}) collective-permute-start(bf16[4,8,48,384]{3,2,1,0:T(8,128)(2,1)S(1)} %all-to-all-done.1.refs_0_), channel_id=1, source_target_pairs={{20,0},{11,8},{21,1},{8,9},{22,2},{9,10},{23,3},{10,11},{0,4},{15,... | collective-permute-start | bytes 3538952 | tf_op jit(solution)/shard_map/ppermute | solution.py:44
  44.2 3.1 %collective-permute-start.4 = (s32[2,12,2]{2,1,0:T(8,128)S(1)}, s32[2,12,2]{2,1,0:T(8,128)S(1)}, u32[]{:S(2)}, u32[]{:S(2)}) collective-permute-start(s32[2,12,2]{2,1,0:T(8,128)S(1)} %copy.9.own_ref), channel_id=1, source_target_pairs={{8,0},{0,8},{9,1},{1,9},{10,2},{2,10},{11,3},{3,11},{12,4},{4,12},... | collective-permute-start | bytes 584 | tf_op jit(solution)/shard_map/ppermute | solution.py:34
  50.3 2.3 %copy-start = (bf16[2,384,3072]{2,1,0:T(8,128)(2,1)S(1)}, bf16[2,384,3072]{2,1,0:T(8,128)(2,1)}, u32[]{:S(2)}) copy-start(bf16[2,384,3072]{2,1,0:T(8,128)(2,1)} %refs_3_.1) | copy-start | bytes 14155780
  52.7 9.2 %copy-start.1 = (bf16[2,384,3072]{2,1,0:T(8,128)(2,1)S(1)}, bf16[2,384,3072]{2,1,0:T(8,128)(2,1)}, u32[]{:S(2)}) copy-start(bf16[2,384,3072]{2,1,0:T(8,128)(2,1)} %refs_3_.1) | copy-start | bytes 14155780
  57.0 1.7 %copy-start.2 = (bf16[97,128,128]{2,1,0:T(8,128)(2,1)}, bf16[97,128,128]{2,1,0:T(8,128)(2,1)S(1)}, u32[]{:S(2)}) copy-start(bf16[97,128,128]{2,1,0:T(8,128)(2,1)S(1)} %get-tuple-element.28.left_ref) | copy-start | bytes 9535492
  60.0 9.1 %collective-permute-start.5 = (bf16[2,8,48,384]{3,2,1,0:T(8,128)(2,1)S(1)}, bf16[2,8,48,384]{3,2,1,0:T(8,128)(2,1)S(1)}, u32[]{:S(2)}, u32[]{:S(2)}) collective-permute-start(bf16[2,8,48,384]{3,2,1,0:T(8,128)(2,1)S(1)} %slice.6), channel_id=1, source_target_pairs={{4,0},{9,8},{5,1},{10,9},{6,2},{11,10},{7,3},{8,11},{16,4},{13,12}... | collective-permute-start | bytes 1769480 | tf_op jit(solution)/shard_map/ppermute | solution.py:44
  60.2 10.5 %copy-start.6 = (s32[12]{0:T(128)S(1)}, s32[12]{0:T(128)}, u32[]{:S(2)}) copy-start(s32[12]{0:T(128)} %sizes_ref.1) | copy-start | bytes 148
  60.2 10.5 %copy-start.8 = (s32[24]{0:T(128)S(1)}, s32[24]{0:T(128)}, u32[]{:S(2)}) copy-start(s32[24]{0:T(128)} %right_ref.3) | copy-start | bytes 292
  60.2 10.5 %collective-permute-start.6 = (bf16[2,8,48,384]{3,2,1,0:T(8,128)(2,1)S(1)}, bf16[2,8,48,384]{3,2,1,0:T(8,128)(2,1)S(1)}, u32[]{:S(2)}, u32[]{:S(2)}) collective-permute-start(bf16[2,8,48,384]{3,2,1,0:T(8,128)(2,1)S(1)} %slice.7), channel_id=1, source_target_pairs={{20,0},{11,8},{21,1},{8,9},{22,2},{9,10},{23,3},{10,11},{0,4},{15,... | collective-permute-start | bytes 1769480 | tf_op jit(solution)/shard_map/ppermute | solution.py:44
  61.9 8.8 %copy-start.3 = (bf16[97,128,128]{2,1,0:T(8,128)(2,1)S(1)}, bf16[97,128,128]{2,1,0:T(8,128)(2,1)}, u32[]{:S(2)}) copy-start(bf16[97,128,128]{2,1,0:T(8,128)(2,1)} %copy-done.2) | copy-start | bytes 9535492
  77.6 5.7 %collective-permute-start.7 = (bf16[16,48,384]{2,1,0:T(8,128)(2,1)S(1)}, bf16[16,48,384]{2,1,0:T(8,128)(2,1)S(1)}, u32[]{:S(2)}, u32[]{:S(2)}) collective-permute-start(bf16[16,48,384]{2,1,0:T(8,128)(2,1)S(1)} %get-tuple-element.30), channel_id=1, source_target_pairs={{8,0},{0,8},{9,1},{1,9},{10,2},{2,10},{11,3},{3,11},{12,4},{4,12},... | collective-permute-start | bytes 1769480 | tf_op jit(solution)/shard_map/ppermute | solution.py:34

commit v6 on v5

--- a/solution.py
+++ b/solution.py
@@ -10,7 +10,6 @@
 BLK = 128
 NZ, NXH, NC, NXL, NY = 8, 2, 2, 2, 4
 NX = NXH * NXL
-RING = 4
 AXES = ("pair", "panel")
 VMEM_LIMIT = 28 * 1024 * 1024
 SMALL_LIMIT = 2 * 1024 * 1024
@@ -36,10 +35,11 @@
     )
 
 
-def last_shift(value, step):
+def partner(value, ring, step):
     perm = []
     for z, x, y, c in everywhere():
-        source = flat(z, (x + step) % NX, y, c) if c == 0 else flat(z, x, (y + step) % NY, c)
+        along_x = (ring == "last") == (c == 0)
+        source = flat(z, x ^ step, y, c) if along_x else flat(z, x, y ^ step, c)
         perm.append((source, flat(z, x, y, c)))
     return lax.ppermute(value, AXES, perm)
 
@@ -54,12 +54,6 @@
     return [
         [flat(z, x, y, c) for z in range(NZ)] for x in range(NX) for y in range(NY) for c in range(NC)
     ]
-
-
-def middle_groups():
-    along_y = [[flat(z, x, y, 0) for y in range(NY)] for z in range(NZ) for x in range(NX)]
-    along_x = [[flat(z, x, y, 1) for x in range(NX)] for z in range(NZ) for y in range(NY)]
-    return along_y + along_x
 
 
 def position():
@@ -95,7 +89,6 @@
         out_shape=jax.ShapeDtypeStruct((NZ,) + psi.shape, psi.dtype),
         in_specs=[SMEM_SPEC, SMEM_SPEC, VMEM_SPEC],
         out_specs=VMEM_SPEC,
-        compiler_params=pltpu.CompilerParams(vmem_limit_bytes=SMALL_LIMIT),
         name="mask_psi",
     )(left_sizes, right_sizes, psi)
 
@@ -107,24 +100,24 @@
         (side, pair, block, s)
         for side in range(2)
         for pair in range(shape[0])
-        for block in range(shape[1])
-        for s in range(shape[2])
+        for block in range(shape[2])
+        for s in range(shape[1])
     ]
 
     def row_of(slot):
-        return (own_ref, other_ref)[slot[0]][slot[1], slot[2], slot[3]]
+        return (own_ref, other_ref)[slot[0]][slot[1], slot[3], slot[2]]
 
     for place in range(slots_ref.shape[0]):
         slots_ref[place] = 2 * count
     for place in range(rows_ref.shape[0]):
         rows_ref[place] = 0
-    for row in range(shape[1]):
+    for row in range(shape[2]):
         next_ref[row] = 0
     for slot in slots:
         row = row_of(slot)
         next_ref[row] = next_ref[row] + 1
     start = jnp.int32(0)
-    for row in range(shape[1]):
+    for row in range(shape[2]):
         pairs = (next_ref[row] + 1) // 2
         next_ref[row] = 2 * start
 
@@ -141,7 +134,7 @@
 
 
 def plan(own, other):
-    pairs = own.size + own.shape[1] // 2
+    pairs = own.size + own.shape[2] // 2
     return pl.pallas_call(
         plan_kernel,
         out_shape=(
@@ -150,18 +143,13 @@
         ),
         in_specs=[SMEM_SPEC, SMEM_SPEC],
         out_specs=(SMEM_SPEC, SMEM_SPEC),
-        scratch_shapes=[pltpu.SMEM((own.shape[1],), jnp.int32)],
+        scratch_shapes=[pltpu.SMEM((own.shape[2],), jnp.int32)],
         compiler_params=pltpu.CompilerParams(vmem_limit_bytes=SMALL_LIMIT),
         name="plan",
     )(own, other)
 
 
-def two_specs(steps, counts):
-    return [
-        (number, spot, step, start + spot)
-        for number, ((step, start), count) in enumerate(zip(steps, counts))
-        for spot in range(0, count, 2)
-    ]
+NEAR, AWAY = (0, 1), (3, 2)
 
 
 def two_copies(twos, right, buffer, sem):
@@ -169,12 +157,11 @@
     x = xh * NXL + xl
     cols = right[0].shape[1]
     copies, halves = [], []
-    for index, (_, _, step, place) in enumerate(twos):
-        far_x, far_y = lax.rem(x + step, NX), lax.rem(y + step, NY)
+    for index, (step, places) in enumerate(twos):
         copies.append([])
-        for way in range(2):
-            unit_x = jnp.where(core == 0, far_x, place + way)
-            unit_y = jnp.where(core == 0, place + way, far_y)
+        for way, place in enumerate(places):
+            unit_x = jnp.where(core == 0, x ^ step, x ^ place)
+            unit_y = jnp.where(core == 0, y ^ place, y ^ step)
             column = pl.multiple_of((lax.rem(unit_x, NXL) * NY + unit_y) * cols, BLK)
             for side in range(2):
                 copies[-1].append(
@@ -188,9 +175,9 @@
     return copies, halves
 
 
-def wide(array, spot):
+def wide(array):
     rows = array.shape[1] * array.shape[2]
-    return jnp.concatenate([array[spot + way].reshape(rows, array.shape[3]) for way in range(2)], axis=1)
+    return jnp.concatenate([array[way].reshape(rows, array.shape[3]) for way in range(2)], axis=1)
 
 
 def times(left_side, right_side):
@@ -203,17 +190,16 @@
     return buffer[index, side].reshape(buffer.shape[2] * buffer.shape[3], buffer.shape[4])
 
 
-def sums_kernel(steps, ahead, *refs):
+def sums_kernel(twos, ahead, *refs):
     refs = list(refs)
     acc_in = refs.pop(0) if ahead else None
-    arrays = [refs.pop(0) for _ in steps]
+    arrays = [refs.pop(0) for _ in twos]
     right = (refs.pop(0), refs.pop(0))
     left = None if ahead else (refs.pop(0), refs.pop(0))
     acc, later_ref, rbuf, sem, later_sem = refs
-    twos = two_specs(steps, [array.shape[0] for array in arrays])
     copies, halves = two_copies(twos, right, rbuf, sem)
     if ahead:
-        later = sum(two_copies(two_specs(ahead, [RING // 2] * 2), right, later_ref, later_sem)[0], [])
+        later = sum(two_copies(ahead, right, later_ref, later_sem)[0], [])
     else:
         count = left[0].shape[0]
         later = [
@@ -226,13 +212,13 @@
     for copy in sum(copies, []) + later:
         copy.start()
     acc[...] = acc_in[...] if ahead else jnp.zeros_like(acc)
-    for index, (number, spot, _, _) in enumerate(twos):
+    for index, array in enumerate(arrays):
         for copy in copies[index]:
             copy.wait()
 
         @pl.loop(0, 2)
         def _(side):
-            acc[halves[index], side] += times(wide(arrays[number], spot), operator(rbuf, index, side))
+            acc[halves[index], side] += times(wide(array), operator(rbuf, index, side))
 
     for copy in later:
         copy.wait()
@@ -240,17 +226,17 @@
 
 def sums(acc, pieces, right, left=None, ahead=()):
     arrays = [array for array, _, _ in pieces]
-    steps = tuple((step, start) for _, step, start in pieces)
+    twos = tuple((step, places) for _, step, places in pieces)
     group, cols = arrays[0].shape[2:]
     pairs = right[0].shape[0]
-    units = sum(array.shape[0] for array in arrays)
+    units = 2 * len(arrays)
     near, away = ([acc] if ahead else []) + arrays, list(right) + ([] if ahead else list(left))
     if ahead:
         later = (2, 2, pairs, cols, 2 * cols)
     else:
         later = (2 * left[0].shape[0] + 1,) + left[0].shape[1:]
     return pl.pallas_call(
-        functools.partial(sums_kernel, steps, ahead),
+        functools.partial(sums_kernel, twos, ahead),
         out_shape=[
             jax.ShapeDtypeStruct((NXH, 2, NZ * group, pairs * cols), jnp.float32),
             jax.ShapeDtypeStruct(later, jnp.bfloat16),
@@ -276,13 +262,12 @@
 UNROLL = 6
 
 
-def terms_kernel(steps, slots_ref, rows_ref, sizes_ref, right_ref, acc, low, high, far_ref, left_ref, *refs):
+def terms_kernel(slots_ref, rows_ref, sizes_ref, right_ref, acc, far_near, far_away, far_ref, left_ref, *refs):
     keep_ref, send_ref, part, total = refs
     _, xh, core, xl, y = position()
-    arrays = (low, high)
-    group, cols = low.shape[2:]
+    arrays = (far_near, far_away)
+    group, cols = far_near.shape[2:]
     pairs = far_ref.shape[2]
-    twos = two_specs(steps, [array.shape[0] for array in arrays])
     lane = lax.broadcasted_iota(jnp.int32, (1, BLK), 1)
     start = (xl * NY + y) * (cols // BLK)
     live = jnp.concatenate(
@@ -308,15 +293,14 @@
         def _():
             far = 1 - xh
             place(xh, side, acc[xh, side])
-            left_side = jnp.concatenate([wide(arrays[n], spot) for n, spot, _, _ in twos], axis=1)
-            right_side = jnp.concatenate([operator(far_ref, i, side) for i in range(len(twos))], axis=1)
+            left_side = jnp.concatenate([wide(array) for array in arrays], axis=1)
+            right_side = jnp.concatenate([operator(far_ref, i, side) for i in range(2)], axis=1)
             place(far, side, acc[far, side] + times(left_side, right_side))
 
         @pl.when(core == 1)
         def _():
-            for index, (n, spot, _, middle) in enumerate(twos):
-                half = middle // NXL
-                place(half, side, acc[half, side] + times(wide(arrays[n], spot), operator(far_ref, index, side)))
+            for index, (array, half) in enumerate(zip(arrays, (xh, 1 - xh))):
+                place(half, side, acc[half, side] + times(wide(array), operator(far_ref, index, side)))
 
     last_block = 2 * pairs * height // BLK - 1
 
@@ -343,13 +327,13 @@
         send_ref[q] = other.astype(send_ref.dtype)
 
 
-def terms(steps, slots, rows, left_sizes, right_sizes, acc, low, high, far, left):
-    group, cols = low.shape[2:]
+def terms(slots, rows, left_sizes, right_sizes, acc, far_near, far_away, far, left):
+    group, cols = far_near.shape[2:]
     height = NZ * NXH * NC * group
     pairs = 2 * far.shape[2]
     assert rows.shape[0] % UNROLL == 0
     return pl.pallas_call(
-        functools.partial(terms_kernel, steps),
+        terms_kernel,
         out_shape=(
             jax.ShapeDtypeStruct((NZ * NXH, group, cols), jnp.float32),
             jax.ShapeDtypeStruct((NZ * NXH, group, cols), jnp.bfloat16),
@@ -362,7 +346,7 @@
         ],
         compiler_params=pltpu.CompilerParams(vmem_limit_bytes=VMEM_LIMIT),
         name="terms",
-    )(slots, rows, left_sizes, right_sizes, acc, low, high, far, left)
+    )(slots, rows, left_sizes, right_sizes, acc, far_near, far_away, far, left)
 
 
 def local(psi, left_ops, a_rows, right_ops, left_sizes, right_sizes):
@@ -370,22 +354,30 @@
     right = (right_ops, core_swap(right_ops))
     flat_left = left_ops.reshape((-1, BLK, BLK))
     left = (flat_left, core_swap(flat_left))
-    slots, rows = plan(a_rows, core_swap(a_rows))
+    rows_by_slot = jnp.transpose(a_rows, (0, 2, 1))
+    slots, rows = plan(rows_by_slot, core_swap(rows_by_slot))
 
     along_z = exchange(copies, z_groups())
-    near = exchange(jnp.broadcast_to(along_z[None], (RING,) + along_z.shape), middle_groups())
-    plus = last_shift(near, 1)
-    minus = last_shift(near, -1)
-    acc, both = sums(None, [(near, 0, 0)], right, left)
-    half = RING // 2
-    plus, minus, acc, slots, rows = lax.optimization_barrier((plus, minus, acc, slots, rows))
-    far_low = last_shift(plus[:half], 1)
-    far_high = last_shift(minus[half:], -1)
-    last_steps = ((2, 0), (2, half))
-    acc, far = sums(acc, [(plus, 1, 0), (minus, 3, 0)], right, ahead=last_steps)
-    keep, send = terms(
-        last_steps, slots, rows, left_sizes, right_sizes, acc, far_low, far_high, far, both
-    )
+    beside = partner(along_z, "middle", 1)
+    across = partner(along_z, "middle", 3)
+    beside, slots, rows = lax.optimization_barrier((beside, slots, rows))
+    near = jnp.stack([along_z, beside])
+    near_1 = partner(near, "last", 1)
+    near_3 = partner(near, "last", 3)
+    away = jnp.stack([across, partner(across, "middle", 1)])
+    away_1 = partner(away, "last", 1)
+    away_3 = partner(away, "last", 3)
+    acc, both = sums(None, [(near, 0, NEAR), (away, 0, AWAY)], right, left)
+    near_3, away_1, acc = lax.optimization_barrier((near_3, away_1, acc))
+    near_2 = partner(near_3, "last", 1)
+    away_2 = partner(away_1, "last", 3)
+    acc, far = sums(
+        acc,
+        [(near_1, 1, NEAR), (near_3, 3, NEAR), (away_1, 1, AWAY), (away_3, 3, AWAY)],
+        right,
+        ahead=((2, NEAR), (2, AWAY)),
+    )
+    keep, send = terms(slots, rows, left_sizes, right_sizes, acc, near_2, away_2, far, both)
     mine = (keep + core_swap(send).astype(jnp.float32)).astype(jnp.bfloat16)
     groups = [
         [flat(z, xh * NXL + xl, y, c) for z in range(NZ) for xh in range(NXH)]

time: 108 us -> 98.5 us (0.912)
  the two profiles are of different devices: /device:TPU:1 before, /device:TPU:24 now
where the time goes in v6:
time: 98.5 us; the launch traced here: 97.4 us
  blocking collectives  46.2 us (47%)
  Pallas kernels  22.7 us (23%)
  waiting for transfers between devices  13.7 us (14%)
  starting transfers between devices  10.7 us (11%)
  local copies, waits for them, and re-layouts  3.04 us (3%)
    all_to_all x2, blocking collectives, exchange(): lax.all_to_all(copies, AXES, split_axis=0, concat_axis=0, axis_index_grou...  46.2 us
    pallas_call x2, Pallas kernels, sums(): pl.pallas_call(functools.partial(sums_kernel, twos, ahead), out_shape=[ja...  11.6 us
    ppermute x9, waiting for transfers between devices, partner(): return lax.ppermute(value, AXES, perm)  10.3 us
    ppermute x9, starting transfers between devices, partner(): return lax.ppermute(value, AXES, perm)  10.1 us
    pallas_call x1, Pallas kernels, terms(): pl.pallas_call(terms_kernel, out_shape=(jax.ShapeDtypeStruct((NZ * NXH, g...  7.07 us
    ppermute x4, waiting for transfers between devices, core_swap(): lax.ppermute(value, AXES, [(flat(z, x, y, 1 - c), flat(z, x, y, c)) for z...  3.36 us
    unnamed x12, local copies, waits for them, and re-layouts  3.04 us
    pallas_call x1, Pallas kernels, plan(): pl.pallas_call(plan_kernel, out_shape=(jax.ShapeDtypeStruct((2 * pairs,),...  2.54 us
  transfers between devices with their start and end apart: 13, of which 4 were waited for; matrix products, arithmetic and copies ran while one was open for 0% of the time, Pallas kernels for 16%

profile of v6, /device:TPU:24, one launch (start us, length us, event | category | flops | bytes accessed | tf_op | source)
XLA Modules:
  0.0 97.4 jit_solution(4296342153705174631)
XLA Ops:
  0.0 0.0 collective-permute-start.6
  0.0 0.0 copy-start.2
  0.0 0.5 collective-permute-start.7
  0.5 1.6 %mask_psi.1 = bf16[8,48,384]{2,1,0:T(8,128)(2,1)} custom-call(s32[12]{0:T(128)} %sizes_ref.1, s32[24]{0:T(128)} %right_ref.3, bf16[48,384]{1,0:T(8,128)(2,1)} %psi_ref.1), custom_call_target="tpu_custom_call" | custom-call | tf_op jit(solution)/shard_map/mask_psi/pallas_call | solution.py:87
  2.1 21.4 %all_to_all.10 = bf16[8,48,384]{2,1,0:T(8,128)(2,1)S(1)} all-to-all(bf16[8,48,384]{2,1,0:T(8,128)(2,1)} %mask_psi.1), channel_id=1, replica_groups={{0,32,64,96,128,160,192,224},{8,40,72,104,136,168,200,232},{1,33,65,97,..., dimensions={0} | all-to-all | bytes 589824 | tf_op jit(solution)/shard_map/all_to_all | solution.py:48
  23.5 0.2 collective-permute-start.3
  23.7 1.0 collective-permute-start
  24.7 6.7 %collective-permute-done.3 = bf16[8,48,384]{2,1,0:T(8,128)(2,1)S(1)} collective-permute-done((bf16[8,48,384]{2,1,0:T(8,128)(2,1)S(1)}, bf16[8,48,384]{2,1,0:T(8,128)(2,1)S(1)}, u32[]{:S(2)}, u32[]{:S(2)}) %collective-permute-start.3) | collective-permute-done | bytes 294944 | tf_op jit(solution)/shard_map/ppermute | solution.py:44
  31.4 0.0 collective-permute-start.4
  31.4 0.0 collective-permute-start.1
  31.4 1.4 %collective-permute-done.1.other_ref = s32[2,2,12]{2,1,0:T(2,128)S(1)} collective-permute-done((s32[2,2,12]{2,1,0:T(2,128)}, s32[2,2,12]{2,1,0:T(2,128)S(1)}, u32[]{:S(2)}, u32[]{:S(2)}) %collective-permute-start.1) | collective-permute-done | bytes 224 | tf_op jit(solution)/shard_map/ppermute | solution.py:33
  32.8 0.0 copy-start.5
  32.8 0.7 copy-done.5
  33.5 2.5 %plan.1 = (s32[108]{0:T(128)S(1)}, s32[54]{0:T(128)S(1)}) custom-call(s32[2,2,12]{2,1,0:T(2,128)S(1)} %bitcast.9, s32[2,2,12]{2,1,0:T(2,128)S(1)} %collective-permute-done.1.other_ref), custom_call_target="tpu_custom_call" | custom-call | tf_op jit(solution)/shard_map/plan/pallas_call | solution.py:138
  36.0 0.0 collective-permute-done
  36.0 0.1 pad_maximum_fusion.refs_0_
  36.1 2.8 %collective-permute-start.2 = (bf16[2,8,48,384]{3,2,1,0:T(8,128)(2,1)S(1)}, bf16[2,8,48,384]{3,2,1,0:T(8,128)(2,1)S(1)}, u32[]{:S(2)}, u32[]{:S(2)}) collective-permute-start(bf16[2,8,48,384]{3,2,1,0:T(8,128)(2,1)S(1)} %pad_maximum_fusion.refs_0_), channel_id=1, source_target_pairs={{20,0},{11,8},{21,1},{10,9},{22,2},{9,10},{23,3},{8,11},{16,4},{15... | collective-permute-start | bytes 1769480 | tf_op jit(solution)/shard_map/ppermute | solution.py:44
  38.9 0.0 collective-permute-done.4
  39.0 0.1 pad_maximum_fusion.1.refs_1_
  39.0 0.8 collective-permute-start.5
  39.8 1.4 %collective-permute-start.8 = (bf16[2,8,48,384]{3,2,1,0:T(8,128)(2,1)S(1)}, bf16[2,8,48,384]{3,2,1,0:T(8,128)(2,1)S(1)}, u32[]{:S(2)}, u32[]{:S(2)}) collective-permute-start(bf16[2,8,48,384]{3,2,1,0:T(8,128)(2,1)S(1)} %pad_maximum_fusion.refs_0_), channel_id=1, source_target_pairs={{4,0},{9,8},{5,1},{8,9},{6,2},{11,10},{7,3},{10,11},{0,4},{13,12},... | collective-permute-start | bytes 1769480 | tf_op jit(solution)/shard_map/ppermute | solution.py:44
  41.1 0.0 collective-permute-done.7.refs_5_
  41.1 1.9 %collective-permute-start.9 = (bf16[2,8,48,384]{3,2,1,0:T(8,128)(2,1)S(1)}, bf16[2,8,48,384]{3,2,1,0:T(8,128)(2,1)S(1)}, u32[]{:S(2)}, u32[]{:S(2)}) collective-permute-start(bf16[2,8,48,384]{3,2,1,0:T(8,128)(2,1)S(1)} %pad_maximum_fusion.1.refs_1_), channel_id=1, source_target_pairs={{20,0},{11,8},{21,1},{10,9},{22,2},{9,10},{23,3},{8,11},{16,4},{15... | collective-permute-start | bytes 1769480 | tf_op jit(solution)/shard_map/ppermute | solution.py:44
  43.1 0.0 collective-permute-done.6.refs_3_.refs_6_
  43.1 0.0 copy-done.2
  43.1 0.0 copy-start
  43.1 2.3 %copy-done = bf16[2,384,3072]{2,1,0:T(8,128)(2,1)S(1)} copy-done((bf16[2,384,3072]{2,1,0:T(8,128)(2,1)S(1)}, bf16[2,384,3072]{2,1,0:T(8,128)(2,1)}, u32[]{:S(2)}) %copy-start) | copy-done | bytes 4718616
  45.4 0.0 copy-start.1
  45.4 4.3 %sums_4.1 = (f32[2,2,384,768]{3,2,1,0:T(8,128)S(1)}, bf16[97,128,128]{2,1,0:T(8,128)(2,1)S(1)}) custom-call(bf16[2,8,48,384]{3,2,1,0:T(8,128)(2,1)S(1)} %pad_maximum_fusion.refs_0_, bf16[2,8,48,384]{3,2,1,0:T(8,128)(2,1)S(1)} %pad_maximum_fusion.1.refs_1_, bf16[2,384,3072]{2,1,0:T(8,128)(2,1)S(1)} %copy-done, ...), custom_call_target="tpu_custom_call" | custom-call | flops 1811939328 | bytes 4718592 | tf_op jit(solution)/shard_map/sums_4/pallas_call | solution.py:238
  49.7 0.0 collective-permute-done.2.refs_2_
  49.7 0.0 collective-permute-done.5.refs_3_
  49.8 0.0 copy-start.3
  49.8 0.0 copy-start.4
  49.8 0.3 collective-permute-start.10
  50.1 1.7 %collective-permute-start.11 = (bf16[2,8,48,384]{3,2,1,0:T(8,128)(2,1)S(1)}, bf16[2,8,48,384]{3,2,1,0:T(8,128)(2,1)S(1)}, u32[]{:S(2)}, u32[]{:S(2)}) collective-permute-start(bf16[2,8,48,384]{3,2,1,0:T(8,128)(2,1)S(1)} %collective-permute-done.5.refs_3_), channel_id=1, source_target_pairs={{20,0},{11,8},{21,1},{10,9},{22,2},{9,10},{23,3},{8,11},{16,4},{15... | collective-permute-start | bytes 1769480 | tf_op jit(solution)/shard_map/ppermute | solution.py:44
  51.8 3.5 %collective-permute-done.8.refs_1_ = bf16[2,8,48,384]{3,2,1,0:T(8,128)(2,1)S(1)} collective-permute-done((bf16[2,8,48,384]{3,2,1,0:T(8,128)(2,1)S(1)}, bf16[2,8,48,384]{3,2,1,0:T(8,128)(2,1)S(1)}, u32[]{:S(2)}, u32[]{:S(2)}) %collective-permute-start.8) | collective-permute-done | bytes 589856 | tf_op jit(solution)/shard_map/ppermute | solution.py:44
  55.3 0.0 collective-permute-done.9.refs_4_
  55.3 0.0 copy-done.1
  55.3 7.3 %sums_8.1 = (f32[2,2,384,768]{3,2,1,0:T(8,128)S(1)}, bf16[2,2,2,384,768]{4,3,2,1,0:T(8,128)(2,1)S(1)}) custom-call(f32[2,2,384,768]{3,2,1,0:T(8,128)S(1)} %get-tuple-element.25.refs_0_, bf16[2,8,48,384]{3,2,1,0:T(8,128)(2,1)S(1)} %collective-permute-done.8.refs_1_, ...), custom_call_target="tpu_custom_call", output_to_operand_aliasing={{0}: (0, {})} | custom-call | flops 3623878656 | bytes 9437184 | tf_op jit(solution)/shard_map/sums_8/pallas_call | solution.py:238
  62.6 0.0 collective-permute-done.10.far_near
  62.6 0.0 collective-permute-done.11.far_away
  62.6 0.0 copy-done.3
  62.6 0.0 copy-done.4
  62.6 7.1 %terms.1 = (f32[16,48,384]{2,1,0:T(8,128)S(1)}, bf16[16,48,384]{2,1,0:T(8,128)(2,1)S(1)}) custom-call(s32[108]{0:T(128)S(1)} %get-tuple-element.21.slots_ref, s32[54]{0:T(128)S(1)} %get-tuple-element.22.rows_ref, s32[12]{0:T(128)S(1)} %copy-done.3, s32[24]{0:T(128)S(1)} %copy-done.4, f32[2,2,384,768]{3,2,1,0:T(8,128)S(1)} %get-tuple-element.28.acc, ...), custom_call_target="tpu_custom_call" | custom-call | tf_op jit(solution)/shard_map/terms/pallas_call | solution.py:335
  69.7 0.1 collective-permute-start.12
  69.8 2.0 %collective-permute-done.12 = bf16[16,48,384]{2,1,0:T(8,128)(2,1)S(1)} collective-permute-done((bf16[16,48,384]{2,1,0:T(8,128)(2,1)S(1)}, bf16[16,48,384]{2,1,0:T(8,128)(2,1)S(1)}, u32[]{:S(2)}, u32[]{:S(2)}) %collective-permute-start.12) | collective-permute-done | bytes 589856 | tf_op jit(solution)/shard_map/ppermute | solution.py:33
  71.8 0.1 add_convert_fusion
  71.9 24.8 %all_to_all.11 = bf16[16,48,384]{2,1,0:T(8,128)(2,1)S(1)} all-to-all(bf16[16,48,384]{2,1,0:T(8,128)(2,1)S(1)} %add_convert_fusion), channel_id=1, replica_groups={{0,16,32,48,64,80,96,112,128,144,160,176,192,208,224,240},{1,17,33,49,6..., dimensions={0} | all-to-all | bytes 1179648 | tf_op jit(solution)/shard_map/all_to_all | solution.py:48
  96.7 0.7 convert_reduce_fusion
Async XLA Ops:
  0.0 43.1 %collective-permute-start.6 = (bf16[2,384,3072]{2,1,0:T(8,128)(2,1)}, bf16[2,384,3072]{2,1,0:T(8,128)(2,1)}, u32[]{:S(2)}, u32[]{:S(2)}) collective-permute-start(bf16[2,384,3072]{2,1,0:T(8,128)(2,1)} %refs_5_.1), channel_id=1, source_target_pairs={{8,0},{0,8},{9,1},{1,9},{10,2},{2,10},{11,3},{3,11},{12,4},{4,12},... | collective-permute-start | bytes 14155784 | tf_op jit(solution)/shard_map/ppermute | solution.py:33
  0.0 43.1 %copy-start.2 = (bf16[2,12,2,128,128]{4,3,2,1,0:T(8,128)(2,1)S(1)}, bf16[2,12,2,128,128]{4,3,2,1,0:T(8,128)(2,1)}, u32[]{:S(2)}) copy-start(bf16[2,12,2,128,128]{4,3,2,1,0:T(8,128)(2,1)} %param.7) | copy-start | bytes 4718596
  0.0 41.1 %collective-permute-start.7 = (bf16[48,128,128]{2,1,0:T(8,128)(2,1)}, bf16[48,128,128]{2,1,0:T(8,128)(2,1)S(1)}, u32[]{:S(2)}, u32[]{:S(2)}) collective-permute-start(bf16[48,128,128]{2,1,0:T(8,128)(2,1)} %bitcast.6), channel_id=1, source_target_pairs={{8,0},{0,8},{9,1},{1,9},{10,2},{2,10},{11,3},{3,11},{12,4},{4,12},... | collective-permute-start | bytes 4718600 | tf_op jit(solution)/shard_map/ppermute | solution.py:33
  23.5 7.9 %collective-permute-start.3 = (bf16[8,48,384]{2,1,0:T(8,128)(2,1)S(1)}, bf16[8,48,384]{2,1,0:T(8,128)(2,1)S(1)}, u32[]{:S(2)}, u32[]{:S(2)}) collective-permute-start(bf16[8,48,384]{2,1,0:T(8,128)(2,1)S(1)} %all_to_all.10), channel_id=1, source_target_pairs={{3,0},{28,8},{2,1},{29,9},{1,2},{30,10},{0,3},{31,11},{7,4},{24,12... | collective-permute-start | bytes 884744 | tf_op jit(solution)/shard_map/ppermute | solution.py:44
  23.7 12.3 %collective-permute-start = (bf16[8,48,384]{2,1,0:T(8,128)(2,1)S(1)}, bf16[8,48,384]{2,1,0:T(8,128)(2,1)S(1)}, u32[]{:S(2)}, u32[]{:S(2)}) collective-permute-start(bf16[8,48,384]{2,1,0:T(8,128)(2,1)S(1)} %all_to_all.10), channel_id=1, source_target_pairs={{1,0},{12,8},{0,1},{13,9},{3,2},{14,10},{2,3},{15,11},{5,4},{8,12}... | collective-permute-start | bytes 884744 | tf_op jit(solution)/shard_map/ppermute | solution.py:44
  31.4 7.5 %collective-permute-start.4 = (bf16[8,48,384]{2,1,0:T(8,128)(2,1)S(1)}, bf16[8,48,384]{2,1,0:T(8,128)(2,1)S(1)}, u32[]{:S(2)}, u32[]{:S(2)}) collective-permute-start(bf16[8,48,384]{2,1,0:T(8,128)(2,1)S(1)} %collective-permute-done.3), channel_id=1, source_target_pairs={{1,0},{12,8},{0,1},{13,9},{3,2},{14,10},{2,3},{15,11},{5,4},{8,12}... | collective-permute-start | bytes 884744 | tf_op jit(solution)/shard_map/ppermute | solution.py:44
  31.4 1.4 %collective-permute-start.1 = (s32[2,2,12]{2,1,0:T(2,128)}, s32[2,2,12]{2,1,0:T(2,128)S(1)}, u32[]{:S(2)}, u32[]{:S(2)}) collective-permute-start(s32[2,2,12]{2,1,0:T(2,128)} %bitcast.8), channel_id=1, source_target_pairs={{8,0},{0,8},{9,1},{1,9},{10,2},{2,10},{11,3},{3,11},{12,4},{4,12},... | collective-permute-start | bytes 584 | tf_op jit(solution)/shard_map/ppermute | solution.py:33
  32.8 0.7 copy-start.5
  36.1 13.6 %collective-permute-start.2 = (bf16[2,8,48,384]{3,2,1,0:T(8,128)(2,1)S(1)}, bf16[2,8,48,384]{3,2,1,0:T(8,128)(2,1)S(1)}, u32[]{:S(2)}, u32[]{:S(2)}) collective-permute-start(bf16[2,8,48,384]{3,2,1,0:T(8,128)(2,1)S(1)} %pad_maximum_fusion.refs_0_), channel_id=1, source_target_pairs={{20,0},{11,8},{21,1},{10,9},{22,2},{9,10},{23,3},{8,11},{16,4},{15... | collective-permute-start | bytes 1769480 | tf_op jit(solution)/shard_map/ppermute | solution.py:44
  39.0 10.7 %collective-permute-start.5 = (bf16[2,8,48,384]{3,2,1,0:T(8,128)(2,1)S(1)}, bf16[2,8,48,384]{3,2,1,0:T(8,128)(2,1)S(1)}, u32[]{:S(2)}, u32[]{:S(2)}) collective-permute-start(bf16[2,8,48,384]{3,2,1,0:T(8,128)(2,1)S(1)} %pad_maximum_fusion.1.refs_1_), channel_id=1, source_target_pairs={{4,0},{9,8},{5,1},{8,9},{6,2},{11,10},{7,3},{10,11},{0,4},{13,12},... | collective-permute-start | bytes 1769480 | tf_op jit(solution)/shard_map/ppermute | solution.py:44
  39.8 15.5 %collective-permute-start.8 = (bf16[2,8,48,384]{3,2,1,0:T(8,128)(2,1)S(1)}, bf16[2,8,48,384]{3,2,1,0:T(8,128)(2,1)S(1)}, u32[]{:S(2)}, u32[]{:S(2)}) collective-permute-start(bf16[2,8,48,384]{3,2,1,0:T(8,128)(2,1)S(1)} %pad_maximum_fusion.refs_0_), channel_id=1, source_target_pairs={{4,0},{9,8},{5,1},{8,9},{6,2},{11,10},{7,3},{10,11},{0,4},{13,12},... | collective-permute-start | bytes 1769480 | tf_op jit(solution)/shard_map/ppermute | solution.py:44
  41.1 14.2 %collective-permute-start.9 = (bf16[2,8,48,384]{3,2,1,0:T(8,128)(2,1)S(1)}, bf16[2,8,48,384]{3,2,1,0:T(8,128)(2,1)S(1)}, u32[]{:S(2)}, u32[]{:S(2)}) collective-permute-start(bf16[2,8,48,384]{3,2,1,0:T(8,128)(2,1)S(1)} %pad_maximum_fusion.1.refs_1_), channel_id=1, source_target_pairs={{20,0},{11,8},{21,1},{10,9},{22,2},{9,10},{23,3},{8,11},{16,4},{15... | collective-permute-start | bytes 1769480 | tf_op jit(solution)/shard_map/ppermute | solution.py:44
  43.1 2.3 %copy-start = (bf16[2,384,3072]{2,1,0:T(8,128)(2,1)S(1)}, bf16[2,384,3072]{2,1,0:T(8,128)(2,1)}, u32[]{:S(2)}) copy-start(bf16[2,384,3072]{2,1,0:T(8,128)(2,1)} %refs_5_.1) | copy-start | bytes 14155780
  45.4 9.9 %copy-start.1 = (bf16[2,384,3072]{2,1,0:T(8,128)(2,1)S(1)}, bf16[2,384,3072]{2,1,0:T(8,128)(2,1)}, u32[]{:S(2)}) copy-start(bf16[2,384,3072]{2,1,0:T(8,128)(2,1)} %refs_5_.1) | copy-start | bytes 14155780
  49.8 12.9 %copy-start.3 = (s32[12]{0:T(128)S(1)}, s32[12]{0:T(128)}, u32[]{:S(2)}) copy-start(s32[12]{0:T(128)} %sizes_ref.1) | copy-start | bytes 148
  49.8 12.9 %copy-start.4 = (s32[24]{0:T(128)S(1)}, s32[24]{0:T(128)}, u32[]{:S(2)}) copy-start(s32[24]{0:T(128)} %right_ref.3) | copy-start | bytes 292
  49.8 12.8 %collective-permute-start.10 = (bf16[2,8,48,384]{3,2,1,0:T(8,128)(2,1)S(1)}, bf16[2,8,48,384]{3,2,1,0:T(8,128)(2,1)S(1)}, u32[]{:S(2)}, u32[]{:S(2)}) collective-permute-start(bf16[2,8,48,384]{3,2,1,0:T(8,128)(2,1)S(1)} %collective-permute-done.2.refs_2_), channel_id=1, source_target_pairs={{4,0},{9,8},{5,1},{8,9},{6,2},{11,10},{7,3},{10,11},{0,4},{13,12},... | collective-permute-start | bytes 1769480 | tf_op jit(solution)/shard_map/ppermute | solution.py:44
  50.1 12.5 %collective-permute-start.11 = (bf16[2,8,48,384]{3,2,1,0:T(8,128)(2,1)S(1)}, bf16[2,8,48,384]{3,2,1,0:T(8,128)(2,1)S(1)}, u32[]{:S(2)}, u32[]{:S(2)}) collective-permute-start(bf16[2,8,48,384]{3,2,1,0:T(8,128)(2,1)S(1)} %collective-permute-done.5.refs_3_), channel_id=1, source_target_pairs={{20,0},{11,8},{21,1},{10,9},{22,2},{9,10},{23,3},{8,11},{16,4},{15... | collective-permute-start | bytes 1769480 | tf_op jit(solution)/shard_map/ppermute | solution.py:44
  69.7 2.1 %collective-permute-start.12 = (bf16[16,48,384]{2,1,0:T(8,128)(2,1)S(1)}, bf16[16,48,384]{2,1,0:T(8,128)(2,1)S(1)}, u32[]{:S(2)}, u32[]{:S(2)}) collective-permute-start(bf16[16,48,384]{2,1,0:T(8,128)(2,1)S(1)} %get-tuple-element.32), channel_id=1, source_target_pairs={{8,0},{0,8},{9,1},{1,9},{10,2},{2,10},{11,3},{3,11},{12,4},{4,12},... | collective-permute-start | bytes 1769480 | tf_op jit(solution)/shard_map/ppermute | solution.py:33

commit v7 on v6

--- a/solution.py
+++ b/solution.py
@@ -190,17 +190,20 @@
     return buffer[index, side].reshape(buffer.shape[2] * buffer.shape[3], buffer.shape[4])
 
 
-def sums_kernel(twos, ahead, *refs):
+def sums_kernel(twos, first, ahead, *refs):
     refs = list(refs)
-    acc_in = refs.pop(0) if ahead else None
+    acc_in = None if first else refs.pop(0)
     arrays = [refs.pop(0) for _ in twos]
     right = (refs.pop(0), refs.pop(0))
-    left = None if ahead else (refs.pop(0), refs.pop(0))
-    acc, later_ref, rbuf, sem, later_sem = refs
+    left = (refs.pop(0), refs.pop(0)) if first else None
+    acc = refs.pop(0)
+    later_ref = refs.pop(0) if first or ahead else None
+    rbuf, sem, later_sem = refs
     copies, halves = two_copies(twos, right, rbuf, sem)
+    later = []
     if ahead:
         later = sum(two_copies(ahead, right, later_ref, later_sem)[0], [])
-    else:
+    if first:
         count = left[0].shape[0]
         later = [
             pltpu.make_async_copy(
@@ -211,7 +214,7 @@
         later_ref[2 * count] = jnp.zeros(later_ref.shape[1:], later_ref.dtype)
     for copy in sum(copies, []) + later:
         copy.start()
-    acc[...] = acc_in[...] if ahead else jnp.zeros_like(acc)
+    acc[...] = jnp.zeros_like(acc) if first else acc_in[...]
     for index, array in enumerate(arrays):
         for copy in copies[index]:
             copy.wait()
@@ -230,32 +233,32 @@
     group, cols = arrays[0].shape[2:]
     pairs = right[0].shape[0]
     units = 2 * len(arrays)
-    near, away = ([acc] if ahead else []) + arrays, list(right) + ([] if ahead else list(left))
+    first = acc is None
+    near, away = ([] if first else [acc]) + arrays, list(right) + (list(left) if first else [])
+    out_shape = [jax.ShapeDtypeStruct((NXH, 2, NZ * group, pairs * cols), jnp.float32)]
+    if first:
+        later = (2 * left[0].shape[0] + 1,) + left[0].shape[1:]
+        out_shape.append(jax.ShapeDtypeStruct(later, jnp.bfloat16))
     if ahead:
-        later = (2, 2, pairs, cols, 2 * cols)
-    else:
-        later = (2 * left[0].shape[0] + 1,) + left[0].shape[1:]
+        out_shape.append(jax.ShapeDtypeStruct((2, 2, pairs, cols, 2 * cols), jnp.bfloat16))
     return pl.pallas_call(
-        functools.partial(sums_kernel, twos, ahead),
-        out_shape=[
-            jax.ShapeDtypeStruct((NXH, 2, NZ * group, pairs * cols), jnp.float32),
-            jax.ShapeDtypeStruct(later, jnp.bfloat16),
-        ],
+        functools.partial(sums_kernel, twos, first, ahead),
+        out_shape=out_shape,
         in_specs=[VMEM_SPEC] * len(near) + [HBM_SPEC] * len(away),
-        out_specs=[VMEM_SPEC] * 2,
+        out_specs=[VMEM_SPEC] * len(out_shape),
         scratch_shapes=[
             pltpu.VMEM((units // 2, 2, pairs, cols, 2 * cols), jnp.bfloat16),
             pltpu.SemaphoreType.DMA((units // 2, 2, 2)),
             pltpu.SemaphoreType.DMA((2, 2, 2) if ahead else (2,)),
         ],
-        input_output_aliases={0: 0} if ahead else {},
+        input_output_aliases={} if first else {0: 0},
         compiler_params=pltpu.CompilerParams(vmem_limit_bytes=VMEM_LIMIT),
         cost_estimate=pl.CostEstimate(
             flops=2 * units * 2 * pairs * NZ * group * cols * cols,
             bytes_accessed=units * 2 * pairs * cols * cols * 2,
             transcendentals=0,
         ),
-        name=f"sums_{units}",
+        name=f"sums_{'first' if first else 'last' if ahead else 'middle'}",
     )(*near, *away)
 
 
@@ -355,12 +358,11 @@
     flat_left = left_ops.reshape((-1, BLK, BLK))
     left = (flat_left, core_swap(flat_left))
     rows_by_slot = jnp.transpose(a_rows, (0, 2, 1))
-    slots, rows = plan(rows_by_slot, core_swap(rows_by_slot))
+    rows_other = core_swap(rows_by_slot)
 
     along_z = exchange(copies, z_groups())
     beside = partner(along_z, "middle", 1)
     across = partner(along_z, "middle", 3)
-    beside, slots, rows = lax.optimization_barrier((beside, slots, rows))
     near = jnp.stack([along_z, beside])
     near_1 = partner(near, "last", 1)
     near_3 = partner(near, "last", 3)
@@ -368,15 +370,15 @@
     away_1 = partner(away, "last", 1)
     away_3 = partner(away, "last", 3)
     acc, both = sums(None, [(near, 0, NEAR), (away, 0, AWAY)], right, left)
+    (acc,) = sums(acc, [(near_1, 1, NEAR), (near_3, 3, NEAR)], right)
     near_3, away_1, acc = lax.optimization_barrier((near_3, away_1, acc))
     near_2 = partner(near_3, "last", 1)
     away_2 = partner(away_1, "last", 3)
     acc, far = sums(
-        acc,
-        [(near_1, 1, NEAR), (near_3, 3, NEAR), (away_1, 1, AWAY), (away_3, 3, AWAY)],
-        right,
-        ahead=((2, NEAR), (2, AWAY)),
-    )
+        acc, [(away_1, 1, AWAY), (away_3, 3, AWAY)], right, ahead=((2, NEAR), (2, AWAY))
+    )
+    rows_other, acc = lax.optimization_barrier((rows_other, acc))
+    slots, rows = plan(rows_by_slot, rows_other)
     keep, send = terms(slots, rows, left_sizes, right_sizes, acc, near_2, away_2, far, both)
     mine = (keep + core_swap(send).astype(jnp.float32)).astype(jnp.bfloat16)
     groups = [

time: 98.5 us -> 102 us (1.036)
  waiting for transfers between devices: 13.7 us -> 18.4 us
    ppermute x9, waiting for transfers between devices: 10.3 us -> 16.4 us  [partner(): return lax.ppermute(value, AXES, perm)]
    ppermute x4, waiting for transfers between devices: 3.36 us -> 2 us  [core_swap(): lax.ppermute(value, AXES, [(flat(z, x, y, 1 - c), flat(z, x, y, c)) for z...]
    pallas_call x2 -> x3, Pallas kernels: 11.6 us -> 12.5 us  [sums(): pl.pallas_call(functools.partial(sums_kernel, twos, first, ahead), out_sh...]
where the time goes in v7:
time: 102 us; the launch traced here: 101 us
  blocking collectives  45.6 us (45%)
  Pallas kernels  23.6 us (23%)
  waiting for transfers between devices  18.4 us (18%)
  starting transfers between devices  10.1 us (10%)
  local copies, waits for them, and re-layouts  2.36 us (2%)
    all_to_all x2, blocking collectives, exchange(): lax.all_to_all(copies, AXES, split_axis=0, concat_axis=0, axis_index_grou...  45.6 us
    ppermute x9, waiting for transfers between devices, partner(): return lax.ppermute(value, AXES, perm)  16.4 us
    pallas_call x3, Pallas kernels, sums(): pl.pallas_call(functools.partial(sums_kernel, twos, first, ahead), out_sh...  12.5 us
    ppermute x9, starting transfers between devices, partner(): return lax.ppermute(value, AXES, perm)  9.2 us
    pallas_call x1, Pallas kernels, terms(): pl.pallas_call(terms_kernel, out_shape=(jax.ShapeDtypeStruct((NZ * NXH, g...  6.98 us
    pallas_call x1, Pallas kernels, plan(): pl.pallas_call(plan_kernel, out_shape=(jax.ShapeDtypeStruct((2 * pairs,),...  2.55 us
    unnamed x12, local copies, waits for them, and re-layouts  2.36 us
  transfers between devices with their start and end apart: 13, of which 4 were waited for; matrix products, arithmetic and copies ran while one was open for 0% of the time, Pallas kernels for 16%

profile of v7, /device:TPU:24, one launch (start us, length us, event | category | flops | bytes accessed | tf_op | source)
XLA Modules:
  0.0 101.2 jit_solution(6867637526064994804)
XLA Ops:
  0.0 0.0 copy-start.2
  0.0 0.0 collective-permute-start.6
  0.0 0.5 collective-permute-start.7
  0.5 1.6 %mask_psi.1 = bf16[8,48,384]{2,1,0:T(8,128)(2,1)} custom-call(s32[12]{0:T(128)} %sizes_ref.1, s32[24]{0:T(128)} %right_ref.3, bf16[48,384]{1,0:T(8,128)(2,1)} %psi_ref.1), custom_call_target="tpu_custom_call" | custom-call | tf_op jit(solution)/shard_map/mask_psi/pallas_call | solution.py:87
  2.1 21.3 %all_to_all.10 = bf16[8,48,384]{2,1,0:T(8,128)(2,1)S(1)} all-to-all(bf16[8,48,384]{2,1,0:T(8,128)(2,1)} %mask_psi.1), channel_id=1, replica_groups={{0,32,64,96,128,160,192,224},{8,40,72,104,136,168,200,232},{1,33,65,97,..., dimensions={0} | all-to-all | bytes 589824 | tf_op jit(solution)/shard_map/all_to_all | solution.py:48
  23.4 0.2 collective-permute-start.3
  23.6 1.0 collective-permute-start.1
  24.6 6.7 %collective-permute-done.3 = bf16[8,48,384]{2,1,0:T(8,128)(2,1)S(1)} collective-permute-done((bf16[8,48,384]{2,1,0:T(8,128)(2,1)S(1)}, bf16[8,48,384]{2,1,0:T(8,128)(2,1)S(1)}, u32[]{:S(2)}, u32[]{:S(2)}) %collective-permute-start.3) | collective-permute-done | bytes 294944 | tf_op jit(solution)/shard_map/ppermute | solution.py:44
  31.3 0.0 collective-permute-start.4
  31.3 0.0 collective-permute-done.1
  31.3 0.1 pad_maximum_fusion.refs_0_
  31.4 2.8 %collective-permute-start.2 = (bf16[2,8,48,384]{3,2,1,0:T(8,128)(2,1)S(1)}, bf16[2,8,48,384]{3,2,1,0:T(8,128)(2,1)S(1)}, u32[]{:S(2)}, u32[]{:S(2)}) collective-permute-start(bf16[2,8,48,384]{3,2,1,0:T(8,128)(2,1)S(1)} %pad_maximum_fusion.refs_0_), channel_id=1, source_target_pairs={{20,0},{11,8},{21,1},{10,9},{22,2},{9,10},{23,3},{8,11},{16,4},{15... | collective-permute-start | bytes 1769480 | tf_op jit(solution)/shard_map/ppermute | solution.py:44
  34.2 0.2 collective-permute-start.8
  34.5 6.8 %collective-permute-done.4 = bf16[8,48,384]{2,1,0:T(8,128)(2,1)S(1)} collective-permute-done((bf16[8,48,384]{2,1,0:T(8,128)(2,1)S(1)}, bf16[8,48,384]{2,1,0:T(8,128)(2,1)S(1)}, u32[]{:S(2)}, u32[]{:S(2)}) %collective-permute-start.4) | collective-permute-done | bytes 294944 | tf_op jit(solution)/shard_map/ppermute | solution.py:44
  41.2 0.1 pad_maximum_fusion.1.refs_1_
  41.3 1.6 %collective-permute-start.5 = (bf16[2,8,48,384]{3,2,1,0:T(8,128)(2,1)S(1)}, bf16[2,8,48,384]{3,2,1,0:T(8,128)(2,1)S(1)}, u32[]{:S(2)}, u32[]{:S(2)}) collective-permute-start(bf16[2,8,48,384]{3,2,1,0:T(8,128)(2,1)S(1)} %pad_maximum_fusion.1.refs_1_), channel_id=1, source_target_pairs={{4,0},{9,8},{5,1},{8,9},{6,2},{11,10},{7,3},{10,11},{0,4},{13,12},... | collective-permute-start | bytes 1769480 | tf_op jit(solution)/shard_map/ppermute | solution.py:44
  42.9 0.0 collective-permute-done.7.refs_5_
  42.9 2.1 %collective-permute-start.9 = (bf16[2,8,48,384]{3,2,1,0:T(8,128)(2,1)S(1)}, bf16[2,8,48,384]{3,2,1,0:T(8,128)(2,1)S(1)}, u32[]{:S(2)}, u32[]{:S(2)}) collective-permute-start(bf16[2,8,48,384]{3,2,1,0:T(8,128)(2,1)S(1)} %pad_maximum_fusion.1.refs_1_), channel_id=1, source_target_pairs={{20,0},{11,8},{21,1},{10,9},{22,2},{9,10},{23,3},{8,11},{16,4},{15... | collective-permute-start | bytes 1769480 | tf_op jit(solution)/shard_map/ppermute | solution.py:44
  45.0 0.0 collective-permute-done.6.refs_3_.refs_4_
  45.0 0.0 copy-done.2
  45.0 0.0 copy-start
  45.0 2.3 %copy-done = bf16[2,384,3072]{2,1,0:T(8,128)(2,1)S(1)} copy-done((bf16[2,384,3072]{2,1,0:T(8,128)(2,1)S(1)}, bf16[2,384,3072]{2,1,0:T(8,128)(2,1)}, u32[]{:S(2)}) %copy-start) | copy-done | bytes 4718616
  47.3 0.0 copy-start.1
  47.4 4.2 %sums_first.1 = (f32[2,2,384,768]{3,2,1,0:T(8,128)S(1)}, bf16[97,128,128]{2,1,0:T(8,128)(2,1)S(1)}) custom-call(bf16[2,8,48,384]{3,2,1,0:T(8,128)(2,1)S(1)} %pad_maximum_fusion.refs_0_, bf16[2,8,48,384]{3,2,1,0:T(8,128)(2,1)S(1)} %pad_maximum_fusion.1.refs_1_, bf16[2,384,3072]{2,1,0:T(8,128)(2,1)S(1)} %copy-done, ...), custom_call_target="tpu_custom_call" | custom-call | flops 1811939328 | bytes 4718592 | tf_op jit(solution)/shard_map/sums_first/pallas_call | solution.py:244
  51.6 0.0 collective-permute-done.2.refs_2_
  51.6 0.0 collective-permute-done.8.refs_1_
  51.6 0.0 copy-done.1
  51.6 0.0 copy-start.5
  51.6 4.1 %sums_middle.1.refs_0_ = f32[2,2,384,768]{3,2,1,0:T(8,128)S(1)} custom-call(f32[2,2,384,768]{3,2,1,0:T(8,128)S(1)} %get-tuple-element.18.refs_0_, bf16[2,8,48,384]{3,2,1,0:T(8,128)(2,1)S(1)} %collective-permute-done.8.refs_1_, bf16[2,8,48,384]{3,2,1,0:T(8,128)(2,1)S(1)} %collective-permute-done.2.refs_2_, ...), custom_call_target="tpu_custom_call", output_to_operand_aliasing={{}: (0, {})} | custom-call | flops 1811939328 | bytes 4718592 | tf_op jit(solution)/shard_map/sums_middle/pallas_call | solution.py:244
  55.7 0.0 collective-permute-done.5.refs_1_
  55.7 1.2 %collective-permute-start.11 = (bf16[2,8,48,384]{3,2,1,0:T(8,128)(2,1)S(1)}, bf16[2,8,48,384]{3,2,1,0:T(8,128)(2,1)S(1)}, u32[]{:S(2)}, u32[]{:S(2)}) collective-permute-start(bf16[2,8,48,384]{3,2,1,0:T(8,128)(2,1)S(1)} %collective-permute-done.5.refs_1_), channel_id=1, source_target_pairs={{20,0},{11,8},{21,1},{10,9},{22,2},{9,10},{23,3},{8,11},{16,4},{15... | collective-permute-start | bytes 1769480 | tf_op jit(solution)/shard_map/ppermute | solution.py:44
  57.0 0.0 collective-permute-start.10
  57.0 0.0 copy-done.5
  57.0 0.0 copy-start.3
  57.0 0.0 copy-start.4
  57.0 0.3 collective-permute-start
  57.3 0.0 collective-permute-done.9.refs_2_
  57.3 4.2 %sums_last.1 = (f32[2,2,384,768]{3,2,1,0:T(8,128)S(1)}, bf16[2,2,2,384,768]{4,3,2,1,0:T(8,128)(2,1)S(1)}) custom-call(f32[2,2,384,768]{3,2,1,0:T(8,128)S(1)} %sums_middle.1.refs_0_, bf16[2,8,48,384]{3,2,1,0:T(8,128)(2,1)S(1)} %collective-permute-done.5.refs_1_, ...), custom_call_target="tpu_custom_call", output_to_operand_aliasing={{0}: (0, {})} | custom-call | flops 1811939328 | bytes 4718592 | tf_op jit(solution)/shard_map/sums_last/pallas_call | solution.py:244
  61.5 0.0 collective-permute-done.other_ref
  61.5 2.6 %plan.1 = (s32[108]{0:T(128)S(1)}, s32[54]{0:T(128)S(1)}) custom-call(s32[2,2,12]{2,1,0:T(2,128)S(1)} %bitcast.9, s32[2,2,12]{2,1,0:T(2,128)S(1)} %collective-permute-done.other_ref), custom_call_target="tpu_custom_call" | custom-call | tf_op jit(solution)/shard_map/plan/pallas_call | solution.py:138
  64.1 2.9 %collective-permute-done.11.far_away = bf16[2,8,48,384]{3,2,1,0:T(8,128)(2,1)S(1)} collective-permute-done((bf16[2,8,48,384]{3,2,1,0:T(8,128)(2,1)S(1)}, bf16[2,8,48,384]{3,2,1,0:T(8,128)(2,1)S(1)}, u32[]{:S(2)}, u32[]{:S(2)}) %collective-permute-start.11) | collective-permute-done | bytes 589856 | tf_op jit(solution)/shard_map/ppermute | solution.py:44
  66.9 0.0 collective-permute-done.10.far_near
  66.9 0.0 copy-done.3
  66.9 0.0 copy-done.4
  66.9 7.0 %terms.1 = (f32[16,48,384]{2,1,0:T(8,128)S(1)}, bf16[16,48,384]{2,1,0:T(8,128)(2,1)S(1)}) custom-call(s32[108]{0:T(128)S(1)} %get-tuple-element.23.slots_ref, s32[54]{0:T(128)S(1)} %get-tuple-element.24.rows_ref, s32[12]{0:T(128)S(1)} %copy-done.3, s32[24]{0:T(128)S(1)} %copy-done.4, f32[2,2,384,768]{3,2,1,0:T(8,128)S(1)} %get-tuple-element.25.acc, ...), custom_call_target="tpu_custom_call" | custom-call | tf_op jit(solution)/shard_map/terms/pallas_call | solution.py:338
  73.9 0.1 collective-permute-start.12
  74.0 2.0 %collective-permute-done.12 = bf16[16,48,384]{2,1,0:T(8,128)(2,1)S(1)} collective-permute-done((bf16[16,48,384]{2,1,0:T(8,128)(2,1)S(1)}, bf16[16,48,384]{2,1,0:T(8,128)(2,1)S(1)}, u32[]{:S(2)}, u32[]{:S(2)}) %collective-permute-start.12) | collective-permute-done | bytes 589856 | tf_op jit(solution)/shard_map/ppermute | solution.py:33
  76.0 0.2 add_convert_fusion
  76.2 24.3 %all_to_all.11 = bf16[16,48,384]{2,1,0:T(8,128)(2,1)S(1)} all-to-all(bf16[16,48,384]{2,1,0:T(8,128)(2,1)S(1)} %add_convert_fusion), channel_id=1, replica_groups={{0,16,32,48,64,80,96,112,128,144,160,176,192,208,224,240},{1,17,33,49,6..., dimensions={0} | all-to-all | bytes 1179648 | tf_op jit(solution)/shard_map/all_to_all | solution.py:48
  100.5 0.7 convert_reduce_fusion
Async XLA Ops:
  0.0 45.0 %copy-start.2 = (bf16[2,12,2,128,128]{4,3,2,1,0:T(8,128)(2,1)S(1)}, bf16[2,12,2,128,128]{4,3,2,1,0:T(8,128)(2,1)}, u32[]{:S(2)}) copy-start(bf16[2,12,2,128,128]{4,3,2,1,0:T(8,128)(2,1)} %param.7) | copy-start | bytes 4718596
  0.0 45.0 %collective-permute-start.6 = (bf16[2,384,3072]{2,1,0:T(8,128)(2,1)}, bf16[2,384,3072]{2,1,0:T(8,128)(2,1)}, u32[]{:S(2)}, u32[]{:S(2)}) collective-permute-start(bf16[2,384,3072]{2,1,0:T(8,128)(2,1)} %refs_3_.3), channel_id=1, source_target_pairs={{8,0},{0,8},{9,1},{1,9},{10,2},{2,10},{11,3},{3,11},{12,4},{4,12},... | collective-permute-start | bytes 14155784 | tf_op jit(solution)/shard_map/ppermute | solution.py:33
  0.0 42.9 %collective-permute-start.7 = (bf16[48,128,128]{2,1,0:T(8,128)(2,1)}, bf16[48,128,128]{2,1,0:T(8,128)(2,1)S(1)}, u32[]{:S(2)}, u32[]{:S(2)}) collective-permute-start(bf16[48,128,128]{2,1,0:T(8,128)(2,1)} %bitcast.6), channel_id=1, source_target_pairs={{8,0},{0,8},{9,1},{1,9},{10,2},{2,10},{11,3},{3,11},{12,4},{4,12},... | collective-permute-start | bytes 4718600 | tf_op jit(solution)/shard_map/ppermute | solution.py:33
  23.4 7.9 %collective-permute-start.3 = (bf16[8,48,384]{2,1,0:T(8,128)(2,1)S(1)}, bf16[8,48,384]{2,1,0:T(8,128)(2,1)S(1)}, u32[]{:S(2)}, u32[]{:S(2)}) collective-permute-start(bf16[8,48,384]{2,1,0:T(8,128)(2,1)S(1)} %all_to_all.10), channel_id=1, source_target_pairs={{3,0},{28,8},{2,1},{29,9},{1,2},{30,10},{0,3},{31,11},{7,4},{24,12... | collective-permute-start | bytes 884744 | tf_op jit(solution)/shard_map/ppermute | solution.py:44
  23.6 7.7 %collective-permute-start.1 = (bf16[8,48,384]{2,1,0:T(8,128)(2,1)S(1)}, bf16[8,48,384]{2,1,0:T(8,128)(2,1)S(1)}, u32[]{:S(2)}, u32[]{:S(2)}) collective-permute-start(bf16[8,48,384]{2,1,0:T(8,128)(2,1)S(1)} %all_to_all.10), channel_id=1, source_target_pairs={{1,0},{12,8},{0,1},{13,9},{3,2},{14,10},{2,3},{15,11},{5,4},{8,12}... | collective-permute-start | bytes 884744 | tf_op jit(solution)/shard_map/ppermute | solution.py:44
  31.3 9.9 %collective-permute-start.4 = (bf16[8,48,384]{2,1,0:T(8,128)(2,1)S(1)}, bf16[8,48,384]{2,1,0:T(8,128)(2,1)S(1)}, u32[]{:S(2)}, u32[]{:S(2)}) collective-permute-start(bf16[8,48,384]{2,1,0:T(8,128)(2,1)S(1)} %collective-permute-done.3), channel_id=1, source_target_pairs={{1,0},{12,8},{0,1},{13,9},{3,2},{14,10},{2,3},{15,11},{5,4},{8,12}... | collective-permute-start | bytes 884744 | tf_op jit(solution)/shard_map/ppermute | solution.py:44
  31.4 20.2 %collective-permute-start.2 = (bf16[2,8,48,384]{3,2,1,0:T(8,128)(2,1)S(1)}, bf16[2,8,48,384]{3,2,1,0:T(8,128)(2,1)S(1)}, u32[]{:S(2)}, u32[]{:S(2)}) collective-permute-start(bf16[2,8,48,384]{3,2,1,0:T(8,128)(2,1)S(1)} %pad_maximum_fusion.refs_0_), channel_id=1, source_target_pairs={{20,0},{11,8},{21,1},{10,9},{22,2},{9,10},{23,3},{8,11},{16,4},{15... | collective-permute-start | bytes 1769480 | tf_op jit(solution)/shard_map/ppermute | solution.py:44
  34.2 17.4 %collective-permute-start.8 = (bf16[2,8,48,384]{3,2,1,0:T(8,128)(2,1)S(1)}, bf16[2,8,48,384]{3,2,1,0:T(8,128)(2,1)S(1)}, u32[]{:S(2)}, u32[]{:S(2)}) collective-permute-start(bf16[2,8,48,384]{3,2,1,0:T(8,128)(2,1)S(1)} %pad_maximum_fusion.refs_0_), channel_id=1, source_target_pairs={{4,0},{9,8},{5,1},{8,9},{6,2},{11,10},{7,3},{10,11},{0,4},{13,12},... | collective-permute-start | bytes 1769480 | tf_op jit(solution)/shard_map/ppermute | solution.py:44
  41.3 14.4 %collective-permute-start.5 = (bf16[2,8,48,384]{3,2,1,0:T(8,128)(2,1)S(1)}, bf16[2,8,48,384]{3,2,1,0:T(8,128)(2,1)S(1)}, u32[]{:S(2)}, u32[]{:S(2)}) collective-permute-start(bf16[2,8,48,384]{3,2,1,0:T(8,128)(2,1)S(1)} %pad_maximum_fusion.1.refs_1_), channel_id=1, source_target_pairs={{4,0},{9,8},{5,1},{8,9},{6,2},{11,10},{7,3},{10,11},{0,4},{13,12},... | collective-permute-start | bytes 1769480 | tf_op jit(solution)/shard_map/ppermute | solution.py:44
  42.9 14.4 %collective-permute-start.9 = (bf16[2,8,48,384]{3,2,1,0:T(8,128)(2,1)S(1)}, bf16[2,8,48,384]{3,2,1,0:T(8,128)(2,1)S(1)}, u32[]{:S(2)}, u32[]{:S(2)}) collective-permute-start(bf16[2,8,48,384]{3,2,1,0:T(8,128)(2,1)S(1)} %pad_maximum_fusion.1.refs_1_), channel_id=1, source_target_pairs={{20,0},{11,8},{21,1},{10,9},{22,2},{9,10},{23,3},{8,11},{16,4},{15... | collective-permute-start | bytes 1769480 | tf_op jit(solution)/shard_map/ppermute | solution.py:44
  45.0 2.3 %copy-start = (bf16[2,384,3072]{2,1,0:T(8,128)(2,1)S(1)}, bf16[2,384,3072]{2,1,0:T(8,128)(2,1)}, u32[]{:S(2)}) copy-start(bf16[2,384,3072]{2,1,0:T(8,128)(2,1)} %refs_3_.3) | copy-start | bytes 14155780
  47.3 4.2 %copy-start.1 = (bf16[2,384,3072]{2,1,0:T(8,128)(2,1)S(1)}, bf16[2,384,3072]{2,1,0:T(8,128)(2,1)}, u32[]{:S(2)}) copy-start(bf16[2,384,3072]{2,1,0:T(8,128)(2,1)} %refs_3_.3) | copy-start | bytes 14155780
  51.6 5.4 %copy-start.5 = (s32[2,12,2]{1,2,0:T(2,128)S(1)}, s32[2,12,2]{1,2,0:T(2,128)}, u32[]{:S(2)}) copy-start(s32[2,12,2]{1,2,0:T(2,128)} %param.8) | copy-start | bytes 580
  55.7 11.2 %collective-permute-start.11 = (bf16[2,8,48,384]{3,2,1,0:T(8,128)(2,1)S(1)}, bf16[2,8,48,384]{3,2,1,0:T(8,128)(2,1)S(1)}, u32[]{:S(2)}, u32[]{:S(2)}) collective-permute-start(bf16[2,8,48,384]{3,2,1,0:T(8,128)(2,1)S(1)} %collective-permute-done.5.refs_1_), channel_id=1, source_target_pairs={{20,0},{11,8},{21,1},{10,9},{22,2},{9,10},{23,3},{8,11},{16,4},{15... | collective-permute-start | bytes 1769480 | tf_op jit(solution)/shard_map/ppermute | solution.py:44
  57.0 10.0 %collective-permute-start.10 = (bf16[2,8,48,384]{3,2,1,0:T(8,128)(2,1)S(1)}, bf16[2,8,48,384]{3,2,1,0:T(8,128)(2,1)S(1)}, u32[]{:S(2)}, u32[]{:S(2)}) collective-permute-start(bf16[2,8,48,384]{3,2,1,0:T(8,128)(2,1)S(1)} %collective-permute-done.2.refs_2_), channel_id=1, source_target_pairs={{4,0},{9,8},{5,1},{8,9},{6,2},{11,10},{7,3},{10,11},{0,4},{13,12},... | collective-permute-start | bytes 1769480 | tf_op jit(solution)/shard_map/ppermute | solution.py:44
  57.0 10.0 %copy-start.3 = (s32[12]{0:T(128)S(1)}, s32[12]{0:T(128)}, u32[]{:S(2)}) copy-start(s32[12]{0:T(128)} %sizes_ref.1) | copy-start | bytes 148
  57.0 10.0 %copy-start.4 = (s32[24]{0:T(128)S(1)}, s32[24]{0:T(128)}, u32[]{:S(2)}) copy-start(s32[24]{0:T(128)} %right_ref.3) | copy-start | bytes 292
  57.0 4.5 %collective-permute-start = (s32[2,2,12]{2,1,0:T(2,128)S(1)}, s32[2,2,12]{2,1,0:T(2,128)S(1)}, u32[]{:S(2)}, u32[]{:S(2)}) collective-permute-start(s32[2,2,12]{2,1,0:T(2,128)S(1)} %bitcast.8), channel_id=1, source_target_pairs={{8,0},{0,8},{9,1},{1,9},{10,2},{2,10},{11,3},{3,11},{12,4},{4,12},... | collective-permute-start | bytes 584 | tf_op jit(solution)/shard_map/ppermute | solution.py:33
  73.9 2.1 %collective-permute-start.12 = (bf16[16,48,384]{2,1,0:T(8,128)(2,1)S(1)}, bf16[16,48,384]{2,1,0:T(8,128)(2,1)S(1)}, u32[]{:S(2)}, u32[]{:S(2)}) collective-permute-start(bf16[16,48,384]{2,1,0:T(8,128)(2,1)S(1)} %get-tuple-element.30), channel_id=1, source_target_pairs={{8,0},{0,8},{9,1},{1,9},{10,2},{2,10},{11,3},{3,11},{12,4},{4,12},... | collective-permute-start | bytes 1769480 | tf_op jit(solution)/shard_map/ppermute | solution.py:33

commit v8 on v7

--- a/solution.py
+++ b/solution.py
@@ -363,22 +363,23 @@
     along_z = exchange(copies, z_groups())
     beside = partner(along_z, "middle", 1)
     across = partner(along_z, "middle", 3)
-    near = jnp.stack([along_z, beside])
+    opposite = partner(across, "middle", 1)
+    near, away = jnp.stack([along_z, beside]), jnp.stack([across, opposite])
+    near, away, rows_other = lax.optimization_barrier((near, away, rows_other))
+    near_3 = partner(near, "last", 3)
+    away_1 = partner(away, "last", 1)
     near_1 = partner(near, "last", 1)
-    near_3 = partner(near, "last", 3)
-    away = jnp.stack([across, partner(across, "middle", 1)])
-    away_1 = partner(away, "last", 1)
     away_3 = partner(away, "last", 3)
+    slots, rows = plan(rows_by_slot, rows_other)
+    near, slots, rows = lax.optimization_barrier((near, slots, rows))
     acc, both = sums(None, [(near, 0, NEAR), (away, 0, AWAY)], right, left)
-    (acc,) = sums(acc, [(near_1, 1, NEAR), (near_3, 3, NEAR)], right)
     near_3, away_1, acc = lax.optimization_barrier((near_3, away_1, acc))
     near_2 = partner(near_3, "last", 1)
     away_2 = partner(away_1, "last", 3)
+    (acc,) = sums(acc, [(near_3, 3, NEAR), (away_1, 1, AWAY)], right)
     acc, far = sums(
-        acc, [(away_1, 1, AWAY), (away_3, 3, AWAY)], right, ahead=((2, NEAR), (2, AWAY))
-    )
-    rows_other, acc = lax.optimization_barrier((rows_other, acc))
-    slots, rows = plan(rows_by_slot, rows_other)
+        acc, [(near_1, 1, NEAR), (away_3, 3, AWAY)], right, ahead=((2, NEAR), (2, AWAY))
+    )
     keep, send = terms(slots, rows, left_sizes, right_sizes, acc, near_2, away_2, far, both)
     mine = (keep + core_swap(send).astype(jnp.float32)).astype(jnp.bfloat16)
     groups = [

time: 102 us -> 101 us (level)
  blocking collectives: 45.6 us -> 26.3 us
  waiting for transfers between devices: 18.4 us -> 28.4 us
  starting transfers between devices: 10.1 us -> 18.4 us
    all_to_all x2 -> x1, blocking collectives: 45.6 us -> 26.3 us  [exchange(): lax.all_to_all(copies, AXES, split_axis=0, concat_axis=0, axis_index_grou...]
    all_to_all x0 -> x1, waiting for transfers between devices: none -> 13 us  [exchange(): lax.all_to_all(copies, AXES, split_axis=0, concat_axis=0, axis_index_grou...]
    all_to_all x0 -> x1, starting transfers between devices: none -> 8.48 us  [exchange(): lax.all_to_all(copies, AXES, split_axis=0, concat_axis=0, axis_index_grou...]
    ppermute x9, waiting for transfers between devices: 16.4 us -> 13.4 us  [partner(): return lax.ppermute(value, AXES, perm)]
  transfers between devices with their start and end apart: 13 -> 14, of which waited for: 4 -> 4; matrix products, arithmetic and copies ran while one was open for 0% -> 0% of each run, Pallas kernels for 16% -> 17%
where the time goes in v8:
time: 101 us
  waiting for transfers between devices  28.4 us (28%)
  blocking collectives  26.3 us (26%)
  Pallas kernels  24 us (24%)
  starting transfers between devices  18.4 us (18%)
  local copies, waits for them, and re-layouts  2.36 us (2%)
  other arithmetic  1.01 us (1%)
    all_to_all x1, blocking collectives, exchange(): lax.all_to_all(copies, AXES, split_axis=0, concat_axis=0, axis_index_grou...  26.3 us
    ppermute x9, waiting for transfers between devices, partner(): return lax.ppermute(value, AXES, perm)  13.4 us
    all_to_all x1, waiting for transfers between devices, exchange(): lax.all_to_all(copies, AXES, split_axis=0, concat_axis=0, axis_index_grou...  13 us
    pallas_call x3, Pallas kernels, sums(): pl.pallas_call(functools.partial(sums_kernel, twos, first, ahead), out_sh...  12.7 us
    ppermute x9, starting transfers between devices, partner(): return lax.ppermute(value, AXES, perm)  9.76 us
    all_to_all x1, starting transfers between devices, exchange(): lax.all_to_all(copies, AXES, split_axis=0, concat_axis=0, axis_index_grou...  8.48 us
    pallas_call x1, Pallas kernels, terms(): pl.pallas_call(terms_kernel, out_shape=(jax.ShapeDtypeStruct((NZ * NXH, g...  7.08 us
    pallas_call x1, Pallas kernels, plan(): pl.pallas_call(plan_kernel, out_shape=(jax.ShapeDtypeStruct((2 * pairs,),...  2.54 us
  transfers between devices with their start and end apart: 14, of which 4 were waited for; matrix products, arithmetic and copies ran while one was open for 0% of the time, Pallas kernels for 17%

profile of v8, /device:TPU:24, one launch (start us, length us, event | category | flops | bytes accessed | tf_op | source)
XLA Modules:
  0.0 100.7 jit_solution(2628745908508896988)
XLA Ops:
  0.0 0.0 copy-start.2
  0.0 0.0 copy-start.5
  0.0 0.0 collective-permute-start.6
  0.0 1.7 %mask_psi.1 = bf16[8,48,384]{2,1,0:T(8,128)(2,1)} custom-call(s32[12]{0:T(128)} %sizes_ref.1, s32[24]{0:T(128)} %right_ref.3, bf16[48,384]{1,0:T(8,128)(2,1)} %psi_ref.1), custom_call_target="tpu_custom_call" | custom-call | tf_op jit(solution)/shard_map/mask_psi/pallas_call | solution.py:87
  1.7 8.5 %all-to-all-start = ((bf16[8,48,384]{2,1,0:T(8,128)(2,1)}), bf16[8,48,384]{2,1,0:T(8,128)(2,1)S(1)}, u32[]{:S(2)}, u32[]{:S(2)}) async-start(bf16[8,48,384]{2,1,0:T(8,128)(2,1)} %mask_psi.1), calls=%async_computation | async-start | bytes 589824 | tf_op jit(solution)/shard_map/all_to_all | solution.py:48
  10.2 0.1 collective-permute-start.7
  10.3 13.0 %all-to-all-done = bf16[8,48,384]{2,1,0:T(8,128)(2,1)S(1)} async-done(((bf16[8,48,384]{2,1,0:T(8,128)(2,1)}), bf16[8,48,384]{2,1,0:T(8,128)(2,1)S(1)}, u32[]{:S(2)}, u32[]{:S(2)}) %all-to-all-start) | async-done | bytes 294944 | tf_op jit(solution)/shard_map/all_to_all | solution.py:48
  23.3 0.2 collective-permute-start.1
  23.5 1.0 collective-permute-start
  24.5 6.7 %collective-permute-done.1 = bf16[8,48,384]{2,1,0:T(8,128)(2,1)S(1)} collective-permute-done((bf16[8,48,384]{2,1,0:T(8,128)(2,1)S(1)}, bf16[8,48,384]{2,1,0:T(8,128)(2,1)S(1)}, u32[]{:S(2)}, u32[]{:S(2)}) %collective-permute-start.1) | collective-permute-done | bytes 294944 | tf_op jit(solution)/shard_map/ppermute | solution.py:44
  31.2 0.0 collective-permute-start.2
  31.2 0.0 collective-permute-start.3
  31.2 0.0 collective-permute-done
  31.2 0.1 pad_maximum_fusion.refs_0_
  31.3 6.6 %collective-permute-done.2 = bf16[8,48,384]{2,1,0:T(8,128)(2,1)S(1)} collective-permute-done((bf16[8,48,384]{2,1,0:T(8,128)(2,1)S(1)}, bf16[8,48,384]{2,1,0:T(8,128)(2,1)S(1)}, u32[]{:S(2)}, u32[]{:S(2)}) %collective-permute-start.2) | collective-permute-done | bytes 294944 | tf_op jit(solution)/shard_map/ppermute | solution.py:44
  37.9 0.1 pad_maximum_fusion.1.refs_1_
  38.0 0.0 collective-permute-done.3.other_ref
  38.0 2.8 %collective-permute-start.4 = (bf16[2,8,48,384]{3,2,1,0:T(8,128)(2,1)S(1)}, bf16[2,8,48,384]{3,2,1,0:T(8,128)(2,1)S(1)}, u32[]{:S(2)}, u32[]{:S(2)}) collective-permute-start(bf16[2,8,48,384]{3,2,1,0:T(8,128)(2,1)S(1)} %pad_maximum_fusion.refs_0_), channel_id=1, source_target_pairs={{20,0},{11,8},{21,1},{10,9},{22,2},{9,10},{23,3},{8,11},{16,4},{15... | collective-permute-start | bytes 1769480 | tf_op jit(solution)/shard_map/ppermute | solution.py:44
  40.9 0.2 collective-permute-start.5
  41.1 1.8 %collective-permute-start.8 = (bf16[2,8,48,384]{3,2,1,0:T(8,128)(2,1)S(1)}, bf16[2,8,48,384]{3,2,1,0:T(8,128)(2,1)S(1)}, u32[]{:S(2)}, u32[]{:S(2)}) collective-permute-start(bf16[2,8,48,384]{3,2,1,0:T(8,128)(2,1)S(1)} %pad_maximum_fusion.refs_0_), channel_id=1, source_target_pairs={{4,0},{9,8},{5,1},{8,9},{6,2},{11,10},{7,3},{10,11},{0,4},{13,12},... | collective-permute-start | bytes 1769480 | tf_op jit(solution)/shard_map/ppermute | solution.py:44
  42.9 0.0 copy-done.5
  42.9 2.5 %plan.1 = (s32[108]{0:T(128)S(1)}, s32[54]{0:T(128)S(1)}) custom-call(s32[2,2,12]{2,1,0:T(2,128)S(1)} %bitcast.9, s32[2,2,12]{2,1,0:T(2,128)S(1)} %collective-permute-done.3.other_ref), custom_call_target="tpu_custom_call" | custom-call | tf_op jit(solution)/shard_map/plan/pallas_call | solution.py:138
  45.5 0.0 collective-permute-done.7.refs_5_
  45.5 0.6 collective-permute-start.9
  46.0 0.0 collective-permute-done.6.refs_3_.refs_4_
  46.0 0.0 copy-done.2
  46.0 0.0 copy-start
  46.0 2.3 %copy-done = bf16[2,384,3072]{2,1,0:T(8,128)(2,1)S(1)} copy-done((bf16[2,384,3072]{2,1,0:T(8,128)(2,1)S(1)}, bf16[2,384,3072]{2,1,0:T(8,128)(2,1)}, u32[]{:S(2)}) %copy-start) | copy-done | bytes 4718616
  48.4 0.0 copy-start.1
  48.4 4.3 %sums_first.1 = (f32[2,2,384,768]{3,2,1,0:T(8,128)S(1)}, bf16[97,128,128]{2,1,0:T(8,128)(2,1)S(1)}) custom-call(bf16[2,8,48,384]{3,2,1,0:T(8,128)(2,1)S(1)} %pad_maximum_fusion.refs_0_, bf16[2,8,48,384]{3,2,1,0:T(8,128)(2,1)S(1)} %pad_maximum_fusion.1.refs_1_, bf16[2,384,3072]{2,1,0:T(8,128)(2,1)S(1)} %copy-done, ...), custom_call_target="tpu_custom_call" | custom-call | flops 1811939328 | bytes 4718592 | tf_op jit(solution)/shard_map/sums_first/pallas_call | solution.py:244
  52.7 0.0 collective-permute-done.4.refs_1_
  52.7 0.0 collective-permute-done.5.refs_2_
  52.7 0.4 collective-permute-start.10
  53.1 2.8 %collective-permute-start.11 = (bf16[2,8,48,384]{3,2,1,0:T(8,128)(2,1)S(1)}, bf16[2,8,48,384]{3,2,1,0:T(8,128)(2,1)S(1)}, u32[]{:S(2)}, u32[]{:S(2)}) collective-permute-start(bf16[2,8,48,384]{3,2,1,0:T(8,128)(2,1)S(1)} %collective-permute-done.5.refs_2_), channel_id=1, source_target_pairs={{20,0},{11,8},{21,1},{10,9},{22,2},{9,10},{23,3},{8,11},{16,4},{15... | collective-permute-start | bytes 1769480 | tf_op jit(solution)/shard_map/ppermute | solution.py:44
  55.8 0.0 copy-done.1
  55.8 4.2 %sums_middle.1.refs_0_ = f32[2,2,384,768]{3,2,1,0:T(8,128)S(1)} custom-call(f32[2,2,384,768]{3,2,1,0:T(8,128)S(1)} %get-tuple-element.31.refs_0_, bf16[2,8,48,384]{3,2,1,0:T(8,128)(2,1)S(1)} %collective-permute-done.4.refs_1_, bf16[2,8,48,384]{3,2,1,0:T(8,128)(2,1)S(1)} %collective-permute-done.5.refs_2_, ...), custom_call_target="tpu_custom_call", output_to_operand_aliasing={{}: (0, {})} | custom-call | flops 1811939328 | bytes 4718592 | tf_op jit(solution)/shard_map/sums_middle/pallas_call | solution.py:244
  60.0 0.0 copy-start.3
  60.0 0.0 copy-start.4
  60.0 0.0 collective-permute-done.8.refs_1_
  60.0 0.0 collective-permute-done.9.refs_2_
  60.0 4.3 %sums_last.1 = (f32[2,2,384,768]{3,2,1,0:T(8,128)S(1)}, bf16[2,2,2,384,768]{4,3,2,1,0:T(8,128)(2,1)S(1)}) custom-call(f32[2,2,384,768]{3,2,1,0:T(8,128)S(1)} %sums_middle.1.refs_0_, bf16[2,8,48,384]{3,2,1,0:T(8,128)(2,1)S(1)} %collective-permute-done.8.refs_1_, ...), custom_call_target="tpu_custom_call", output_to_operand_aliasing={{0}: (0, {})} | custom-call | flops 1811939328 | bytes 4718592 | tf_op jit(solution)/shard_map/sums_last/pallas_call | solution.py:244
  64.3 0.0 collective-permute-done.10.far_near
  64.3 0.0 collective-permute-done.11.far_away
  64.3 0.0 copy-done.3
  64.4 0.0 copy-done.4
  64.4 7.1 %terms.1 = (f32[16,48,384]{2,1,0:T(8,128)S(1)}, bf16[16,48,384]{2,1,0:T(8,128)(2,1)S(1)}) custom-call(s32[108]{0:T(128)S(1)} %get-tuple-element.26.slots_ref, s32[54]{0:T(128)S(1)} %get-tuple-element.27.rows_ref, s32[12]{0:T(128)S(1)} %copy-done.3, s32[24]{0:T(128)S(1)} %copy-done.4, f32[2,2,384,768]{3,2,1,0:T(8,128)S(1)} %get-tuple-element.34.acc, ...), custom_call_target="tpu_custom_call" | custom-call | tf_op jit(solution)/shard_map/terms/pallas_call | solution.py:338
  71.5 0.1 collective-permute-start.12
  71.6 2.0 %collective-permute-done.12 = bf16[16,48,384]{2,1,0:T(8,128)(2,1)S(1)} collective-permute-done((bf16[16,48,384]{2,1,0:T(8,128)(2,1)S(1)}, bf16[16,48,384]{2,1,0:T(8,128)(2,1)S(1)}, u32[]{:S(2)}, u32[]{:S(2)}) %collective-permute-start.12) | collective-permute-done | bytes 589856 | tf_op jit(solution)/shard_map/ppermute | solution.py:33
  73.5 0.2 add_convert_fusion
  73.7 26.3 %all_to_all.10 = bf16[16,48,384]{2,1,0:T(8,128)(2,1)S(1)} all-to-all(bf16[16,48,384]{2,1,0:T(8,128)(2,1)S(1)} %add_convert_fusion), channel_id=1, replica_groups={{0,16,32,48,64,80,96,112,128,144,160,176,192,208,224,240},{1,17,33,49,6..., dimensions={0} | all-to-all | bytes 1179648 | tf_op jit(solution)/shard_map/all_to_all | solution.py:48
  100.0 0.7 convert_reduce_fusion
Async XLA Ops:
  0.0 46.0 %copy-start.2 = (bf16[2,12,2,128,128]{4,3,2,1,0:T(8,128)(2,1)S(1)}, bf16[2,12,2,128,128]{4,3,2,1,0:T(8,128)(2,1)}, u32[]{:S(2)}) copy-start(bf16[2,12,2,128,128]{4,3,2,1,0:T(8,128)(2,1)} %param.7) | copy-start | bytes 4718596
  0.0 42.9 %copy-start.5 = (s32[2,12,2]{1,2,0:T(2,128)S(1)}, s32[2,12,2]{1,2,0:T(2,128)}, u32[]{:S(2)}) copy-start(s32[2,12,2]{1,2,0:T(2,128)} %param.8) | copy-start | bytes 580
  0.0 46.0 %collective-permute-start.6 = (bf16[2,384,3072]{2,1,0:T(8,128)(2,1)}, bf16[2,384,3072]{2,1,0:T(8,128)(2,1)}, u32[]{:S(2)}, u32[]{:S(2)}) collective-permute-start(bf16[2,384,3072]{2,1,0:T(8,128)(2,1)} %refs_3_.3), channel_id=1, source_target_pairs={{8,0},{0,8},{9,1},{1,9},{10,2},{2,10},{11,3},{3,11},{12,4},{4,12},... | collective-permute-start | bytes 14155784 | tf_op jit(solution)/shard_map/ppermute | solution.py:33
  1.7 21.6 %all-to-all-start = ((bf16[8,48,384]{2,1,0:T(8,128)(2,1)}), bf16[8,48,384]{2,1,0:T(8,128)(2,1)S(1)}, u32[]{:S(2)}, u32[]{:S(2)}) async-start(bf16[8,48,384]{2,1,0:T(8,128)(2,1)} %mask_psi.1), calls=%async_computation | async-start | bytes 589824 | tf_op jit(solution)/shard_map/all_to_all | solution.py:48
  10.2 35.3 %collective-permute-start.7 = (bf16[48,128,128]{2,1,0:T(8,128)(2,1)}, bf16[48,128,128]{2,1,0:T(8,128)(2,1)S(1)}, u32[]{:S(2)}, u32[]{:S(2)}) collective-permute-start(bf16[48,128,128]{2,1,0:T(8,128)(2,1)} %bitcast.6), channel_id=1, source_target_pairs={{8,0},{0,8},{9,1},{1,9},{10,2},{2,10},{11,3},{3,11},{12,4},{4,12},... | collective-permute-start | bytes 4718600 | tf_op jit(solution)/shard_map/ppermute | solution.py:33
  23.3 7.9 %collective-permute-start.1 = (bf16[8,48,384]{2,1,0:T(8,128)(2,1)S(1)}, bf16[8,48,384]{2,1,0:T(8,128)(2,1)S(1)}, u32[]{:S(2)}, u32[]{:S(2)}) collective-permute-start(bf16[8,48,384]{2,1,0:T(8,128)(2,1)S(1)} %all-to-all-done), channel_id=1, source_target_pairs={{3,0},{28,8},{2,1},{29,9},{1,2},{30,10},{0,3},{31,11},{7,4},{24,12... | collective-permute-start | bytes 884744 | tf_op jit(solution)/shard_map/ppermute | solution.py:44
  23.5 7.7 %collective-permute-start = (bf16[8,48,384]{2,1,0:T(8,128)(2,1)S(1)}, bf16[8,48,384]{2,1,0:T(8,128)(2,1)S(1)}, u32[]{:S(2)}, u32[]{:S(2)}) collective-permute-start(bf16[8,48,384]{2,1,0:T(8,128)(2,1)S(1)} %all-to-all-done), channel_id=1, source_target_pairs={{1,0},{12,8},{0,1},{13,9},{3,2},{14,10},{2,3},{15,11},{5,4},{8,12}... | collective-permute-start | bytes 884744 | tf_op jit(solution)/shard_map/ppermute | solution.py:44
  31.2 6.7 %collective-permute-start.2 = (bf16[8,48,384]{2,1,0:T(8,128)(2,1)S(1)}, bf16[8,48,384]{2,1,0:T(8,128)(2,1)S(1)}, u32[]{:S(2)}, u32[]{:S(2)}) collective-permute-start(bf16[8,48,384]{2,1,0:T(8,128)(2,1)S(1)} %collective-permute-done.1), channel_id=1, source_target_pairs={{1,0},{12,8},{0,1},{13,9},{3,2},{14,10},{2,3},{15,11},{5,4},{8,12}... | collective-permute-start | bytes 884744 | tf_op jit(solution)/shard_map/ppermute | solution.py:44
  31.2 6.8 %collective-permute-start.3 = (s32[2,2,12]{2,1,0:T(2,128)}, s32[2,2,12]{2,1,0:T(2,128)S(1)}, u32[]{:S(2)}, u32[]{:S(2)}) collective-permute-start(s32[2,2,12]{2,1,0:T(2,128)} %bitcast.8), channel_id=1, source_target_pairs={{8,0},{0,8},{9,1},{1,9},{10,2},{2,10},{11,3},{3,11},{12,4},{4,12},... | collective-permute-start | bytes 584 | tf_op jit(solution)/shard_map/ppermute | solution.py:33
  38.0 14.7 %collective-permute-start.4 = (bf16[2,8,48,384]{3,2,1,0:T(8,128)(2,1)S(1)}, bf16[2,8,48,384]{3,2,1,0:T(8,128)(2,1)S(1)}, u32[]{:S(2)}, u32[]{:S(2)}) collective-permute-start(bf16[2,8,48,384]{3,2,1,0:T(8,128)(2,1)S(1)} %pad_maximum_fusion.refs_0_), channel_id=1, source_target_pairs={{20,0},{11,8},{21,1},{10,9},{22,2},{9,10},{23,3},{8,11},{16,4},{15... | collective-permute-start | bytes 1769480 | tf_op jit(solution)/shard_map/ppermute | solution.py:44
  40.9 11.8 %collective-permute-start.5 = (bf16[2,8,48,384]{3,2,1,0:T(8,128)(2,1)S(1)}, bf16[2,8,48,384]{3,2,1,0:T(8,128)(2,1)S(1)}, u32[]{:S(2)}, u32[]{:S(2)}) collective-permute-start(bf16[2,8,48,384]{3,2,1,0:T(8,128)(2,1)S(1)} %pad_maximum_fusion.1.refs_1_), channel_id=1, source_target_pairs={{4,0},{9,8},{5,1},{8,9},{6,2},{11,10},{7,3},{10,11},{0,4},{13,12},... | collective-permute-start | bytes 1769480 | tf_op jit(solution)/shard_map/ppermute | solution.py:44
  41.1 18.9 %collective-permute-start.8 = (bf16[2,8,48,384]{3,2,1,0:T(8,128)(2,1)S(1)}, bf16[2,8,48,384]{3,2,1,0:T(8,128)(2,1)S(1)}, u32[]{:S(2)}, u32[]{:S(2)}) collective-permute-start(bf16[2,8,48,384]{3,2,1,0:T(8,128)(2,1)S(1)} %pad_maximum_fusion.refs_0_), channel_id=1, source_target_pairs={{4,0},{9,8},{5,1},{8,9},{6,2},{11,10},{7,3},{10,11},{0,4},{13,12},... | collective-permute-start | bytes 1769480 | tf_op jit(solution)/shard_map/ppermute | solution.py:44
  45.5 14.6 %collective-permute-start.9 = (bf16[2,8,48,384]{3,2,1,0:T(8,128)(2,1)S(1)}, bf16[2,8,48,384]{3,2,1,0:T(8,128)(2,1)S(1)}, u32[]{:S(2)}, u32[]{:S(2)}) collective-permute-start(bf16[2,8,48,384]{3,2,1,0:T(8,128)(2,1)S(1)} %pad_maximum_fusion.1.refs_1_), channel_id=1, source_target_pairs={{20,0},{11,8},{21,1},{10,9},{22,2},{9,10},{23,3},{8,11},{16,4},{15... | collective-permute-start | bytes 1769480 | tf_op jit(solution)/shard_map/ppermute | solution.py:44
  46.0 2.3 %copy-start = (bf16[2,384,3072]{2,1,0:T(8,128)(2,1)S(1)}, bf16[2,384,3072]{2,1,0:T(8,128)(2,1)}, u32[]{:S(2)}) copy-start(bf16[2,384,3072]{2,1,0:T(8,128)(2,1)} %refs_3_.3) | copy-start | bytes 14155780
  48.4 7.5 %copy-start.1 = (bf16[2,384,3072]{2,1,0:T(8,128)(2,1)S(1)}, bf16[2,384,3072]{2,1,0:T(8,128)(2,1)}, u32[]{:S(2)}) copy-start(bf16[2,384,3072]{2,1,0:T(8,128)(2,1)} %refs_3_.3) | copy-start | bytes 14155780
  52.7 11.6 %collective-permute-start.10 = (bf16[2,8,48,384]{3,2,1,0:T(8,128)(2,1)S(1)}, bf16[2,8,48,384]{3,2,1,0:T(8,128)(2,1)S(1)}, u32[]{:S(2)}, u32[]{:S(2)}) collective-permute-start(bf16[2,8,48,384]{3,2,1,0:T(8,128)(2,1)S(1)} %collective-permute-done.4.refs_1_), channel_id=1, source_target_pairs={{4,0},{9,8},{5,1},{8,9},{6,2},{11,10},{7,3},{10,11},{0,4},{13,12},... | collective-permute-start | bytes 1769480 | tf_op jit(solution)/shard_map/ppermute | solution.py:44
  53.1 11.3 %collective-permute-start.11 = (bf16[2,8,48,384]{3,2,1,0:T(8,128)(2,1)S(1)}, bf16[2,8,48,384]{3,2,1,0:T(8,128)(2,1)S(1)}, u32[]{:S(2)}, u32[]{:S(2)}) collective-permute-start(bf16[2,8,48,384]{3,2,1,0:T(8,128)(2,1)S(1)} %collective-permute-done.5.refs_2_), channel_id=1, source_target_pairs={{20,0},{11,8},{21,1},{10,9},{22,2},{9,10},{23,3},{8,11},{16,4},{15... | collective-permute-start | bytes 1769480 | tf_op jit(solution)/shard_map/ppermute | solution.py:44
  60.0 4.4 %copy-start.3 = (s32[12]{0:T(128)S(1)}, s32[12]{0:T(128)}, u32[]{:S(2)}) copy-start(s32[12]{0:T(128)} %sizes_ref.1) | copy-start | bytes 148
  60.0 4.4 %copy-start.4 = (s32[24]{0:T(128)S(1)}, s32[24]{0:T(128)}, u32[]{:S(2)}) copy-start(s32[24]{0:T(128)} %right_ref.3) | copy-start | bytes 292
  71.5 2.1 %collective-permute-start.12 = (bf16[16,48,384]{2,1,0:T(8,128)(2,1)S(1)}, bf16[16,48,384]{2,1,0:T(8,128)(2,1)S(1)}, u32[]{:S(2)}, u32[]{:S(2)}) collective-permute-start(bf16[16,48,384]{2,1,0:T(8,128)(2,1)S(1)} %get-tuple-element.38), channel_id=1, source_target_pairs={{8,0},{0,8},{9,1},{1,9},{10,2},{2,10},{11,3},{3,11},{12,4},{4,12},... | collective-permute-start | bytes 1769480 | tf_op jit(solution)/shard_map/ppermute | solution.py:33

commit v9 on v6

--- a/solution.py
+++ b/solution.py
@@ -41,6 +41,14 @@
         along_x = (ring == "last") == (c == 0)
         source = flat(z, x ^ step, y, c) if along_x else flat(z, x, y ^ step, c)
         perm.append((source, flat(z, x, y, c)))
+    return lax.ppermute(value, AXES, perm)
+
+
+def to_owner(value, step):
+    perm = []
+    for z, x, y, c in everywhere():
+        q = (z * NXH + x // NXL) ^ step
+        perm.append((flat(q // NXH, (q % NXH) * NXL + x % NXL, y, c), flat(z, x, y, c)))
     return lax.ppermute(value, AXES, perm)
 
 
@@ -264,7 +272,7 @@
 
 def terms_kernel(slots_ref, rows_ref, sizes_ref, right_ref, acc, far_near, far_away, far_ref, left_ref, *refs):
     keep_ref, send_ref, part, total = refs
-    _, xh, core, xl, y = position()
+    z, xh, core, xl, y = position()
     arrays = (far_near, far_away)
     group, cols = far_near.shape[2:]
     pairs = far_ref.shape[2]
@@ -319,12 +327,13 @@
             )
             total[pl.ds(pl.multiple_of(rows_ref[number] * BLK, BLK), BLK), :] += result
 
-    for q in range(NZ * NXH):
+    for step in range(NZ * NXH):
+        q = (z * NXH + xh) ^ step
         mine = pl.multiple_of((q * NC + core) * group, 16)
         theirs = pl.multiple_of((q * NC + 1 - core) * group, 16)
-        keep_ref[q] = jnp.where(row_live(mine, sizes_ref, group), total[pl.ds(mine, group), :], 0.0)
+        keep_ref[step] = jnp.where(row_live(mine, sizes_ref, group), total[pl.ds(mine, group), :], 0.0)
         other = jnp.where(row_live(theirs, sizes_ref, group), total[pl.ds(theirs, group), :], 0.0)
-        send_ref[q] = other.astype(send_ref.dtype)
+        send_ref[step] = other.astype(send_ref.dtype)
 
 
 def terms(slots, rows, left_sizes, right_sizes, acc, far_near, far_away, far, left):
@@ -378,15 +387,12 @@
         ahead=((2, NEAR), (2, AWAY)),
     )
     keep, send = terms(slots, rows, left_sizes, right_sizes, acc, near_2, away_2, far, both)
-    mine = (keep + core_swap(send).astype(jnp.float32)).astype(jnp.bfloat16)
-    groups = [
-        [flat(z, xh * NXL + xl, y, c) for z in range(NZ) for xh in range(NXH)]
-        for c in range(NC)
-        for xl in range(NXL)
-        for y in range(NY)
-    ]
-    parts = exchange(mine, groups)
-    return parts.astype(jnp.float32).sum(axis=0)
+    chip = keep + core_swap(send).astype(jnp.float32)
+    rounded = chip.astype(jnp.bfloat16)
+    summed = chip[0]
+    for step in range(1, NZ * NXH):
+        summed = summed + to_owner(rounded[step], step).astype(jnp.float32)
+    return summed
 
 
 def solution(mesh):

time: 98.5 us -> 114 us (1.16)
  starting transfers between devices: 10.7 us -> 48.1 us
  blocking collectives: 46.2 us -> 21.4 us
  waiting for transfers between devices: 13.7 us -> 17.3 us
    ppermute x0 -> x15, starting transfers between devices: none -> 37.4 us  [to_owner(): return lax.ppermute(value, AXES, perm)]
    all_to_all x2 -> x1, blocking collectives: 46.2 us -> 21.4 us  [exchange(): lax.all_to_all(copies, AXES, split_axis=0, concat_axis=0, axis_index_grou...]
    ppermute x0 -> x15, waiting for transfers between devices: none -> 3.6 us  [to_owner(): return lax.ppermute(value, AXES, perm)]
  transfers between devices with their start and end apart: 13 -> 28, of which waited for: 4 -> 6; matrix products, arithmetic and copies ran while one was open for 0% -> 0% of each run, Pallas kernels for 16% -> 14%
where the time goes in v9:
time: 114 us
  starting transfers between devices  48.1 us (42%)
  Pallas kernels  22.8 us (20%)
  blocking collectives  21.4 us (19%)
  waiting for transfers between devices  17.3 us (15%)
  local copies, waits for them, and re-layouts  3.1 us (3%)
    ppermute x15, starting transfers between devices, to_owner(): return lax.ppermute(value, AXES, perm)  37.4 us
    all_to_all x1, blocking collectives, exchange(): lax.all_to_all(copies, AXES, split_axis=0, concat_axis=0, axis_index_grou...  21.4 us
    pallas_call x2, Pallas kernels, sums(): pl.pallas_call(functools.partial(sums_kernel, twos, ahead), out_shape=[ja...  11.6 us
    ppermute x9, waiting for transfers between devices, partner(): return lax.ppermute(value, AXES, perm)  10.3 us
    ppermute x9, starting transfers between devices, partner(): return lax.ppermute(value, AXES, perm)  10.1 us
    pallas_call x1, Pallas kernels, terms(): pl.pallas_call(terms_kernel, out_shape=(jax.ShapeDtypeStruct((NZ * NXH, g...  7.15 us
    ppermute x15, waiting for transfers between devices, to_owner(): return lax.ppermute(value, AXES, perm)  3.6 us
    ppermute x4, waiting for transfers between devices, core_swap(): lax.ppermute(value, AXES, [(flat(z, x, y, 1 - c), flat(z, x, y, c)) for z...  3.36 us
  transfers between devices with their start and end apart: 28, of which 6 were waited for; matrix products, arithmetic and copies ran while one was open for 0% of the time, Pallas kernels for 14%

profile of v9, /device:TPU:24, one launch (start us, length us, event | category | flops | bytes accessed | tf_op | source)
XLA Modules:
  0.0 113.8 jit_solution(615127565398568738)
XLA Ops:
  0.0 0.0 collective-permute-start.6
  0.0 0.5 collective-permute-start.7
  0.5 1.6 %mask_psi.1 = bf16[8,48,384]{2,1,0:T(8,128)(2,1)} custom-call(s32[12]{0:T(128)} %sizes_ref.1, s32[24]{0:T(128)} %right_ref.3, bf16[48,384]{1,0:T(8,128)(2,1)} %psi_ref.1), custom_call_target="tpu_custom_call" | custom-call | tf_op jit(solution)/shard_map/mask_psi/pallas_call | solution.py:95
  2.1 21.4 %all_to_all.5 = bf16[8,48,384]{2,1,0:T(8,128)(2,1)S(1)} all-to-all(bf16[8,48,384]{2,1,0:T(8,128)(2,1)} %mask_psi.1), channel_id=1, replica_groups={{0,32,64,96,128,160,192,224},{8,40,72,104,136,168,200,232},{1,33,65,97,..., dimensions={0} | all-to-all | bytes 589824 | tf_op jit(solution)/shard_map/all_to_all | solution.py:56
  23.5 0.2 collective-permute-start.3
  23.7 1.0 collective-permute-start
  24.7 6.7 %collective-permute-done.3 = bf16[8,48,384]{2,1,0:T(8,128)(2,1)S(1)} collective-permute-done((bf16[8,48,384]{2,1,0:T(8,128)(2,1)S(1)}, bf16[8,48,384]{2,1,0:T(8,128)(2,1)S(1)}, u32[]{:S(2)}, u32[]{:S(2)}) %collective-permute-start.3) | collective-permute-done | bytes 294944 | tf_op jit(solution)/shard_map/ppermute | solution.py:44
  31.4 0.0 collective-permute-start.4
  31.4 0.0 collective-permute-start.1
  31.4 1.4 %collective-permute-done.1.other_ref = s32[2,2,12]{2,1,0:T(2,128)S(1)} collective-permute-done((s32[2,2,12]{2,1,0:T(2,128)}, s32[2,2,12]{2,1,0:T(2,128)S(1)}, u32[]{:S(2)}, u32[]{:S(2)}) %collective-permute-start.1) | collective-permute-done | bytes 224 | tf_op jit(solution)/shard_map/ppermute | solution.py:33
  32.8 0.7 copy-done.5
  33.5 2.5 %plan.1 = (s32[108]{0:T(128)S(1)}, s32[54]{0:T(128)S(1)}) custom-call(s32[2,2,12]{2,1,0:T(2,128)S(1)} %bitcast.71, s32[2,2,12]{2,1,0:T(2,128)S(1)} %collective-permute-done.1.other_ref), custom_call_target="tpu_custom_call" | custom-call | tf_op jit(solution)/shard_map/plan/pallas_call | solution.py:146
  36.0 0.0 collective-permute-done
  36.0 0.1 pad_maximum_fusion.refs_0_
  36.1 2.9 %collective-permute-start.2 = (bf16[2,8,48,384]{3,2,1,0:T(8,128)(2,1)S(1)}, bf16[2,8,48,384]{3,2,1,0:T(8,128)(2,1)S(1)}, u32[]{:S(2)}, u32[]{:S(2)}) collective-permute-start(bf16[2,8,48,384]{3,2,1,0:T(8,128)(2,1)S(1)} %pad_maximum_fusion.refs_0_), channel_id=1, source_target_pairs={{20,0},{11,8},{21,1},{10,9},{22,2},{9,10},{23,3},{8,11},{16,4},{15... | collective-permute-start | bytes 1769480 | tf_op jit(solution)/shard_map/ppermute | solution.py:44
  39.0 0.0 collective-permute-done.4
  39.0 0.1 pad_maximum_fusion.1.refs_1_
  39.0 0.8 collective-permute-start.5
  39.8 1.4 %collective-permute-start.8 = (bf16[2,8,48,384]{3,2,1,0:T(8,128)(2,1)S(1)}, bf16[2,8,48,384]{3,2,1,0:T(8,128)(2,1)S(1)}, u32[]{:S(2)}, u32[]{:S(2)}) collective-permute-start(bf16[2,8,48,384]{3,2,1,0:T(8,128)(2,1)S(1)} %pad_maximum_fusion.refs_0_), channel_id=1, source_target_pairs={{4,0},{9,8},{5,1},{8,9},{6,2},{11,10},{7,3},{10,11},{0,4},{13,12},... | collective-permute-start | bytes 1769480 | tf_op jit(solution)/shard_map/ppermute | solution.py:44
  41.1 0.0 collective-permute-done.7.refs_5_
  41.2 1.9 %collective-permute-start.9 = (bf16[2,8,48,384]{3,2,1,0:T(8,128)(2,1)S(1)}, bf16[2,8,48,384]{3,2,1,0:T(8,128)(2,1)S(1)}, u32[]{:S(2)}, u32[]{:S(2)}) collective-permute-start(bf16[2,8,48,384]{3,2,1,0:T(8,128)(2,1)S(1)} %pad_maximum_fusion.1.refs_1_), channel_id=1, source_target_pairs={{20,0},{11,8},{21,1},{10,9},{22,2},{9,10},{23,3},{8,11},{16,4},{15... | collective-permute-start | bytes 1769480 | tf_op jit(solution)/shard_map/ppermute | solution.py:44
  43.1 0.0 collective-permute-done.6.refs_3_.refs_6_
  43.1 2.3 %copy-done = bf16[2,384,3072]{2,1,0:T(8,128)(2,1)S(1)} copy-done((bf16[2,384,3072]{2,1,0:T(8,128)(2,1)S(1)}, bf16[2,384,3072]{2,1,0:T(8,128)(2,1)}, u32[]{:S(2)}) %copy-start) | copy-done | bytes 4718616
  45.4 4.3 %sums_4.1 = (f32[2,2,384,768]{3,2,1,0:T(8,128)S(1)}, bf16[97,128,128]{2,1,0:T(8,128)(2,1)S(1)}) custom-call(bf16[2,8,48,384]{3,2,1,0:T(8,128)(2,1)S(1)} %pad_maximum_fusion.refs_0_, bf16[2,8,48,384]{3,2,1,0:T(8,128)(2,1)S(1)} %pad_maximum_fusion.1.refs_1_, bf16[2,384,3072]{2,1,0:T(8,128)(2,1)S(1)} %copy-done, ...), custom_call_target="tpu_custom_call" | custom-call | flops 1811939328 | bytes 4718592 | tf_op jit(solution)/shard_map/sums_4/pallas_call | solution.py:246
  49.7 0.0 collective-permute-done.2.refs_2_
  49.8 0.0 collective-permute-done.5.refs_3_
  49.8 0.0 copy-start.3
  49.8 0.0 copy-start.4
  49.8 0.3 collective-permute-start.10
  50.1 1.7 %collective-permute-start.11 = (bf16[2,8,48,384]{3,2,1,0:T(8,128)(2,1)S(1)}, bf16[2,8,48,384]{3,2,1,0:T(8,128)(2,1)S(1)}, u32[]{:S(2)}, u32[]{:S(2)}) collective-permute-start(bf16[2,8,48,384]{3,2,1,0:T(8,128)(2,1)S(1)} %collective-permute-done.5.refs_3_), channel_id=1, source_target_pairs={{20,0},{11,8},{21,1},{10,9},{22,2},{9,10},{23,3},{8,11},{16,4},{15... | collective-permute-start | bytes 1769480 | tf_op jit(solution)/shard_map/ppermute | solution.py:44
  51.8 3.6 %collective-permute-done.8.refs_1_ = bf16[2,8,48,384]{3,2,1,0:T(8,128)(2,1)S(1)} collective-permute-done((bf16[2,8,48,384]{3,2,1,0:T(8,128)(2,1)S(1)}, bf16[2,8,48,384]{3,2,1,0:T(8,128)(2,1)S(1)}, u32[]{:S(2)}, u32[]{:S(2)}) %collective-permute-start.8) | collective-permute-done | bytes 589856 | tf_op jit(solution)/shard_map/ppermute | solution.py:44
  55.3 7.3 %sums_8.1 = (f32[2,2,384,768]{3,2,1,0:T(8,128)S(1)}, bf16[2,2,2,384,768]{4,3,2,1,0:T(8,128)(2,1)S(1)}) custom-call(f32[2,2,384,768]{3,2,1,0:T(8,128)S(1)} %get-tuple-element.25.refs_0_, bf16[2,8,48,384]{3,2,1,0:T(8,128)(2,1)S(1)} %collective-permute-done.8.refs_1_, ...), custom_call_target="tpu_custom_call", output_to_operand_aliasing={{0}: (0, {})} | custom-call | flops 3623878656 | bytes 9437184 | tf_op jit(solution)/shard_map/sums_8/pallas_call | solution.py:246
  62.6 0.0 collective-permute-done.10.far_near
  62.6 7.2 %terms.1 = (f32[16,48,384]{2,1,0:T(8,128)S(1)}, bf16[16,48,384]{2,1,0:T(8,128)(2,1)S(1)}) custom-call(s32[108]{0:T(128)S(1)} %get-tuple-element.21.slots_ref, s32[54]{0:T(128)S(1)} %get-tuple-element.22.rows_ref, s32[12]{0:T(128)S(1)} %copy-done.3, s32[24]{0:T(128)S(1)} %copy-done.4, f32[2,2,384,768]{3,2,1,0:T(8,128)S(1)} %get-tuple-element.28.acc, ...), custom_call_target="tpu_custom_call" | custom-call | tf_op jit(solution)/shard_map/terms/pallas_call | solution.py:344
  69.8 0.1 collective-permute-start.12
  69.9 2.0 %collective-permute-done.12 = bf16[16,48,384]{2,1,0:T(8,128)(2,1)S(1)} collective-permute-done((bf16[16,48,384]{2,1,0:T(8,128)(2,1)S(1)}, bf16[16,48,384]{2,1,0:T(8,128)(2,1)S(1)}, u32[]{:S(2)}, u32[]{:S(2)}) %collective-permute-start.12) | collective-permute-done | bytes 589856 | tf_op jit(solution)/shard_map/ppermute | solution.py:33
  71.9 0.1 fusion.15
  72.0 0.1 slice_bitcast_fusion.15
  72.1 2.3 %collective-permute-start.13 = (bf16[48,384]{1,0:T(8,128)(2,1)S(1)}, bf16[48,384]{1,0:T(8,128)(2,1)S(1)}, u32[]{:S(2)}, u32[]{:S(2)}) collective-permute-start(bf16[48,384]{1,0:T(8,128)(2,1)S(1)} %get-tuple-element.35), channel_id=1, source_target_pairs={{16,0},{24,8},{17,1},{25,9},{18,2},{26,10},{19,3},{27,11},{20,4},{... | collective-permute-start | bytes 110600 | tf_op jit(solution)/shard_map/ppermute | solution.py:52
  74.4 1.1 collective-permute-start.27
  75.5 2.9 %collective-permute-start.26 = (bf16[48,384]{1,0:T(8,128)(2,1)S(1)}, bf16[48,384]{1,0:T(8,128)(2,1)S(1)}, u32[]{:S(2)}, u32[]{:S(2)}) collective-permute-start(bf16[48,384]{1,0:T(8,128)(2,1)S(1)} %get-tuple-element.37), channel_id=1, source_target_pairs={{224,0},{232,8},{225,1},{233,9},{226,2},{234,10},{227,3},{235,11},... | collective-permute-start | bytes 110600 | tf_op jit(solution)/shard_map/ppermute | solution.py:52
  78.4 3.9 %collective-permute-start.25 = (bf16[48,384]{1,0:T(8,128)(2,1)S(1)}, bf16[48,384]{1,0:T(8,128)(2,1)S(1)}, u32[]{:S(2)}, u32[]{:S(2)}) collective-permute-start(bf16[48,384]{1,0:T(8,128)(2,1)S(1)} %get-tuple-element.38), channel_id=1, source_target_pairs={{208,0},{216,8},{209,1},{217,9},{210,2},{218,10},{211,3},{219,11},... | collective-permute-start | bytes 110600 | tf_op jit(solution)/shard_map/ppermute | solution.py:52
  82.3 1.9 %collective-permute-start.24 = (bf16[48,384]{1,0:T(8,128)(2,1)S(1)}, bf16[48,384]{1,0:T(8,128)(2,1)S(1)}, u32[]{:S(2)}, u32[]{:S(2)}) collective-permute-start(bf16[48,384]{1,0:T(8,128)(2,1)S(1)} %get-tuple-element.39), channel_id=1, source_target_pairs={{192,0},{200,8},{193,1},{201,9},{194,2},{202,10},{195,3},{203,11},... | collective-permute-start | bytes 110600 | tf_op jit(solution)/shard_map/ppermute | solution.py:52
  84.2 0.0 collective-permute-done.13
  84.2 3.1 %collective-permute-start.23 = (bf16[48,384]{1,0:T(8,128)(2,1)S(1)}, bf16[48,384]{1,0:T(8,128)(2,1)S(1)}, u32[]{:S(2)}, u32[]{:S(2)}) collective-permute-start(bf16[48,384]{1,0:T(8,128)(2,1)S(1)} %get-tuple-element.40), channel_id=1, source_target_pairs={{176,0},{184,8},{177,1},{185,9},{178,2},{186,10},{179,3},{187,11},... | collective-permute-start | bytes 110600 | tf_op jit(solution)/shard_map/ppermute | solution.py:52
  87.3 2.7 %collective-permute-start.22 = (bf16[48,384]{1,0:T(8,128)(2,1)S(1)}, bf16[48,384]{1,0:T(8,128)(2,1)S(1)}, u32[]{:S(2)}, u32[]{:S(2)}) collective-permute-start(bf16[48,384]{1,0:T(8,128)(2,1)S(1)} %get-tuple-element.41), channel_id=1, source_target_pairs={{160,0},{168,8},{161,1},{169,9},{162,2},{170,10},{163,3},{171,11},... | collective-permute-start | bytes 110600 | tf_op jit(solution)/shard_map/ppermute | solution.py:52
  90.0 3.5 %collective-permute-start.21 = (bf16[48,384]{1,0:T(8,128)(2,1)S(1)}, bf16[48,384]{1,0:T(8,128)(2,1)S(1)}, u32[]{:S(2)}, u32[]{:S(2)}) collective-permute-start(bf16[48,384]{1,0:T(8,128)(2,1)S(1)} %get-tuple-element.42), channel_id=1, source_target_pairs={{144,0},{152,8},{145,1},{153,9},{146,2},{154,10},{147,3},{155,11},... | collective-permute-start | bytes 110600 | tf_op jit(solution)/shard_map/ppermute | solution.py:52
  93.5 0.0 collective-permute-done.25
  93.5 4.1 %collective-permute-start.20 = (bf16[48,384]{1,0:T(8,128)(2,1)S(1)}, bf16[48,384]{1,0:T(8,128)(2,1)S(1)}, u32[]{:S(2)}, u32[]{:S(2)}) collective-permute-start(bf16[48,384]{1,0:T(8,128)(2,1)S(1)} %get-tuple-element.43), channel_id=1, source_target_pairs={{128,0},{136,8},{129,1},{137,9},{130,2},{138,10},{131,3},{139,11},... | collective-permute-start | bytes 110600 | tf_op jit(solution)/shard_map/ppermute | solution.py:52
  97.6 0.0 collective-permute-done.24
  97.6 1.2 %collective-permute-start.19 = (bf16[48,384]{1,0:T(8,128)(2,1)S(1)}, bf16[48,384]{1,0:T(8,128)(2,1)S(1)}, u32[]{:S(2)}, u32[]{:S(2)}) collective-permute-start(bf16[48,384]{1,0:T(8,128)(2,1)S(1)} %get-tuple-element.44), channel_id=1, source_target_pairs={{112,0},{120,8},{113,1},{121,9},{114,2},{122,10},{115,3},{123,11},... | collective-permute-start | bytes 110600 | tf_op jit(solution)/shard_map/ppermute | solution.py:52
  98.8 0.0 collective-permute-done.23
  98.8 3.3 %collective-permute-start.18 = (bf16[48,384]{1,0:T(8,128)(2,1)S(1)}, bf16[48,384]{1,0:T(8,128)(2,1)S(1)}, u32[]{:S(2)}, u32[]{:S(2)}) collective-permute-start(bf16[48,384]{1,0:T(8,128)(2,1)S(1)} %get-tuple-element.45), channel_id=1, source_target_pairs={{96,0},{104,8},{97,1},{105,9},{98,2},{106,10},{99,3},{107,11},{100... | collective-permute-start | bytes 110600 | tf_op jit(solution)/shard_map/ppermute | solution.py:52
  102.2 0.0 collective-permute-done.22
  102.2 2.2 %collective-permute-start.17 = (bf16[48,384]{1,0:T(8,128)(2,1)S(1)}, bf16[48,384]{1,0:T(8,128)(2,1)S(1)}, u32[]{:S(2)}, u32[]{:S(2)}) collective-permute-start(bf16[48,384]{1,0:T(8,128)(2,1)S(1)} %get-tuple-element.46), channel_id=1, source_target_pairs={{80,0},{88,8},{81,1},{89,9},{82,2},{90,10},{83,3},{91,11},{84,4},{... | collective-permute-start | bytes 110600 | tf_op jit(solution)/shard_map/ppermute | solution.py:52
  104.3 0.0 collective-permute-done.21
  104.3 2.4 %collective-permute-start.16 = (bf16[48,384]{1,0:T(8,128)(2,1)S(1)}, bf16[48,384]{1,0:T(8,128)(2,1)S(1)}, u32[]{:S(2)}, u32[]{:S(2)}) collective-permute-start(bf16[48,384]{1,0:T(8,128)(2,1)S(1)} %get-tuple-element.47), channel_id=1, source_target_pairs={{64,0},{72,8},{65,1},{73,9},{66,2},{74,10},{67,3},{75,11},{68,4},{... | collective-permute-start | bytes 110600 | tf_op jit(solution)/shard_map/ppermute | solution.py:52
  106.7 0.0 collective-permute-done.20
  106.7 1.3 %collective-permute-start.15 = (bf16[48,384]{1,0:T(8,128)(2,1)S(1)}, bf16[48,384]{1,0:T(8,128)(2,1)S(1)}, u32[]{:S(2)}, u32[]{:S(2)}) collective-permute-start(bf16[48,384]{1,0:T(8,128)(2,1)S(1)} %get-tuple-element.48), channel_id=1, source_target_pairs={{48,0},{56,8},{49,1},{57,9},{50,2},{58,10},{51,3},{59,11},{52,4},{... | collective-permute-start | bytes 110600 | tf_op jit(solution)/shard_map/ppermute | solution.py:52
  108.1 1.5 %collective-permute-start.14 = (bf16[48,384]{1,0:T(8,128)(2,1)S(1)}, bf16[48,384]{1,0:T(8,128)(2,1)S(1)}, u32[]{:S(2)}, u32[]{:S(2)}) collective-permute-start(bf16[48,384]{1,0:T(8,128)(2,1)S(1)} %get-tuple-element.49), channel_id=1, source_target_pairs={{32,0},{40,8},{33,1},{41,9},{34,2},{42,10},{35,3},{43,11},{36,4},{... | collective-permute-start | bytes 110600 | tf_op jit(solution)/shard_map/ppermute | solution.py:52
  109.5 0.7 collective-permute-done.17
  110.2 0.0 collective-permute-done.16
  110.2 2.9 %collective-permute-done.15 = bf16[48,384]{1,0:T(8,128)(2,1)S(1)} collective-permute-done((bf16[48,384]{1,0:T(8,128)(2,1)S(1)}, bf16[48,384]{1,0:T(8,128)(2,1)S(1)}, u32[]{:S(2)}, u32[]{:S(2)}) %collective-permute-start.15) | collective-permute-done | bytes 36896 | tf_op jit(solution)/shard_map/ppermute | solution.py:52
  113.1 0.7 fusion.14
  (15 shorter events, 0.0 us)
Async XLA Ops:
  0.0 43.1 %collective-permute-start.6 = (bf16[2,384,3072]{2,1,0:T(8,128)(2,1)}, bf16[2,384,3072]{2,1,0:T(8,128)(2,1)}, u32[]{:S(2)}, u32[]{:S(2)}) collective-permute-start(bf16[2,384,3072]{2,1,0:T(8,128)(2,1)} %refs_5_.1), channel_id=1, source_target_pairs={{8,0},{0,8},{9,1},{1,9},{10,2},{2,10},{11,3},{3,11},{12,4},{4,12},... | collective-permute-start | bytes 14155784 | tf_op jit(solution)/shard_map/ppermute | solution.py:33
  0.0 43.1 %copy-start.2 = (bf16[2,12,2,128,128]{4,3,2,1,0:T(8,128)(2,1)S(1)}, bf16[2,12,2,128,128]{4,3,2,1,0:T(8,128)(2,1)}, u32[]{:S(2)}) copy-start(bf16[2,12,2,128,128]{4,3,2,1,0:T(8,128)(2,1)} %param.7) | copy-start | bytes 4718596
  0.0 41.1 %collective-permute-start.7 = (bf16[48,128,128]{2,1,0:T(8,128)(2,1)}, bf16[48,128,128]{2,1,0:T(8,128)(2,1)S(1)}, u32[]{:S(2)}, u32[]{:S(2)}) collective-permute-start(bf16[48,128,128]{2,1,0:T(8,128)(2,1)} %bitcast.68), channel_id=1, source_target_pairs={{8,0},{0,8},{9,1},{1,9},{10,2},{2,10},{11,3},{3,11},{12,4},{4,12},... | collective-permute-start | bytes 4718600 | tf_op jit(solution)/shard_map/ppermute | solution.py:33
  23.5 7.9 %collective-permute-start.3 = (bf16[8,48,384]{2,1,0:T(8,128)(2,1)S(1)}, bf16[8,48,384]{2,1,0:T(8,128)(2,1)S(1)}, u32[]{:S(2)}, u32[]{:S(2)}) collective-permute-start(bf16[8,48,384]{2,1,0:T(8,128)(2,1)S(1)} %all_to_all.5), channel_id=1, source_target_pairs={{3,0},{28,8},{2,1},{29,9},{1,2},{30,10},{0,3},{31,11},{7,4},{24,12... | collective-permute-start | bytes 884744 | tf_op jit(solution)/shard_map/ppermute | solution.py:44
  23.7 12.3 %collective-permute-start = (bf16[8,48,384]{2,1,0:T(8,128)(2,1)S(1)}, bf16[8,48,384]{2,1,0:T(8,128)(2,1)S(1)}, u32[]{:S(2)}, u32[]{:S(2)}) collective-permute-start(bf16[8,48,384]{2,1,0:T(8,128)(2,1)S(1)} %all_to_all.5), channel_id=1, source_target_pairs={{1,0},{12,8},{0,1},{13,9},{3,2},{14,10},{2,3},{15,11},{5,4},{8,12}... | collective-permute-start | bytes 884744 | tf_op jit(solution)/shard_map/ppermute | solution.py:44
  31.4 7.5 %collective-permute-start.4 = (bf16[8,48,384]{2,1,0:T(8,128)(2,1)S(1)}, bf16[8,48,384]{2,1,0:T(8,128)(2,1)S(1)}, u32[]{:S(2)}, u32[]{:S(2)}) collective-permute-start(bf16[8,48,384]{2,1,0:T(8,128)(2,1)S(1)} %collective-permute-done.3), channel_id=1, source_target_pairs={{1,0},{12,8},{0,1},{13,9},{3,2},{14,10},{2,3},{15,11},{5,4},{8,12}... | collective-permute-start | bytes 884744 | tf_op jit(solution)/shard_map/ppermute | solution.py:44
  31.4 1.4 %collective-permute-start.1 = (s32[2,2,12]{2,1,0:T(2,128)}, s32[2,2,12]{2,1,0:T(2,128)S(1)}, u32[]{:S(2)}, u32[]{:S(2)}) collective-permute-start(s32[2,2,12]{2,1,0:T(2,128)} %bitcast.70), channel_id=1, source_target_pairs={{8,0},{0,8},{9,1},{1,9},{10,2},{2,10},{11,3},{3,11},{12,4},{4,12},... | collective-permute-start | bytes 584 | tf_op jit(solution)/shard_map/ppermute | solution.py:33
  32.8 0.7 copy-start.5
  36.1 13.6 %collective-permute-start.2 = (bf16[2,8,48,384]{3,2,1,0:T(8,128)(2,1)S(1)}, bf16[2,8,48,384]{3,2,1,0:T(8,128)(2,1)S(1)}, u32[]{:S(2)}, u32[]{:S(2)}) collective-permute-start(bf16[2,8,48,384]{3,2,1,0:T(8,128)(2,1)S(1)} %pad_maximum_fusion.refs_0_), channel_id=1, source_target_pairs={{20,0},{11,8},{21,1},{10,9},{22,2},{9,10},{23,3},{8,11},{16,4},{15... | collective-permute-start | bytes 1769480 | tf_op jit(solution)/shard_map/ppermute | solution.py:44
  39.0 10.7 %collective-permute-start.5 = (bf16[2,8,48,384]{3,2,1,0:T(8,128)(2,1)S(1)}, bf16[2,8,48,384]{3,2,1,0:T(8,128)(2,1)S(1)}, u32[]{:S(2)}, u32[]{:S(2)}) collective-permute-start(bf16[2,8,48,384]{3,2,1,0:T(8,128)(2,1)S(1)} %pad_maximum_fusion.1.refs_1_), channel_id=1, source_target_pairs={{4,0},{9,8},{5,1},{8,9},{6,2},{11,10},{7,3},{10,11},{0,4},{13,12},... | collective-permute-start | bytes 1769480 | tf_op jit(solution)/shard_map/ppermute | solution.py:44
  39.8 15.5 %collective-permute-start.8 = (bf16[2,8,48,384]{3,2,1,0:T(8,128)(2,1)S(1)}, bf16[2,8,48,384]{3,2,1,0:T(8,128)(2,1)S(1)}, u32[]{:S(2)}, u32[]{:S(2)}) collective-permute-start(bf16[2,8,48,384]{3,2,1,0:T(8,128)(2,1)S(1)} %pad_maximum_fusion.refs_0_), channel_id=1, source_target_pairs={{4,0},{9,8},{5,1},{8,9},{6,2},{11,10},{7,3},{10,11},{0,4},{13,12},... | collective-permute-start | bytes 1769480 | tf_op jit(solution)/shard_map/ppermute | solution.py:44
  41.2 14.2 %collective-permute-start.9 = (bf16[2,8,48,384]{3,2,1,0:T(8,128)(2,1)S(1)}, bf16[2,8,48,384]{3,2,1,0:T(8,128)(2,1)S(1)}, u32[]{:S(2)}, u32[]{:S(2)}) collective-permute-start(bf16[2,8,48,384]{3,2,1,0:T(8,128)(2,1)S(1)} %pad_maximum_fusion.1.refs_1_), channel_id=1, source_target_pairs={{20,0},{11,8},{21,1},{10,9},{22,2},{9,10},{23,3},{8,11},{16,4},{15... | collective-permute-start | bytes 1769480 | tf_op jit(solution)/shard_map/ppermute | solution.py:44
  43.1 2.3 %copy-start = (bf16[2,384,3072]{2,1,0:T(8,128)(2,1)S(1)}, bf16[2,384,3072]{2,1,0:T(8,128)(2,1)}, u32[]{:S(2)}) copy-start(bf16[2,384,3072]{2,1,0:T(8,128)(2,1)} %refs_5_.1) | copy-start | bytes 14155780
  45.4 9.9 %copy-start.1 = (bf16[2,384,3072]{2,1,0:T(8,128)(2,1)S(1)}, bf16[2,384,3072]{2,1,0:T(8,128)(2,1)}, u32[]{:S(2)}) copy-start(bf16[2,384,3072]{2,1,0:T(8,128)(2,1)} %refs_5_.1) | copy-start | bytes 14155780
  49.8 12.9 %copy-start.3 = (s32[12]{0:T(128)S(1)}, s32[12]{0:T(128)}, u32[]{:S(2)}) copy-start(s32[12]{0:T(128)} %sizes_ref.1) | copy-start | bytes 148
  49.8 12.9 %copy-start.4 = (s32[24]{0:T(128)S(1)}, s32[24]{0:T(128)}, u32[]{:S(2)}) copy-start(s32[24]{0:T(128)} %right_ref.3) | copy-start | bytes 292
  49.8 12.8 %collective-permute-start.10 = (bf16[2,8,48,384]{3,2,1,0:T(8,128)(2,1)S(1)}, bf16[2,8,48,384]{3,2,1,0:T(8,128)(2,1)S(1)}, u32[]{:S(2)}, u32[]{:S(2)}) collective-permute-start(bf16[2,8,48,384]{3,2,1,0:T(8,128)(2,1)S(1)} %collective-permute-done.2.refs_2_), channel_id=1, source_target_pairs={{4,0},{9,8},{5,1},{8,9},{6,2},{11,10},{7,3},{10,11},{0,4},{13,12},... | collective-permute-start | bytes 1769480 | tf_op jit(solution)/shard_map/ppermute | solution.py:44
  50.1 12.5 %collective-permute-start.11 = (bf16[2,8,48,384]{3,2,1,0:T(8,128)(2,1)S(1)}, bf16[2,8,48,384]{3,2,1,0:T(8,128)(2,1)S(1)}, u32[]{:S(2)}, u32[]{:S(2)}) collective-permute-start(bf16[2,8,48,384]{3,2,1,0:T(8,128)(2,1)S(1)} %collective-permute-done.5.refs_3_), channel_id=1, source_target_pairs={{20,0},{11,8},{21,1},{10,9},{22,2},{9,10},{23,3},{8,11},{16,4},{15... | collective-permute-start | bytes 1769480 | tf_op jit(solution)/shard_map/ppermute | solution.py:44
  69.8 2.1 %collective-permute-start.12 = (bf16[16,48,384]{2,1,0:T(8,128)(2,1)S(1)}, bf16[16,48,384]{2,1,0:T(8,128)(2,1)S(1)}, u32[]{:S(2)}, u32[]{:S(2)}) collective-permute-start(bf16[16,48,384]{2,1,0:T(8,128)(2,1)S(1)} %get-tuple-element.32), channel_id=1, source_target_pairs={{8,0},{0,8},{9,1},{1,9},{10,2},{2,10},{11,3},{3,11},{12,4},{4,12},... | collective-permute-start | bytes 1769480 | tf_op jit(solution)/shard_map/ppermute | solution.py:33
  72.1 12.1 %collective-permute-start.13 = (bf16[48,384]{1,0:T(8,128)(2,1)S(1)}, bf16[48,384]{1,0:T(8,128)(2,1)S(1)}, u32[]{:S(2)}, u32[]{:S(2)}) collective-permute-start(bf16[48,384]{1,0:T(8,128)(2,1)S(1)} %get-tuple-element.35), channel_id=1, source_target_pairs={{16,0},{24,8},{17,1},{25,9},{18,2},{26,10},{19,3},{27,11},{20,4},{... | collective-permute-start | bytes 110600 | tf_op jit(solution)/shard_map/ppermute | solution.py:52
  74.4 12.9 %collective-permute-start.27 = (bf16[48,384]{1,0:T(8,128)(2,1)S(1)}, bf16[48,384]{1,0:T(8,128)(2,1)S(1)}, u32[]{:S(2)}, u32[]{:S(2)}) collective-permute-start(bf16[48,384]{1,0:T(8,128)(2,1)S(1)} %get-tuple-element.36), channel_id=1, source_target_pairs={{240,0},{248,8},{241,1},{249,9},{242,2},{250,10},{243,3},{251,11},... | collective-permute-start | bytes 110600 | tf_op jit(solution)/shard_map/ppermute | solution.py:52
  75.5 14.5 %collective-permute-start.26 = (bf16[48,384]{1,0:T(8,128)(2,1)S(1)}, bf16[48,384]{1,0:T(8,128)(2,1)S(1)}, u32[]{:S(2)}, u32[]{:S(2)}) collective-permute-start(bf16[48,384]{1,0:T(8,128)(2,1)S(1)} %get-tuple-element.37), channel_id=1, source_target_pairs={{224,0},{232,8},{225,1},{233,9},{226,2},{234,10},{227,3},{235,11},... | collective-permute-start | bytes 110600 | tf_op jit(solution)/shard_map/ppermute | solution.py:52
  78.4 15.1 %collective-permute-start.25 = (bf16[48,384]{1,0:T(8,128)(2,1)S(1)}, bf16[48,384]{1,0:T(8,128)(2,1)S(1)}, u32[]{:S(2)}, u32[]{:S(2)}) collective-permute-start(bf16[48,384]{1,0:T(8,128)(2,1)S(1)} %get-tuple-element.38), channel_id=1, source_target_pairs={{208,0},{216,8},{209,1},{217,9},{210,2},{218,10},{211,3},{219,11},... | collective-permute-start | bytes 110600 | tf_op jit(solution)/shard_map/ppermute | solution.py:52
  82.3 15.3 %collective-permute-start.24 = (bf16[48,384]{1,0:T(8,128)(2,1)S(1)}, bf16[48,384]{1,0:T(8,128)(2,1)S(1)}, u32[]{:S(2)}, u32[]{:S(2)}) collective-permute-start(bf16[48,384]{1,0:T(8,128)(2,1)S(1)} %get-tuple-element.39), channel_id=1, source_target_pairs={{192,0},{200,8},{193,1},{201,9},{194,2},{202,10},{195,3},{203,11},... | collective-permute-start | bytes 110600 | tf_op jit(solution)/shard_map/ppermute | solution.py:52
  84.2 14.6 %collective-permute-start.23 = (bf16[48,384]{1,0:T(8,128)(2,1)S(1)}, bf16[48,384]{1,0:T(8,128)(2,1)S(1)}, u32[]{:S(2)}, u32[]{:S(2)}) collective-permute-start(bf16[48,384]{1,0:T(8,128)(2,1)S(1)} %get-tuple-element.40), channel_id=1, source_target_pairs={{176,0},{184,8},{177,1},{185,9},{178,2},{186,10},{179,3},{187,11},... | collective-permute-start | bytes 110600 | tf_op jit(solution)/shard_map/ppermute | solution.py:52
  87.3 14.9 %collective-permute-start.22 = (bf16[48,384]{1,0:T(8,128)(2,1)S(1)}, bf16[48,384]{1,0:T(8,128)(2,1)S(1)}, u32[]{:S(2)}, u32[]{:S(2)}) collective-permute-start(bf16[48,384]{1,0:T(8,128)(2,1)S(1)} %get-tuple-element.41), channel_id=1, source_target_pairs={{160,0},{168,8},{161,1},{169,9},{162,2},{170,10},{163,3},{171,11},... | collective-permute-start | bytes 110600 | tf_op jit(solution)/shard_map/ppermute | solution.py:52
  90.0 14.3 %collective-permute-start.21 = (bf16[48,384]{1,0:T(8,128)(2,1)S(1)}, bf16[48,384]{1,0:T(8,128)(2,1)S(1)}, u32[]{:S(2)}, u32[]{:S(2)}) collective-permute-start(bf16[48,384]{1,0:T(8,128)(2,1)S(1)} %get-tuple-element.42), channel_id=1, source_target_pairs={{144,0},{152,8},{145,1},{153,9},{146,2},{154,10},{147,3},{155,11},... | collective-permute-start | bytes 110600 | tf_op jit(solution)/shard_map/ppermute | solution.py:52
  93.5 13.2 %collective-permute-start.20 = (bf16[48,384]{1,0:T(8,128)(2,1)S(1)}, bf16[48,384]{1,0:T(8,128)(2,1)S(1)}, u32[]{:S(2)}, u32[]{:S(2)}) collective-permute-start(bf16[48,384]{1,0:T(8,128)(2,1)S(1)} %get-tuple-element.43), channel_id=1, source_target_pairs={{128,0},{136,8},{129,1},{137,9},{130,2},{138,10},{131,3},{139,11},... | collective-permute-start | bytes 110600 | tf_op jit(solution)/shard_map/ppermute | solution.py:52
  97.6 10.5 %collective-permute-start.19 = (bf16[48,384]{1,0:T(8,128)(2,1)S(1)}, bf16[48,384]{1,0:T(8,128)(2,1)S(1)}, u32[]{:S(2)}, u32[]{:S(2)}) collective-permute-start(bf16[48,384]{1,0:T(8,128)(2,1)S(1)} %get-tuple-element.44), channel_id=1, source_target_pairs={{112,0},{120,8},{113,1},{121,9},{114,2},{122,10},{115,3},{123,11},... | collective-permute-start | bytes 110600 | tf_op jit(solution)/shard_map/ppermute | solution.py:52
  98.8 10.7 %collective-permute-start.18 = (bf16[48,384]{1,0:T(8,128)(2,1)S(1)}, bf16[48,384]{1,0:T(8,128)(2,1)S(1)}, u32[]{:S(2)}, u32[]{:S(2)}) collective-permute-start(bf16[48,384]{1,0:T(8,128)(2,1)S(1)} %get-tuple-element.45), channel_id=1, source_target_pairs={{96,0},{104,8},{97,1},{105,9},{98,2},{106,10},{99,3},{107,11},{100... | collective-permute-start | bytes 110600 | tf_op jit(solution)/shard_map/ppermute | solution.py:52
  102.2 8.1 %collective-permute-start.17 = (bf16[48,384]{1,0:T(8,128)(2,1)S(1)}, bf16[48,384]{1,0:T(8,128)(2,1)S(1)}, u32[]{:S(2)}, u32[]{:S(2)}) collective-permute-start(bf16[48,384]{1,0:T(8,128)(2,1)S(1)} %get-tuple-element.46), channel_id=1, source_target_pairs={{80,0},{88,8},{81,1},{89,9},{82,2},{90,10},{83,3},{91,11},{84,4},{... | collective-permute-start | bytes 110600 | tf_op jit(solution)/shard_map/ppermute | solution.py:52
  104.3 5.9 %collective-permute-start.16 = (bf16[48,384]{1,0:T(8,128)(2,1)S(1)}, bf16[48,384]{1,0:T(8,128)(2,1)S(1)}, u32[]{:S(2)}, u32[]{:S(2)}) collective-permute-start(bf16[48,384]{1,0:T(8,128)(2,1)S(1)} %get-tuple-element.47), channel_id=1, source_target_pairs={{64,0},{72,8},{65,1},{73,9},{66,2},{74,10},{67,3},{75,11},{68,4},{... | collective-permute-start | bytes 110600 | tf_op jit(solution)/shard_map/ppermute | solution.py:52
  106.7 6.4 %collective-permute-start.15 = (bf16[48,384]{1,0:T(8,128)(2,1)S(1)}, bf16[48,384]{1,0:T(8,128)(2,1)S(1)}, u32[]{:S(2)}, u32[]{:S(2)}) collective-permute-start(bf16[48,384]{1,0:T(8,128)(2,1)S(1)} %get-tuple-element.48), channel_id=1, source_target_pairs={{48,0},{56,8},{49,1},{57,9},{50,2},{58,10},{51,3},{59,11},{52,4},{... | collective-permute-start | bytes 110600 | tf_op jit(solution)/shard_map/ppermute | solution.py:52
  108.1 5.0 %collective-permute-start.14 = (bf16[48,384]{1,0:T(8,128)(2,1)S(1)}, bf16[48,384]{1,0:T(8,128)(2,1)S(1)}, u32[]{:S(2)}, u32[]{:S(2)}) collective-permute-start(bf16[48,384]{1,0:T(8,128)(2,1)S(1)} %get-tuple-element.49), channel_id=1, source_target_pairs={{32,0},{40,8},{33,1},{41,9},{34,2},{42,10},{35,3},{43,11},{36,4},{... | collective-permute-start | bytes 110600 | tf_op jit(solution)/shard_map/ppermute | solution.py:52

commit v10 on v8

--- a/solution.py
+++ b/solution.py
@@ -365,13 +365,13 @@
     across = partner(along_z, "middle", 3)
     opposite = partner(across, "middle", 1)
     near, away = jnp.stack([along_z, beside]), jnp.stack([across, opposite])
-    near, away, rows_other = lax.optimization_barrier((near, away, rows_other))
     near_3 = partner(near, "last", 3)
+    near, rows_other = lax.optimization_barrier((near, rows_other))
+    slots, rows = plan(rows_by_slot, rows_other)
+    near, away, slots, rows = lax.optimization_barrier((near, away, slots, rows))
     away_1 = partner(away, "last", 1)
     near_1 = partner(near, "last", 1)
     away_3 = partner(away, "last", 3)
-    slots, rows = plan(rows_by_slot, rows_other)
-    near, slots, rows = lax.optimization_barrier((near, slots, rows))
     acc, both = sums(None, [(near, 0, NEAR), (away, 0, AWAY)], right, left)
     near_3, away_1, acc = lax.optimization_barrier((near_3, away_1, acc))
     near_2 = partner(near_3, "last", 1)

time: 101 us -> 96.6 us (0.956)
  waiting for transfers between devices: 28.4 us -> 23.8 us
  blocking collectives: 26.3 us -> 24.6 us
  starting transfers between devices: 18.4 us -> 19.6 us
    ppermute x9, waiting for transfers between devices: 13.4 us -> 8.75 us  [partner(): return lax.ppermute(value, AXES, perm)]
    all_to_all x1, blocking collectives: 26.3 us -> 24.6 us  [exchange(): lax.all_to_all(copies, AXES, split_axis=0, concat_axis=0, axis_index_grou...]
    ppermute x9, starting transfers between devices: 9.76 us -> 11 us  [partner(): return lax.ppermute(value, AXES, perm)]
  transfers between devices with their start and end apart: 14 -> 14, of which waited for: 4 -> 6; matrix products, arithmetic and copies ran while one was open for 0% -> 0% of each run, Pallas kernels for 17% -> 18%
where the time goes in v10:
time: 96.6 us; the launch traced here: 96.3 us
  blocking collectives  24.6 us (25%)
  Pallas kernels  24 us (25%)
  waiting for transfers between devices  23.8 us (25%)
  starting transfers between devices  19.6 us (20%)
  local copies, waits for them, and re-layouts  3.04 us (3%)
  other arithmetic  1.01 us (1%)
    all_to_all x1, blocking collectives, exchange(): lax.all_to_all(copies, AXES, split_axis=0, concat_axis=0, axis_index_grou...  24.6 us
    all_to_all x1, waiting for transfers between devices, exchange(): lax.all_to_all(copies, AXES, split_axis=0, concat_axis=0, axis_index_grou...  13 us
    pallas_call x3, Pallas kernels, sums(): pl.pallas_call(functools.partial(sums_kernel, twos, first, ahead), out_sh...  12.7 us
    ppermute x9, starting transfers between devices, partner(): return lax.ppermute(value, AXES, perm)  11 us
    ppermute x9, waiting for transfers between devices, partner(): return lax.ppermute(value, AXES, perm)  8.75 us
    all_to_all x1, starting transfers between devices, exchange(): lax.all_to_all(copies, AXES, split_axis=0, concat_axis=0, axis_index_grou...  8.49 us
    pallas_call x1, Pallas kernels, terms(): pl.pallas_call(terms_kernel, out_shape=(jax.ShapeDtypeStruct((NZ * NXH, g...  7.07 us
    unnamed x12, local copies, waits for them, and re-layouts  3.04 us
  transfers between devices with their start and end apart: 14, of which 6 were waited for; matrix products, arithmetic and copies ran while one was open for 0% of the time, Pallas kernels for 18%

profile of v10, /device:TPU:24, one launch (start us, length us, event | category | flops | bytes accessed | tf_op | source)
XLA Modules:
  0.0 96.3 jit_solution(9139141390818207498)
XLA Ops:
  0.0 0.0 copy-start.2
  0.0 0.0 collective-permute-start.6
  0.0 1.7 %mask_psi.1 = bf16[8,48,384]{2,1,0:T(8,128)(2,1)} custom-call(s32[12]{0:T(128)} %sizes_ref.1, s32[24]{0:T(128)} %right_ref.3, bf16[48,384]{1,0:T(8,128)(2,1)} %psi_ref.1), custom_call_target="tpu_custom_call" | custom-call | tf_op jit(solution)/shard_map/mask_psi/pallas_call | solution.py:87
  1.7 8.5 %all-to-all-start = ((bf16[8,48,384]{2,1,0:T(8,128)(2,1)}), bf16[8,48,384]{2,1,0:T(8,128)(2,1)S(1)}, u32[]{:S(2)}, u32[]{:S(2)}) async-start(bf16[8,48,384]{2,1,0:T(8,128)(2,1)} %mask_psi.1), calls=%async_computation | async-start | bytes 589824 | tf_op jit(solution)/shard_map/all_to_all | solution.py:48
  10.2 0.1 collective-permute-start.7
  10.3 13.0 %all-to-all-done = bf16[8,48,384]{2,1,0:T(8,128)(2,1)S(1)} async-done(((bf16[8,48,384]{2,1,0:T(8,128)(2,1)}), bf16[8,48,384]{2,1,0:T(8,128)(2,1)S(1)}, u32[]{:S(2)}, u32[]{:S(2)}) %all-to-all-start) | async-done | bytes 294944 | tf_op jit(solution)/shard_map/all_to_all | solution.py:48
  23.3 0.2 collective-permute-start.2
  23.5 1.0 %collective-permute-start = (bf16[8,48,384]{2,1,0:T(8,128)(2,1)S(1)}, bf16[8,48,384]{2,1,0:T(8,128)(2,1)S(1)}, u32[]{:S(2)}, u32[]{:S(2)}) collective-permute-start(bf16[8,48,384]{2,1,0:T(8,128)(2,1)S(1)} %all-to-all-done), channel_id=1, source_target_pairs={{1,0},{12,8},{0,1},{13,9},{3,2},{14,10},{2,3},{15,11},{5,4},{8,12}... | collective-permute-start | bytes 884744 | tf_op jit(solution)/shard_map/ppermute | solution.py:44
  24.5 6.7 %collective-permute-done.2 = bf16[8,48,384]{2,1,0:T(8,128)(2,1)S(1)} collective-permute-done((bf16[8,48,384]{2,1,0:T(8,128)(2,1)S(1)}, bf16[8,48,384]{2,1,0:T(8,128)(2,1)S(1)}, u32[]{:S(2)}, u32[]{:S(2)}) %collective-permute-start.2) | collective-permute-done | bytes 294944 | tf_op jit(solution)/shard_map/ppermute | solution.py:44
  31.2 0.0 collective-permute-start.3
  31.2 0.0 collective-permute-start.1
  31.2 0.0 collective-permute-done
  31.2 0.1 pad_maximum_fusion.refs_0_
  31.3 2.8 %collective-permute-start.4 = (bf16[2,8,48,384]{3,2,1,0:T(8,128)(2,1)S(1)}, bf16[2,8,48,384]{3,2,1,0:T(8,128)(2,1)S(1)}, u32[]{:S(2)}, u32[]{:S(2)}) collective-permute-start(bf16[2,8,48,384]{3,2,1,0:T(8,128)(2,1)S(1)} %pad_maximum_fusion.refs_0_), channel_id=1, source_target_pairs={{20,0},{11,8},{21,1},{10,9},{22,2},{9,10},{23,3},{8,11},{16,4},{15... | collective-permute-start | bytes 1769480 | tf_op jit(solution)/shard_map/ppermute | solution.py:44
  34.2 0.0 collective-permute-done.1.other_ref
  34.2 0.0 copy-start.5
  34.2 0.7 copy-done.5
  34.8 2.5 %plan.1 = (s32[108]{0:T(128)S(1)}, s32[54]{0:T(128)S(1)}) custom-call(s32[2,2,12]{2,1,0:T(2,128)S(1)} %bitcast.9, s32[2,2,12]{2,1,0:T(2,128)S(1)} %collective-permute-done.1.other_ref), custom_call_target="tpu_custom_call" | custom-call | tf_op jit(solution)/shard_map/plan/pallas_call | solution.py:138
  37.4 0.5 collective-permute-done.3
  37.9 0.1 pad_maximum_fusion.1.refs_1_
  38.0 1.6 %collective-permute-start.5 = (bf16[2,8,48,384]{3,2,1,0:T(8,128)(2,1)S(1)}, bf16[2,8,48,384]{3,2,1,0:T(8,128)(2,1)S(1)}, u32[]{:S(2)}, u32[]{:S(2)}) collective-permute-start(bf16[2,8,48,384]{3,2,1,0:T(8,128)(2,1)S(1)} %pad_maximum_fusion.1.refs_1_), channel_id=1, source_target_pairs={{4,0},{9,8},{5,1},{8,9},{6,2},{11,10},{7,3},{10,11},{0,4},{13,12},... | collective-permute-start | bytes 1769480 | tf_op jit(solution)/shard_map/ppermute | solution.py:44
  39.6 2.1 %collective-permute-start.9 = (bf16[2,8,48,384]{3,2,1,0:T(8,128)(2,1)S(1)}, bf16[2,8,48,384]{3,2,1,0:T(8,128)(2,1)S(1)}, u32[]{:S(2)}, u32[]{:S(2)}) collective-permute-start(bf16[2,8,48,384]{3,2,1,0:T(8,128)(2,1)S(1)} %pad_maximum_fusion.1.refs_1_), channel_id=1, source_target_pairs={{20,0},{11,8},{21,1},{10,9},{22,2},{9,10},{23,3},{8,11},{16,4},{15... | collective-permute-start | bytes 1769480 | tf_op jit(solution)/shard_map/ppermute | solution.py:44
  41.7 0.0 collective-permute-done.7.refs_5_
  41.7 0.6 collective-permute-start.8
  42.3 0.0 collective-permute-done.6.refs_3_.refs_4_
  42.3 0.0 copy-done.2
  42.3 0.0 copy-start
  42.3 2.3 %copy-done = bf16[2,384,3072]{2,1,0:T(8,128)(2,1)S(1)} copy-done((bf16[2,384,3072]{2,1,0:T(8,128)(2,1)S(1)}, bf16[2,384,3072]{2,1,0:T(8,128)(2,1)}, u32[]{:S(2)}) %copy-start) | copy-done | bytes 4718616
  44.6 0.0 copy-start.1
  44.6 4.3 %sums_first.1 = (f32[2,2,384,768]{3,2,1,0:T(8,128)S(1)}, bf16[97,128,128]{2,1,0:T(8,128)(2,1)S(1)}) custom-call(bf16[2,8,48,384]{3,2,1,0:T(8,128)(2,1)S(1)} %pad_maximum_fusion.refs_0_, bf16[2,8,48,384]{3,2,1,0:T(8,128)(2,1)S(1)} %pad_maximum_fusion.1.refs_1_, bf16[2,384,3072]{2,1,0:T(8,128)(2,1)S(1)} %copy-done, ...), custom_call_target="tpu_custom_call" | custom-call | flops 1811939328 | bytes 4718592 | tf_op jit(solution)/shard_map/sums_first/pallas_call | solution.py:244
  48.9 0.0 collective-permute-done.4.refs_1_
  49.0 0.0 collective-permute-done.5.refs_2_
  49.0 1.5 %collective-permute-start.10 = (bf16[2,8,48,384]{3,2,1,0:T(8,128)(2,1)S(1)}, bf16[2,8,48,384]{3,2,1,0:T(8,128)(2,1)S(1)}, u32[]{:S(2)}, u32[]{:S(2)}) collective-permute-start(bf16[2,8,48,384]{3,2,1,0:T(8,128)(2,1)S(1)} %collective-permute-done.4.refs_1_), channel_id=1, source_target_pairs={{4,0},{9,8},{5,1},{8,9},{6,2},{11,10},{7,3},{10,11},{0,4},{13,12},... | collective-permute-start | bytes 1769480 | tf_op jit(solution)/shard_map/ppermute | solution.py:44
  50.5 1.1 %collective-permute-start.11 = (bf16[2,8,48,384]{3,2,1,0:T(8,128)(2,1)S(1)}, bf16[2,8,48,384]{3,2,1,0:T(8,128)(2,1)S(1)}, u32[]{:S(2)}, u32[]{:S(2)}) collective-permute-start(bf16[2,8,48,384]{3,2,1,0:T(8,128)(2,1)S(1)} %collective-permute-done.5.refs_2_), channel_id=1, source_target_pairs={{20,0},{11,8},{21,1},{10,9},{22,2},{9,10},{23,3},{8,11},{16,4},{15... | collective-permute-start | bytes 1769480 | tf_op jit(solution)/shard_map/ppermute | solution.py:44
  51.6 0.0 copy-done.1
  51.6 4.2 %sums_middle.1.refs_0_ = f32[2,2,384,768]{3,2,1,0:T(8,128)S(1)} custom-call(f32[2,2,384,768]{3,2,1,0:T(8,128)S(1)} %get-tuple-element.31.refs_0_, bf16[2,8,48,384]{3,2,1,0:T(8,128)(2,1)S(1)} %collective-permute-done.4.refs_1_, bf16[2,8,48,384]{3,2,1,0:T(8,128)(2,1)S(1)} %collective-permute-done.5.refs_2_, ...), custom_call_target="tpu_custom_call", output_to_operand_aliasing={{}: (0, {})} | custom-call | flops 1811939328 | bytes 4718592 | tf_op jit(solution)/shard_map/sums_middle/pallas_call | solution.py:244
  55.8 0.0 copy-start.3
  55.8 0.0 copy-start.4
  55.8 0.0 collective-permute-done.8.refs_1_
  55.8 0.0 collective-permute-done.9.refs_2_
  55.8 4.3 %sums_last.1 = (f32[2,2,384,768]{3,2,1,0:T(8,128)S(1)}, bf16[2,2,2,384,768]{4,3,2,1,0:T(8,128)(2,1)S(1)}) custom-call(f32[2,2,384,768]{3,2,1,0:T(8,128)S(1)} %sums_middle.1.refs_0_, bf16[2,8,48,384]{3,2,1,0:T(8,128)(2,1)S(1)} %collective-permute-done.8.refs_1_, ...), custom_call_target="tpu_custom_call", output_to_operand_aliasing={{0}: (0, {})} | custom-call | flops 1811939328 | bytes 4718592 | tf_op jit(solution)/shard_map/sums_last/pallas_call | solution.py:244
  60.1 0.5 collective-permute-done.10.far_near
  60.6 1.0 collective-permute-done.11.far_away
  61.6 0.0 copy-done.3
  61.6 0.0 copy-done.4
  61.6 7.1 %terms.1 = (f32[16,48,384]{2,1,0:T(8,128)S(1)}, bf16[16,48,384]{2,1,0:T(8,128)(2,1)S(1)}) custom-call(s32[108]{0:T(128)S(1)} %get-tuple-element.26.slots_ref, s32[54]{0:T(128)S(1)} %get-tuple-element.27.rows_ref, s32[12]{0:T(128)S(1)} %copy-done.3, s32[24]{0:T(128)S(1)} %copy-done.4, f32[2,2,384,768]{3,2,1,0:T(8,128)S(1)} %get-tuple-element.34.acc, ...), custom_call_target="tpu_custom_call" | custom-call | tf_op jit(solution)/shard_map/terms/pallas_call | solution.py:338
  68.7 0.1 collective-permute-start.12
  68.8 2.0 %collective-permute-done.12 = bf16[16,48,384]{2,1,0:T(8,128)(2,1)S(1)} collective-permute-done((bf16[16,48,384]{2,1,0:T(8,128)(2,1)S(1)}, bf16[16,48,384]{2,1,0:T(8,128)(2,1)S(1)}, u32[]{:S(2)}, u32[]{:S(2)}) %collective-permute-start.12) | collective-permute-done | bytes 589856 | tf_op jit(solution)/shard_map/ppermute | solution.py:33
  70.8 0.2 add_convert_fusion
  70.9 24.6 %all_to_all.10 = bf16[16,48,384]{2,1,0:T(8,128)(2,1)S(1)} all-to-all(bf16[16,48,384]{2,1,0:T(8,128)(2,1)S(1)} %add_convert_fusion), channel_id=1, replica_groups={{0,16,32,48,64,80,96,112,128,144,160,176,192,208,224,240},{1,17,33,49,6..., dimensions={0} | all-to-all | bytes 1179648 | tf_op jit(solution)/shard_map/all_to_all | solution.py:48
  95.6 0.7 convert_reduce_fusion
Async XLA Ops:
  0.0 42.3 %copy-start.2 = (bf16[2,12,2,128,128]{4,3,2,1,0:T(8,128)(2,1)S(1)}, bf16[2,12,2,128,128]{4,3,2,1,0:T(8,128)(2,1)}, u32[]{:S(2)}) copy-start(bf16[2,12,2,128,128]{4,3,2,1,0:T(8,128)(2,1)} %param.7) | copy-start | bytes 4718596
  0.0 42.3 %collective-permute-start.6 = (bf16[2,384,3072]{2,1,0:T(8,128)(2,1)}, bf16[2,384,3072]{2,1,0:T(8,128)(2,1)}, u32[]{:S(2)}, u32[]{:S(2)}) collective-permute-start(bf16[2,384,3072]{2,1,0:T(8,128)(2,1)} %refs_3_.3), channel_id=1, source_target_pairs={{8,0},{0,8},{9,1},{1,9},{10,2},{2,10},{11,3},{3,11},{12,4},{4,12},... | collective-permute-start | bytes 14155784 | tf_op jit(solution)/shard_map/ppermute | solution.py:33
  1.7 21.6 %all-to-all-start = ((bf16[8,48,384]{2,1,0:T(8,128)(2,1)}), bf16[8,48,384]{2,1,0:T(8,128)(2,1)S(1)}, u32[]{:S(2)}, u32[]{:S(2)}) async-start(bf16[8,48,384]{2,1,0:T(8,128)(2,1)} %mask_psi.1), calls=%async_computation | async-start | bytes 589824 | tf_op jit(solution)/shard_map/all_to_all | solution.py:48
  10.2 31.5 %collective-permute-start.7 = (bf16[48,128,128]{2,1,0:T(8,128)(2,1)}, bf16[48,128,128]{2,1,0:T(8,128)(2,1)S(1)}, u32[]{:S(2)}, u32[]{:S(2)}) collective-permute-start(bf16[48,128,128]{2,1,0:T(8,128)(2,1)} %bitcast.6), channel_id=1, source_target_pairs={{8,0},{0,8},{9,1},{1,9},{10,2},{2,10},{11,3},{3,11},{12,4},{4,12},... | collective-permute-start | bytes 4718600 | tf_op jit(solution)/shard_map/ppermute | solution.py:33
  23.3 7.9 %collective-permute-start.2 = (bf16[8,48,384]{2,1,0:T(8,128)(2,1)S(1)}, bf16[8,48,384]{2,1,0:T(8,128)(2,1)S(1)}, u32[]{:S(2)}, u32[]{:S(2)}) collective-permute-start(bf16[8,48,384]{2,1,0:T(8,128)(2,1)S(1)} %all-to-all-done), channel_id=1, source_target_pairs={{3,0},{28,8},{2,1},{29,9},{1,2},{30,10},{0,3},{31,11},{7,4},{24,12... | collective-permute-start | bytes 884744 | tf_op jit(solution)/shard_map/ppermute | solution.py:44
  23.5 7.7 %collective-permute-start = (bf16[8,48,384]{2,1,0:T(8,128)(2,1)S(1)}, bf16[8,48,384]{2,1,0:T(8,128)(2,1)S(1)}, u32[]{:S(2)}, u32[]{:S(2)}) collective-permute-start(bf16[8,48,384]{2,1,0:T(8,128)(2,1)S(1)} %all-to-all-done), channel_id=1, source_target_pairs={{1,0},{12,8},{0,1},{13,9},{3,2},{14,10},{2,3},{15,11},{5,4},{8,12}... | collective-permute-start | bytes 884744 | tf_op jit(solution)/shard_map/ppermute | solution.py:44
  31.2 6.7 %collective-permute-start.3 = (bf16[8,48,384]{2,1,0:T(8,128)(2,1)S(1)}, bf16[8,48,384]{2,1,0:T(8,128)(2,1)S(1)}, u32[]{:S(2)}, u32[]{:S(2)}) collective-permute-start(bf16[8,48,384]{2,1,0:T(8,128)(2,1)S(1)} %collective-permute-done.2), channel_id=1, source_target_pairs={{1,0},{12,8},{0,1},{13,9},{3,2},{14,10},{2,3},{15,11},{5,4},{8,12}... | collective-permute-start | bytes 884744 | tf_op jit(solution)/shard_map/ppermute | solution.py:44
  31.2 2.9 %collective-permute-start.1 = (s32[2,2,12]{2,1,0:T(2,128)}, s32[2,2,12]{2,1,0:T(2,128)S(1)}, u32[]{:S(2)}, u32[]{:S(2)}) collective-permute-start(s32[2,2,12]{2,1,0:T(2,128)} %bitcast.8), channel_id=1, source_target_pairs={{8,0},{0,8},{9,1},{1,9},{10,2},{2,10},{11,3},{3,11},{12,4},{4,12},... | collective-permute-start | bytes 584 | tf_op jit(solution)/shard_map/ppermute | solution.py:33
  31.3 17.6 %collective-permute-start.4 = (bf16[2,8,48,384]{3,2,1,0:T(8,128)(2,1)S(1)}, bf16[2,8,48,384]{3,2,1,0:T(8,128)(2,1)S(1)}, u32[]{:S(2)}, u32[]{:S(2)}) collective-permute-start(bf16[2,8,48,384]{3,2,1,0:T(8,128)(2,1)S(1)} %pad_maximum_fusion.refs_0_), channel_id=1, source_target_pairs={{20,0},{11,8},{21,1},{10,9},{22,2},{9,10},{23,3},{8,11},{16,4},{15... | collective-permute-start | bytes 1769480 | tf_op jit(solution)/shard_map/ppermute | solution.py:44
  34.2 0.7 copy-start.5
  38.0 10.9 %collective-permute-start.5 = (bf16[2,8,48,384]{3,2,1,0:T(8,128)(2,1)S(1)}, bf16[2,8,48,384]{3,2,1,0:T(8,128)(2,1)S(1)}, u32[]{:S(2)}, u32[]{:S(2)}) collective-permute-start(bf16[2,8,48,384]{3,2,1,0:T(8,128)(2,1)S(1)} %pad_maximum_fusion.1.refs_1_), channel_id=1, source_target_pairs={{4,0},{9,8},{5,1},{8,9},{6,2},{11,10},{7,3},{10,11},{0,4},{13,12},... | collective-permute-start | bytes 1769480 | tf_op jit(solution)/shard_map/ppermute | solution.py:44
  39.6 16.2 %collective-permute-start.9 = (bf16[2,8,48,384]{3,2,1,0:T(8,128)(2,1)S(1)}, bf16[2,8,48,384]{3,2,1,0:T(8,128)(2,1)S(1)}, u32[]{:S(2)}, u32[]{:S(2)}) collective-permute-start(bf16[2,8,48,384]{3,2,1,0:T(8,128)(2,1)S(1)} %pad_maximum_fusion.1.refs_1_), channel_id=1, source_target_pairs={{20,0},{11,8},{21,1},{10,9},{22,2},{9,10},{23,3},{8,11},{16,4},{15... | collective-permute-start | bytes 1769480 | tf_op jit(solution)/shard_map/ppermute | solution.py:44
  41.7 14.1 %collective-permute-start.8 = (bf16[2,8,48,384]{3,2,1,0:T(8,128)(2,1)S(1)}, bf16[2,8,48,384]{3,2,1,0:T(8,128)(2,1)S(1)}, u32[]{:S(2)}, u32[]{:S(2)}) collective-permute-start(bf16[2,8,48,384]{3,2,1,0:T(8,128)(2,1)S(1)} %pad_maximum_fusion.refs_0_), channel_id=1, source_target_pairs={{4,0},{9,8},{5,1},{8,9},{6,2},{11,10},{7,3},{10,11},{0,4},{13,12},... | collective-permute-start | bytes 1769480 | tf_op jit(solution)/shard_map/ppermute | solution.py:44
  42.3 2.3 %copy-start = (bf16[2,384,3072]{2,1,0:T(8,128)(2,1)S(1)}, bf16[2,384,3072]{2,1,0:T(8,128)(2,1)}, u32[]{:S(2)}) copy-start(bf16[2,384,3072]{2,1,0:T(8,128)(2,1)} %refs_3_.3) | copy-start | bytes 14155780
  44.6 7.0 %copy-start.1 = (bf16[2,384,3072]{2,1,0:T(8,128)(2,1)S(1)}, bf16[2,384,3072]{2,1,0:T(8,128)(2,1)}, u32[]{:S(2)}) copy-start(bf16[2,384,3072]{2,1,0:T(8,128)(2,1)} %refs_3_.3) | copy-start | bytes 14155780
  49.0 11.7 %collective-permute-start.10 = (bf16[2,8,48,384]{3,2,1,0:T(8,128)(2,1)S(1)}, bf16[2,8,48,384]{3,2,1,0:T(8,128)(2,1)S(1)}, u32[]{:S(2)}, u32[]{:S(2)}) collective-permute-start(bf16[2,8,48,384]{3,2,1,0:T(8,128)(2,1)S(1)} %collective-permute-done.4.refs_1_), channel_id=1, source_target_pairs={{4,0},{9,8},{5,1},{8,9},{6,2},{11,10},{7,3},{10,11},{0,4},{13,12},... | collective-permute-start | bytes 1769480 | tf_op jit(solution)/shard_map/ppermute | solution.py:44
  50.5 11.1 %collective-permute-start.11 = (bf16[2,8,48,384]{3,2,1,0:T(8,128)(2,1)S(1)}, bf16[2,8,48,384]{3,2,1,0:T(8,128)(2,1)S(1)}, u32[]{:S(2)}, u32[]{:S(2)}) collective-permute-start(bf16[2,8,48,384]{3,2,1,0:T(8,128)(2,1)S(1)} %collective-permute-done.5.refs_2_), channel_id=1, source_target_pairs={{20,0},{11,8},{21,1},{10,9},{22,2},{9,10},{23,3},{8,11},{16,4},{15... | collective-permute-start | bytes 1769480 | tf_op jit(solution)/shard_map/ppermute | solution.py:44
  55.8 5.8 %copy-start.3 = (s32[12]{0:T(128)S(1)}, s32[12]{0:T(128)}, u32[]{:S(2)}) copy-start(s32[12]{0:T(128)} %sizes_ref.1) | copy-start | bytes 148
  55.8 5.8 %copy-start.4 = (s32[24]{0:T(128)S(1)}, s32[24]{0:T(128)}, u32[]{:S(2)}) copy-start(s32[24]{0:T(128)} %right_ref.3) | copy-start | bytes 292
  68.7 2.1 %collective-permute-start.12 = (bf16[16,48,384]{2,1,0:T(8,128)(2,1)S(1)}, bf16[16,48,384]{2,1,0:T(8,128)(2,1)S(1)}, u32[]{:S(2)}, u32[]{:S(2)}) collective-permute-start(bf16[16,48,384]{2,1,0:T(8,128)(2,1)S(1)} %get-tuple-element.38), channel_id=1, source_target_pairs={{8,0},{0,8},{9,1},{1,9},{10,2},{2,10},{11,3},{3,11},{12,4},{4,12},... | collective-permute-start | bytes 1769480 | tf_op jit(solution)/shard_map/ppermute | solution.py:33

commit v11 on v8

--- a/solution.py
+++ b/solution.py
@@ -365,8 +365,8 @@
     across = partner(along_z, "middle", 3)
     opposite = partner(across, "middle", 1)
     near, away = jnp.stack([along_z, beside]), jnp.stack([across, opposite])
-    near, away, rows_other = lax.optimization_barrier((near, away, rows_other))
     near_3 = partner(near, "last", 3)
+    near, away, rows_other, right, left = lax.optimization_barrier((near, away, rows_other, right, left))
     away_1 = partner(away, "last", 1)
     near_1 = partner(near, "last", 1)
     away_3 = partner(away, "last", 3)

time: 101 us -> 99.9 us (0.989)
  blocking collectives: 26.3 us -> 46.1 us
  waiting for transfers between devices: 28.4 us -> 13.5 us
  starting transfers between devices: 18.4 us -> 12.9 us
    all_to_all x1 -> x2, blocking collectives: 26.3 us -> 46.1 us  [exchange(): lax.all_to_all(copies, AXES, split_axis=0, concat_axis=0, axis_index_grou...]
    all_to_all x1 -> x0, waiting for transfers between devices: 13 us -> none  [exchange(): lax.all_to_all(copies, AXES, split_axis=0, concat_axis=0, axis_index_grou...]
    all_to_all x1 -> x0, starting transfers between devices: 8.48 us -> none  [exchange(): lax.all_to_all(copies, AXES, split_axis=0, concat_axis=0, axis_index_grou...]
    ppermute x9, starting transfers between devices: 9.76 us -> 12.3 us  [partner(): return lax.ppermute(value, AXES, perm)]
    ppermute x9, waiting for transfers between devices: 13.4 us -> 11.5 us  [partner(): return lax.ppermute(value, AXES, perm)]
    unnamed x12 -> x14, local copies, waits for them, and re-layouts: 2.36 us -> 2.36 us
  transfers between devices with their start and end apart: 14 -> 13, of which waited for: 4 -> 4; matrix products, arithmetic and copies ran while one was open for 0% -> 0% of each run, Pallas kernels for 17% -> 17%
where the time goes in v11:
time: 99.9 us; the launch traced here: 99.6 us
  blocking collectives  46.1 us (46%)
  Pallas kernels  23.6 us (24%)
  waiting for transfers between devices  13.5 us (14%)
  starting transfers between devices  12.9 us (13%)
  local copies, waits for them, and re-layouts  2.36 us (2%)
    all_to_all x2, blocking collectives, exchange(): lax.all_to_all(copies, AXES, split_axis=0, concat_axis=0, axis_index_grou...  46.1 us
    pallas_call x3, Pallas kernels, sums(): pl.pallas_call(functools.partial(sums_kernel, twos, first, ahead), out_sh...  12.5 us
    ppermute x9, starting transfers between devices, partner(): return lax.ppermute(value, AXES, perm)  12.3 us
    ppermute x9, waiting for transfers between devices, partner(): return lax.ppermute(value, AXES, perm)  11.5 us
    pallas_call x1, Pallas kernels, terms(): pl.pallas_call(terms_kernel, out_shape=(jax.ShapeDtypeStruct((NZ * NXH, g...  6.96 us
    pallas_call x1, Pallas kernels, plan(): pl.pallas_call(plan_kernel, out_shape=(jax.ShapeDtypeStruct((2 * pairs,),...  2.55 us
    unnamed x14, local copies, waits for them, and re-layouts  2.36 us
    ppermute x4, waiting for transfers between devices, core_swap(): lax.ppermute(value, AXES, [(flat(z, x, y, 1 - c), flat(z, x, y, c)) for z...  2 us
  transfers between devices with their start and end apart: 13, of which 4 were waited for; matrix products, arithmetic and copies ran while one was open for 0% of the time, Pallas kernels for 17%

profile of v11, /device:TPU:24, one launch (start us, length us, event | category | flops | bytes accessed | tf_op | source)
XLA Modules:
  0.0 99.6 jit_solution(2314572528172489370)
XLA Ops:
  0.0 0.0 copy-start.1
  0.0 0.0 copy-start.4
  0.0 0.0 collective-permute-start.4
  0.0 0.5 collective-permute-start.5
  0.5 0.0 slice-start
  0.5 1.6 %mask_psi.1 = bf16[8,48,384]{2,1,0:T(8,128)(2,1)} custom-call(s32[12]{0:T(128)} %sizes_ref.1, s32[24]{0:T(128)} %right_ref.3, bf16[48,384]{1,0:T(8,128)(2,1)} %psi_ref.1), custom_call_target="tpu_custom_call" | custom-call | tf_op jit(solution)/shard_map/mask_psi/pallas_call | solution.py:87
  2.1 21.3 %all_to_all.10 = bf16[8,48,384]{2,1,0:T(8,128)(2,1)S(1)} all-to-all(bf16[8,48,384]{2,1,0:T(8,128)(2,1)} %mask_psi.1), channel_id=1, replica_groups={{0,32,64,96,128,160,192,224},{8,40,72,104,136,168,200,232},{1,33,65,97,..., dimensions={0} | all-to-all | bytes 589824 | tf_op jit(solution)/shard_map/all_to_all | solution.py:48
  23.4 0.2 collective-permute-start.1
  23.7 1.0 collective-permute-start
  24.6 6.7 %collective-permute-done.1 = bf16[8,48,384]{2,1,0:T(8,128)(2,1)S(1)} collective-permute-done((bf16[8,48,384]{2,1,0:T(8,128)(2,1)S(1)}, bf16[8,48,384]{2,1,0:T(8,128)(2,1)S(1)}, u32[]{:S(2)}, u32[]{:S(2)}) %collective-permute-start.1) | collective-permute-done | bytes 294944 | tf_op jit(solution)/shard_map/ppermute | solution.py:44
  31.4 0.0 collective-permute-start.2
  31.4 0.0 collective-permute-start.3
  31.4 0.0 collective-permute-done
  31.4 0.1 pad_maximum_fusion.refs_0_
  31.5 2.8 %collective-permute-start.6 = (bf16[2,8,48,384]{3,2,1,0:T(8,128)(2,1)S(1)}, bf16[2,8,48,384]{3,2,1,0:T(8,128)(2,1)S(1)}, u32[]{:S(2)}, u32[]{:S(2)}) collective-permute-start(bf16[2,8,48,384]{3,2,1,0:T(8,128)(2,1)S(1)} %pad_maximum_fusion.refs_0_), channel_id=1, source_target_pairs={{20,0},{11,8},{21,1},{10,9},{22,2},{9,10},{23,3},{8,11},{16,4},{15... | collective-permute-start | bytes 1769480 | tf_op jit(solution)/shard_map/ppermute | solution.py:44
  34.3 3.8 %collective-permute-done.2 = bf16[8,48,384]{2,1,0:T(8,128)(2,1)S(1)} collective-permute-done((bf16[8,48,384]{2,1,0:T(8,128)(2,1)S(1)}, bf16[8,48,384]{2,1,0:T(8,128)(2,1)S(1)}, u32[]{:S(2)}, u32[]{:S(2)}) %collective-permute-start.2) | collective-permute-done | bytes 294944 | tf_op jit(solution)/shard_map/ppermute | solution.py:44
  38.1 0.1 pad_maximum_fusion.1.refs_1_
  38.2 0.0 collective-permute-done.3.other_ref
  38.2 0.0 collective-permute-done.5.refs_5_
  38.2 0.0 collective-permute-done.4.refs_3_.refs_4_
  38.2 2.9 %collective-permute-start.7 = (bf16[2,8,48,384]{3,2,1,0:T(8,128)(2,1)S(1)}, bf16[2,8,48,384]{3,2,1,0:T(8,128)(2,1)S(1)}, u32[]{:S(2)}, u32[]{:S(2)}) collective-permute-start(bf16[2,8,48,384]{3,2,1,0:T(8,128)(2,1)S(1)} %pad_maximum_fusion.1.refs_1_), channel_id=1, source_target_pairs={{4,0},{9,8},{5,1},{8,9},{6,2},{11,10},{7,3},{10,11},{0,4},{13,12},... | collective-permute-start | bytes 1769480 | tf_op jit(solution)/shard_map/ppermute | solution.py:44
  41.1 1.4 %collective-permute-start.9 = (bf16[2,8,48,384]{3,2,1,0:T(8,128)(2,1)S(1)}, bf16[2,8,48,384]{3,2,1,0:T(8,128)(2,1)S(1)}, u32[]{:S(2)}, u32[]{:S(2)}) collective-permute-start(bf16[2,8,48,384]{3,2,1,0:T(8,128)(2,1)S(1)} %pad_maximum_fusion.1.refs_1_), channel_id=1, source_target_pairs={{20,0},{11,8},{21,1},{10,9},{22,2},{9,10},{23,3},{8,11},{16,4},{15... | collective-permute-start | bytes 1769480 | tf_op jit(solution)/shard_map/ppermute | solution.py:44
  42.5 0.0 copy-done.4
  42.5 2.6 %plan.1 = (s32[108]{0:T(128)S(1)}, s32[54]{0:T(128)S(1)}) custom-call(s32[2,2,12]{2,1,0:T(2,128)S(1)} %bitcast.11, s32[2,2,12]{2,1,0:T(2,128)S(1)} %collective-permute-done.3.other_ref), custom_call_target="tpu_custom_call" | custom-call | tf_op jit(solution)/shard_map/plan/pallas_call | solution.py:138
  45.1 0.1 collective-permute-start.8
  45.2 0.0 copy-done.1
  45.2 0.0 copy-start
  45.2 2.3 %copy-done = bf16[2,384,3072]{2,1,0:T(8,128)(2,1)S(1)} copy-done((bf16[2,384,3072]{2,1,0:T(8,128)(2,1)S(1)}, bf16[2,384,3072]{2,1,0:T(8,128)(2,1)}, u32[]{:S(2)}) %copy-start) | copy-done | bytes 4718616
  47.5 0.0 slice-start.1
  47.5 4.2 %sums_first.1 = (f32[2,2,384,768]{3,2,1,0:T(8,128)S(1)}, bf16[97,128,128]{2,1,0:T(8,128)(2,1)S(1)}) custom-call(bf16[2,8,48,384]{3,2,1,0:T(8,128)(2,1)S(1)} %pad_maximum_fusion.refs_0_, bf16[2,8,48,384]{3,2,1,0:T(8,128)(2,1)S(1)} %pad_maximum_fusion.1.refs_1_, bf16[2,384,3072]{2,1,0:T(8,128)(2,1)S(1)} %copy-done, ...), custom_call_target="tpu_custom_call" | custom-call | flops 1811939328 | bytes 4718592 | tf_op jit(solution)/shard_map/sums_first/pallas_call | solution.py:244
  51.8 0.0 collective-permute-done.6.refs_1_
  51.8 0.0 collective-permute-done.7.refs_2_
  51.8 2.1 %collective-permute-start.10 = (bf16[2,8,48,384]{3,2,1,0:T(8,128)(2,1)S(1)}, bf16[2,8,48,384]{3,2,1,0:T(8,128)(2,1)S(1)}, u32[]{:S(2)}, u32[]{:S(2)}) collective-permute-start(bf16[2,8,48,384]{3,2,1,0:T(8,128)(2,1)S(1)} %collective-permute-done.6.refs_1_), channel_id=1, source_target_pairs={{4,0},{9,8},{5,1},{8,9},{6,2},{11,10},{7,3},{10,11},{0,4},{13,12},... | collective-permute-start | bytes 1769480 | tf_op jit(solution)/shard_map/ppermute | solution.py:44
  53.9 1.8 %collective-permute-start.11 = (bf16[2,8,48,384]{3,2,1,0:T(8,128)(2,1)S(1)}, bf16[2,8,48,384]{3,2,1,0:T(8,128)(2,1)S(1)}, u32[]{:S(2)}, u32[]{:S(2)}) collective-permute-start(bf16[2,8,48,384]{3,2,1,0:T(8,128)(2,1)S(1)} %collective-permute-done.7.refs_2_), channel_id=1, source_target_pairs={{20,0},{11,8},{21,1},{10,9},{22,2},{9,10},{23,3},{8,11},{16,4},{15... | collective-permute-start | bytes 1769480 | tf_op jit(solution)/shard_map/ppermute | solution.py:44
  55.7 0.0 slice-done
  55.7 0.0 slice-done.1
  55.7 4.1 %sums_middle.1.refs_0_ = f32[2,2,384,768]{3,2,1,0:T(8,128)S(1)} custom-call(f32[2,2,384,768]{3,2,1,0:T(8,128)S(1)} %get-tuple-element.39.refs_0_, bf16[2,8,48,384]{3,2,1,0:T(8,128)(2,1)S(1)} %collective-permute-done.6.refs_1_, bf16[2,8,48,384]{3,2,1,0:T(8,128)(2,1)S(1)} %collective-permute-done.7.refs_2_, ...), custom_call_target="tpu_custom_call", output_to_operand_aliasing={{}: (0, {})} | custom-call | flops 1811939328 | bytes 4718592 | tf_op jit(solution)/shard_map/sums_middle/pallas_call | solution.py:244
  59.8 0.0 copy-start.2
  59.8 0.0 copy-start.3
  59.8 0.0 collective-permute-done.8.refs_1_
  59.8 0.0 collective-permute-done.9.refs_2_
  59.8 4.2 %sums_last.1 = (f32[2,2,384,768]{3,2,1,0:T(8,128)S(1)}, bf16[2,2,2,384,768]{4,3,2,1,0:T(8,128)(2,1)S(1)}) custom-call(f32[2,2,384,768]{3,2,1,0:T(8,128)S(1)} %sums_middle.1.refs_0_, bf16[2,8,48,384]{3,2,1,0:T(8,128)(2,1)S(1)} %collective-permute-done.8.refs_1_, ...), custom_call_target="tpu_custom_call", output_to_operand_aliasing={{0}: (0, {})} | custom-call | flops 1811939328 | bytes 4718592 | tf_op jit(solution)/shard_map/sums_last/pallas_call | solution.py:244
  64.0 0.0 collective-permute-done.10.far_near
  64.0 0.9 collective-permute-done.11.far_away
  65.0 0.0 copy-done.2
  65.0 0.0 copy-done.3
  65.0 7.0 %terms.1 = (f32[16,48,384]{2,1,0:T(8,128)S(1)}, bf16[16,48,384]{2,1,0:T(8,128)(2,1)S(1)}) custom-call(s32[108]{0:T(128)S(1)} %get-tuple-element.30.slots_ref, s32[54]{0:T(128)S(1)} %get-tuple-element.31.rows_ref, s32[12]{0:T(128)S(1)} %copy-done.2, s32[24]{0:T(128)S(1)} %copy-done.3, f32[2,2,384,768]{3,2,1,0:T(8,128)S(1)} %get-tuple-element.42.acc, ...), custom_call_target="tpu_custom_call" | custom-call | tf_op jit(solution)/shard_map/terms/pallas_call | solution.py:338
  71.9 0.1 collective-permute-start.12
  72.0 2.0 %collective-permute-done.12 = bf16[16,48,384]{2,1,0:T(8,128)(2,1)S(1)} collective-permute-done((bf16[16,48,384]{2,1,0:T(8,128)(2,1)S(1)}, bf16[16,48,384]{2,1,0:T(8,128)(2,1)S(1)}, u32[]{:S(2)}, u32[]{:S(2)}) %collective-permute-start.12) | collective-permute-done | bytes 589856 | tf_op jit(solution)/shard_map/ppermute | solution.py:33
  74.0 0.1 add_convert_fusion
  74.1 24.8 %all_to_all.11 = bf16[16,48,384]{2,1,0:T(8,128)(2,1)S(1)} all-to-all(bf16[16,48,384]{2,1,0:T(8,128)(2,1)S(1)} %add_convert_fusion), channel_id=1, replica_groups={{0,16,32,48,64,80,96,112,128,144,160,176,192,208,224,240},{1,17,33,49,6..., dimensions={0} | all-to-all | bytes 1179648 | tf_op jit(solution)/shard_map/all_to_all | solution.py:48
  98.9 0.7 convert_reduce_fusion
  (1 shorter events, 0.0 us)
Async XLA Ops:
  0.0 45.2 %copy-start.1 = (bf16[2,12,2,128,128]{4,3,2,1,0:T(8,128)(2,1)S(1)}, bf16[2,12,2,128,128]{4,3,2,1,0:T(8,128)(2,1)}, u32[]{:S(2)}) copy-start(bf16[2,12,2,128,128]{4,3,2,1,0:T(8,128)(2,1)} %param.7) | copy-start | bytes 4718596
  0.0 42.5 %copy-start.4 = (s32[2,12,2]{1,2,0:T(2,128)S(1)}, s32[2,12,2]{1,2,0:T(2,128)}, u32[]{:S(2)}) copy-start(s32[2,12,2]{1,2,0:T(2,128)} %param.8) | copy-start | bytes 580
  0.0 38.2 %collective-permute-start.4 = (bf16[2,384,3072]{2,1,0:T(8,128)(2,1)}, bf16[2,384,3072]{2,1,0:T(8,128)(2,1)}, u32[]{:S(2)}, u32[]{:S(2)}) collective-permute-start(bf16[2,384,3072]{2,1,0:T(8,128)(2,1)} %refs_3_.1), channel_id=1, source_target_pairs={{8,0},{0,8},{9,1},{1,9},{10,2},{2,10},{11,3},{3,11},{12,4},{4,12},... | collective-permute-start | bytes 14155784 | tf_op jit(solution)/shard_map/ppermute | solution.py:33
  0.0 38.2 %collective-permute-start.5 = (bf16[48,128,128]{2,1,0:T(8,128)(2,1)}, bf16[48,128,128]{2,1,0:T(8,128)(2,1)}, u32[]{:S(2)}, u32[]{:S(2)}) collective-permute-start(bf16[48,128,128]{2,1,0:T(8,128)(2,1)} %bitcast.8), channel_id=1, source_target_pairs={{8,0},{0,8},{9,1},{1,9},{10,2},{2,10},{11,3},{3,11},{12,4},{4,12},... | collective-permute-start | bytes 4718600 | tf_op jit(solution)/shard_map/ppermute | solution.py:33
  0.5 55.2 %slice-start = ((s8[4718592]{0:T(1024)(128)(4,1)}), s8[524288]{0:T(1024)(128)(4,1)S(1)}, s32[]{:S(2)}) async-start(s8[4718592]{0:T(1024)(128)(4,1)} %bitcast.6), calls=%async_computation.2 | async-start | bytes 1048576
  23.4 7.9 %collective-permute-start.1 = (bf16[8,48,384]{2,1,0:T(8,128)(2,1)S(1)}, bf16[8,48,384]{2,1,0:T(8,128)(2,1)S(1)}, u32[]{:S(2)}, u32[]{:S(2)}) collective-permute-start(bf16[8,48,384]{2,1,0:T(8,128)(2,1)S(1)} %all_to_all.10), channel_id=1, source_target_pairs={{3,0},{28,8},{2,1},{29,9},{1,2},{30,10},{0,3},{31,11},{7,4},{24,12... | collective-permute-start | bytes 884744 | tf_op jit(solution)/shard_map/ppermute | solution.py:44
  23.7 7.7 %collective-permute-start = (bf16[8,48,384]{2,1,0:T(8,128)(2,1)S(1)}, bf16[8,48,384]{2,1,0:T(8,128)(2,1)S(1)}, u32[]{:S(2)}, u32[]{:S(2)}) collective-permute-start(bf16[8,48,384]{2,1,0:T(8,128)(2,1)S(1)} %all_to_all.10), channel_id=1, source_target_pairs={{1,0},{12,8},{0,1},{13,9},{3,2},{14,10},{2,3},{15,11},{5,4},{8,12}... | collective-permute-start | bytes 884744 | tf_op jit(solution)/shard_map/ppermute | solution.py:44
  31.4 6.7 %collective-permute-start.2 = (bf16[8,48,384]{2,1,0:T(8,128)(2,1)S(1)}, bf16[8,48,384]{2,1,0:T(8,128)(2,1)S(1)}, u32[]{:S(2)}, u32[]{:S(2)}) collective-permute-start(bf16[8,48,384]{2,1,0:T(8,128)(2,1)S(1)} %collective-permute-done.1), channel_id=1, source_target_pairs={{1,0},{12,8},{0,1},{13,9},{3,2},{14,10},{2,3},{15,11},{5,4},{8,12}... | collective-permute-start | bytes 884744 | tf_op jit(solution)/shard_map/ppermute | solution.py:44
  31.4 6.8 %collective-permute-start.3 = (s32[2,2,12]{2,1,0:T(2,128)}, s32[2,2,12]{2,1,0:T(2,128)S(1)}, u32[]{:S(2)}, u32[]{:S(2)}) collective-permute-start(s32[2,2,12]{2,1,0:T(2,128)} %bitcast.10), channel_id=1, source_target_pairs={{8,0},{0,8},{9,1},{1,9},{10,2},{2,10},{11,3},{3,11},{12,4},{4,12},... | collective-permute-start | bytes 584 | tf_op jit(solution)/shard_map/ppermute | solution.py:33
  31.5 20.3 %collective-permute-start.6 = (bf16[2,8,48,384]{3,2,1,0:T(8,128)(2,1)S(1)}, bf16[2,8,48,384]{3,2,1,0:T(8,128)(2,1)S(1)}, u32[]{:S(2)}, u32[]{:S(2)}) collective-permute-start(bf16[2,8,48,384]{3,2,1,0:T(8,128)(2,1)S(1)} %pad_maximum_fusion.refs_0_), channel_id=1, source_target_pairs={{20,0},{11,8},{21,1},{10,9},{22,2},{9,10},{23,3},{8,11},{16,4},{15... | collective-permute-start | bytes 1769480 | tf_op jit(solution)/shard_map/ppermute | solution.py:44
  38.2 13.6 %collective-permute-start.7 = (bf16[2,8,48,384]{3,2,1,0:T(8,128)(2,1)S(1)}, bf16[2,8,48,384]{3,2,1,0:T(8,128)(2,1)S(1)}, u32[]{:S(2)}, u32[]{:S(2)}) collective-permute-start(bf16[2,8,48,384]{3,2,1,0:T(8,128)(2,1)S(1)} %pad_maximum_fusion.1.refs_1_), channel_id=1, source_target_pairs={{4,0},{9,8},{5,1},{8,9},{6,2},{11,10},{7,3},{10,11},{0,4},{13,12},... | collective-permute-start | bytes 1769480 | tf_op jit(solution)/shard_map/ppermute | solution.py:44
  41.1 18.7 %collective-permute-start.9 = (bf16[2,8,48,384]{3,2,1,0:T(8,128)(2,1)S(1)}, bf16[2,8,48,384]{3,2,1,0:T(8,128)(2,1)S(1)}, u32[]{:S(2)}, u32[]{:S(2)}) collective-permute-start(bf16[2,8,48,384]{3,2,1,0:T(8,128)(2,1)S(1)} %pad_maximum_fusion.1.refs_1_), channel_id=1, source_target_pairs={{20,0},{11,8},{21,1},{10,9},{22,2},{9,10},{23,3},{8,11},{16,4},{15... | collective-permute-start | bytes 1769480 | tf_op jit(solution)/shard_map/ppermute | solution.py:44
  45.1 14.7 %collective-permute-start.8 = (bf16[2,8,48,384]{3,2,1,0:T(8,128)(2,1)S(1)}, bf16[2,8,48,384]{3,2,1,0:T(8,128)(2,1)S(1)}, u32[]{:S(2)}, u32[]{:S(2)}) collective-permute-start(bf16[2,8,48,384]{3,2,1,0:T(8,128)(2,1)S(1)} %pad_maximum_fusion.refs_0_), channel_id=1, source_target_pairs={{4,0},{9,8},{5,1},{8,9},{6,2},{11,10},{7,3},{10,11},{0,4},{13,12},... | collective-permute-start | bytes 1769480 | tf_op jit(solution)/shard_map/ppermute | solution.py:44
  45.2 2.3 %copy-start = (bf16[2,384,3072]{2,1,0:T(8,128)(2,1)S(1)}, bf16[2,384,3072]{2,1,0:T(8,128)(2,1)}, u32[]{:S(2)}) copy-start(bf16[2,384,3072]{2,1,0:T(8,128)(2,1)} %refs_3_.1) | copy-start | bytes 14155780
  47.5 8.1 %slice-start.1 = ((s8[4718592]{0:T(1024)(128)(4,1)}), s8[4194304]{0:T(1024)(128)(4,1)S(1)}, s32[]{:S(2)}) async-start(s8[4718592]{0:T(1024)(128)(4,1)} %bitcast.6), calls=%async_computation.3 | async-start | bytes 8388608
  51.8 12.2 %collective-permute-start.10 = (bf16[2,8,48,384]{3,2,1,0:T(8,128)(2,1)S(1)}, bf16[2,8,48,384]{3,2,1,0:T(8,128)(2,1)S(1)}, u32[]{:S(2)}, u32[]{:S(2)}) collective-permute-start(bf16[2,8,48,384]{3,2,1,0:T(8,128)(2,1)S(1)} %collective-permute-done.6.refs_1_), channel_id=1, source_target_pairs={{4,0},{9,8},{5,1},{8,9},{6,2},{11,10},{7,3},{10,11},{0,4},{13,12},... | collective-permute-start | bytes 1769480 | tf_op jit(solution)/shard_map/ppermute | solution.py:44
  53.9 11.1 %collective-permute-start.11 = (bf16[2,8,48,384]{3,2,1,0:T(8,128)(2,1)S(1)}, bf16[2,8,48,384]{3,2,1,0:T(8,128)(2,1)S(1)}, u32[]{:S(2)}, u32[]{:S(2)}) collective-permute-start(bf16[2,8,48,384]{3,2,1,0:T(8,128)(2,1)S(1)} %collective-permute-done.7.refs_2_), channel_id=1, source_target_pairs={{20,0},{11,8},{21,1},{10,9},{22,2},{9,10},{23,3},{8,11},{16,4},{15... | collective-permute-start | bytes 1769480 | tf_op jit(solution)/shard_map/ppermute | solution.py:44
  59.8 5.2 %copy-start.2 = (s32[12]{0:T(128)S(1)}, s32[12]{0:T(128)}, u32[]{:S(2)}) copy-start(s32[12]{0:T(128)} %sizes_ref.1) | copy-start | bytes 148
  59.8 5.2 %copy-start.3 = (s32[24]{0:T(128)S(1)}, s32[24]{0:T(128)}, u32[]{:S(2)}) copy-start(s32[24]{0:T(128)} %right_ref.3) | copy-start | bytes 292
  71.9 2.1 %collective-permute-start.12 = (bf16[16,48,384]{2,1,0:T(8,128)(2,1)S(1)}, bf16[16,48,384]{2,1,0:T(8,128)(2,1)S(1)}, u32[]{:S(2)}, u32[]{:S(2)}) collective-permute-start(bf16[16,48,384]{2,1,0:T(8,128)(2,1)S(1)} %get-tuple-element.46), channel_id=1, source_target_pairs={{8,0},{0,8},{9,1},{1,9},{10,2},{2,10},{11,3},{3,11},{12,4},{4,12},... | collective-permute-start | bytes 1769480 | tf_op jit(solution)/shard_map/ppermute | solution.py:33

commit v12 on v10

--- a/solution.py
+++ b/solution.py
@@ -262,7 +262,7 @@
     )(*near, *away)
 
 
-UNROLL = 6
+UNROLL = 18
 
 
 def terms_kernel(slots_ref, rows_ref, sizes_ref, right_ref, acc, far_near, far_away, far_ref, left_ref, *refs):

time: 96.6 us -> 95.7 us (level)
  no operation moved by 1% of the time
where the time goes in v12:
time: 95.7 us; the launch traced here: 95.4 us
  blocking collectives  24.6 us (26%)
  waiting for transfers between devices  23.8 us (25%)
  Pallas kernels  23.1 us (24%)
  starting transfers between devices  19.6 us (20%)
  local copies, waits for them, and re-layouts  3.04 us (3%)
  other arithmetic  1.01 us (1%)
    all_to_all x1, blocking collectives, exchange(): lax.all_to_all(copies, AXES, split_axis=0, concat_axis=0, axis_index_grou...  24.6 us
    all_to_all x1, waiting for transfers between devices, exchange(): lax.all_to_all(copies, AXES, split_axis=0, concat_axis=0, axis_index_grou...  13 us
    pallas_call x3, Pallas kernels, sums(): pl.pallas_call(functools.partial(sums_kernel, twos, first, ahead), out_sh...  12.7 us
    ppermute x9, starting transfers between devices, partner(): return lax.ppermute(value, AXES, perm)  11 us
    ppermute x9, waiting for transfers between devices, partner(): return lax.ppermute(value, AXES, perm)  8.75 us
    all_to_all x1, starting transfers between devices, exchange(): lax.all_to_all(copies, AXES, split_axis=0, concat_axis=0, axis_index_grou...  8.49 us
    pallas_call x1, Pallas kernels, terms(): pl.pallas_call(terms_kernel, out_shape=(jax.ShapeDtypeStruct((NZ * NXH, g...  6.16 us
    unnamed x12, local copies, waits for them, and re-layouts  3.04 us
  transfers between devices with their start and end apart: 14, of which 6 were waited for; matrix products, arithmetic and copies ran while one was open for 0% of the time, Pallas kernels for 18%

profile of v12, /device:TPU:24, one launch (start us, length us, event | category | flops | bytes accessed | tf_op | source)
XLA Modules:
  0.0 95.4 jit_solution(8280297680711834414)
XLA Ops:
  0.0 0.0 copy-start.2
  0.0 0.0 collective-permute-start.6
  0.0 1.7 %mask_psi.1 = bf16[8,48,384]{2,1,0:T(8,128)(2,1)} custom-call(s32[12]{0:T(128)} %sizes_ref.1, s32[24]{0:T(128)} %right_ref.3, bf16[48,384]{1,0:T(8,128)(2,1)} %psi_ref.1), custom_call_target="tpu_custom_call" | custom-call | tf_op jit(solution)/shard_map/mask_psi/pallas_call | solution.py:87
  1.7 8.5 %all-to-all-start = ((bf16[8,48,384]{2,1,0:T(8,128)(2,1)}), bf16[8,48,384]{2,1,0:T(8,128)(2,1)S(1)}, u32[]{:S(2)}, u32[]{:S(2)}) async-start(bf16[8,48,384]{2,1,0:T(8,128)(2,1)} %mask_psi.1), calls=%async_computation | async-start | bytes 589824 | tf_op jit(solution)/shard_map/all_to_all | solution.py:48
  10.2 0.1 collective-permute-start.7
  10.3 13.0 %all-to-all-done = bf16[8,48,384]{2,1,0:T(8,128)(2,1)S(1)} async-done(((bf16[8,48,384]{2,1,0:T(8,128)(2,1)}), bf16[8,48,384]{2,1,0:T(8,128)(2,1)S(1)}, u32[]{:S(2)}, u32[]{:S(2)}) %all-to-all-start) | async-done | bytes 294944 | tf_op jit(solution)/shard_map/all_to_all | solution.py:48
  23.3 0.2 collective-permute-start.2
  23.5 1.0 %collective-permute-start = (bf16[8,48,384]{2,1,0:T(8,128)(2,1)S(1)}, bf16[8,48,384]{2,1,0:T(8,128)(2,1)S(1)}, u32[]{:S(2)}, u32[]{:S(2)}) collective-permute-start(bf16[8,48,384]{2,1,0:T(8,128)(2,1)S(1)} %all-to-all-done), channel_id=1, source_target_pairs={{1,0},{12,8},{0,1},{13,9},{3,2},{14,10},{2,3},{15,11},{5,4},{8,12}... | collective-permute-start | bytes 884744 | tf_op jit(solution)/shard_map/ppermute | solution.py:44
  24.5 6.7 %collective-permute-done.2 = bf16[8,48,384]{2,1,0:T(8,128)(2,1)S(1)} collective-permute-done((bf16[8,48,384]{2,1,0:T(8,128)(2,1)S(1)}, bf16[8,48,384]{2,1,0:T(8,128)(2,1)S(1)}, u32[]{:S(2)}, u32[]{:S(2)}) %collective-permute-start.2) | collective-permute-done | bytes 294944 | tf_op jit(solution)/shard_map/ppermute | solution.py:44
  31.2 0.0 collective-permute-start.3
  31.2 0.0 collective-permute-start.1
  31.2 0.0 collective-permute-done
  31.2 0.1 pad_maximum_fusion.refs_0_
  31.3 2.8 %collective-permute-start.4 = (bf16[2,8,48,384]{3,2,1,0:T(8,128)(2,1)S(1)}, bf16[2,8,48,384]{3,2,1,0:T(8,128)(2,1)S(1)}, u32[]{:S(2)}, u32[]{:S(2)}) collective-permute-start(bf16[2,8,48,384]{3,2,1,0:T(8,128)(2,1)S(1)} %pad_maximum_fusion.refs_0_), channel_id=1, source_target_pairs={{20,0},{11,8},{21,1},{10,9},{22,2},{9,10},{23,3},{8,11},{16,4},{15... | collective-permute-start | bytes 1769480 | tf_op jit(solution)/shard_map/ppermute | solution.py:44
  34.2 0.0 collective-permute-done.1.other_ref
  34.2 0.0 copy-start.5
  34.2 0.7 copy-done.5
  34.8 2.5 %plan.1 = (s32[108]{0:T(128)S(1)}, s32[54]{0:T(128)S(1)}) custom-call(s32[2,2,12]{2,1,0:T(2,128)S(1)} %bitcast.9, s32[2,2,12]{2,1,0:T(2,128)S(1)} %collective-permute-done.1.other_ref), custom_call_target="tpu_custom_call" | custom-call | tf_op jit(solution)/shard_map/plan/pallas_call | solution.py:138
  37.4 0.5 collective-permute-done.3
  37.9 0.1 pad_maximum_fusion.1.refs_1_
  38.0 1.6 %collective-permute-start.5 = (bf16[2,8,48,384]{3,2,1,0:T(8,128)(2,1)S(1)}, bf16[2,8,48,384]{3,2,1,0:T(8,128)(2,1)S(1)}, u32[]{:S(2)}, u32[]{:S(2)}) collective-permute-start(bf16[2,8,48,384]{3,2,1,0:T(8,128)(2,1)S(1)} %pad_maximum_fusion.1.refs_1_), channel_id=1, source_target_pairs={{4,0},{9,8},{5,1},{8,9},{6,2},{11,10},{7,3},{10,11},{0,4},{13,12},... | collective-permute-start | bytes 1769480 | tf_op jit(solution)/shard_map/ppermute | solution.py:44
  39.6 2.1 %collective-permute-start.9 = (bf16[2,8,48,384]{3,2,1,0:T(8,128)(2,1)S(1)}, bf16[2,8,48,384]{3,2,1,0:T(8,128)(2,1)S(1)}, u32[]{:S(2)}, u32[]{:S(2)}) collective-permute-start(bf16[2,8,48,384]{3,2,1,0:T(8,128)(2,1)S(1)} %pad_maximum_fusion.1.refs_1_), channel_id=1, source_target_pairs={{20,0},{11,8},{21,1},{10,9},{22,2},{9,10},{23,3},{8,11},{16,4},{15... | collective-permute-start | bytes 1769480 | tf_op jit(solution)/shard_map/ppermute | solution.py:44
  41.7 0.0 collective-permute-done.7.refs_5_
  41.7 0.6 collective-permute-start.8
  42.3 0.0 collective-permute-done.6.refs_3_.refs_4_
  42.3 0.0 copy-done.2
  42.3 0.0 copy-start
  42.3 2.3 %copy-done = bf16[2,384,3072]{2,1,0:T(8,128)(2,1)S(1)} copy-done((bf16[2,384,3072]{2,1,0:T(8,128)(2,1)S(1)}, bf16[2,384,3072]{2,1,0:T(8,128)(2,1)}, u32[]{:S(2)}) %copy-start) | copy-done | bytes 4718616
  44.6 0.0 copy-start.1
  44.6 4.3 %sums_first.1 = (f32[2,2,384,768]{3,2,1,0:T(8,128)S(1)}, bf16[97,128,128]{2,1,0:T(8,128)(2,1)S(1)}) custom-call(bf16[2,8,48,384]{3,2,1,0:T(8,128)(2,1)S(1)} %pad_maximum_fusion.refs_0_, bf16[2,8,48,384]{3,2,1,0:T(8,128)(2,1)S(1)} %pad_maximum_fusion.1.refs_1_, bf16[2,384,3072]{2,1,0:T(8,128)(2,1)S(1)} %copy-done, ...), custom_call_target="tpu_custom_call" | custom-call | flops 1811939328 | bytes 4718592 | tf_op jit(solution)/shard_map/sums_first/pallas_call | solution.py:244
  48.9 0.0 collective-permute-done.4.refs_1_
  49.0 0.0 collective-permute-done.5.refs_2_
  49.0 1.5 %collective-permute-start.10 = (bf16[2,8,48,384]{3,2,1,0:T(8,128)(2,1)S(1)}, bf16[2,8,48,384]{3,2,1,0:T(8,128)(2,1)S(1)}, u32[]{:S(2)}, u32[]{:S(2)}) collective-permute-start(bf16[2,8,48,384]{3,2,1,0:T(8,128)(2,1)S(1)} %collective-permute-done.4.refs_1_), channel_id=1, source_target_pairs={{4,0},{9,8},{5,1},{8,9},{6,2},{11,10},{7,3},{10,11},{0,4},{13,12},... | collective-permute-start | bytes 1769480 | tf_op jit(solution)/shard_map/ppermute | solution.py:44
  50.5 1.1 %collective-permute-start.11 = (bf16[2,8,48,384]{3,2,1,0:T(8,128)(2,1)S(1)}, bf16[2,8,48,384]{3,2,1,0:T(8,128)(2,1)S(1)}, u32[]{:S(2)}, u32[]{:S(2)}) collective-permute-start(bf16[2,8,48,384]{3,2,1,0:T(8,128)(2,1)S(1)} %collective-permute-done.5.refs_2_), channel_id=1, source_target_pairs={{20,0},{11,8},{21,1},{10,9},{22,2},{9,10},{23,3},{8,11},{16,4},{15... | collective-permute-start | bytes 1769480 | tf_op jit(solution)/shard_map/ppermute | solution.py:44
  51.6 0.0 copy-done.1
  51.6 4.2 %sums_middle.1.refs_0_ = f32[2,2,384,768]{3,2,1,0:T(8,128)S(1)} custom-call(f32[2,2,384,768]{3,2,1,0:T(8,128)S(1)} %get-tuple-element.31.refs_0_, bf16[2,8,48,384]{3,2,1,0:T(8,128)(2,1)S(1)} %collective-permute-done.4.refs_1_, bf16[2,8,48,384]{3,2,1,0:T(8,128)(2,1)S(1)} %collective-permute-done.5.refs_2_, ...), custom_call_target="tpu_custom_call", output_to_operand_aliasing={{}: (0, {})} | custom-call | flops 1811939328 | bytes 4718592 | tf_op jit(solution)/shard_map/sums_middle/pallas_call | solution.py:244
  55.8 0.0 copy-start.3
  55.8 0.0 copy-start.4
  55.8 0.0 collective-permute-done.8.refs_1_
  55.8 0.0 collective-permute-done.9.refs_2_
  55.8 4.3 %sums_last.1 = (f32[2,2,384,768]{3,2,1,0:T(8,128)S(1)}, bf16[2,2,2,384,768]{4,3,2,1,0:T(8,128)(2,1)S(1)}) custom-call(f32[2,2,384,768]{3,2,1,0:T(8,128)S(1)} %sums_middle.1.refs_0_, bf16[2,8,48,384]{3,2,1,0:T(8,128)(2,1)S(1)} %collective-permute-done.8.refs_1_, ...), custom_call_target="tpu_custom_call", output_to_operand_aliasing={{0}: (0, {})} | custom-call | flops 1811939328 | bytes 4718592 | tf_op jit(solution)/shard_map/sums_last/pallas_call | solution.py:244
  60.1 0.5 collective-permute-done.10.far_near
  60.6 1.0 collective-permute-done.11.far_away
  61.6 0.0 copy-done.3
  61.6 0.0 copy-done.4
  61.6 6.2 %terms.1 = (f32[16,48,384]{2,1,0:T(8,128)S(1)}, bf16[16,48,384]{2,1,0:T(8,128)(2,1)S(1)}) custom-call(s32[108]{0:T(128)S(1)} %get-tuple-element.26.slots_ref, s32[54]{0:T(128)S(1)} %get-tuple-element.27.rows_ref, s32[12]{0:T(128)S(1)} %copy-done.3, s32[24]{0:T(128)S(1)} %copy-done.4, f32[2,2,384,768]{3,2,1,0:T(8,128)S(1)} %get-tuple-element.34.acc, ...), custom_call_target="tpu_custom_call" | custom-call | tf_op jit(solution)/shard_map/terms/pallas_call | solution.py:338
  67.8 0.1 collective-permute-start.12
  67.9 2.0 %collective-permute-done.12 = bf16[16,48,384]{2,1,0:T(8,128)(2,1)S(1)} collective-permute-done((bf16[16,48,384]{2,1,0:T(8,128)(2,1)S(1)}, bf16[16,48,384]{2,1,0:T(8,128)(2,1)S(1)}, u32[]{:S(2)}, u32[]{:S(2)}) %collective-permute-start.12) | collective-permute-done | bytes 589856 | tf_op jit(solution)/shard_map/ppermute | solution.py:33
  69.8 0.2 add_convert_fusion
  70.0 24.6 %all_to_all.10 = bf16[16,48,384]{2,1,0:T(8,128)(2,1)S(1)} all-to-all(bf16[16,48,384]{2,1,0:T(8,128)(2,1)S(1)} %add_convert_fusion), channel_id=1, replica_groups={{0,16,32,48,64,80,96,112,128,144,160,176,192,208,224,240},{1,17,33,49,6..., dimensions={0} | all-to-all | bytes 1179648 | tf_op jit(solution)/shard_map/all_to_all | solution.py:48
  94.6 0.7 convert_reduce_fusion
Async XLA Ops:
  0.0 42.3 %copy-start.2 = (bf16[2,12,2,128,128]{4,3,2,1,0:T(8,128)(2,1)S(1)}, bf16[2,12,2,128,128]{4,3,2,1,0:T(8,128)(2,1)}, u32[]{:S(2)}) copy-start(bf16[2,12,2,128,128]{4,3,2,1,0:T(8,128)(2,1)} %param.7) | copy-start | bytes 4718596
  0.0 42.3 %collective-permute-start.6 = (bf16[2,384,3072]{2,1,0:T(8,128)(2,1)}, bf16[2,384,3072]{2,1,0:T(8,128)(2,1)}, u32[]{:S(2)}, u32[]{:S(2)}) collective-permute-start(bf16[2,384,3072]{2,1,0:T(8,128)(2,1)} %refs_3_.3), channel_id=1, source_target_pairs={{8,0},{0,8},{9,1},{1,9},{10,2},{2,10},{11,3},{3,11},{12,4},{4,12},... | collective-permute-start | bytes 14155784 | tf_op jit(solution)/shard_map/ppermute | solution.py:33
  1.7 21.6 %all-to-all-start = ((bf16[8,48,384]{2,1,0:T(8,128)(2,1)}), bf16[8,48,384]{2,1,0:T(8,128)(2,1)S(1)}, u32[]{:S(2)}, u32[]{:S(2)}) async-start(bf16[8,48,384]{2,1,0:T(8,128)(2,1)} %mask_psi.1), calls=%async_computation | async-start | bytes 589824 | tf_op jit(solution)/shard_map/all_to_all | solution.py:48
  10.2 31.5 %collective-permute-start.7 = (bf16[48,128,128]{2,1,0:T(8,128)(2,1)}, bf16[48,128,128]{2,1,0:T(8,128)(2,1)S(1)}, u32[]{:S(2)}, u32[]{:S(2)}) collective-permute-start(bf16[48,128,128]{2,1,0:T(8,128)(2,1)} %bitcast.6), channel_id=1, source_target_pairs={{8,0},{0,8},{9,1},{1,9},{10,2},{2,10},{11,3},{3,11},{12,4},{4,12},... | collective-permute-start | bytes 4718600 | tf_op jit(solution)/shard_map/ppermute | solution.py:33
  23.3 7.9 %collective-permute-start.2 = (bf16[8,48,384]{2,1,0:T(8,128)(2,1)S(1)}, bf16[8,48,384]{2,1,0:T(8,128)(2,1)S(1)}, u32[]{:S(2)}, u32[]{:S(2)}) collective-permute-start(bf16[8,48,384]{2,1,0:T(8,128)(2,1)S(1)} %all-to-all-done), channel_id=1, source_target_pairs={{3,0},{28,8},{2,1},{29,9},{1,2},{30,10},{0,3},{31,11},{7,4},{24,12... | collective-permute-start | bytes 884744 | tf_op jit(solution)/shard_map/ppermute | solution.py:44
  23.5 7.7 %collective-permute-start = (bf16[8,48,384]{2,1,0:T(8,128)(2,1)S(1)}, bf16[8,48,384]{2,1,0:T(8,128)(2,1)S(1)}, u32[]{:S(2)}, u32[]{:S(2)}) collective-permute-start(bf16[8,48,384]{2,1,0:T(8,128)(2,1)S(1)} %all-to-all-done), channel_id=1, source_target_pairs={{1,0},{12,8},{0,1},{13,9},{3,2},{14,10},{2,3},{15,11},{5,4},{8,12}... | collective-permute-start | bytes 884744 | tf_op jit(solution)/shard_map/ppermute | solution.py:44
  31.2 6.7 %collective-permute-start.3 = (bf16[8,48,384]{2,1,0:T(8,128)(2,1)S(1)}, bf16[8,48,384]{2,1,0:T(8,128)(2,1)S(1)}, u32[]{:S(2)}, u32[]{:S(2)}) collective-permute-start(bf16[8,48,384]{2,1,0:T(8,128)(2,1)S(1)} %collective-permute-done.2), channel_id=1, source_target_pairs={{1,0},{12,8},{0,1},{13,9},{3,2},{14,10},{2,3},{15,11},{5,4},{8,12}... | collective-permute-start | bytes 884744 | tf_op jit(solution)/shard_map/ppermute | solution.py:44
  31.2 2.9 %collective-permute-start.1 = (s32[2,2,12]{2,1,0:T(2,128)}, s32[2,2,12]{2,1,0:T(2,128)S(1)}, u32[]{:S(2)}, u32[]{:S(2)}) collective-permute-start(s32[2,2,12]{2,1,0:T(2,128)} %bitcast.8), channel_id=1, source_target_pairs={{8,0},{0,8},{9,1},{1,9},{10,2},{2,10},{11,3},{3,11},{12,4},{4,12},... | collective-permute-start | bytes 584 | tf_op jit(solution)/shard_map/ppermute | solution.py:33
  31.3 17.6 %collective-permute-start.4 = (bf16[2,8,48,384]{3,2,1,0:T(8,128)(2,1)S(1)}, bf16[2,8,48,384]{3,2,1,0:T(8,128)(2,1)S(1)}, u32[]{:S(2)}, u32[]{:S(2)}) collective-permute-start(bf16[2,8,48,384]{3,2,1,0:T(8,128)(2,1)S(1)} %pad_maximum_fusion.refs_0_), channel_id=1, source_target_pairs={{20,0},{11,8},{21,1},{10,9},{22,2},{9,10},{23,3},{8,11},{16,4},{15... | collective-permute-start | bytes 1769480 | tf_op jit(solution)/shard_map/ppermute | solution.py:44
  34.2 0.7 copy-start.5
  38.0 10.9 %collective-permute-start.5 = (bf16[2,8,48,384]{3,2,1,0:T(8,128)(2,1)S(1)}, bf16[2,8,48,384]{3,2,1,0:T(8,128)(2,1)S(1)}, u32[]{:S(2)}, u32[]{:S(2)}) collective-permute-start(bf16[2,8,48,384]{3,2,1,0:T(8,128)(2,1)S(1)} %pad_maximum_fusion.1.refs_1_), channel_id=1, source_target_pairs={{4,0},{9,8},{5,1},{8,9},{6,2},{11,10},{7,3},{10,11},{0,4},{13,12},... | collective-permute-start | bytes 1769480 | tf_op jit(solution)/shard_map/ppermute | solution.py:44
  39.6 16.2 %collective-permute-start.9 = (bf16[2,8,48,384]{3,2,1,0:T(8,128)(2,1)S(1)}, bf16[2,8,48,384]{3,2,1,0:T(8,128)(2,1)S(1)}, u32[]{:S(2)}, u32[]{:S(2)}) collective-permute-start(bf16[2,8,48,384]{3,2,1,0:T(8,128)(2,1)S(1)} %pad_maximum_fusion.1.refs_1_), channel_id=1, source_target_pairs={{20,0},{11,8},{21,1},{10,9},{22,2},{9,10},{23,3},{8,11},{16,4},{15... | collective-permute-start | bytes 1769480 | tf_op jit(solution)/shard_map/ppermute | solution.py:44
  41.7 14.1 %collective-permute-start.8 = (bf16[2,8,48,384]{3,2,1,0:T(8,128)(2,1)S(1)}, bf16[2,8,48,384]{3,2,1,0:T(8,128)(2,1)S(1)}, u32[]{:S(2)}, u32[]{:S(2)}) collective-permute-start(bf16[2,8,48,384]{3,2,1,0:T(8,128)(2,1)S(1)} %pad_maximum_fusion.refs_0_), channel_id=1, source_target_pairs={{4,0},{9,8},{5,1},{8,9},{6,2},{11,10},{7,3},{10,11},{0,4},{13,12},... | collective-permute-start | bytes 1769480 | tf_op jit(solution)/shard_map/ppermute | solution.py:44
  42.3 2.3 %copy-start = (bf16[2,384,3072]{2,1,0:T(8,128)(2,1)S(1)}, bf16[2,384,3072]{2,1,0:T(8,128)(2,1)}, u32[]{:S(2)}) copy-start(bf16[2,384,3072]{2,1,0:T(8,128)(2,1)} %refs_3_.3) | copy-start | bytes 14155780
  44.6 7.0 %copy-start.1 = (bf16[2,384,3072]{2,1,0:T(8,128)(2,1)S(1)}, bf16[2,384,3072]{2,1,0:T(8,128)(2,1)}, u32[]{:S(2)}) copy-start(bf16[2,384,3072]{2,1,0:T(8,128)(2,1)} %refs_3_.3) | copy-start | bytes 14155780
  49.0 11.7 %collective-permute-start.10 = (bf16[2,8,48,384]{3,2,1,0:T(8,128)(2,1)S(1)}, bf16[2,8,48,384]{3,2,1,0:T(8,128)(2,1)S(1)}, u32[]{:S(2)}, u32[]{:S(2)}) collective-permute-start(bf16[2,8,48,384]{3,2,1,0:T(8,128)(2,1)S(1)} %collective-permute-done.4.refs_1_), channel_id=1, source_target_pairs={{4,0},{9,8},{5,1},{8,9},{6,2},{11,10},{7,3},{10,11},{0,4},{13,12},... | collective-permute-start | bytes 1769480 | tf_op jit(solution)/shard_map/ppermute | solution.py:44
  50.5 11.1 %collective-permute-start.11 = (bf16[2,8,48,384]{3,2,1,0:T(8,128)(2,1)S(1)}, bf16[2,8,48,384]{3,2,1,0:T(8,128)(2,1)S(1)}, u32[]{:S(2)}, u32[]{:S(2)}) collective-permute-start(bf16[2,8,48,384]{3,2,1,0:T(8,128)(2,1)S(1)} %collective-permute-done.5.refs_2_), channel_id=1, source_target_pairs={{20,0},{11,8},{21,1},{10,9},{22,2},{9,10},{23,3},{8,11},{16,4},{15... | collective-permute-start | bytes 1769480 | tf_op jit(solution)/shard_map/ppermute | solution.py:44
  55.8 5.8 %copy-start.3 = (s32[12]{0:T(128)S(1)}, s32[12]{0:T(128)}, u32[]{:S(2)}) copy-start(s32[12]{0:T(128)} %sizes_ref.1) | copy-start | bytes 148
  55.8 5.8 %copy-start.4 = (s32[24]{0:T(128)S(1)}, s32[24]{0:T(128)}, u32[]{:S(2)}) copy-start(s32[24]{0:T(128)} %right_ref.3) | copy-start | bytes 292
  67.8 2.1 %collective-permute-start.12 = (bf16[16,48,384]{2,1,0:T(8,128)(2,1)S(1)}, bf16[16,48,384]{2,1,0:T(8,128)(2,1)S(1)}, u32[]{:S(2)}, u32[]{:S(2)}) collective-permute-start(bf16[16,48,384]{2,1,0:T(8,128)(2,1)S(1)} %get-tuple-element.38), channel_id=1, source_target_pairs={{8,0},{0,8},{9,1},{1,9},{10,2},{2,10},{11,3},{3,11},{12,4},{4,12},... | collective-permute-start | bytes 1769480 | tf_op jit(solution)/shard_map/ppermute | solution.py:33
